TPU v7x, 32 devices: a whole 2x2x4 slice. The times are simulated.
32 devices in a mesh: dp: 8 (over y, x, core), tensor: 4 (over z).
Axes of the slice: x: 2, y: 2, z: 4, core: 2. Of those that a mesh axis runs over, the one named last changes fastest.
Arguments:
- layer_input: bfloat16 [32768, 1024], P(('dp', 'tensor')), may hold values from -15 to 15
- grad_output: bfloat16 [32768, 1024], P(('dp', 'tensor')), may hold values from -6 to 6
- doc_lengths: int32 [64, 4], P('dp'), may hold values from 1 to 256, 512 in all within a row
- ranges: float32 [4], replicated, may hold values from 0.5 to 6
- w_qkv: bfloat16 [3, 1024, 1024], P(None, None, 'tensor'), may hold values from -0.1875 to 0.1875
- bias_qv: bfloat16 [2, 1024], P(None, 'tensor'), may hold values from -3 to 3
- w_out: bfloat16 [1024, 1024], P('tensor'), may hold values from -0.75 to 0.75
- b_out: bfloat16 [1024], replicated, may hold values from -3 to 3
- gain_one: bfloat16 [1024], replicated, may hold values from 0.5 to 1.5
- shift_one: bfloat16 [1024], replicated, may hold values from -3 to 3
- w_in: bfloat16 [1024, 4096], P(None, 'tensor'), may hold values from -0.1875 to 0.1875
- b_in: bfloat16 [4096], P('tensor'), may hold values from -3 to 3
- w_down: bfloat16 [4096, 1024], P('tensor'), may hold values from -0.1875 to 0.1875
- b_down: bfloat16 [1024], replicated, may hold values from -3 to 3
- gain_two: bfloat16 [1024], replicated, may hold values from 0.5 to 1.5
- shift_two: bfloat16 [1024], replicated, may hold values from -3 to 3
Outputs:
- output: bfloat16 [32768, 1024], P(('dp', 'tensor'))
- grad_x: bfloat16 [32768, 1024], P(('dp', 'tensor'))
- grad_w_qkv: float32 [3, 1024, 1024], P(None, None, 'tensor')
- grad_bias_qv: float32 [2, 1024], P(None, 'tensor')
- grad_w_out: float32 [1024, 1024], P('tensor')
- grad_b_out: float32 [1024], replicated
- grad_gain_one: float32 [1024], replicated
- grad_shift_one: float32 [1024], replicated
- grad_w_in: float32 [1024, 4096], P(None, 'tensor')
- grad_b_in: float32 [4096], P('tensor')
- grad_w_down: float32 [4096, 1024], P('tensor')
- grad_b_down: float32 [1024], replicated
- grad_gain_two: float32 [1024], replicated
- grad_shift_two: float32 [1024], replicated
- new_ranges: float32 [4], replicated
Inputs may be any that keep to these rules, and one draw needn't show every extreme that they name: `doc_lengths`: each packed row holds 4 documents whose lengths sum to 512.
All inputs are finite; a program needn't handle non-finite values. Where the computation divides by a largest or mean magnitude, that divisor is 1e-20 or more.
Results may differ from a plain program's by a relative error of at most 0.013.
The roundings to bfloat16 on the way count: a program that leaves them out, or rounds other values in their place, can miss the bound.
Values may be sent and summed in bfloat16 or wider, within the bound.
A program may use at most 320 MiB of HBM per device.

v0:
```python
from functools import partial

import jax
import jax.numpy as jnp
from jax import lax
from jax.sharding import PartitionSpec as P

HD = 64
SEQ = 512


EPS = 1e-06
DECAY = 0.9
MASKED = -1e30


def soft_clip(values, clip_level):
    return clip_level * jnp.tanh(values / clip_level)


def clip_slope(values, clip_level):
    tangent = jnp.tanh(values / clip_level)
    return 1.0 - tangent * tangent


def product(first_operand, second_operand):
    return jnp.dot(first_operand, second_operand, preferred_element_type=jnp.float32)


def contract_rows(first_operand, second_operand):
    return lax.dot_general(
        first_operand, second_operand, (((0,), (0,)), ((), ())), preferred_element_type=jnp.float32
    )


def contract_cols(first_operand, second_operand):
    return lax.dot_general(
        first_operand, second_operand, (((1,), (1,)), ((), ())), preferred_element_type=jnp.float32
    )


def norm_forward(summed, norm_gain, norm_shift):
    center = summed - jnp.mean(summed, axis=-1, keepdims=True)
    inverse = lax.rsqrt(jnp.mean(center * center, axis=-1, keepdims=True) + EPS)
    normal = center * inverse
    return (normal * norm_gain + norm_shift, normal, inverse)


def norm_backward(upstream, normal, inverse, norm_gain):
    grad_gain = jnp.sum(upstream * normal, axis=0)
    grad_shift = jnp.sum(upstream, axis=0)
    scaled = upstream * norm_gain
    centered_grad = (
        scaled
        - jnp.mean(scaled, axis=-1, keepdims=True)
        - normal * jnp.mean(scaled * normal, axis=-1, keepdims=True)
    )
    return (inverse * centered_grad, grad_gain, grad_shift)


def doc_segments(doc_lengths, length):
    doc_ends = jnp.cumsum(doc_lengths, axis=1, dtype=jnp.int32)
    places = jnp.arange(length, dtype=jnp.int32)
    return jnp.sum(
        (places[None, :, None] >= doc_ends[:, None, :]).astype(jnp.int32), axis=2, dtype=jnp.int32
    )


def sequence_scores(queries, key_rows, segments, factor):
    raw_scores = jnp.einsum("qhd,khd->hqk", queries, key_rows, preferred_element_type=jnp.float32)
    same_doc = segments[:, None] == segments[None, :]
    return jnp.where(same_doc[None], raw_scores * factor, MASKED)


def attend_forward(queries, key_rows, value_rows, segments, factor):
    scores = sequence_scores(queries, key_rows, segments, factor)
    row_max = jnp.max(scores, axis=-1, keepdims=True)
    exponent = jnp.exp(scores - row_max)
    totals = jnp.sum(exponent, axis=-1, keepdims=True)
    probs_low = (exponent / totals).astype(jnp.bfloat16)
    context = jnp.einsum("hqk,khd->qhd", probs_low, value_rows, preferred_element_type=jnp.float32)
    return (context, (row_max + jnp.log(totals))[..., 0])


def attend_backward(queries, key_rows, value_rows, segments, logsum, grad_context, factor):
    scores = sequence_scores(queries, key_rows, segments, factor)
    attn_probs = jnp.exp(scores - logsum[..., None])
    probs_low = attn_probs.astype(jnp.bfloat16)
    grad_values = jnp.einsum(
        "hqk,qhd->khd", probs_low, grad_context, preferred_element_type=jnp.float32
    )
    grad_probs = jnp.einsum(
        "qhd,khd->hqk", grad_context, value_rows, preferred_element_type=jnp.float32
    )
    mean_grad = jnp.sum(attn_probs * grad_probs, axis=-1, keepdims=True)
    grad_scores = (factor * attn_probs * (grad_probs - mean_grad)).astype(jnp.bfloat16)
    grad_queries = jnp.einsum(
        "hqk,khd->qhd", grad_scores, key_rows, preferred_element_type=jnp.float32
    )
    grad_keys = jnp.einsum("hqk,qhd->khd", grad_scores, queries, preferred_element_type=jnp.float32)
    return (
        grad_queries.astype(jnp.bfloat16),
        grad_keys.astype(jnp.bfloat16),
        grad_values.astype(jnp.bfloat16),
    )


def local(
    layer_input,
    grad_output,
    doc_lengths,
    ranges,
    w_qkv,
    bias_qv,
    w_out,
    b_out,
    gain_one,
    shift_one,
    w_in,
    b_in,
    w_down,
    b_down,
    gain_two,
    shift_two,
):
    qkv_float = w_qkv.astype(jnp.float32)
    out_float = w_out.astype(jnp.float32)
    in_float = w_in.astype(jnp.float32)
    down_float = w_down.astype(jnp.float32)
    inputs = layer_input.astype(jnp.float32)
    local_peaks = jnp.concatenate(
        [
            jnp.max(jnp.abs(qkv_float), axis=(1, 2)),
            jnp.stack(
                [
                    jnp.max(jnp.abs(out_float)),
                    jnp.max(jnp.abs(in_float)),
                    jnp.max(jnp.abs(down_float)),
                    jnp.max(jnp.abs(inputs)),
                ]
            ),
        ]
    )
    all_peaks = lax.pmax(local_peaks, ("dp", "tensor"))
    weight_levels = 0.5 * all_peaks[:6]
    qkv_levels = weight_levels[:3][:, None, None]
    level_input = DECAY * ranges[0] + (1.0 - DECAY) * all_peaks[6]
    quant_qkv = soft_clip(qkv_float, qkv_levels).astype(jnp.bfloat16)
    quant_out = soft_clip(out_float, weight_levels[3]).astype(jnp.bfloat16)
    quant_in = soft_clip(in_float, weight_levels[4]).astype(jnp.bfloat16)
    quant_down = soft_clip(down_float, weight_levels[5]).astype(jnp.bfloat16)
    quant_input = soft_clip(inputs, level_input).astype(jnp.bfloat16)
    qkv_weights, bias_pair, out_weights, in_weights, bias_hidden, down_weights = (
        quant_qkv,
        bias_qv,
        quant_out,
        quant_in,
        b_in,
        quant_down,
    )
    attend_rows = lax.all_gather(quant_input, "tensor", axis=0, tiled=True)
    bias_float = bias_pair.astype(jnp.float32)
    queries = (product(attend_rows, qkv_weights[0]) + bias_float[0]).astype(jnp.bfloat16)
    key_rows = product(attend_rows, qkv_weights[1]).astype(jnp.bfloat16)
    value_rows = (product(attend_rows, qkv_weights[2]) + bias_float[1]).astype(jnp.bfloat16)
    heads_here = queries.shape[1] // HD
    blocked = (-1, SEQ, heads_here, HD)
    segments = doc_segments(doc_lengths, SEQ)
    factor = HD ** (-0.5)

    def forward_one(block_items):
        return attend_forward(
            block_items[0], block_items[1], block_items[2], block_items[3], factor
        )

    context, logsum = lax.map(
        forward_one,
        (
            queries.reshape(blocked),
            key_rows.reshape(blocked),
            value_rows.reshape(blocked),
            segments,
        ),
    )
    context = context.reshape(queries.shape)
    level_context = DECAY * ranges[1] + (1.0 - DECAY) * lax.pmax(
        jnp.max(jnp.abs(context)), ("dp", "tensor")
    )
    quant_context = soft_clip(context, level_context).astype(jnp.bfloat16)
    partial_attn = product(quant_context, out_weights)
    attention_out = lax.psum_scatter(partial_attn, "tensor", scatter_dimension=0, tiled=True)
    gain_first = gain_one.astype(jnp.float32)
    gain_second = gain_two.astype(jnp.float32)
    normed, normal_one, inverse_one = norm_forward(
        inputs + attention_out + b_out.astype(jnp.float32),
        gain_first,
        shift_one.astype(jnp.float32),
    )
    level_normed = DECAY * ranges[2] + (1.0 - DECAY) * lax.pmax(
        jnp.max(jnp.abs(normed)), ("dp", "tensor")
    )
    quant_normed = soft_clip(normed, level_normed).astype(jnp.bfloat16)
    ffn_rows = lax.all_gather(quant_normed, "tensor", axis=0, tiled=True)
    hidden = product(ffn_rows, in_weights) + bias_hidden.astype(jnp.float32)
    active = jax.nn.gelu(hidden, approximate=False)
    level_active = DECAY * ranges[3] + (1.0 - DECAY) * lax.pmax(
        jnp.max(jnp.abs(active)), ("dp", "tensor")
    )
    quant_active = soft_clip(active, level_active).astype(jnp.bfloat16)
    partial_ffn = product(quant_active, down_weights)
    branch = lax.psum_scatter(partial_ffn, "tensor", scatter_dimension=0, tiled=True)
    result, normal_two, inverse_two = norm_forward(
        normed + branch + b_down.astype(jnp.float32), gain_second, shift_two.astype(jnp.float32)
    )
    output = result.astype(jnp.bfloat16)
    grad_sum_two, grad_gain_two, grad_shift_two = norm_backward(
        grad_output.astype(jnp.float32), normal_two, inverse_two, gain_second
    )
    grad_b_down = jnp.sum(grad_sum_two, axis=0)
    grad_branch = grad_sum_two.astype(jnp.bfloat16)
    branch_rows = lax.all_gather(grad_branch, "tensor", axis=0, tiled=True)
    quant_down_grad = contract_rows(quant_active, branch_rows)
    grad_active = contract_cols(branch_rows, down_weights) * clip_slope(active, level_active)
    _, gelu_pull = jax.vjp(partial(jax.nn.gelu, approximate=False), hidden)
    grad_hidden = gelu_pull(grad_active)[0].astype(jnp.bfloat16)
    grad_b_in = jnp.sum(grad_hidden.astype(jnp.float32), axis=0)
    quant_in_grad = contract_rows(ffn_rows, grad_hidden)
    partial_normed = contract_cols(grad_hidden, in_weights)
    grad_quant_normed = lax.psum_scatter(partial_normed, "tensor", scatter_dimension=0, tiled=True)
    grad_normed = grad_sum_two + grad_quant_normed * clip_slope(normed, level_normed)
    grad_sum_one, grad_gain_one, grad_shift_one = norm_backward(
        grad_normed, normal_one, inverse_one, gain_first
    )
    grad_b_out = jnp.sum(grad_sum_one, axis=0)
    grad_attention = grad_sum_one.astype(jnp.bfloat16)
    attention_rows = lax.all_gather(grad_attention, "tensor", axis=0, tiled=True)
    quant_out_grad = contract_rows(quant_context, attention_rows)
    grad_context = (
        contract_cols(attention_rows, out_weights) * clip_slope(context, level_context)
    ).astype(jnp.bfloat16)

    def backward_one(block_items):
        return attend_backward(
            block_items[0],
            block_items[1],
            block_items[2],
            block_items[3],
            block_items[4],
            block_items[5],
            factor,
        )

    grad_queries, grad_keys, grad_values = lax.map(
        backward_one,
        (
            queries.reshape(blocked),
            key_rows.reshape(blocked),
            value_rows.reshape(blocked),
            segments,
            logsum,
            grad_context.reshape(blocked),
        ),
    )
    grad_queries = grad_queries.reshape(queries.shape)
    grad_keys = grad_keys.reshape(queries.shape)
    grad_values = grad_values.reshape(queries.shape)
    grad_bias_pair = jnp.stack(
        [
            jnp.sum(grad_queries.astype(jnp.float32), axis=0),
            jnp.sum(grad_values.astype(jnp.float32), axis=0),
        ]
    )
    quant_qkv_grad = jnp.stack(
        [
            contract_rows(attend_rows, grad_queries),
            contract_rows(attend_rows, grad_keys),
            contract_rows(attend_rows, grad_values),
        ]
    )
    partial_input = (
        contract_cols(grad_queries, qkv_weights[0])
        + contract_cols(grad_keys, qkv_weights[1])
        + contract_cols(grad_values, qkv_weights[2])
    )
    grad_quant_input = lax.psum_scatter(partial_input, "tensor", scatter_dimension=0, tiled=True)
    grad_x = (grad_sum_one + grad_quant_input * clip_slope(inputs, level_input)).astype(
        jnp.bfloat16
    )
    weight_terms = (
        quant_qkv_grad,
        grad_bias_pair,
        quant_out_grad,
        quant_in_grad,
        grad_b_in,
        quant_down_grad,
    )
    local_terms = (
        weight_terms[0] * clip_slope(qkv_float, qkv_levels),
        weight_terms[1],
        weight_terms[2] * clip_slope(out_float, weight_levels[3]),
        weight_terms[3] * clip_slope(in_float, weight_levels[4]),
        weight_terms[4],
        weight_terms[5] * clip_slope(down_float, weight_levels[5]),
    )
    summed_terms = lax.psum(
        (
            local_terms[0],
            local_terms[1],
            local_terms[2],
            local_terms[3],
            local_terms[4],
            local_terms[5],
        ),
        "dp",
    )
    row_terms = lax.psum(
        jnp.stack(
            [grad_b_out, grad_gain_one, grad_shift_one, grad_b_down, grad_gain_two, grad_shift_two]
        ),
        ("dp", "tensor"),
    )
    new_ranges = jnp.stack([level_input, level_context, level_normed, level_active])
    return (
        output,
        grad_x,
        summed_terms[0],
        summed_terms[1],
        summed_terms[2],
        row_terms[0],
        row_terms[1],
        row_terms[2],
        summed_terms[3],
        summed_terms[4],
        summed_terms[5],
        row_terms[3],
        row_terms[4],
        row_terms[5],
        new_ranges,
    )


def solution(mesh):
    in_specs = (
        P(("dp", "tensor"), None),
        P(("dp", "tensor"), None),
        P("dp", None),
        P(),
        P(None, None, "tensor"),
        P(None, "tensor"),
        P("tensor", None),
        P(),
        P(),
        P(),
        P(None, "tensor"),
        P("tensor"),
        P("tensor", None),
        P(),
        P(),
        P(),
    )
    out_specs = (
        P(("dp", "tensor"), None),
        P(("dp", "tensor"), None),
        P(None, None, "tensor"),
        P(None, "tensor"),
        P("tensor", None),
        P(),
        P(),
        P(),
        P(None, "tensor"),
        P("tensor"),
        P("tensor", None),
        P(),
        P(),
        P(),
        P(),
    )
    return jax.shard_map(local, mesh=mesh, in_specs=in_specs, out_specs=out_specs, check_vma=False)
```

profile of v0, /device:TPU:0, one launch (start us, length us, event | category | flops | bytes accessed | tf_op | source)
XLA Modules:
  0.0 2585.5 jit_solution(2142261974662647699)
XLA Ops:
  18.9 42.0 %pmax.28 = f32[7]{0:T(128)S(1)} all-reduce(f32[7]{0:T(128)S(1)} %concatenate.3), channel_id=1, replica_groups=mesh['dp'=8,'tensor'=4] {'dp','tensor'}, use_global_device_ids=true, to_apply=%region_5.0 | all-reduce | flops 7 | bytes 56 | tf_op jit(solution)/shard_map/pmax | solution.py:144
  68.8 145.6 %all-gather.5.cloned.1.call-done = bf16[4096,1024]{1,0:T(8,128)(2,1)} async-done(((bf16[1024,1024]{1,0:T(8,128)(2,1)}), bf16[4096,1024]{1,0:T(8,128)(2,1)}) %all-gather.5.cloned.1.call-update) | async-done | bytes 8388624 | tf_op jit(solution)/shard_map/all_gather | solution.py:161
  277.8 54.8 %while.26 = (s32[]{:T(128)}, f32[8,512,4,64]{1,3,2,0:T(8,128)}, f32[8,4,512]{2,1,0:T(4,128)}, bf16[8,512,4,64]{1,3,2,0:T(8,128)(2,1)}, s32[8,512]{1,0:T(8,128)S(...) while((s32[]{:T(128)}, f32[8,512,4,64]{1,3,2,0:T(8,128)}, ...), condition=%wide.region_11.12_spmd, body=%wide.region_8.11_spmd.sunk | while | flops 281278464 | bytes 15016537 | solution.py:176
  336.5 38.7 %pmax.29 = f32[]{:T(128)} all-reduce(f32[]{:T(128)} %abs_reduce_fusion.2), channel_id=1, replica_groups=mesh['dp'=8,'tensor'=4] {'dp','tensor'}, use_global_device_ids=true, to_apply=%region_13.14 | all-reduce | flops 1 | bytes 8 | tf_op jit(solution)/shard_map/pmax | solution.py:186
  394.7 279.1 %reduce-scatter.5.cloned.1.call-done = f32[1024,1024]{1,0:T(8,128)} async-done(((f32[4096,1024]{1,0:T(8,128)}), f32[1024,1024]{1,0:T(8,128)}) %reduce-scatter.5.cloned.1.call-update) | async-done | bytes 4194320 | tf_op jit(solution)/shard_map/reduce_scatter | solution.py:191
  682.2 41.2 %pmax.30 = f32[]{:T(128)} all-reduce(f32[]{:T(128)} %get-tuple-element.220), channel_id=1, replica_groups=mesh['dp'=8,'tensor'=4] {'dp','tensor'}, use_global_device_ids=true, to_apply=%region_18.19 | all-reduce | flops 1 | bytes 8 | tf_op jit(solution)/shard_map/pmax | solution.py:199
  729.3 149.0 %all-gather.7.cloned.1.call-done = bf16[4096,1024]{1,0:T(8,128)(2,1)} async-done(((bf16[1024,1024]{1,0:T(8,128)(2,1)}), bf16[4096,1024]{1,0:T(8,128)(2,1)}) %all-gather.7.cloned.1.call-update) | async-done | bytes 8388624 | tf_op jit(solution)/shard_map/all_gather | solution.py:203
  878.3 50.4 %abs_reduce_fusion = (f32[]{:T(128)}, f32[4096,1024]{1,0:T(8,128)}, f32[4096,1024]{1,0:T(8,128)}) fusion(f32[1024]{0:T(1024)S(1)} %convert_element_type.157, bf16[4096,1024]{1,0:T(8,128)(2,1)} %all-gather.7.cloned.1.call-done, bf16[1024,1024]{1,0:T(8,128)(2,1)S(1)} %copy-done.23, f32[]{:T(128)} %bitcast.33), kind=kOutput, calls=%fused_computation.70 | convolution fusion | flops 8875147264 | bytes 44044296 | tf_op jit(solution)/shard_map/dot_general | solution.py:27
  928.7 38.8 %pmax.31 = f32[]{:T(128)} all-reduce(f32[]{:T(128)} %get-tuple-element.218), channel_id=1, replica_groups=mesh['dp'=8,'tensor'=4] {'dp','tensor'}, use_global_device_ids=true, to_apply=%region_20.21 | all-reduce | flops 1 | bytes 8 | tf_op jit(solution)/shard_map/pmax | solution.py:206
  983.4 12.4 fusion.89
  996.5 279.8 %reduce-scatter.7.cloned.1.call-done = f32[1024,1024]{1,0:T(8,128)} async-done(((f32[4096,1024]{1,0:T(8,128)}), f32[1024,1024]{1,0:T(8,128)}) %reduce-scatter.7.cloned.1.call-update) | async-done | bytes 4194320 | tf_op jit(solution)/shard_map/reduce_scatter | solution.py:211
  1292.4 150.5 %all-gather.9.cloned.1.call-done = bf16[4096,1024]{1,0:T(8,128)(2,1)} async-done(((bf16[1024,1024]{1,0:T(8,128)(2,1)}), bf16[4096,1024]{1,0:T(8,128)(2,1)}) %all-gather.9.cloned.1.call-update) | async-done | bytes 8388624 | tf_op jit(solution)/shard_map/all_gather | solution.py:221
  1442.9 27.5 %convert_reduce_fusion = (f32[1024]{0:T(1024)}, bf16[4096,1024]{1,0:T(8,128)(2,1)}) fusion(f32[4096,1024]{1,0:T(8,128)} %get-tuple-element.219, f32[]{:T(128)} %add.170, bf16[4096,1024]{1,0:T(8,128)(2,1)} %all-gather.9.cloned.1.call-done, bf16[1024,1024]{1,0:T(8,128)(2,1)S(1)} %copy-done.22, f32[]{:T(128)} %bitcast.34, ...), kind=kOutput, calls=%fused_computation.65 | convolution fusion | flops 8686402560 | bytes 52437000 | tf_op jit(solution)/shard_map/dot_general | solution.py:37
  1470.4 15.3 fusion.87
  1485.7 278.6 %reduce-scatter.9.cloned.1.call-done = f32[1024,1024]{1,0:T(8,128)} async-done(((f32[4096,1024]{1,0:T(8,128)}), f32[1024,1024]{1,0:T(8,128)}) %reduce-scatter.9.cloned.1.call-update) | async-done | bytes 4194320 | tf_op jit(solution)/shard_map/reduce_scatter | solution.py:229
  1794.5 132.6 %all-gather.11.cloned.1.call-done = bf16[4096,1024]{1,0:T(8,128)(2,1)} async-done(((bf16[1024,1024]{1,0:T(8,128)(2,1)}), bf16[4096,1024]{1,0:T(8,128)(2,1)}) %all-gather.11.cloned.1.call-update) | async-done | bytes 8388624 | tf_op jit(solution)/shard_map/all_gather | solution.py:236
  1944.8 118.8 %while.27 = (s32[]{:T(128)}, bf16[8,512,4,64]{1,3,2,0:T(8,128)(2,1)}, bf16[8,512,4,64]{1,3,2,0:T(8,128)(2,1)}, bf16[8,512,4,64]{1,3,2,0:T(8,128)(2,1)}, bf16[8,5...) while((s32[]{:T(128)}, ...), condition=%wide.region_31.32_spmd, body=%wide.region_29.31_spmd.sunk | while | flops 688519168 | bytes 35196020 | solution.py:253
  2089.2 19.8 add_add_fusion
  2109.0 17.5 subtract_multiply_fusion
  2126.6 16.7 subtract_multiply_fusion.1
  2157.9 42.5 %psum.52 = f32[6,1024]{1,0:T(8,128)S(1)} all-reduce(f32[6,1024]{1,0:T(8,128)S(1)} %stack.84), channel_id=1, replica_groups=mesh['dp'=8,'tensor'=4] {'dp','tensor'}, use_global_device_ids=true, to_apply=%region_44.45 | all-reduce | flops 6144 | bytes 49152 | tf_op jit(solution)/shard_map/psum | solution.py:316
  2205.2 14.3 all-reduce
  2219.5 169.2 %reduce-scatter.11.cloned.1.call-done = f32[1024,1024]{1,0:T(8,128)} async-done(((f32[4096,1024]{1,0:T(8,128)}), f32[1024,1024]{1,0:T(8,128)}) %reduce-scatter.11.cloned.1.call-update) | async-done | bytes 4194320 | tf_op jit(solution)/shard_map/reduce_scatter | solution.py:285
  2394.8 173.1 %all-reduce.4.cloned.1.call-done = (f32[3,1024,256]{2,1,0:T(8,128)}, f32[256,1024]{1,0:T(8,128)}, f32[1024,1024]{1,0:T(8,128)}, f32[1024,1024]{1,0:T(8,128)}) async-done(((f32[3,1024,256]{2,1,0:T(8,128)}, f32[256,1024]{1,0:T(8,128)}, f32[1024,1024]{1,0:T(8,128)}, f32[1024,1024]{1,0:T(8,128)}), (f32[3,1024,256]{2,1,0:T(8,128)}, f32[256,1024]{1,0:T(8,128)}, f32[1024,1024]{1,0:T(8,128)}, ...) | async-done | bytes 12582928 | tf_op jit(solution)/shard_map/psum | solution.py:305
  (348 shorter events, 430.0 us)
Async XLA Ops:
  7.2 207.2 %all-gather.5.cloned.1.call-start = ((), (), s32[]{:S(2)}) async-start(), calls=%async_computation.4 | async-start | bytes 10485760 | tf_op jit(solution)/shard_map/all_gather | solution.py:161
  15.4 49.4 %copy-start.53 = (s32[8,4]{0,1:T(4,128)S(1)}, s32[8,4]{0,1:T(4,128)}, u32[]{:S(2)}) copy-start(s32[8,4]{0,1:T(4,128)} %param.22) | copy-start | bytes 388
  15.4 50.2 %copy-start.45 = (bf16[2,256]{1,0:T(2,128)(2,1)S(1)}, bf16[2,256]{1,0:T(2,128)(2,1)}, u32[]{:S(2)}) copy-start(bf16[2,256]{1,0:T(2,128)(2,1)} %param.25) | copy-start | bytes 3076
  64.8 609.0 %reduce-scatter.5.cloned.1.call-start = ((), (), s32[]{:S(2)}) async-start(), calls=%async_computation.5 | async-start | bytes 20971520 | tf_op jit(solution)/shard_map/reduce_scatter | solution.py:191
  332.6 48.5 %copy-start.32 = (s32[8,512]{1,0:T(8,128)}, s32[8,512]{1,0:T(8,128)S(1)}, u32[]{:S(2)}) copy-start(s32[8,512]{1,0:T(8,128)S(1)} %get-tuple-element.480) | copy-start | bytes 49156
  393.3 485.0 %all-gather.7.cloned.1.call-start = ((), (), s32[]{:S(2)}) async-start(), calls=%async_computation.6 | async-start | bytes 10485760 | tf_op jit(solution)/shard_map/all_gather | solution.py:203
  394.0 330.0 %copy-start.28 = (f32[1024]{0:T(1024)}, f32[1024]{0:T(1024)S(1)}, u32[]{:S(2)}) copy-start(f32[1024]{0:T(1024)S(1)} %convert_element_type.153) | copy-start | bytes 12292
  394.0 330.1 %copy-start.30 = (f32[1024]{0:T(1024)}, f32[1024]{0:T(1024)S(1)}, u32[]{:S(2)}) copy-start(f32[1024]{0:T(1024)S(1)} %convert_element_type.154) | copy-start | bytes 12292
  724.1 154.2 %copy-start.23 = (bf16[1024,1024]{1,0:T(8,128)(2,1)S(1)}, bf16[1024,1024]{1,0:T(8,128)(2,1)}, u32[]{:S(2)}) copy-start(bf16[1024,1024]{1,0:T(8,128)(2,1)} %param.30) | copy-start | bytes 6291460
  728.5 547.8 %reduce-scatter.7.cloned.1.call-start = ((), (), s32[]{:S(2)}) async-start(), calls=%async_computation.7 | async-start | bytes 20971520 | tf_op jit(solution)/shard_map/reduce_scatter | solution.py:211
  995.8 280.6 %copy-start.29 = (f32[1024]{0:T(1024)S(1)}, f32[1024]{0:T(1024)}, u32[]{:S(2)}) copy-start(f32[1024]{0:T(1024)} %copy-done.28) | copy-start | bytes 12292
  995.8 280.5 %copy-start.31 = (f32[1024]{0:T(1024)S(1)}, f32[1024]{0:T(1024)}, u32[]{:S(2)}) copy-start(f32[1024]{0:T(1024)} %copy-done.30) | copy-start | bytes 12292
  995.9 447.0 %all-gather.9.cloned.1.call-start = ((), (), s32[]{:S(2)}) async-start(), calls=%async_computation.8 | async-start | bytes 10485760 | tf_op jit(solution)/shard_map/all_gather | solution.py:221
  1290.6 152.3 %copy-start.22 = (bf16[1024,1024]{1,0:T(8,128)(2,1)S(1)}, bf16[1024,1024]{1,0:T(8,128)(2,1)}, u32[]{:S(2)}) copy-start(bf16[1024,1024]{1,0:T(8,128)(2,1)} %param.32) | copy-start | bytes 6291460
  1292.3 472.0 %reduce-scatter.9.cloned.1.call-start = ((), (), s32[]{:S(2)}) async-start(), calls=%async_computation.9 | async-start | bytes 20971520 | tf_op jit(solution)/shard_map/reduce_scatter | solution.py:229
  1442.9 27.5 %copy-start.24 = (bf16[1024,1024]{1,0:T(8,128)(2,1)S(1)}, bf16[1024,1024]{1,0:T(8,128)(2,1)}, u32[]{:S(2)}) copy-start(bf16[1024,1024]{1,0:T(8,128)(2,1)} %param.30) | copy-start | bytes 6291460
  1485.7 285.4 %copy-start.34 = (f32[1024]{0:T(1024)S(1)}, f32[1024]{0:T(1024)}, u32[]{:S(2)}) copy-start(f32[1024]{0:T(1024)} %copy-done.33) | copy-start | bytes 12292
  1485.7 441.4 %all-gather.11.cloned.1.call-start = ((), (), s32[]{:S(2)}) async-start(), calls=%async_computation.10 | async-start | bytes 10485760 | tf_op jit(solution)/shard_map/all_gather | solution.py:236
  1776.6 612.1 %reduce-scatter.11.cloned.1.call-start = ((), (), s32[]{:S(2)}) async-start(), calls=%async_computation.11 | async-start | bytes 20971520 | tf_op jit(solution)/shard_map/reduce_scatter | solution.py:285
  1785.5 141.6 %copy-start.20 = (bf16[256,1024]{1,0:T(8,128)(2,1)S(1)}, bf16[256,1024]{1,0:T(8,128)(2,1)}, u32[]{:S(2)}) copy-start(bf16[256,1024]{1,0:T(8,128)(2,1)} %param.26) | copy-start | bytes 1572868
  2109.0 459.0 %all-reduce.4.cloned.1.call-start = ((), (), s32[]{:S(2)}) async-start(), calls=%async_computation.12 | async-start | bytes 25165824 | tf_op jit(solution)/shard_map/psum | solution.py:305
  2109.0 34.2 %slice-start = ((s8[8388608]{0:T(1024)(128)(4,1)}), s8[4194304]{0:T(1024)(128)(4,1)S(1)}, s32[]{:S(2)}) async-start(s8[8388608]{0:T(1024)(128)(4,1)} %bitcast.228), calls=%async_computation.13 | async-start | bytes 8388608
  2157.1 48.0 %copy-start.44 = (f32[1024]{0:T(1024)S(1)}, f32[1024]{0:T(1024)}, u32[]{:S(2)}) copy-start(f32[1024]{0:T(1024)} %get-tuple-element.245) | copy-start | bytes 12292
  2157.1 231.6 %copy-start.2 = (bf16[1024,1024]{1,0:T(8,128)(2,1)S(1)}, bf16[1024,1024]{1,0:T(8,128)(2,1)}, u32[]{:S(2)}) copy-start(bf16[1024,1024]{1,0:T(8,128)(2,1)} %param.20) | copy-start | bytes 6291460
  (43 other events, 186.2 us)
Sparse Core Ops, SparseCore 0:
  64.9 149.4 all-gather.4
  393.4 280.3 reduce-scatter.4
  728.7 149.5 all-gather.6
  996.0 280.3 reduce-scatter.6
  1292.5 150.3 all-gather.8
  1485.8 278.5 reduce-scatter.8
  1776.7 150.3 all-gather.10
  2109.1 279.5 reduce-scatter.10
  2393.8 174.0 all-reduce.3
where the time goes:
time: 2590 us
  waiting for transfers between devices  1760 us (68%)
  matrix products  360 us (14%)
  blocking collectives  218 us (8%)
  local copies, waits for them, and re-layouts  120 us (5%)
  other arithmetic  109 us (4%)
    reduce_scatter x1, waiting for transfers between devices, local(): lax.psum_scatter(partial_ffn, 'tensor', scatter_dimension=0, tiled=True)  280 us
    reduce_scatter x1, waiting for transfers between devices, local(): lax.psum_scatter(partial_attn, 'tensor', scatter_dimension=0, tiled=True)  279 us
    reduce_scatter x1, waiting for transfers between devices, local(): lax.psum_scatter(partial_normed, 'tensor', scatter_dimension=0, tiled=True)  279 us
    psum x1, waiting for transfers between devices, local(): lax.psum((local_terms[0], local_terms[1], local_terms[2], local_terms[3],...  173 us
    reduce_scatter x1, waiting for transfers between devices, local(): lax.psum_scatter(partial_input, 'tensor', scatter_dimension=0, tiled=True)  169 us
    all_gather x1, waiting for transfers between devices, local(): branch_rows = lax.all_gather(grad_branch, 'tensor', axis=0, tiled=True)  150 us
    all_gather x1, waiting for transfers between devices, local(): ffn_rows = lax.all_gather(quant_normed, 'tensor', axis=0, tiled=True)  149 us
    all_gather x1, waiting for transfers between devices, local(): attend_rows = lax.all_gather(quant_input, 'tensor', axis=0, tiled=True)  146 us
  transfers between devices with their start and end apart: 9, of which 9 were waited for; matrix products, arithmetic and copies ran while one was open for 3% of the time, Pallas kernels for 0%

commit v1 on v0

v1 whole, which is shorter than its diff:
```python
from functools import partial

import jax
import jax.numpy as jnp
from jax import lax
from jax.experimental import pallas as pl
from jax.experimental.pallas import tpu as pltpu
from jax.sharding import PartitionSpec as P

HD = 64
SEQ = 512
LANES = 128

EPS = 1e-06
DECAY = 0.9
MASKED = -1e30
MESH = pl.DeviceIdType.MESH
F32 = jnp.float32
BF16 = jnp.bfloat16
MIB = 1024 * 1024


def shape_of(dims, kind):
    return jax.ShapeDtypeStruct(dims, kind)


def params(mib=48, **rest):
    return pltpu.CompilerParams(vmem_limit_bytes=mib * MIB, **rest)


def in_smem():
    return pl.BlockSpec(memory_space=pltpu.SMEM)


def cost(flops, moved):
    return pl.CostEstimate(flops=int(flops), bytes_accessed=int(moved), transcendentals=0)


def dot(first, second):
    return jnp.dot(first, second, preferred_element_type=F32)


def dot_cols(first, second):
    return lax.dot_general(first, second, (((1,), (1,)), ((), ())), preferred_element_type=F32)


def dot_rows(first, second):
    return lax.dot_general(first, second, (((0,), (0,)), ((), ())), preferred_element_type=F32)


def flat(block):
    return block.reshape(block.shape[0] * block.shape[1], block.shape[2])


def exchange_kernel(kind, x_ref, range_ref, o_ref, near, far, mid, near_send, near_recv, far_send, far_recv):
    data, part = lax.axis_index("dp"), lax.axis_index("tensor")
    datas, parts = lax.axis_size("dp"), lax.axis_size("tensor")
    barrier = pltpu.get_barrier_semaphore()

    def to_data(step):
        return (lax.rem(data + step, datas), part)

    def to_part(step):
        return (data, lax.rem(part + step, parts))

    def greet(target):
        def run(step, carry):
            pl.semaphore_signal(barrier, inc=1, device_id=target(step), device_id_type=MESH)
            return carry

        return run

    lax.fori_loop(1, datas, greet(to_data), 0)
    lax.fori_loop(1, parts, greet(to_part), 0)
    pl.semaphore_wait(barrier, datas + parts - 2)

    def exchange(source, slots, send, recv, target, count):
        def copy(step):
            return pltpu.make_async_remote_copy(
                src_ref=source,
                dst_ref=slots.at[step],
                send_sem=send.at[step],
                recv_sem=recv.at[step],
                device_id=target(step),
                device_id_type=MESH,
            )

        def start(step, carry):
            copy(step).start()
            return carry

        def finish(step, carry):
            copy(step).wait()
            return carry

        lax.fori_loop(1, count, start, 0)
        slots[0] = source[...]
        lax.fori_loop(1, count, finish, 0)
        if kind == "sum":
            return jnp.sum(slots[...], axis=0)
        return jnp.max(slots[...], axis=0)

    mid[...] = exchange(x_ref, near, near_send, near_recv, to_data, datas)
    total = exchange(mid, far, far_send, far_recv, to_part, parts)
    if kind == "rows":
        total = jnp.broadcast_to(jnp.max(total, axis=1, keepdims=True), total.shape)
    if kind == "level":
        peak = jnp.max(total, keepdims=True)
        total = jnp.broadcast_to(DECAY * range_ref[0] + (1.0 - DECAY) * peak, total.shape)
    o_ref[...] = total


def exchange_all(values, mesh, kind, previous):
    datas, parts = mesh.shape["dp"], mesh.shape["tensor"]
    dims = values.shape
    copies = pltpu.SemaphoreType.DMA
    return pl.pallas_call(
        partial(exchange_kernel, kind),
        out_shape=shape_of(dims, F32),
        in_specs=[pl.BlockSpec(memory_space=pltpu.VMEM), in_smem()],
        out_specs=pl.BlockSpec(memory_space=pltpu.VMEM),
        scratch_shapes=[
            pltpu.VMEM((datas,) + dims, F32),
            pltpu.VMEM((parts,) + dims, F32),
            pltpu.VMEM(dims, F32),
            copies((datas,)),
            copies((datas,)),
            copies((parts,)),
            copies((parts,)),
        ],
        compiler_params=pltpu.CompilerParams(
            collective_id={"rows": 0, "level": 1, "sum": 2}[kind], has_side_effects=True
        ),
        name="exchange_" + kind,
    )(values, previous)


def swap(values, axis, bit):
    count = lax.axis_size(axis)
    return lax.ppermute(values, axis, [(i, i ^ (1 << bit)) for i in range(count)])


def bits_of(axis):
    return lax.axis_size(axis).bit_length() - 1


def plane_orders():
    plane = list(range(1, bits_of("dp")))
    return plane, (plane[::-1], plane)


def spread_plane(values, order):
    held = []
    for bit in order:
        other = swap(values, "dp", bit)
        place = sum(1 for seen in held if seen > bit)
        values = jnp.stack([values, other], axis=place)
        held.append(bit)
    return values.reshape((-1,) + values.shape[len(held) :])


def gather(piece):
    held = piece[None]
    for bit in reversed(range(bits_of("tensor"))):
        other = swap(held, "tensor", bit)
        held = jnp.stack([held, other], axis=1).reshape((-1,) + piece.shape)
    half = held.shape[0] // 2
    _, orders = plane_orders()
    sides = [spread_plane(held[:half], orders[0]), spread_plane(held[half:], orders[1])]
    near = jnp.concatenate(sides, axis=1)
    return near, swap(near, "dp", 0)


def low(values):
    return values.astype(BF16)


def scatter_side(values, order):
    plane, _ = plane_orders()
    values = values.reshape((2,) * len(plane) + values.shape[1:])
    left = plane[::-1]
    for bit in order:
        place = left.index(bit)
        keep = lax.index_in_dim(values, 0, place, keepdims=False)
        send = lax.index_in_dim(values, 1, place, keepdims=False)
        values = keep + swap(low(send), "dp", bit).astype(F32)
        left.remove(bit)
    for bit in range(bits_of("tensor") - 1):
        pairs = values.reshape((-1, 2) + values.shape[1:])
        values = pairs[:, 0] + swap(low(pairs[:, 1]), "tensor", bit).astype(F32)
    return values[0]


def scatter(keep, send):
    summed = keep + swap(send, "dp", 0).astype(F32)
    half = summed.shape[1] // 2
    _, orders = plane_orders()
    near = scatter_side(summed[:, :half], orders[0])
    far = scatter_side(summed[:, half:], orders[1])
    return near + swap(low(far), "tensor", bits_of("tensor") - 1).astype(F32)


def spread(piece):
    half = piece.shape[1] // 2
    _, orders = plane_orders()
    sides = [spread_plane(piece[:, :half], orders[0]), spread_plane(piece[:, half:], orders[1])]
    near = jnp.concatenate(sides, axis=2)
    return jnp.concatenate([near, swap(near, "dp", 0)], axis=0)


def take_blocks(ref, order_ref):
    return jnp.concatenate(
        [
            ref[:, pl.ds(pl.multiple_of(order_ref[j] * LANES, LANES), LANES)]
            for j in range(ref.shape[1] // LANES)
        ],
        axis=1,
    )


def put_blocks(ref, order_ref, values):
    for j in range(ref.shape[1] // LANES):
        ref[:, pl.ds(pl.multiple_of(order_ref[j] * LANES, LANES), LANES)] = values[
            :, j * LANES : (j + 1) * LANES
        ]


def fold_peak(values):
    return jnp.max(jnp.abs(values).reshape(-1, 8, LANES), axis=0)


def column_peak(values):
    peak = fold_peak(values[:, :LANES])
    for j in range(1, values.shape[1] // LANES):
        peak = jnp.maximum(peak, fold_peak(values[:, j * LANES : (j + 1) * LANES]))
    return peak


def quant_kernel(order_ref, x_ref, level_ref, o_ref):
    level = level_ref[0:1, 0:1]
    x = take_blocks(x_ref, order_ref).astype(F32)
    o_ref[...] = low(level * jnp.tanh(x / level))


def quant_rows(x, level, order):
    tokens, width = x.shape
    rows = 256
    return pl.pallas_call(
        quant_kernel,
        grid=(tokens // rows,),
        in_specs=[
            in_smem(),
            pl.BlockSpec((rows, width), lambda t: (t, 0)),
            pl.BlockSpec((8, LANES), lambda t: (0, 0)),
        ],
        out_specs=pl.BlockSpec((rows, width), lambda t: (t, 0)),
        out_shape=shape_of((tokens, width), BF16),
        compiler_params=params(32),
        name="quant_input",
    )(order, x, level)


def qkv_kernel(x_ref, near_ref, far_ref, b_ref, o_ref):
    half = x_ref.shape[1] // 2
    total = dot(x_ref[:, :half], flat(near_ref[...])) + dot(x_ref[:, half:], flat(far_ref[...]))
    o_ref[...] = low(total + b_ref[...])


def qkv_rows(x, weights, bias):
    near, far = weights
    plane, parts, kinds, rows, c = near.shape
    tokens, width = x.shape
    weight_spec = pl.BlockSpec((plane, None, None, rows, c), lambda r, i: (0, r, i, 0, 0))
    return pl.pallas_call(
        qkv_kernel,
        grid=(parts, kinds),
        in_specs=[
            pl.BlockSpec((tokens, width), lambda r, i: (0, 0)),
            weight_spec,
            weight_spec,
            pl.BlockSpec((None, 1, c), lambda r, i: (i, 0, r)),
        ],
        out_specs=pl.BlockSpec((None, tokens, c), lambda r, i: (i, 0, r)),
        out_shape=shape_of((kinds, tokens, parts * c), BF16),
        compiler_params=params(32),
        cost_estimate=cost(2 * tokens * width * kinds * parts * c, 14 * MIB),
        name="qkv",
    )(x, near, far, bias)


def fill_mask(mask_ref, col_ref, row_ref):
    mask_ref[...] = jnp.where(col_ref[...] == row_ref[...], 0.0, MASKED).astype(F32)


def attend_kernel(q_ref, k_ref, v_ref, col_ref, row_ref, o_ref, lse_ref, peak_ref, mask_ref, sums_ref):
    row, pair = pl.program_id(0), pl.program_id(1)
    factor = HD ** (-0.5)

    @pl.when(pair == 0)
    def _():
        fill_mask(mask_ref, col_ref, row_ref)
        sums_ref[...] = jnp.zeros_like(sums_ref)

    @pl.when((pair == 0) & (row == 0))
    def _():
        peak_ref[...] = jnp.zeros_like(peak_ref)

    rows = 256
    lanes = lax.broadcasted_iota(jnp.int32, (rows, LANES), 1)
    for start in range(0, SEQ, rows):
        here = pl.ds(start, rows)
        q = q_ref[here, :] * jnp.asarray(factor, BF16)
        parts = []
        sums = sums_ref[here, :]
        for head in range(LANES // HD):
            own = lanes // HD == head
            scores = dot_cols(jnp.where(own, q, jnp.zeros_like(q)), k_ref[...]) + mask_ref[here, :]
            row_max = jnp.max(scores, axis=-1, keepdims=True)
            exponent = jnp.exp(scores - row_max)
            totals = jnp.sum(exponent, axis=-1, keepdims=True)
            probs = low(exponent * (1.0 / totals))
            parts.append(dot(probs, v_ref[...]))
            sums = jnp.where(lanes == pair * (LANES // HD) + head, row_max + jnp.log(totals), sums)
        context = parts[0]
        for head in range(1, LANES // HD):
            context = jnp.where(lanes // HD == head, parts[head], context)
        o_ref[here, :] = context
        sums_ref[here, :] = sums
        peak_ref[...] = jnp.maximum(peak_ref[...], fold_peak(context))

    @pl.when(pair == pl.num_programs(1) - 1)
    def _():
        lse_ref[...] = sums_ref[...].T


def attend(qkv, cols, rows):
    _, tokens, width = qkv.shape
    held = tokens // SEQ

    def side(i):
        return pl.BlockSpec((None, SEQ, LANES), lambda r, j: (i, r, j))

    return pl.pallas_call(
        attend_kernel,
        grid=(held, width // LANES),
        in_specs=[
            side(0),
            side(1),
            side(2),
            pl.BlockSpec((None, SEQ, 1), lambda r, j: (r, 0, 0)),
            pl.BlockSpec((None, 1, SEQ), lambda r, j: (r, 0, 0)),
        ],
        out_specs=[
            pl.BlockSpec((SEQ, LANES), lambda r, j: (r, j)),
            pl.BlockSpec((None, LANES, SEQ), lambda r, j: (r, 0, 0)),
            pl.BlockSpec((8, LANES), lambda r, j: (0, 0)),
        ],
        out_shape=[
            shape_of((tokens, width), F32),
            shape_of((held, LANES, SEQ), F32),
            shape_of((8, LANES), F32),
        ],
        scratch_shapes=[pltpu.VMEM((SEQ, SEQ), F32), pltpu.VMEM((SEQ, LANES), F32)],
        compiler_params=params(40),
        cost_estimate=cost(30e9, 16 * MIB),
        name="attend",
    )(qkv, qkv, qkv, cols, rows)


def attend_back_kernel(
    q_ref, k_ref, v_ref, g_ref, col_ref, row_ref, lse_ref, dq_ref, dk_ref, dv_ref, sum_ref, mask_ref
):
    pair = pl.program_id(1)
    factor = HD ** (-0.5)

    @pl.when(pair == 0)
    def _():
        fill_mask(mask_ref, col_ref, row_ref)

    lanes = lax.broadcasted_iota(jnp.int32, (SEQ, LANES), 1)
    q, k, v, g = q_ref[...], k_ref[...], v_ref[...], g_ref[...]
    q_sums, k_sums, v_sums = [], [], []
    for head in range(LANES // HD):
        own = lanes // HD == head
        zero = jnp.zeros_like(q)
        q_own = jnp.where(own, q * jnp.asarray(factor, BF16), zero)
        g_own = jnp.where(own, g, zero)
        logsum = lse_ref[pl.ds(pair * (LANES // HD) + head, 1), :]
        probs = jnp.exp(dot_cols(k, q_own) + mask_ref[...] - logsum)
        v_sums.append(dot(low(probs), g))
        grad_probs = dot_cols(v, g_own)
        mean_grad = jnp.sum(probs * grad_probs, axis=0, keepdims=True)
        grad_scores = low(factor * probs * (grad_probs - mean_grad))
        k_sums.append(dot(grad_scores, q))
        q_sums.append(dot_rows(grad_scores, k))

    def join(parts):
        joined = parts[0]
        for head in range(1, LANES // HD):
            joined = jnp.where(lanes // HD == head, parts[head], joined)
        return low(joined)

    dq, dv = join(q_sums), join(v_sums)
    dq_ref[...] = dq
    dk_ref[...] = join(k_sums)
    dv_ref[...] = dv
    sum_ref[0:1, :] = jnp.sum(dq.astype(F32), axis=0, keepdims=True)
    sum_ref[1:2, :] = jnp.sum(dv.astype(F32), axis=0, keepdims=True)


def attend_back(qkv, grad, cols, rows, lse):
    _, tokens, width = qkv.shape
    held = tokens // SEQ

    def side(i):
        return pl.BlockSpec((None, SEQ, LANES), lambda r, j: (i, r, j))

    block = pl.BlockSpec((SEQ, LANES), lambda r, j: (r, j))
    return pl.pallas_call(
        attend_back_kernel,
        grid=(held, width // LANES),
        in_specs=[
            side(0),
            side(1),
            side(2),
            block,
            pl.BlockSpec((None, SEQ, 1), lambda r, j: (r, 0, 0)),
            pl.BlockSpec((None, 1, SEQ), lambda r, j: (r, 0, 0)),
            pl.BlockSpec((None, LANES, SEQ), lambda r, j: (r, 0, 0)),
        ],
        out_specs=[block, block, block, pl.BlockSpec((None, 8, LANES), lambda r, j: (r, 0, j))],
        out_shape=[shape_of((tokens, width), BF16)] * 3 + [shape_of((held, 8, width), F32)],
        scratch_shapes=[pltpu.VMEM((SEQ, SEQ), F32)],
        compiler_params=params(40),
        cost_estimate=cost(60e9, 16 * MIB),
        name="attend_back",
    )(qkv, qkv, qkv, grad, cols, rows, lse)


def project(values, near_ref, far_ref):
    parts, c = near_ref.shape[1], near_ref.shape[3]
    halves = []
    for ref in (near_ref, far_ref):
        total = None
        for r in range(parts):
            term = dot_cols(values[:, r * c : (r + 1) * c], flat(ref[:, r]))
            total = term if total is None else total + term
        halves.append(total)
    return jnp.concatenate(halves, axis=1)


def norm_parts(summed):
    center = summed - jnp.mean(summed, axis=-1, keepdims=True)
    inverse = lax.rsqrt(jnp.mean(center * center, axis=-1, keepdims=True) + EPS)
    return center * inverse, inverse


def norm_back(upstream, normal, inverse, gain):
    scaled = upstream * gain
    return inverse * (
        scaled
        - jnp.mean(scaled, axis=-1, keepdims=True)
        - normal * jnp.mean(scaled * normal, axis=-1, keepdims=True)
    )


def add_sums(ref, sums):
    @pl.when(pl.program_id(0) == 0)
    def _():
        ref[...] = jnp.zeros_like(ref)

    for i, values in enumerate(sums):
        ref[i : i + 1, :] += jnp.sum(values, axis=0, keepdims=True)


def first_norm_kernel(
    order_ref, ctx_ref, level_ref, near_ref, far_ref, x_ref, row_ref, quant_ref, normed_ref, normal_ref,
    inverse_ref, peak_ref
):
    level = level_ref[0:1, 0:1]
    quant = low(level * jnp.tanh(ctx_ref[...] / level))
    quant_ref[...] = quant
    summed = take_blocks(x_ref, order_ref).astype(F32) + project(quant, near_ref, far_ref)
    normal, inverse = norm_parts(summed + row_ref[0:1, :])
    normed = normal * row_ref[1:2, :] + row_ref[2:3, :]
    normed_ref[...] = normed
    normal_ref[...] = normal
    inverse_ref[...] = inverse

    @pl.when(pl.program_id(0) == 0)
    def _():
        peak_ref[...] = jnp.zeros_like(peak_ref)

    peak_ref[...] = jnp.maximum(peak_ref[...], column_peak(normed))


def whole(values):
    dims = values.shape
    return pl.BlockSpec(dims, lambda *steps: (0,) * len(dims))


def first_norm(context, level, weights, x, vectors, order):
    near, far = weights
    tokens, width = x.shape
    inner = context.shape[1]
    rows = 256

    def block(columns):
        return pl.BlockSpec((rows, columns), lambda t: (t, 0))

    return pl.pallas_call(
        first_norm_kernel,
        grid=(tokens // rows,),
        in_specs=[
            in_smem(),
            block(inner),
            whole(level),
            whole(near),
            whole(far),
            block(width),
            whole(vectors),
        ],
        out_specs=[
            block(inner),
            block(width),
            block(width),
            block(1),
            pl.BlockSpec((8, LANES), lambda t: (0, 0)),
        ],
        out_shape=[
            shape_of((tokens, inner), BF16),
            shape_of((tokens, width), F32),
            shape_of((tokens, width), F32),
            shape_of((tokens, 1), F32),
            shape_of((8, LANES), F32),
        ],
        compiler_params=params(48),
        cost_estimate=cost(2 * tokens * width * inner, 20 * MIB),
        name="first_norm",
    )(order, context, level, near, far, x, vectors)


def hidden_kernel(normed_ref, level_ref, near_ref, far_ref, b_ref, quant_ref, act_ref, slope_ref, peak_ref):
    tokens, width = normed_ref.shape
    half = width // 2
    rows = 128

    @pl.when(pl.program_id(0) == 0)
    def _():
        peak_ref[...] = jnp.zeros_like(peak_ref)
        level = level_ref[0:1, 0:1]

        @pl.loop(0, tokens // rows)
        def _(step):
            here = pl.ds(step * rows, rows)
            quant_ref[here, :] = low(level * jnp.tanh(normed_ref[here, :] / level))

    @pl.loop(0, tokens // rows)
    def _(step):
        here = pl.ds(pl.multiple_of(step * rows, rows), rows)
        hidden = dot(quant_ref[here, :half], flat(near_ref[...]))
        hidden = hidden + dot(quant_ref[here, half:], flat(far_ref[...])) + b_ref[...]
        share = 0.5 + 0.5 * lax.erf(hidden * (0.5**0.5))
        active = hidden * share
        act_ref[here, :] = active
        slope_ref[here, :] = share + hidden * (
            (0.5 / jnp.pi) ** 0.5 * jnp.exp(-0.5 * hidden * hidden)
        )
        peak_ref[...] = jnp.maximum(peak_ref[...], column_peak(active))


def hidden_rows(normed, level, weights, bias):
    near, far = weights
    plane, parts, rows, c = near.shape
    tokens, width = normed.shape
    step = min(c, 512)
    cuts = c // step
    weight_spec = pl.BlockSpec((plane, None, rows, step), lambda s: (0, s // cuts, 0, s % cuts))
    block = pl.BlockSpec((tokens, step), lambda s: (0, s))
    return pl.pallas_call(
        hidden_kernel,
        grid=(parts * cuts,),
        in_specs=[
            whole(normed),
            whole(level),
            weight_spec,
            weight_spec,
            pl.BlockSpec((1, step), lambda s: (0, s)),
        ],
        out_specs=[
            pl.BlockSpec((tokens, width), lambda s: (0, 0)),
            block,
            block,
            pl.BlockSpec((8, LANES), lambda s: (0, 0)),
        ],
        out_shape=[
            shape_of((tokens, width), BF16),
            shape_of((tokens, parts * c), F32),
            shape_of((tokens, parts * c), F32),
            shape_of((8, LANES), F32),
        ],
        compiler_params=params(48),
        cost_estimate=cost(2 * tokens * width * parts * c, 50 * MIB),
        name="hidden",
    )(normed, level, near, far, bias)


def second_norm_kernel(
    order_ref, act_ref, slope_ref, level_ref, near_ref, far_ref, normed_ref, grad_ref, row_ref,
    quant_ref, back_ref, out_ref, sum_ref, branch_ref, terms_ref
):
    level = level_ref[0:1, 0:1]
    tangent = jnp.tanh(act_ref[...] / level)
    quant = low(level * tangent)
    quant_ref[...] = quant
    back_ref[...] = (1.0 - tangent * tangent) * slope_ref[...]
    summed = normed_ref[...] + project(quant, near_ref, far_ref) + row_ref[0:1, :]
    normal, inverse = norm_parts(summed)
    gain = row_ref[1:2, :]
    put_blocks(out_ref, order_ref, low(normal * gain + row_ref[2:3, :]))
    upstream = take_blocks(grad_ref, order_ref).astype(F32)
    grad_sum = norm_back(upstream, normal, inverse, gain)
    sum_ref[...] = grad_sum
    branch_ref[...] = low(grad_sum)
    add_sums(terms_ref, (grad_sum, upstream * normal, upstream))


def second_norm(active, slope, level, weights, normed, grad, vectors, order):
    near, far = weights
    tokens, width = normed.shape
    inner = active.shape[1]
    rows = 128

    def block(columns):
        return pl.BlockSpec((rows, columns), lambda t: (t, 0))

    return pl.pallas_call(
        second_norm_kernel,
        grid=(tokens // rows,),
        in_specs=[
            in_smem(),
            block(inner),
            block(inner),
            whole(level),
            whole(near),
            whole(far),
            block(width),
            block(width),
            whole(vectors),
        ],
        out_specs=[
            block(inner),
            block(inner),
            block(width),
            block(width),
            block(width),
            pl.BlockSpec((8, width), lambda t: (0, 0)),
        ],
        out_shape=[
            shape_of((tokens, inner), BF16),
            shape_of((tokens, inner), F32),
            shape_of((tokens, width), BF16),
            shape_of((tokens, width), F32),
            shape_of((tokens, width), BF16),
            shape_of((8, width), F32),
        ],
        compiler_params=params(56),
        cost_estimate=cost(2 * tokens * width * inner, 80 * MIB),
        name="second_norm",
    )(order, active, slope, level, near, far, normed, grad, vectors)


def weight_grad_kernel(count, x_ref, *refs):
    h_refs, (keep_ref, send_ref, turned_ref) = refs[:count], refs[count:]
    half = turned_ref.shape[0] // 2

    @pl.when((pl.program_id(0) == 0) & (pl.program_id(1) == 0))
    def _():
        turned_ref[...] = x_ref[...].T

    for i, h_ref in enumerate(h_refs):
        h = h_ref[...]
        keep_ref[:, i] = dot(turned_ref[:half, :], h).reshape(keep_ref.shape[0], -1, h.shape[1])
        send_ref[:, i] = low(dot(turned_ref[half:, :], h)).reshape(keep_ref.shape[0], -1, h.shape[1])


def weight_grad(x, grads, parts, plane):
    tokens, width = x.shape
    count = len(grads)
    c = grads[0].shape[1] // parts
    rows = width // (2 * plane)
    step = min(c, 512)
    cuts = c // step
    dims = (plane, parts, count, rows, c)
    out_spec = pl.BlockSpec((plane, None, count, rows, step), lambda r, j: (0, r, 0, 0, j))
    return pl.pallas_call(
        partial(weight_grad_kernel, count),
        grid=(parts, cuts),
        in_specs=[whole(x)]
        + [pl.BlockSpec((tokens, step), lambda r, j: (0, r * cuts + j))] * count,
        out_specs=[out_spec, out_spec],
        out_shape=[shape_of(dims, F32), shape_of(dims, BF16)],
        scratch_shapes=[pltpu.VMEM((width, tokens), BF16)],
        compiler_params=params(48),
        cost_estimate=cost(2 * tokens * width * parts * c * count, 8 * width * parts * c * count),
        name="weight_grad",
    )(x, *grads)


def grad_hidden_kernel(g_ref, near_ref, far_ref, back_ref, o_ref, sum_ref):
    tokens, width = g_ref.shape
    half = width // 2
    rows = 256
    sum_ref[...] = jnp.zeros_like(sum_ref)

    @pl.loop(0, tokens // rows)
    def _(step):
        here = pl.ds(pl.multiple_of(step * rows, rows), rows)
        grad = dot(g_ref[here, :half], flat(near_ref[...]))
        grad = grad + dot(g_ref[here, half:], flat(far_ref[...]))
        grad = low(grad * back_ref[here, :])
        o_ref[here, :] = grad
        sum_ref[...] += jnp.sum(grad.astype(F32), axis=0, keepdims=True)


def grad_hidden_rows(grad, weights, back):
    near, far = weights
    plane, parts, rows, c = near.shape
    tokens, width = grad.shape
    step = min(c, 512)
    cuts = c // step
    weight_spec = pl.BlockSpec((plane, None, rows, step), lambda s: (0, s // cuts, 0, s % cuts))
    block = pl.BlockSpec((tokens, step), lambda s: (0, s))
    return pl.pallas_call(
        grad_hidden_kernel,
        grid=(parts * cuts,),
        in_specs=[whole(grad), weight_spec, weight_spec, block],
        out_specs=[block, pl.BlockSpec((1, step), lambda s: (0, s))],
        out_shape=[shape_of((tokens, parts * c), BF16), shape_of((1, parts * c), F32)],
        compiler_params=params(48),
        cost_estimate=cost(2 * tokens * width * parts * c, 34 * MIB),
        name="grad_hidden",
    )(grad, near, far, back)


def first_back_kernel(
    g_ref, near_ref, far_ref, normed_ref, normal_ref, inverse_ref, sum_two_ref, level_ref, row_ref,
    sum_ref, low_ref, terms_ref
):
    level = level_ref[0:1, 0:1]
    tangent = jnp.tanh(normed_ref[...] / level)
    grad = project(g_ref[...], near_ref, far_ref) * (1.0 - tangent * tangent) + sum_two_ref[...]
    normal = normal_ref[...]
    grad_sum = norm_back(grad, normal, inverse_ref[...], row_ref[1:2, :])
    sum_ref[...] = grad_sum
    low_ref[...] = low(grad_sum)
    add_sums(terms_ref, (grad_sum, grad * normal, grad))


def first_back(grad, weights, normed, normal, inverse, sum_two, level, vectors):
    near, far = weights
    tokens, width = normed.shape
    inner = grad.shape[1]
    rows = 256

    def block(columns):
        return pl.BlockSpec((rows, columns), lambda t: (t, 0))

    return pl.pallas_call(
        first_back_kernel,
        grid=(tokens // rows,),
        in_specs=[
            block(inner),
            whole(near),
            whole(far),
            block(width),
            block(width),
            block(1),
            block(width),
            whole(level),
            whole(vectors),
        ],
        out_specs=[block(width), block(width), pl.BlockSpec((8, width), lambda t: (0, 0))],
        out_shape=[
            shape_of((tokens, width), F32),
            shape_of((tokens, width), BF16),
            shape_of((8, width), F32),
        ],
        compiler_params=params(56),
        cost_estimate=cost(2 * tokens * width * inner, 36 * MIB),
        name="first_back",
    )(grad, near, far, normed, normal, inverse, sum_two, level, vectors)


def grad_context_kernel(g_ref, near_ref, far_ref, ctx_ref, level_ref, o_ref):
    half = g_ref.shape[1] // 2
    level = level_ref[0:1, 0:1]
    tangent = jnp.tanh(ctx_ref[...] / level)
    grad = dot(g_ref[:, :half], flat(near_ref[...])) + dot(g_ref[:, half:], flat(far_ref[...]))
    o_ref[...] = low(grad * (1.0 - tangent * tangent))


def grad_context_rows(grad, weights, context, level):
    near, far = weights
    plane, parts, rows, c = near.shape
    tokens, width = grad.shape
    weight_spec = pl.BlockSpec((plane, None, rows, c), lambda r: (0, r, 0, 0))
    block = pl.BlockSpec((tokens, c), lambda r: (0, r))
    return pl.pallas_call(
        grad_context_kernel,
        grid=(parts,),
        in_specs=[whole(grad), weight_spec, weight_spec, block, whole(level)],
        out_specs=block,
        out_shape=shape_of((tokens, parts * c), BF16),
        compiler_params=params(40),
        cost_estimate=cost(2 * tokens * width * parts * c, 10 * MIB),
        name="grad_context",
    )(grad, near, far, context, level)


def grad_input_kernel(order_ref, q_ref, k_ref, v_ref, near_ref, far_ref, sum_ref, x_ref, level_ref, o_ref):
    level = level_ref[0:1, 0:1]
    total = None
    for i, ref in enumerate((q_ref, k_ref, v_ref)):
        term = project(ref[...], near_ref.at[:, :, i], far_ref.at[:, :, i])
        total = term if total is None else total + term
    tangent = jnp.tanh(take_blocks(x_ref, order_ref).astype(F32) / level)
    put_blocks(o_ref, order_ref, low(sum_ref[...] + total * (1.0 - tangent * tangent)))


def grad_input(grads, weights, grad_sum, x, level, order):
    near, far = weights
    tokens, width = x.shape
    inner = grads[0].shape[1]
    rows = 256

    def block(columns):
        return pl.BlockSpec((rows, columns), lambda t: (t, 0))

    return pl.pallas_call(
        grad_input_kernel,
        grid=(tokens // rows,),
        in_specs=[
            in_smem(),
            block(inner),
            block(inner),
            block(inner),
            whole(near),
            whole(far),
            block(width),
            block(width),
            whole(level),
        ],
        out_specs=block(width),
        out_shape=shape_of((tokens, width), BF16),
        compiler_params=params(48),
        cost_estimate=cost(6 * tokens * width * inner, 20 * MIB),
        name="grad_input",
    )(order, *grads, near, far, grad_sum, x, level)


def doc_segments(doc_lengths, length):
    doc_ends = jnp.cumsum(doc_lengths, axis=1, dtype=jnp.int32)
    places = jnp.arange(length, dtype=jnp.int32)
    return jnp.sum(
        (places[None, :, None] >= doc_ends[:, None, :]).astype(jnp.int32), axis=2, dtype=jnp.int32
    )


def soft_clip(values, clip_level):
    return clip_level * jnp.tanh(values / clip_level)


def clip_slope(values, clip_level):
    tangent = jnp.tanh(values / clip_level)
    return 1.0 - tangent * tangent


def by_distance(values, axis_name, axis):
    count, me = lax.axis_size(axis_name), lax.axis_index(axis_name)
    dims = values.shape
    split = values.reshape(dims[:axis] + (count, dims[axis] // count) + dims[axis + 1 :])
    moved = jnp.take(split, me ^ jnp.arange(count), axis=axis)
    return moved.reshape(dims)


def own_block(values, axis):
    rows = values.shape[axis] // lax.axis_size("dp")
    return lax.dynamic_slice_in_dim(values, lax.axis_index("dp") * rows, rows, axis)


def local(
    mesh, layer_input, grad_output, doc_lengths, ranges, w_qkv, bias_qv, w_out, b_out, gain_one,
    shift_one, w_in, b_in, w_down, b_down, gain_two, shift_two
):
    datas, parts = lax.axis_size("dp"), lax.axis_size("tensor")
    data, part = lax.axis_index("dp"), lax.axis_index("tensor")
    plane = datas // 2
    tokens, width = layer_input.shape
    rows = width // datas

    places = jnp.arange(datas)
    distance = (places % plane) * 2 + places // plane
    blocks = data ^ distance
    if rows % LANES == 0:
        per_block = rows // LANES
        order = (blocks[:, None] * per_block + jnp.arange(per_block)).reshape(-1).astype(jnp.int32)
    else:
        order = jnp.arange(width // LANES, dtype=jnp.int32)

    def arrange(values):
        split = values.reshape(values.shape[:-1] + (datas, rows))
        return jnp.take(split, blocks, axis=-2).reshape(values.shape)

    def restore(values):
        split = values.reshape(values.shape[:-1] + (datas, rows))
        back = jnp.zeros((datas,), jnp.int32).at[blocks].set(places.astype(jnp.int32))
        return jnp.take(split, back, axis=-2).reshape(values.shape)

    def arrange_rows(values):
        return values if rows % LANES == 0 else arrange(values)

    def restore_rows(values):
        return values if rows % LANES == 0 else restore(values)

    x = arrange_rows(layer_input)
    upstream = arrange_rows(grad_output)
    vectors_one = jnp.zeros((8, width), F32).at[:3].set(
        arrange(jnp.stack([b_out, gain_one, shift_one]).astype(F32))
    )
    vectors_two = jnp.zeros((8, width), F32).at[:3].set(
        arrange(jnp.stack([b_down, gain_two, shift_two]).astype(F32))
    )

    own = [
        own_block(w_qkv, 1),
        own_block(w_out, 1).T[None],
        own_block(w_in, 0)[None],
        own_block(w_down, 1).T[None],
    ]
    own = [values.astype(F32) for values in own]
    peaks = [jnp.max(jnp.abs(own[0][i]), axis=0) for i in range(3)]
    peaks += [jnp.max(jnp.abs(values[0]), axis=0) for values in own[1:]]
    peaks += [jnp.max(jnp.abs(x.astype(F32)), axis=0)]
    peaks = [jnp.max(values.reshape(-1, LANES), axis=0) for values in peaks]
    peaks = jnp.stack(peaks + [jnp.zeros_like(peaks[0])])
    reached = exchange_all(peaks, mesh, "rows", ranges[:1])
    weight_levels = 0.5 * reached[:6, 0]
    level_input = DECAY * ranges[0] + (1.0 - DECAY) * reached[6:7, 0:1]
    level_input = jnp.broadcast_to(level_input, (8, LANES))
    own_levels = [weight_levels[:3][:, None, None]] + [weight_levels[i] for i in (3, 4, 5)]
    quant_own = [low(soft_clip(values, level)) for values, level in zip(own, own_levels)]
    slopes = [clip_slope(values, level) for values, level in zip(own, own_levels)]

    weights_qkv = gather(quant_own[0])
    weights_out, weights_in, weights_down = [
        tuple(side[:, :, 0] for side in gather(values)) for values in quant_own[1:]
    ]
    biases = jnp.concatenate([bias_qv.reshape(-1), b_in]).astype(BF16)[None]
    for bit in reversed(range(bits_of("tensor"))):
        other = swap(biases, "tensor", bit)
        biases = jnp.stack([biases, other], axis=1).reshape(-1, biases.shape[1])
    columns = bias_qv.shape[1]
    bias_q = biases[:, :columns].reshape(1, -1)
    bias_v = biases[:, columns : 2 * columns].reshape(1, -1)
    bias_qkv = jnp.stack([bias_q, jnp.zeros_like(bias_q), bias_v]).astype(F32)
    bias_hidden = biases[:, 2 * columns :].reshape(1, -1).astype(F32)

    held = tokens // SEQ
    lengths_here = lax.dynamic_slice_in_dim(doc_lengths, part * held, held, 0)
    segments = doc_segments(lengths_here, SEQ).astype(F32)
    seg_cols, seg_rows = segments[:, :, None], segments[:, None, :]

    quant_input = quant_rows(x, level_input, order)
    qkv = qkv_rows(quant_input, weights_qkv, bias_qkv)
    context, lse, peak = attend(qkv, seg_cols, seg_rows)
    level_context = exchange_all(peak, mesh, "level", ranges[1:2])
    quant_context, normed, normal_one, inverse_one, peak = first_norm(
        context, level_context, weights_out, x, vectors_one, order
    )
    level_normed = exchange_all(peak, mesh, "level", ranges[2:3])
    quant_normed, active, slope, peak = hidden_rows(normed, level_normed, weights_in, bias_hidden)
    level_active = exchange_all(peak, mesh, "level", ranges[3:4])
    quant_active, back, output, grad_sum_two, grad_branch, terms_two = second_norm(
        active, slope, level_active, weights_down, normed, upstream, vectors_two, order
    )

    def finish(keep, send, slope):
        return spread(low(scatter(keep, send) * slope))

    down = finish(*weight_grad(grad_branch, [quant_active], parts, plane), slopes[3])
    grad_hidden, sum_hidden = grad_hidden_rows(grad_branch, weights_down, back)
    inner = finish(*weight_grad(quant_normed, [grad_hidden], parts, plane), slopes[2])
    grad_sum_one, grad_attention, terms_one = first_back(
        grad_hidden, weights_in, normed, normal_one, inverse_one, grad_sum_two, level_normed, vectors_one
    )
    outer = finish(*weight_grad(grad_attention, [quant_context], parts, plane), slopes[1])
    grad_context = grad_context_rows(grad_attention, weights_out, context, level_context)
    *grads, sum_qv = attend_back(qkv, grad_context, seg_cols, seg_rows, lse)
    first = finish(*weight_grad(quant_input, grads, parts, plane), slopes[0])
    grad_x = grad_input(grads, weights_qkv, grad_sum_one, x, level_input, order)

    back_order = (data ^ jnp.arange(datas)).astype(jnp.int32)
    back_order = (back_order % 2) * plane + back_order // 2

    def own_order(values):
        return jnp.take(values, back_order, axis=0).astype(F32)

    grad_w_qkv = own_order(first).transpose(1, 0, 2, 3).reshape(w_qkv.shape)
    grad_w_in = own_order(inner).reshape(w_in.shape)
    grad_w_out = own_order(outer).reshape(width, -1).T
    grad_w_down = own_order(down).reshape(width, -1).T

    sums = jnp.concatenate([restore(terms_one[:3]), restore(terms_two[:3])])
    sum_qv = jnp.sum(sum_qv, axis=0)[:2]
    sum_qv = by_distance(sum_qv, "tensor", 1)
    sum_hidden = by_distance(sum_hidden, "tensor", 1).reshape(-1, width)
    sums = jnp.concatenate([sums, sum_qv, sum_hidden])
    padded = jnp.zeros((-(-sums.shape[0] // 8) * 8, width), F32).at[: sums.shape[0]].set(sums)
    sums = exchange_all(padded, mesh, "sum", ranges[:1])
    hidden_all = sums[8 : 8 + sum_hidden.shape[0]].reshape(-1)
    grad_bias_qv = lax.dynamic_slice_in_dim(sums[6:8], part * columns, columns, 1)
    grad_b_in = lax.dynamic_slice_in_dim(hidden_all, part * b_in.shape[0], b_in.shape[0], 0)
    new_ranges = jnp.stack(
        [level_input[0, 0], level_context[0, 0], level_normed[0, 0], level_active[0, 0]]
    )
    return (
        restore_rows(output),
        restore_rows(grad_x),
        grad_w_qkv,
        grad_bias_qv,
        grad_w_out,
        sums[0],
        sums[1],
        sums[2],
        grad_w_in,
        grad_b_in,
        grad_w_down,
        sums[3],
        sums[4],
        sums[5],
        new_ranges,
    )


def solution(mesh):
    in_specs = (
        P(("dp", "tensor"), None),
        P(("dp", "tensor"), None),
        P("dp", None),
        P(),
        P(None, None, "tensor"),
        P(None, "tensor"),
        P("tensor", None),
        P(),
        P(),
        P(),
        P(None, "tensor"),
        P("tensor"),
        P("tensor", None),
        P(),
        P(),
        P(),
    )
    out_specs = (
        P(("dp", "tensor"), None),
        P(("dp", "tensor"), None),
        P(None, None, "tensor"),
        P(None, "tensor"),
        P("tensor", None),
        P(),
        P(),
        P(),
        P(None, "tensor"),
        P("tensor"),
        P("tensor", None),
        P(),
        P(),
        P(),
        P(),
    )
    return jax.shard_map(
        partial(local, mesh), mesh=mesh, in_specs=in_specs, out_specs=out_specs, check_vma=False
    )
```

time: 2590 us -> 802 us (0.31)
  waiting for transfers between devices: 1760 us -> 194 us
  matrix products: 360 us -> 0 us
  Pallas kernels: 0 us -> 327 us
  blocking collectives: 218 us -> 0 us
  starting transfers between devices: 0.37 us -> 85.8 us
  local copies, waits for them, and re-layouts: 120 us -> 80.8 us
    reduce_scatter x4 -> x0, waiting for transfers between devices: 1010 us -> none  [the longest x1 280 us: local(): lax.psum_scatter(partial_ffn, 'tensor', scatter_dimension=0, tiled=True)]
    all_gather x4 -> x0, waiting for transfers between devices: 578 us -> none  [the longest x1 150 us: local(): branch_rows = lax.all_gather(grad_branch, 'tensor', axis=0, tiled=True)]
    dot_general x74 -> x0, matrix products: 360 us -> none  [the longest x6 92.9 us: product(): jnp.dot(first_operand, second_operand, preferred_element_type=jnp.float32)]
    pallas_call x0 -> x20, Pallas kernels: none -> 327 us  [the longest x5 64.8 us: exchange_all(): pl.pallas_call(partial(exchange_kernel, kind), out_shape=shape_of(dims, F...]
    ppermute x0 -> x82, waiting for transfers between devices: none -> 194 us  [swap(): return lax.ppermute(values, axis, [(i, i ^ 1 << bit) for i in range(count)])]
    psum x1 -> x0, waiting for transfers between devices: 173 us -> none  [local(): lax.psum((local_terms[0], local_terms[1], local_terms[2], local_terms[3],...]
    pmax x4 -> x0, blocking collectives: 161 us -> none  [the longest x1 42 us: local(): all_peaks = lax.pmax(local_peaks, ('dp', 'tensor'))]
    ppermute x0 -> x82, starting transfers between devices: none -> 85.8 us  [swap(): return lax.ppermute(values, axis, [(i, i ^ 1 << bit) for i in range(count)])]
  transfers between devices with their start and end apart: 9 -> 82, of which waited for: 9 -> 44; matrix products, arithmetic and copies ran while one was open for 3% -> 15% of each run, Pallas kernels for 0% -> 30%
where the time goes in v1:
time: 802 us; the launch traced here: 794 us
  Pallas kernels  327 us (41%)
  waiting for transfers between devices  194 us (24%)
  other arithmetic  103 us (13%)
  starting transfers between devices  85.8 us (11%)
  local copies, waits for them, and re-layouts  80.8 us (10%)
    ppermute x82, waiting for transfers between devices, swap(): return lax.ppermute(values, axis, [(i, i ^ 1 << bit) for i in range(count)])  194 us
    ppermute x82, starting transfers between devices, swap(): return lax.ppermute(values, axis, [(i, i ^ 1 << bit) for i in range(count)])  85.8 us
    pallas_call x5, Pallas kernels, exchange_all(): pl.pallas_call(partial(exchange_kernel, kind), out_shape=shape_of(dims, F...  64.8 us
    pallas_call x4, Pallas kernels, weight_grad(): pl.pallas_call(partial(weight_grad_kernel, count), grid=(parts, cuts), in...  47 us
    pallas_call x1, Pallas kernels, second_norm(): pl.pallas_call(second_norm_kernel, grid=(tokens // rows,), in_specs=[in_s...  36.9 us
    unnamed x177, local copies, waits for them, and re-layouts  34.3 us
    pallas_call x1, Pallas kernels, attend_back(): pl.pallas_call(attend_back_kernel, grid=(held, width // LANES), in_specs=...  34.2 us
    pallas_call x1, Pallas kernels, attend(): pl.pallas_call(attend_kernel, grid=(held, width // LANES), in_specs=[side...  33.5 us
  transfers between devices with their start and end apart: 82, of which 44 were waited for; matrix products, arithmetic and copies ran while one was open for 15% of the time, Pallas kernels for 30%

profile of v1, /device:TPU:0, one launch (start us, length us, event | category | flops | bytes accessed | tf_op | source)
XLA Modules:
  0.0 794.4 jit_solution(8821689335264572998)
XLA Ops:
  7.9 13.6 %exchange_rows.1 = f32[8,128]{1,0:T(8,128)} custom-call(f32[8,128]{1,0:T(8,128)} %stack.397.x_ref, f32[1]{0:T(128)} %get-tuple-element.223.range_ref), custom_call_target="tpu_custom_call" | custom-call | tf_op jit(solution)/shard_map/exchange_rows/pallas_call | solution.py:117
  40.9 17.7 %collective-permute-done = bf16[1,3,128,256]{3,2,1,0:T(8,128)(2,1)S(1)} collective-permute-done((bf16[1,3,128,256]{3,2,1,0:T(8,128)(2,1)S(1)}, bf16[1,3,128,256]{3,2,1,0:T(8,128)(2,1)S(1)}, u32[]{:S(2)}, u32[]{:S(2)}) %collective-permute-start) | collective-permute-done | bytes 196640 | tf_op jit(solution)/shard_map/ppermute | solution.py:140
  156.5 16.2 %collective-permute-done.14 = bf16[2,2,1,128,256]{4,3,0,2,1:T(8,128)(2,1)S(1)} collective-permute-done((bf16[2,2,1,128,256]{4,3,0,2,1:T(8,128)(2,1)S(1)}, bf16[2,2,1,128,256]{4,3,0,2,1:T(8,128)(2,1)S(1)}, u32[]{:S(2)}, u32[]{:S(2)}) %collective-permute-start.14) | collective-permute-done | bytes 262176 | tf_op jit(solution)/shard_map/ppermute | solution.py:140
  185.0 12.6 %collective-permute-done.26 = bf16[2,2,1,128,1024]{4,3,0,2,1:T(8,128)(2,1)S(1)} collective-permute-done((bf16[2,2,1,128,1024]{4,3,0,2,1:T(8,128)(2,1)S(1)}, bf16[2,2,1,128,1024]{4,3,0,2,1:T(8,128)(2,1)S(1)}, u32[]{:S(2)}, u32[]{:S(2)}) %collective-permute-start.26) | collective-permute-done | bytes 1048608 | tf_op jit(solution)/shard_map/ppermute | solution.py:140
  202.0 11.9 %qkv.1.q_ref.k_ref.v_ref = bf16[3,1024,1024]{2,1,0:T(8,128)(2,1)S(1)} custom-call(bf16[1024,1024]{1,0:T(8,128)(2,1)S(1)} %quant_input.1.x_ref, bf16[4,4,3,128,256]{4,3,2,1,0:T(8,128)(2,1)} %pad_maximum_fusion.2.near_ref, bf16[4,4,3,128,256]{4,3,2,1,0:T(8,128)(2,1)} %collective-permute-done.6.far_ref, f32[3,1,1024]{2,1,0:T(1,128)S(1)} %maximum_convert_fusion.b_ref), custom_call_target="tpu_custom_call" | custom-call | flops 6442450944 | bytes 14680064 | tf_op jit(solution)/shard_map/qkv/pallas_call | solution.py:274
  213.9 33.5 %attend.1 = (f32[1024,1024]{1,0:T(8,128)S(1)}, f32[2,128,512]{2,1,0:T(8,128)S(1)}, f32[8,128]{1,0:T(8,128)S(1)}) custom-call(bf16[3,1024,1024]{2,1,0:T(8,128)(2,1)S(1)} %qkv.1.q_ref.k_ref.v_ref, bf16[3,1024,1024]{2,1,0:T(8,128)(2,1)S(1)} %qkv.1.q_ref.k_ref.v_ref, bf16[3,1024,1024]{2,1,0:T(8,128)(2,1)S(1)} %qkv.1.q_ref.k_ref.v_ref, ...), custom_call_target="tpu_custom_call" | custom-call | flops 30000001024 | bytes 16777216 | tf_op jit(solution)/shard_map/attend/pallas_call | solution.py:343
  250.9 11.8 %exchange_level.3.level_ref = f32[8,128]{1,0:T(8,128)} custom-call(f32[8,128]{1,0:T(8,128)} %copy-done.24, f32[1]{0:T(128)} %get-tuple-element.222.range_ref), custom_call_target="tpu_custom_call" | custom-call | tf_op jit(solution)/shard_map/exchange_level/pallas_call | solution.py:117
  264.6 8.9 %first_norm.1 = (bf16[1024,1024]{1,0:T(8,128)(2,1)S(1)}, f32[1024,1024]{1,0:T(8,128)}, f32[1024,1024]{1,0:T(8,128)}, f32[1024,1]{1,0:T(8,128)S(1)}, f32[8,128]{1,0:T(8,128)S(1)}) custom-call(s32[8]{0:T(128)S(1)} %fusion.101.order_ref, f32[1024,1024]{1,0:T(8,128)} %copy-done.3, f32[8,128]{1,0:T(8,128)S(1)} %copy-done.15, ...), custom_call_target="tpu_custom_call" | custom-call | flops 2147483648 | bytes 20971520 | tf_op jit(solution)/shard_map/first_norm/pallas_call | solution.py:511
  276.2 10.3 %exchange_level.4.level_ref = f32[8,128]{1,0:T(8,128)} custom-call(f32[8,128]{1,0:T(8,128)} %copy-done.23, f32[1]{0:T(128)} %get-tuple-element.224.range_ref), custom_call_target="tpu_custom_call" | custom-call | tf_op jit(solution)/shard_map/exchange_level/pallas_call | solution.py:117
  288.4 32.3 %hidden.1 = (bf16[1024,1024]{1,0:T(8,128)(2,1)S(1)}, f32[1024,4096]{1,0:T(8,128)}, f32[1024,4096]{1,0:T(8,128)}, f32[8,128]{1,0:T(8,128)S(1)}) custom-call(f32[1024,1024]{1,0:T(8,128)} %get-tuple-element.90.normed_ref, f32[8,128]{1,0:T(8,128)S(1)} %copy-done.21, bf16[4,4,128,1024]{3,2,1,0:T(8,128)(2,1)} %get-tuple-element.129.near_ref, ...), custom_call_target="tpu_custom_call" | custom-call | flops 8589934592 | bytes 52428800 | tf_op jit(solution)/shard_map/hidden/pallas_call | solution.py:580
  321.4 11.4 %exchange_level.5.level_ref = f32[8,128]{1,0:T(8,128)} custom-call(f32[8,128]{1,0:T(8,128)} %copy-done.22, f32[1]{0:T(128)} %get-tuple-element.221.range_ref), custom_call_target="tpu_custom_call" | custom-call | tf_op jit(solution)/shard_map/exchange_level/pallas_call | solution.py:117
  334.0 36.9 %second_norm.1 = (bf16[1024,4096]{1,0:T(8,128)(2,1)}, f32[1024,4096]{1,0:T(8,128)}, bf16[1024,1024]{1,0:T(8,128)(2,1)}, f32[1024,1024]{1,0:T(8,128)}, bf16[1024,1024]{1,0:T(8,128)(2,1)}, /*index=5*/f32[8,1024]{1,0:T(8,128)}) custom-call(s32[8]{0:T(128)} %copy-done.19, f32[1024,4096]{1,0:T(8,128)} %get-tuple-element.92.act_ref, ...), custom_call_target="tpu_custom_call" | custom-call | flops 8589934592 | bytes 83886080 | tf_op jit(solution)/shard_map/second_norm/pallas_call | solution.py:637
  372.5 19.5 %grad_hidden.1 = (bf16[1024,4096]{1,0:T(8,128)(2,1)}, f32[1,4096]{1,0:T(1,128)S(1)}) custom-call(bf16[1024,1024]{1,0:T(8,128)(2,1)S(1)} %copy-done.26, bf16[4,4,128,1024]{3,2,1,0:T(8,128)(2,1)} %get-tuple-element.127.near_ref, bf16[4,4,128,1024]{3,2,1,0:T(8,128)(2,1)} %bitcast.100.far_ref, f32[1024,4096]{1,0:T(8,128)} %get-tuple-element.97.back_ref), custom_call_target="tpu_custom_call" | custom-call | flops 8589934592 | bytes 35651584 | tf_op jit(solution)/shard_map/grad_hidden/pallas_call | solution.py:734
  392.1 15.2 %weight_grad.6 = (f32[4,4,1,128,1024]{4,3,2,1,0:T(8,128)}, bf16[4,4,1,128,1024]{4,3,2,1,0:T(8,128)(2,1)}) custom-call(bf16[1024,1024]{1,0:T(8,128)(2,1)S(1)} %copy-done.37, bf16[1024,4096]{1,0:T(8,128)(2,1)} %get-tuple-element.98.g_ref.refs_0_), custom_call_target="tpu_custom_call" | custom-call | flops 8589934592 | bytes 33554432 | tf_op jit(solution)/shard_map/weight_grad/pallas_call | solution.py:696
  407.3 15.0 %weight_grad.7 = (f32[4,4,1,128,1024]{4,3,2,1,0:T(8,128)}, bf16[4,4,1,128,1024]{4,3,2,1,0:T(8,128)(2,1)}) custom-call(bf16[1024,1024]{1,0:T(8,128)(2,1)S(1)} %copy-done.27, bf16[1024,4096]{1,0:T(8,128)(2,1)} %get-tuple-element.120.refs_0_), custom_call_target="tpu_custom_call" | custom-call | flops 8589934592 | bytes 33554432 | tf_op jit(solution)/shard_map/weight_grad/pallas_call | solution.py:696
  422.8 18.5 %first_back.1 = (f32[1024,1024]{1,0:T(8,128)}, bf16[1024,1024]{1,0:T(8,128)(2,1)}, f32[8,1024]{1,0:T(8,128)}) custom-call(bf16[1024,4096]{1,0:T(8,128)(2,1)} %get-tuple-element.98.g_ref.refs_0_, bf16[4,4,128,1024]{3,2,1,0:T(8,128)(2,1)} %get-tuple-element.129.near_ref, bf16[4,4,128,1024]{3,2,1,0:T(8,128)(2,1)} %bitcast.80.far_ref, ...), custom_call_target="tpu_custom_call" | custom-call | flops 8589934592 | bytes 37748736 | tf_op jit(solution)/shard_map/first_back/pallas_call | solution.py:769
  459.6 34.2 %attend_back.1 = (bf16[1024,1024]{1,0:T(8,128)(2,1)S(1)}, bf16[1024,1024]{1,0:T(8,128)(2,1)S(1)}, bf16[1024,1024]{1,0:T(8,128)(2,1)S(1)}, f32[2,8,1024]{2,1,0:T(8,128)S(1)}) custom-call(bf16[3,1024,1024]{2,1,0:T(8,128)(2,1)} %copy-done.35, bf16[3,1024,1024]{2,1,0:T(8,128)(2,1)} %copy-done.35, bf16[3,1024,1024]{2,1,0:T(8,128)(2,1)} %copy-done.35, ...), custom_call_target="tpu_custom_call" | custom-call | flops 60000002048 | bytes 16777216 | tf_op jit(solution)/shard_map/attend_back/pallas_call | solution.py:419
  503.8 10.9 %weight_grad.4 = (f32[4,4,3,128,256]{4,3,2,1,0:T(8,128)}, bf16[4,4,3,128,256]{4,3,2,1,0:T(8,128)(2,1)}) custom-call(bf16[1024,1024]{1,0:T(8,128)(2,1)S(1)} %copy-done.9, bf16[1024,1024]{1,0:T(8,128)(2,1)S(1)} %copy-done.30, bf16[1024,1024]{1,0:T(8,128)(2,1)} %copy-done.32, bf16[1024,1024]{1,0:T(8,128)(2,1)} %copy-done.34), custom_call_target="tpu_custom_call" | custom-call | flops 6442450944 | bytes 25165824 | tf_op jit(solution)/shard_map/weight_grad/pallas_call | solution.py:696
  515.4 17.7 %exchange_sum.1 = f32[16,1024]{1,0:T(8,128)} custom-call(f32[16,1024]{1,0:T(8,128)} %select_maximum_fusion.x_ref, f32[1]{0:T(128)} %get-tuple-element.223.range_ref), custom_call_target="tpu_custom_call" | custom-call | tf_op jit(solution)/shard_map/exchange_sum/pallas_call | solution.py:117
  538.0 12.7 %grad_input.1 = bf16[1024,1024]{1,0:T(8,128)(2,1)} custom-call(s32[8]{0:T(128)S(1)} %copy-done.20, bf16[1024,1024]{1,0:T(8,128)(2,1)S(1)} %copy-done.31, bf16[1024,1024]{1,0:T(8,128)(2,1)S(1)} %copy-done.33, bf16[1024,1024]{1,0:T(8,128)(2,1)} %copy-done.34, bf16[4,4,3,128,256]{4,3,2,1,0:T(8,128)(2,1)} %pad_maximum_fusion.2.near_ref, ...), custom_call_target="tpu_custom_call" | custom-call | flops 6442450944 | bytes 20971520 | tf_op jit(solution)/shard_map/grad_input/pallas_call | solution.py:840
  587.2 11.2 %collective-permute-done.53 = bf16[1,64,256]{2,1,0:T(8,128)(2,1)S(1)} collective-permute-done((bf16[1,64,256]{2,1,0:T(8,128)(2,1)S(1)}, bf16[1,64,256]{2,1,0:T(8,128)(2,1)S(1)}, u32[]{:S(2)}, u32[]{:S(2)}) %collective-permute-start.53) | collective-permute-done | bytes 32800 | tf_op jit(solution)/shard_map/ppermute | solution.py:140
  605.6 13.9 %collective-permute-done.31 = bf16[2,2,3,128,256]{4,3,2,1,0:T(8,128)(2,1)S(1)} collective-permute-done((bf16[2,2,3,128,256]{4,3,2,1,0:T(8,128)(2,1)S(1)}, bf16[2,2,3,128,256]{4,3,2,1,0:T(8,128)(2,1)S(1)}, u32[]{:S(2)}, u32[]{:S(2)}) %collective-permute-start.31) | collective-permute-done | bytes 786464 | tf_op jit(solution)/shard_map/ppermute | solution.py:140
  647.4 10.2 %convert_add_fusion = f32[4,4,1,128,1024]{4,3,2,1,0:T(8,128)} fusion(f32[4,4,1,128,1024]{4,3,2,1,0:T(8,128)} %get-tuple-element.121, bf16[4,4,1,128,1024]{4,3,2,1,0:T(8,128)(2,1)} %collective-permute-done.69), kind=kLoop, calls=%fused_computation.11 | loop fusion | flops 4194304 | bytes 20971520 | tf_op jit(solution)/shard_map/add | solution.py:195
  678.1 12.1 %collective-permute-done.70 = bf16[2,2,1,128,1024]{4,3,2,1,0:T(8,128)(2,1)S(1)} collective-permute-done((bf16[2,2,1,128,1024]{4,3,2,1,0:T(8,128)(2,1)S(1)}, bf16[2,2,1,128,1024]{4,3,2,1,0:T(8,128)(2,1)S(1)}, u32[]{:S(2)}, u32[]{:S(2)}) %collective-permute-start.70) | collective-permute-done | bytes 1048608 | tf_op jit(solution)/shard_map/ppermute | solution.py:140
  (581 shorter events, 382.0 us)
Async XLA Ops:
  24.3 76.7 %collective-permute-start.23 = (bf16[1,1,128,1024]{3,2,1,0:T(8,128)(2,1)}, bf16[1,1,128,1024]{3,2,1,0:T(8,128)(2,1)}, u32[]{:S(2)}, u32[]{:S(2)}) collective-permute-start(bf16[1,1,128,1024]{3,2,1,0:T(8,128)(2,1)} %get-tuple-element.175), channel_id=1, source_target_pairs={{0,2},{1,3},{2,0},{3,1},{4,6},{5,7},{6,4},{7,5},{8,10},{9,11},{10,... | collective-permute-start | bytes 786440 | tf_op jit(solution)/shard_map/ppermute | solution.py:140
  29.0 53.1 %collective-permute-start.16 = (bf16[1,1,128,1024]{3,2,1,0:T(8,128)(2,1)}, bf16[1,1,128,1024]{3,2,1,0:T(8,128)(2,1)}, u32[]{:S(2)}, u32[]{:S(2)}) collective-permute-start(bf16[1,1,128,1024]{3,2,1,0:T(8,128)(2,1)} %get-tuple-element.131), channel_id=1, source_target_pairs={{0,2},{1,3},{2,0},{3,1},{4,6},{5,7},{6,4},{7,5},{8,10},{9,11},{10,... | collective-permute-start | bytes 786440 | tf_op jit(solution)/shard_map/ppermute | solution.py:140
  30.9 27.7 %collective-permute-start = (bf16[1,3,128,256]{3,2,1,0:T(8,128)(2,1)S(1)}, bf16[1,3,128,256]{3,2,1,0:T(8,128)(2,1)S(1)}, u32[]{:S(2)}, u32[]{:S(2)}) collective-permute-start(bf16[1,3,128,256]{3,2,1,0:T(8,128)(2,1)S(1)} %fusion.144), channel_id=1, source_target_pairs={{0,2},{1,3},{2,0},{3,1},{4,6},{5,7},{6,4},{7,5},{8,10},{9,11},{10,... | collective-permute-start | bytes 589832 | tf_op jit(solution)/shard_map/ppermute | solution.py:140
  34.3 47.5 %collective-permute-start.7 = (bf16[1,1536]{1,0:T(2,128)(2,1)}, bf16[1,1536]{1,0:T(2,128)(2,1)S(1)}, u32[]{:S(2)}, u32[]{:S(2)}) collective-permute-start(bf16[1,1536]{1,0:T(2,128)(2,1)} %broadcast_in_dim.102), channel_id=1, source_target_pairs={{0,2},{1,3},{2,0},{3,1},{4,6},{5,7},{6,4},{7,5},{8,10},{9,11},{10,... | collective-permute-start | bytes 9224 | tf_op jit(solution)/shard_map/ppermute | solution.py:140
  117.4 84.6 %collective-permute-start.6 = (bf16[4,4,3,128,256]{4,3,2,1,0:T(8,128)(2,1)}, bf16[4,4,3,128,256]{4,3,2,1,0:T(8,128)(2,1)}, u32[]{:S(2)}, u32[]{:S(2)}) collective-permute-start(bf16[4,4,3,128,256]{4,3,2,1,0:T(8,128)(2,1)} %pad_maximum_fusion.2.near_ref), channel_id=1, source_target_pairs={{0,4},{4,0},{8,12},{12,8},{16,20},{20,16},{24,28},{28,24},{1,5},{5... | collective-permute-start | bytes 9437192 | tf_op jit(solution)/shard_map/ppermute | solution.py:140
  136.9 38.7 %collective-permute-start.19 = (bf16[2,2,1,128,1024]{4,3,0,2,1:T(8,128)(2,1)}, bf16[2,2,1,128,1024]{4,3,0,2,1:T(8,128)(2,1)}, u32[]{:S(2)}, u32[]{:S(2)}) collective-permute-start(bf16[2,2,1,128,1024]{4,3,0,2,1:T(8,128)(2,1)} %get-tuple-element.139), channel_id=1, source_target_pairs={{0,8},{4,12},{8,0},{12,4},{16,24},{20,28},{24,16},{28,20},{1,9},{5... | collective-permute-start | bytes 3145736 | tf_op jit(solution)/shard_map/ppermute | solution.py:140
  142.5 34.7 %collective-permute-start.21 = (bf16[2,2,1,128,1024]{4,3,0,2,1:T(8,128)(2,1)}, bf16[2,2,1,128,1024]{4,3,0,2,1:T(8,128)(2,1)}, u32[]{:S(2)}, u32[]{:S(2)}) collective-permute-start(bf16[2,2,1,128,1024]{4,3,0,2,1:T(8,128)(2,1)} %get-tuple-element.143), channel_id=1, source_target_pairs={{0,16},{4,20},{8,24},{12,28},{16,0},{20,4},{24,8},{28,12},{1,17},{... | collective-permute-start | bytes 3145736 | tf_op jit(solution)/shard_map/ppermute | solution.py:140
  144.9 27.9 %collective-permute-start.14 = (bf16[2,2,1,128,256]{4,3,0,2,1:T(8,128)(2,1)S(1)}, bf16[2,2,1,128,256]{4,3,0,2,1:T(8,128)(2,1)S(1)}, u32[]{:S(2)}, u32[]{:S(2)}) collective-permute-start(bf16[2,2,1,128,256]{4,3,0,2,1:T(8,128)(2,1)S(1)} %get-tuple-element.181), channel_id=1, source_target_pairs={{0,16},{4,20},{8,24},{12,28},{16,0},{20,4},{24,8},{28,12},{1,17},{... | collective-permute-start | bytes 786440 | tf_op jit(solution)/shard_map/ppermute | solution.py:140
  153.1 44.5 %collective-permute-start.26 = (bf16[2,2,1,128,1024]{4,3,0,2,1:T(8,128)(2,1)S(1)}, bf16[2,2,1,128,1024]{4,3,0,2,1:T(8,128)(2,1)S(1)}, u32[]{:S(2)}, u32[]{:S(2)}) collective-permute-start(bf16[2,2,1,128,1024]{4,3,0,2,1:T(8,128)(2,1)S(1)} %get-tuple-element.133), channel_id=1, source_target_pairs={{0,8},{4,12},{8,0},{12,4},{16,24},{20,28},{24,16},{28,20},{1,9},{5... | collective-permute-start | bytes 3145736 | tf_op jit(solution)/shard_map/ppermute | solution.py:140
  172.7 25.2 %collective-permute-start.28 = (bf16[2,2,1,128,1024]{4,3,0,2,1:T(8,128)(2,1)S(1)}, bf16[2,2,1,128,1024]{4,3,0,2,1:T(8,128)(2,1)S(1)}, u32[]{:S(2)}, u32[]{:S(2)}) collective-permute-start(bf16[2,2,1,128,1024]{4,3,0,2,1:T(8,128)(2,1)S(1)} %get-tuple-element.137), channel_id=1, source_target_pairs={{0,16},{4,20},{8,24},{12,28},{16,0},{20,4},{24,8},{28,12},{1,17},{... | collective-permute-start | bytes 3145736 | tf_op jit(solution)/shard_map/ppermute | solution.py:140
  183.4 104.4 %collective-permute-start.22 = (bf16[4,4,1,128,1024]{4,3,1,0,2:T(8,128)(2,1)}, bf16[4,4,1,128,1024]{4,3,1,0,2:T(8,128)(2,1)}, u32[]{:S(2)}, u32[]{:S(2)}) collective-permute-start(bf16[4,4,1,128,1024]{4,3,1,0,2:T(8,128)(2,1)} %get-tuple-element.128), channel_id=1, source_target_pairs={{0,4},{4,0},{8,12},{12,8},{16,20},{20,16},{24,28},{28,24},{1,5},{5... | collective-permute-start | bytes 12582920 | tf_op jit(solution)/shard_map/ppermute | solution.py:140
  184.5 79.4 %collective-permute-start.15 = (bf16[4,4,1,128,256]{4,3,1,0,2:T(8,128)(2,1)}, bf16[4,4,1,128,256]{4,3,1,0,2:T(8,128)(2,1)}, u32[]{:S(2)}, u32[]{:S(2)}) collective-permute-start(bf16[4,4,1,128,256]{4,3,1,0,2:T(8,128)(2,1)} %get-tuple-element.144), channel_id=1, source_target_pairs={{0,4},{4,0},{8,12},{12,8},{16,20},{20,16},{24,28},{28,24},{1,5},{5... | collective-permute-start | bytes 3145736 | tf_op jit(solution)/shard_map/ppermute | solution.py:140
  202.0 132.0 %collective-permute-start.29 = (bf16[4,4,1,128,1024]{4,3,1,0,2:T(8,128)(2,1)}, bf16[4,4,1,128,1024]{4,3,1,0,2:T(8,128)(2,1)}, u32[]{:S(2)}, u32[]{:S(2)}) collective-permute-start(bf16[4,4,1,128,1024]{4,3,1,0,2:T(8,128)(2,1)} %get-tuple-element.126), channel_id=1, source_target_pairs={{0,4},{4,0},{8,12},{12,8},{16,20},{20,16},{24,28},{28,24},{1,5},{5... | collective-permute-start | bytes 12582920 | tf_op jit(solution)/shard_map/ppermute | solution.py:140
  407.2 213.0 %collective-permute-start.56 = (bf16[4,4,1,128,1024]{4,3,2,1,0:T(8,128)(2,1)}, bf16[4,4,1,128,1024]{4,3,2,1,0:T(8,128)(2,1)}, u32[]{:S(2)}, u32[]{:S(2)}) collective-permute-start(bf16[4,4,1,128,1024]{4,3,2,1,0:T(8,128)(2,1)} %get-tuple-element.119), channel_id=1, source_target_pairs={{0,4},{4,0},{8,12},{12,8},{16,20},{20,16},{24,28},{28,24},{1,5},{5... | collective-permute-start | bytes 12582920 | tf_op jit(solution)/shard_map/ppermute | solution.py:140
  422.3 225.2 %collective-permute-start.69 = (bf16[4,4,1,128,1024]{4,3,2,1,0:T(8,128)(2,1)}, bf16[4,4,1,128,1024]{4,3,2,1,0:T(8,128)(2,1)}, u32[]{:S(2)}, u32[]{:S(2)}) collective-permute-start(bf16[4,4,1,128,1024]{4,3,2,1,0:T(8,128)(2,1)} %get-tuple-element.122), channel_id=1, source_target_pairs={{0,4},{4,0},{8,12},{12,8},{16,20},{20,16},{24,28},{28,24},{1,5},{5... | collective-permute-start | bytes 12582920 | tf_op jit(solution)/shard_map/ppermute | solution.py:140
  455.8 94.9 %collective-permute-start.43 = (bf16[4,4,1,128,256]{4,3,2,1,0:T(8,128)(2,1)}, bf16[4,4,1,128,256]{4,3,2,1,0:T(8,128)(2,1)}, u32[]{:S(2)}, u32[]{:S(2)}) collective-permute-start(bf16[4,4,1,128,256]{4,3,2,1,0:T(8,128)(2,1)} %get-tuple-element.116), channel_id=1, source_target_pairs={{0,4},{4,0},{8,12},{12,8},{16,20},{20,16},{24,28},{28,24},{1,5},{5... | collective-permute-start | bytes 3145736 | tf_op jit(solution)/shard_map/ppermute | solution.py:140
  533.9 44.9 %collective-permute-start.30 = (bf16[4,4,3,128,256]{4,3,2,1,0:T(8,128)(2,1)}, bf16[4,4,3,128,256]{4,3,2,1,0:T(8,128)(2,1)S(1)}, u32[]{:S(2)}, u32[]{:S(2)}) collective-permute-start(bf16[4,4,3,128,256]{4,3,2,1,0:T(8,128)(2,1)} %get-tuple-element.109), channel_id=1, source_target_pairs={{0,4},{4,0},{8,12},{12,8},{16,20},{20,16},{24,28},{28,24},{1,5},{5... | collective-permute-start | bytes 9437192 | tf_op jit(solution)/shard_map/ppermute | solution.py:140
  604.2 154.7 %collective-permute-start.55 = (bf16[4,1,128,256]{3,2,0,1:T(8,128)(2,1)}, bf16[4,1,128,256]{3,2,0,1:T(8,128)(2,1)}, u32[]{:S(2)}, u32[]{:S(2)}) collective-permute-start(bf16[4,1,128,256]{3,2,0,1:T(8,128)(2,1)} %pad_maximum_fusion.36), channel_id=1, source_target_pairs={{0,4},{4,0},{8,12},{12,8},{16,20},{20,16},{24,28},{28,24},{1,5},{5... | collective-permute-start | bytes 786440 | tf_op jit(solution)/shard_map/ppermute | solution.py:140
  604.5 24.4 %collective-permute-start.35 = (bf16[2,3,128,256]{3,2,1,0:T(8,128)(2,1)S(1)}, bf16[2,3,128,256]{3,2,1,0:T(8,128)(2,1)S(1)}, u32[]{:S(2)}, u32[]{:S(2)}) collective-permute-start(bf16[2,3,128,256]{3,2,1,0:T(8,128)(2,1)S(1)} %fusion.47), channel_id=1, source_target_pairs={{0,16},{4,20},{8,24},{12,28},{16,0},{20,4},{24,8},{28,12},{1,17},{... | collective-permute-start | bytes 1179656 | tf_op jit(solution)/shard_map/ppermute | solution.py:140
  628.0 47.4 %collective-permute-start.57 = (bf16[2,2,1,128,1024]{4,3,2,1,0:T(8,128)(2,1)}, bf16[2,2,1,128,1024]{4,3,2,1,0:T(8,128)(2,1)S(1)}, u32[]{:S(2)}, u32[]{:S(2)}) collective-permute-start(bf16[2,2,1,128,1024]{4,3,2,1,0:T(8,128)(2,1)} %slice.843), channel_id=1, source_target_pairs={{0,16},{4,20},{8,24},{12,28},{16,0},{20,4},{24,8},{28,12},{1,17},{... | collective-permute-start | bytes 3145736 | tf_op jit(solution)/shard_map/ppermute | solution.py:140
  638.6 37.2 %collective-permute-start.60 = (bf16[2,2,1,128,1024]{4,3,1,2,0:T(8,128)(2,1)}, bf16[2,2,1,128,1024]{4,3,1,2,0:T(8,128)(2,1)S(1)}, u32[]{:S(2)}, u32[]{:S(2)}) collective-permute-start(bf16[2,2,1,128,1024]{4,3,1,2,0:T(8,128)(2,1)} %fusion.3), channel_id=1, source_target_pairs={{0,8},{4,12},{8,0},{12,4},{16,24},{20,28},{24,16},{28,20},{1,9},{5... | collective-permute-start | bytes 3145736 | tf_op jit(solution)/shard_map/ppermute | solution.py:140
  675.3 88.6 %collective-permute-start.42 = (bf16[4,3,128,256]{3,2,1,0:T(8,128)(2,1)}, bf16[4,3,128,256]{3,2,1,0:T(8,128)(2,1)}, u32[]{:S(2)}, u32[]{:S(2)}) collective-permute-start(bf16[4,3,128,256]{3,2,1,0:T(8,128)(2,1)} %pad_maximum_fusion.19), channel_id=1, source_target_pairs={{0,4},{4,0},{8,12},{12,8},{16,20},{20,16},{24,28},{28,24},{1,5},{5... | collective-permute-start | bytes 2359304 | tf_op jit(solution)/shard_map/ppermute | solution.py:140
  675.8 28.4 %collective-permute-start.58 = (bf16[2,1,128,1024]{3,2,0,1:T(8,128)(2,1)S(1)}, bf16[2,1,128,1024]{3,2,0,1:T(8,128)(2,1)S(1)}, u32[]{:S(2)}, u32[]{:S(2)}) collective-permute-start(bf16[2,1,128,1024]{3,2,0,1:T(8,128)(2,1)S(1)} %fusion.26), channel_id=1, source_target_pairs={{0,8},{4,12},{8,0},{12,4},{16,24},{20,28},{24,16},{28,20},{1,9},{5... | collective-permute-start | bytes 1572872 | tf_op jit(solution)/shard_map/ppermute | solution.py:140
  705.4 23.8 %collective-permute-start.59 = (bf16[1,1,128,1024]{3,2,1,0:T(8,128)(2,1)S(1)}, bf16[1,1,128,1024]{3,2,1,0:T(8,128)(2,1)S(1)}, u32[]{:S(2)}, u32[]{:S(2)}) collective-permute-start(bf16[1,1,128,1024]{3,2,1,0:T(8,128)(2,1)S(1)} %fusion.59), channel_id=1, source_target_pairs={{0,1},{1,0},{2,3},{3,2},{4,5},{5,4},{6,7},{7,6},{8,9},{9,8},{10,11... | collective-permute-start | bytes 786440 | tf_op jit(solution)/shard_map/ppermute | solution.py:140
  (143 other events, 2248.0 us)

commit v2 on v1

--- a/solution.py
+++ b/solution.py
@@ -96,8 +96,6 @@
         lax.fori_loop(1, count, start, 0)
         slots[0] = source[...]
         lax.fori_loop(1, count, finish, 0)
-        if kind == "sum":
-            return jnp.sum(slots[...], axis=0)
         return jnp.max(slots[...], axis=0)
 
     mid[...] = exchange(x_ref, near, near_send, near_recv, to_data, datas)
@@ -129,15 +127,20 @@
             copies((parts,)),
         ],
         compiler_params=pltpu.CompilerParams(
-            collective_id={"rows": 0, "level": 1, "sum": 2}[kind], has_side_effects=True
+            collective_id={"rows": 0, "level": 1}[kind], has_side_effects=True
         ),
         name="exchange_" + kind,
     )(values, previous)
 
 
-def swap(values, axis, bit):
+def tie(values, others):
+    return lax.optimization_barrier((values, *others))[0]
+
+
+def swap(values, axis, bit, token=None):
     count = lax.axis_size(axis)
-    return lax.ppermute(values, axis, [(i, i ^ (1 << bit)) for i in range(count)])
+    other = lax.ppermute(values, axis, [(i, i ^ (1 << bit)) for i in range(count)])
+    return other if token is None else tie(other, [token])
 
 
 def bits_of(axis):
@@ -149,63 +152,456 @@
     return plane, (plane[::-1], plane)
 
 
-def spread_plane(values, order):
-    held = []
-    for bit in order:
-        other = swap(values, "dp", bit)
-        place = sum(1 for seen in held if seen > bit)
-        values = jnp.stack([values, other], axis=place)
-        held.append(bit)
-    return values.reshape((-1,) + values.shape[len(held) :])
-
-
-def gather(piece):
-    held = piece[None]
-    for bit in reversed(range(bits_of("tensor"))):
-        other = swap(held, "tensor", bit)
-        held = jnp.stack([held, other], axis=1).reshape((-1,) + piece.shape)
-    half = held.shape[0] // 2
-    _, orders = plane_orders()
-    sides = [spread_plane(held[:half], orders[0]), spread_plane(held[half:], orders[1])]
-    near = jnp.concatenate(sides, axis=1)
-    return near, swap(near, "dp", 0)
+def run_all(chain, token=None):
+    try:
+        chain.send(token)
+        while True:
+            next(chain)
+    except StopIteration as done:
+        return done.value
 
 
 def low(values):
     return values.astype(BF16)
 
 
-def scatter_side(values, order):
-    plane, _ = plane_orders()
-    values = values.reshape((2,) * len(plane) + values.shape[1:])
-    left = plane[::-1]
-    for bit in order:
-        place = left.index(bit)
-        keep = lax.index_in_dim(values, 0, place, keepdims=False)
-        send = lax.index_in_dim(values, 1, place, keepdims=False)
-        values = keep + swap(low(send), "dp", bit).astype(F32)
-        left.remove(bit)
+def scatter_plane(keep, send):
+    plane, orders = plane_orders()
+    token = yield [send]
+    values = keep + swap(send, "dp", 0, token).astype(F32)
+    half = values.shape[1] // 2
+    sides = [values[:, :half], values[:, half:]]
+    sides = [side.reshape((2,) * len(plane) + side.shape[1:]) for side in sides]
+    left = [plane[::-1], plane[::-1]]
+    for step in range(len(plane)):
+        places = [left[i].index(orders[i][step]) for i in range(2)]
+        sends = [low(lax.index_in_dim(sides[i], 1, places[i], keepdims=False)) for i in range(2)]
+        token = yield sends
+        for i in range(2):
+            bit = orders[i][step]
+            keep = lax.index_in_dim(sides[i], 0, places[i], keepdims=False)
+            sides[i] = keep + swap(sends[i], "dp", bit, token).astype(F32)
+            left[i].remove(bit)
+    return sides
+
+
+def scatter_all(keep, send):
+    sides = yield from scatter_plane(keep, send)
     for bit in range(bits_of("tensor") - 1):
-        pairs = values.reshape((-1, 2) + values.shape[1:])
-        values = pairs[:, 0] + swap(low(pairs[:, 1]), "tensor", bit).astype(F32)
-    return values[0]
-
-
-def scatter(keep, send):
-    summed = keep + swap(send, "dp", 0).astype(F32)
-    half = summed.shape[1] // 2
-    _, orders = plane_orders()
-    near = scatter_side(summed[:, :half], orders[0])
-    far = scatter_side(summed[:, half:], orders[1])
-    return near + swap(low(far), "tensor", bits_of("tensor") - 1).astype(F32)
-
-
-def spread(piece):
-    half = piece.shape[1] // 2
-    _, orders = plane_orders()
-    sides = [spread_plane(piece[:, :half], orders[0]), spread_plane(piece[:, half:], orders[1])]
-    near = jnp.concatenate(sides, axis=2)
-    return jnp.concatenate([near, swap(near, "dp", 0)], axis=0)
+        pairs = [values.reshape((-1, 2) + values.shape[1:]) for values in sides]
+        sends = [low(values[:, 1]) for values in pairs]
+        token = yield sends
+        sides = [
+            values[:, 0] + swap(send, "tensor", bit, token).astype(F32)
+            for values, send in zip(pairs, sends)
+        ]
+    send = low(sides[1][0])
+    token = yield [send]
+    return sides[0][0] + swap(send, "tensor", bits_of("tensor") - 1, token).astype(F32)
+
+
+def at_distance(axis, r):
+    me, index = lax.axis_index(axis), 0
+    for bit in range(bits_of(axis)):
+        index = index + (me // (1 << bit) + (r >> bit)) % 2 * (1 << bit)
+    return index
+
+
+def plane_moves():
+    plane = 1 << (bits_of("dp") - 1)
+    if plane == 4:
+        return [(1, 2), (2, 4)], [(3, 1, 4, 0), (3, 2, 2, 1)]
+    return [(slot, 2 * slot) for slot in range(1, plane)], []
+
+
+class Mover:
+    def __init__(self, send, recv, local):
+        self.send, self.recv, self.local = send, recv, local
+        self.count, self.local_count = 0, 0
+
+    def remote(self, source, target, axis, r):
+        i = self.count
+        self.count += 1
+        return pltpu.make_async_remote_copy(
+            src_ref=source,
+            dst_ref=target,
+            send_sem=self.send.at[i],
+            recv_sem=self.recv.at[i],
+            device_id={axis: at_distance(axis, r)},
+            device_id_type=MESH,
+        )
+
+    def own(self, source, target):
+        i = self.local_count
+        self.local_count += 1
+        return pltpu.make_async_copy(source, target, self.local.at[i])
+
+
+def greet(distances):
+    barrier = pltpu.get_barrier_semaphore()
+    for axis, r in distances:
+        pl.semaphore_signal(
+            barrier, inc=1, device_id={axis: at_distance(axis, r)}, device_id_type=MESH
+        )
+    pl.semaphore_wait(barrier, len(distances))
+
+
+def part_distances():
+    return [("tensor", r) for r in range(1, 1 << bits_of("tensor"))]
+
+
+def plane_distances():
+    first, second = plane_moves()
+    apart = sorted({move[1] for move in first} | {move[2] for move in second} | {1})
+    return [("dp", r) for r in apart]
+
+
+def halves_of(ref, half):
+    rows = ref.shape[-2] // 2
+    return ref.at[..., half * rows : (half + 1) * rows, :]
+
+
+class AlongParts:
+    def __init__(self, mover, own, held):
+        self.copy = mover.own(own, held.at[0])
+        self.moves = [mover.remote(own, held.at[r], axis, r) for axis, r in part_distances()]
+
+    def start(self):
+        self.copy.start()
+        for move in self.moves:
+            move.start()
+
+    def finish(self):
+        self.copy.wait()
+        for move in self.moves:
+            move.wait()
+
+
+class OverPlane:
+    def __init__(self, mover, held, near, far):
+        first, second = plane_moves()
+        self.copy = mover.own(held, near.at[0])
+        self.first = [mover.remote(held, near.at[slot], "dp", r) for slot, r in first]
+        self.second = [
+            mover.remote(halves_of(near.at[source], half), halves_of(near.at[slot], half), "dp", r)
+            for slot, source, r, half in second
+        ]
+        sources = [held] + [near.at[slot] for slot in range(1, near.shape[0])]
+        self.cores = [mover.remote(source, far.at[i], "dp", 1) for i, source in enumerate(sources)]
+        self.early = 1 + len(first)
+
+    def start(self):
+        self.copy.start()
+        for move in self.first:
+            move.start()
+        self.cores[0].start()
+
+    def relay(self):
+        for move in self.first:
+            move.wait_recv()
+        for move in self.second + self.cores[1 : self.early]:
+            move.start()
+
+    def finish(self):
+        for move in self.second:
+            move.wait_recv()
+        for move in self.cores[self.early :]:
+            move.start()
+        self.copy.wait()
+        for move in self.first + self.second:
+            move.wait_send()
+        for move in self.cores:
+            move.wait()
+
+
+def copy_counts(plans):
+    first, second = plane_moves()
+    parts, plane = 1 << bits_of("tensor"), 1 << (bits_of("dp") - 1)
+    remote = sum(parts - 1 if kind == "parts" else len(first) + len(second) + plane for kind in plans)
+    return remote, len(plans)
+
+
+def copy_semaphores(remote, local):
+    copies = pltpu.SemaphoreType.DMA
+    return [copies((remote,)), copies((remote,)), copies((local,))]
+
+
+def anywhere():
+    return pl.BlockSpec(memory_space=pl.ANY)
+
+
+def hosting(body, counts, plans, relay_step):
+    ins, outs = counts
+
+    def kernel(*refs):
+        extra = sum(1 if kind == "parts" else 2 for kind in plans)
+        body_ins, sources = refs[:ins], list(refs[ins : ins + len(plans)])
+        rest = refs[ins + len(plans) :]
+        body_outs, targets = rest[:outs], list(rest[outs : outs + extra])
+        scratch = rest[outs + extra :]
+        body_scratch, semaphores = scratch[:-3], scratch[-3:]
+        mover = Mover(*semaphores)
+        moves = []
+        for kind in plans:
+            if kind == "parts":
+                moves.append(AlongParts(mover, sources.pop(0), targets.pop(0)))
+            else:
+                moves.append(OverPlane(mover, sources.pop(0), targets.pop(0), targets.pop(0)))
+        step, steps = 0, 1
+        for i in range(HOST_RANK[body]):
+            step = step * pl.num_programs(i) + pl.program_id(i)
+            steps = steps * pl.num_programs(i)
+        apart = plane_distances() if "plane" in plans else []
+        apart = apart + (part_distances() if "parts" in plans else [])
+
+        @pl.when(step == 0)
+        def _():
+            greet(apart)
+            for move in moves:
+                move.start()
+
+        @pl.when(step == relay_step)
+        def _():
+            for move in moves:
+                if isinstance(move, OverPlane):
+                    move.relay()
+
+        body(*body_ins, *body_outs, *body_scratch)
+
+        @pl.when(step == steps - 1)
+        def _():
+            for move in moves:
+                move.finish()
+
+    return kernel
+
+
+def gather_shapes(kind, values):
+    parts, plane = 1 << bits_of("tensor"), 1 << (bits_of("dp") - 1)
+    if kind == "parts":
+        return [shape_of((parts,) + values.shape, values.dtype)]
+    return [shape_of((plane,) + values.shape, values.dtype)] * 2
+
+
+def hosted_call(body, plans, sources, relay_step, cid, *, grid, in_specs, out_specs, out_shape, scratch_shapes=(), mib, **rest):
+    extra = [shape for kind, values in zip(plans, sources) for shape in gather_shapes(kind, values)]
+    counts = (len(in_specs), len(out_specs))
+    call = pl.pallas_call(
+        hosting(body, counts, plans, relay_step),
+        grid=grid,
+        in_specs=in_specs + [anywhere()] * len(sources),
+        out_specs=out_specs + [anywhere()] * len(extra),
+        out_shape=out_shape + extra,
+        scratch_shapes=list(scratch_shapes) + copy_semaphores(*copy_counts(plans)),
+        compiler_params=params(mib, collective_id=cid, has_side_effects=True),
+        **rest,
+    )
+
+    def run(*args):
+        results = call(*args, *sources)
+        return results[: counts[1]], results[counts[1] :]
+
+    return run
+
+
+def first_gather_kernel(first_ref, out_ref, in_ref, near, far, held_out, held_in, send, recv, own):
+    mover = Mover(send, recv, own)
+    parts, plane = near.shape[1], near.shape[0]
+    moves, relays = plane_moves()
+    keep = mover.own(first_ref, near.at[0, 0])
+    along = [mover.remote(first_ref, near.at[0, r], axis, r) for axis, r in part_distances()]
+    sources = [first_ref] + [near.at[0, r] for r in range(1, parts)]
+    over = [[mover.remote(sources[r], near.at[slot, r], "dp", d) for slot, d in moves] for r in range(parts)]
+    again = [
+        [
+            mover.remote(halves_of(near.at[source, r], half), halves_of(near.at[slot, r], half), "dp", d)
+            for slot, source, d, half in relays
+        ]
+        for r in range(parts)
+    ]
+    cores = [
+        [mover.remote(sources[r] if slot == 0 else near.at[slot, r], far.at[slot, r], "dp", 1) for slot in range(plane)]
+        for r in range(parts)
+    ]
+    later = [AlongParts(mover, out_ref, held_out), AlongParts(mover, in_ref, held_in)]
+    greet(part_distances() + plane_distances())
+    for move in along + over[0]:
+        move.start()
+    cores[0][0].start()
+    keep.start()
+    for r in range(1, parts):
+        along[r - 1].wait_recv()
+        for move in over[r] + cores[r][:1]:
+            move.start()
+    for move in along:
+        move.wait_send()
+    for move in later:
+        move.start()
+    for r in range(parts):
+        for i, (slot, _) in enumerate(moves):
+            over[r][i].wait_recv()
+            cores[r][slot].start()
+        for move in again[r]:
+            move.start()
+    for r in range(parts):
+        for move in again[r]:
+            move.wait_recv()
+        for slot in range(1 + len(moves), plane):
+            cores[r][slot].start()
+    keep.wait()
+    for r in range(parts):
+        for move in over[r] + again[r]:
+            move.wait_send()
+        for move in cores[r]:
+            move.wait()
+    for move in later:
+        move.finish()
+
+
+def first_gather(first, outer, inner):
+    parts, plane = 1 << bits_of("tensor"), 1 << (bits_of("dp") - 1)
+    moves, relays = plane_moves()
+    remote = 3 * (parts - 1) + parts * (len(moves) + len(relays) + plane)
+    return pl.pallas_call(
+        first_gather_kernel,
+        in_specs=[anywhere()] * 3,
+        out_specs=[anywhere()] * 4,
+        out_shape=[shape_of((plane, parts) + first.shape, BF16)] * 2
+        + [shape_of((parts,) + values.shape, BF16) for values in (outer, inner)],
+        scratch_shapes=copy_semaphores(remote, 3),
+        compiler_params=params(16, collective_id=3, has_side_effects=True),
+        name="first_gather",
+    )(first, outer, inner)
+
+
+class PartSum:
+    def __init__(self, mover, send, recv, slope, piece, near, far):
+        self.moves = [mover.remote(send.at[r - 1], recv.at[r - 1], axis, r) for axis, r in part_distances()]
+        self.over = OverPlane(mover, piece, near, far)
+        self.send, self.recv, self.slope, self.piece = send, recv, slope, piece
+
+    def push(self, r, values):
+        self.send[r - 1] = low(values)
+        self.moves[r - 1].start()
+
+    def reach(self, own):
+        for move in self.moves:
+            move.wait_recv()
+        total = own + jnp.sum(self.recv[...].astype(F32), axis=0)
+        self.piece[...] = low(total * self.slope[...])
+        self.over.start()
+
+    def relay(self):
+        self.over.relay()
+
+    def finish(self):
+        self.over.finish()
+        for move in self.moves:
+            move.wait_send()
+
+
+def finale_kernel(
+    down_ref, in_a, in_b, out_a, out_b, q_a, q_b, keep_ref, send_ref, slope_in, slope_out, slope_q, sums_ref,
+    near_d, far_d, near_i, far_i, near_o, far_o, near_q, far_q, sums_out,
+    send_i, recv_i, piece_i, send_o, recv_o, piece_o, send_q, recv_q, piece_q, core_recv, plane_send,
+    plane_recv, sums_near, sums_mid, sums_far, send, recv, own
+):
+    mover = Mover(send, recv, own)
+    plane, half = keep_ref.shape[0], keep_ref.shape[1]
+    parts = 2 * half
+    quarter = half // 2
+    datas = sums_near.shape[0]
+    core = mover.remote(send_ref, core_recv, "dp", 1)
+    planes = [
+        mover.remote(plane_send.at[r - 1], plane_recv.at[r - 1], "dp", 2 * r) for r in range(1, plane)
+    ]
+    down = OverPlane(mover, down_ref, near_d, far_d)
+    inner = PartSum(mover, send_i, recv_i, slope_in, piece_i, near_i, far_i)
+    outer = PartSum(mover, send_o, recv_o, slope_out, piece_o, near_o, far_o)
+    first = PartSum(mover, send_q, recv_q, slope_q, piece_q, near_q, far_q)
+    sum_data = [mover.remote(sums_ref, sums_near.at[r], "dp", r) for r in range(1, datas)]
+    sum_part = [mover.remote(sums_mid, sums_far.at[r], axis, r) for axis, r in part_distances()]
+
+    greet([("dp", r) for r in range(1, datas)] + part_distances())
+    core.start()
+    down.start()
+    for move in sum_data:
+        move.start()
+    for r in range(1, half):
+        first.push(r, (q_a if r < quarter else q_b)[r % quarter])
+    for r in range(1, parts):
+        outer.push(r, (out_a if r < half else out_b)[r % half])
+    for r in range(1, parts):
+        inner.push(r, (in_a if r < half else in_b)[r % half])
+
+    core.wait_recv()
+    for r in range(1, plane):
+        plane_send[r - 1] = low(keep_ref[r] + core_recv[r].astype(F32))
+        planes[r - 1].start()
+    for move in sum_data:
+        move.wait()
+    sums_near[0] = sums_ref[...]
+    sums_mid[...] = jnp.sum(sums_near[...], axis=0)
+    for move in sum_part:
+        move.start()
+    down.relay()
+    outer.reach(out_a[0])
+    for move in planes:
+        move.wait_recv()
+    for r in range(half):
+        total = keep_ref[0, r] + core_recv[0, r].astype(F32)
+        for i in range(plane - 1):
+            total = total + plane_recv[i, r].astype(F32)
+        first.push(half + r, total)
+    down.finish()
+    outer.relay()
+    inner.reach(in_a[0])
+    outer.finish()
+    for move in sum_part:
+        move.wait()
+    sums_far[0] = sums_mid[...]
+    sums_out[...] = jnp.sum(sums_far[...], axis=0)
+    first.reach(q_a[0])
+    inner.relay()
+    first.relay()
+    inner.finish()
+    first.finish()
+    core.wait_send()
+    for move in planes:
+        move.wait_send()
+
+
+def finale(down, inner, outer, first, raw, slopes, sums):
+    parts, plane, datas = 1 << bits_of("tensor"), 1 << (bits_of("dp") - 1), 1 << bits_of("dp")
+    keep, send = raw
+    pieces = [down, slopes[1], slopes[2], slopes[0]]
+    first_moves, second_moves = plane_moves()
+    per_plane = len(first_moves) + len(second_moves) + plane
+    remote = 1 + plane - 1 + 4 * per_plane + 4 * (parts - 1) + datas - 1
+    vmem = pl.BlockSpec(memory_space=pltpu.VMEM)
+    scratch = []
+    for piece in pieces[1:]:
+        scratch += [pltpu.VMEM((parts - 1,) + piece.shape, BF16)] * 2 + [pltpu.VMEM(piece.shape, BF16)]
+    scratch += [pltpu.VMEM(keep.shape, BF16)] + [pltpu.VMEM((plane - 1,) + keep.shape[1:], BF16)] * 2
+    scratch += [
+        pltpu.VMEM((datas,) + sums.shape, F32),
+        pltpu.VMEM(sums.shape, F32),
+        pltpu.VMEM((parts,) + sums.shape, F32),
+    ]
+    out_shape = []
+    for piece in pieces:
+        out_shape += [shape_of((plane,) + piece.shape, BF16)] * 2
+    args = (down, *inner, *outer, *first, keep, send, slopes[1], slopes[2], slopes[0], sums)
+    results = pl.pallas_call(
+        finale_kernel,
+        in_specs=[vmem] * 8 + [anywhere()] + [vmem] * 4,
+        out_specs=[anywhere()] * 8 + [vmem],
+        out_shape=out_shape + [shape_of(sums.shape, F32)],
+        scratch_shapes=scratch + copy_semaphores(remote, 4),
+        compiler_params=params(48, collective_id=2, has_side_effects=True),
+        name="finale",
+    )(*args)
+    return [results[2 * i : 2 * i + 2] for i in range(4)], results[8]
 
 
 def take_blocks(ref, order_ref):
@@ -266,13 +662,17 @@
     o_ref[...] = low(total + b_ref[...])
 
 
-def qkv_rows(x, weights, bias):
+def qkv_rows(x, weights, bias, held_out):
     near, far = weights
     plane, parts, kinds, rows, c = near.shape
     tokens, width = x.shape
     weight_spec = pl.BlockSpec((plane, None, None, rows, c), lambda r, i: (0, r, i, 0, 0))
-    return pl.pallas_call(
+    run = hosted_call(
         qkv_kernel,
+        ["plane"],
+        [held_out],
+        parts * kinds // 2,
+        4,
         grid=(parts, kinds),
         in_specs=[
             pl.BlockSpec((tokens, width), lambda r, i: (0, 0)),
@@ -280,12 +680,13 @@
             weight_spec,
             pl.BlockSpec((None, 1, c), lambda r, i: (i, 0, r)),
         ],
-        out_specs=pl.BlockSpec((None, tokens, c), lambda r, i: (i, 0, r)),
-        out_shape=shape_of((kinds, tokens, parts * c), BF16),
-        compiler_params=params(32),
+        out_specs=[pl.BlockSpec((None, tokens, c), lambda r, i: (i, 0, r))],
+        out_shape=[shape_of((kinds, tokens, parts * c), BF16)],
+        mib=32,
         cost_estimate=cost(2 * tokens * width * kinds * parts * c, 14 * MIB),
         name="qkv",
-    )(x, near, far, bias)
+    )
+    return run(x, near, far, bias)
 
 
 def fill_mask(mask_ref, col_ref, row_ref):
@@ -333,15 +734,19 @@
         lse_ref[...] = sums_ref[...].T
 
 
-def attend(qkv, cols, rows):
+def attend(qkv, cols, rows, held_in, own_down):
     _, tokens, width = qkv.shape
     held = tokens // SEQ
 
     def side(i):
         return pl.BlockSpec((None, SEQ, LANES), lambda r, j: (i, r, j))
 
-    return pl.pallas_call(
+    run = hosted_call(
         attend_kernel,
+        ["plane", "parts"],
+        [held_in, own_down],
+        held * width // LANES * 3 // 4,
+        5,
         grid=(held, width // LANES),
         in_specs=[
             side(0),
@@ -361,16 +766,23 @@
             shape_of((8, LANES), F32),
         ],
         scratch_shapes=[pltpu.VMEM((SEQ, SEQ), F32), pltpu.VMEM((SEQ, LANES), F32)],
-        compiler_params=params(40),
-        cost_estimate=cost(30e9, 16 * MIB),
+        mib=40,
+        cost_estimate=cost(30e9, 80 * MIB),
         name="attend",
-    )(qkv, qkv, qkv, cols, rows)
+    )
+    return run(qkv, qkv, qkv, cols, rows)
 
 
 def attend_back_kernel(
-    q_ref, k_ref, v_ref, g_ref, col_ref, row_ref, lse_ref, dq_ref, dk_ref, dv_ref, sum_ref, mask_ref
+    c, first, order_ref, q_ref, k_ref, v_ref, g_ref, col_ref, row_ref, lse_ref, before_ref, dq_ref, dk_ref,
+    dv_ref, sum_ref, mask_ref
 ):
     pair = pl.program_id(1)
+
+    @pl.when((pair == 0) & (pl.program_id(0) == 0))
+    def _():
+        sum_ref[...] = before_ref[...]
+
     factor = HD ** (-0.5)
 
     @pl.when(pair == 0)
@@ -385,7 +797,7 @@
         zero = jnp.zeros_like(q)
         q_own = jnp.where(own, q * jnp.asarray(factor, BF16), zero)
         g_own = jnp.where(own, g, zero)
-        logsum = lse_ref[pl.ds(pair * (LANES // HD) + head, 1), :]
+        logsum = lse_ref[pl.ds((pair + first // LANES) * (LANES // HD) + head, 1), :]
         probs = jnp.exp(dot_cols(k, q_own) + mask_ref[...] - logsum)
         v_sums.append(dot(low(probs), g))
         grad_probs = dot_cols(v, g_own)
@@ -404,22 +816,29 @@
     dq_ref[...] = dq
     dk_ref[...] = join(k_sums)
     dv_ref[...] = dv
-    sum_ref[0:1, :] = jnp.sum(dq.astype(F32), axis=0, keepdims=True)
-    sum_ref[1:2, :] = jnp.sum(dv.astype(F32), axis=0, keepdims=True)
-
-
-def attend_back(qkv, grad, cols, rows, lse):
-    _, tokens, width = qkv.shape
+    column = first + pair * LANES
+    place = order_ref[column // c] * c + column % c
+    here = pl.ds(pl.multiple_of(place, LANES), LANES)
+    sum_ref[0:1, here] += jnp.sum(dq.astype(F32), axis=0, keepdims=True)
+    sum_ref[1:2, here] += jnp.sum(dv.astype(F32), axis=0, keepdims=True)
+
+
+def attend_back(qkv, grad, cols, rows, lse, before, part_order, c, first):
+    _, tokens, inner = qkv.shape
+    width = grad.shape[1]
     held = tokens // SEQ
+    skip = first // LANES
 
     def side(i):
-        return pl.BlockSpec((None, SEQ, LANES), lambda r, j: (i, r, j))
+        return pl.BlockSpec((None, SEQ, LANES), lambda r, j: (i, r, j + skip))
 
     block = pl.BlockSpec((SEQ, LANES), lambda r, j: (r, j))
+    sums = pl.BlockSpec((8, inner), lambda r, j: (0, 0))
     return pl.pallas_call(
-        attend_back_kernel,
+        partial(attend_back_kernel, c, first),
         grid=(held, width // LANES),
         in_specs=[
+            in_smem(),
             side(0),
             side(1),
             side(2),
@@ -427,14 +846,15 @@
             pl.BlockSpec((None, SEQ, 1), lambda r, j: (r, 0, 0)),
             pl.BlockSpec((None, 1, SEQ), lambda r, j: (r, 0, 0)),
             pl.BlockSpec((None, LANES, SEQ), lambda r, j: (r, 0, 0)),
-        ],
-        out_specs=[block, block, block, pl.BlockSpec((None, 8, LANES), lambda r, j: (r, 0, j))],
-        out_shape=[shape_of((tokens, width), BF16)] * 3 + [shape_of((held, 8, width), F32)],
+            sums,
+        ],
+        out_specs=[block, block, block, sums],
+        out_shape=[shape_of((tokens, width), BF16)] * 3 + [shape_of((8, inner), F32)],
         scratch_shapes=[pltpu.VMEM((SEQ, SEQ), F32)],
         compiler_params=params(40),
-        cost_estimate=cost(60e9, 16 * MIB),
+        cost_estimate=cost(15e9, 50 * MIB),
         name="attend_back",
-    )(qkv, qkv, qkv, grad, cols, rows, lse)
+    )(part_order, qkv, qkv, qkv, grad, cols, rows, lse, before)
 
 
 def project(values, near_ref, far_ref):
@@ -464,13 +884,16 @@
     )
 
 
-def add_sums(ref, sums):
+def add_sums(ref, order_ref, sums):
     @pl.when(pl.program_id(0) == 0)
     def _():
         ref[...] = jnp.zeros_like(ref)
 
     for i, values in enumerate(sums):
-        ref[i : i + 1, :] += jnp.sum(values, axis=0, keepdims=True)
+        total = jnp.sum(values, axis=0, keepdims=True)
+        for j in range(ref.shape[1] // LANES):
+            here = pl.ds(pl.multiple_of(order_ref[j] * LANES, LANES), LANES)
+            ref[i : i + 1, here] += total[:, j * LANES : (j + 1) * LANES]
 
 
 def first_norm_kernel(
@@ -480,9 +903,10 @@
     level = level_ref[0:1, 0:1]
     quant = low(level * jnp.tanh(ctx_ref[...] / level))
     quant_ref[...] = quant
+    vectors = take_blocks(row_ref, order_ref)
     summed = take_blocks(x_ref, order_ref).astype(F32) + project(quant, near_ref, far_ref)
-    normal, inverse = norm_parts(summed + row_ref[0:1, :])
-    normed = normal * row_ref[1:2, :] + row_ref[2:3, :]
+    normal, inverse = norm_parts(summed + vectors[0:1, :])
+    normed = normal * vectors[1:2, :] + vectors[2:3, :]
     normed_ref[...] = normed
     normal_ref[...] = normal
     inverse_ref[...] = inverse
@@ -569,7 +993,7 @@
         peak_ref[...] = jnp.maximum(peak_ref[...], column_peak(active))
 
 
-def hidden_rows(normed, level, weights, bias):
+def hidden_rows(normed, level, weights, bias, held_down):
     near, far = weights
     plane, parts, rows, c = near.shape
     tokens, width = normed.shape
@@ -577,8 +1001,12 @@
     cuts = c // step
     weight_spec = pl.BlockSpec((plane, None, rows, step), lambda s: (0, s // cuts, 0, s % cuts))
     block = pl.BlockSpec((tokens, step), lambda s: (0, s))
-    return pl.pallas_call(
+    run = hosted_call(
         hidden_kernel,
+        ["plane"],
+        [held_down],
+        parts * cuts * 3 // 4,
+        6,
         grid=(parts * cuts,),
         in_specs=[
             whole(normed),
@@ -599,10 +1027,11 @@
             shape_of((tokens, parts * c), F32),
             shape_of((8, LANES), F32),
         ],
-        compiler_params=params(48),
+        mib=48,
         cost_estimate=cost(2 * tokens * width * parts * c, 50 * MIB),
         name="hidden",
-    )(normed, level, near, far, bias)
+    )
+    return run(normed, level, near, far, bias)
 
 
 def second_norm_kernel(
@@ -614,15 +1043,16 @@
     quant = low(level * tangent)
     quant_ref[...] = quant
     back_ref[...] = (1.0 - tangent * tangent) * slope_ref[...]
-    summed = normed_ref[...] + project(quant, near_ref, far_ref) + row_ref[0:1, :]
+    vectors = take_blocks(row_ref, order_ref)
+    summed = normed_ref[...] + project(quant, near_ref, far_ref) + vectors[3:4, :]
     normal, inverse = norm_parts(summed)
-    gain = row_ref[1:2, :]
-    put_blocks(out_ref, order_ref, low(normal * gain + row_ref[2:3, :]))
+    gain = vectors[4:5, :]
+    put_blocks(out_ref, order_ref, low(normal * gain + vectors[5:6, :]))
     upstream = take_blocks(grad_ref, order_ref).astype(F32)
     grad_sum = norm_back(upstream, normal, inverse, gain)
     sum_ref[...] = grad_sum
     branch_ref[...] = low(grad_sum)
-    add_sums(terms_ref, (grad_sum, upstream * normal, upstream))
+    add_sums(terms_ref, order_ref, (grad_sum, upstream * normal, upstream))
 
 
 def second_norm(active, slope, level, weights, normed, grad, vectors, order):
@@ -702,28 +1132,36 @@
         out_shape=[shape_of(dims, F32), shape_of(dims, BF16)],
         scratch_shapes=[pltpu.VMEM((width, tokens), BF16)],
         compiler_params=params(48),
-        cost_estimate=cost(2 * tokens * width * parts * c * count, 8 * width * parts * c * count),
+        cost_estimate=cost(2 * tokens * width * parts * c * count, 10 * width * parts * c * count),
         name="weight_grad",
     )(x, *grads)
 
 
-def grad_hidden_kernel(g_ref, near_ref, far_ref, back_ref, o_ref, sum_ref):
+def grad_hidden_kernel(cuts, order_ref, g_ref, near_ref, far_ref, back_ref, o_ref, sum_ref):
     tokens, width = g_ref.shape
     half = width // 2
     rows = 256
-    sum_ref[...] = jnp.zeros_like(sum_ref)
-
-    @pl.loop(0, tokens // rows)
-    def _(step):
+    block = pl.program_id(0)
+    columns = back_ref.shape[1]
+
+    @pl.when(block == 0)
+    def _():
+        sum_ref[...] = jnp.zeros_like(sum_ref)
+
+    def run(step, total):
         here = pl.ds(pl.multiple_of(step * rows, rows), rows)
         grad = dot(g_ref[here, :half], flat(near_ref[...]))
         grad = grad + dot(g_ref[here, half:], flat(far_ref[...]))
         grad = low(grad * back_ref[here, :])
         o_ref[here, :] = grad
-        sum_ref[...] += jnp.sum(grad.astype(F32), axis=0, keepdims=True)
-
-
-def grad_hidden_rows(grad, weights, back):
+        return total + jnp.sum(grad.astype(F32), axis=0, keepdims=True)
+
+    total = lax.fori_loop(0, tokens // rows, run, jnp.zeros((1, columns), F32))
+    start = pl.multiple_of((block % cuts) * columns, LANES)
+    sum_ref[pl.ds(order_ref[block // cuts], 1), pl.ds(start, columns)] = total
+
+
+def grad_hidden_rows(grad, weights, back, part_order):
     near, far = weights
     plane, parts, rows, c = near.shape
     tokens, width = grad.shape
@@ -732,32 +1170,33 @@
     weight_spec = pl.BlockSpec((plane, None, rows, step), lambda s: (0, s // cuts, 0, s % cuts))
     block = pl.BlockSpec((tokens, step), lambda s: (0, s))
     return pl.pallas_call(
-        grad_hidden_kernel,
+        partial(grad_hidden_kernel, cuts),
         grid=(parts * cuts,),
-        in_specs=[whole(grad), weight_spec, weight_spec, block],
-        out_specs=[block, pl.BlockSpec((1, step), lambda s: (0, s))],
-        out_shape=[shape_of((tokens, parts * c), BF16), shape_of((1, parts * c), F32)],
+        in_specs=[in_smem(), whole(grad), weight_spec, weight_spec, block],
+        out_specs=[block, pl.BlockSpec((parts, c), lambda s: (0, 0))],
+        out_shape=[shape_of((tokens, parts * c), BF16), shape_of((parts, c), F32)],
         compiler_params=params(48),
         cost_estimate=cost(2 * tokens * width * parts * c, 34 * MIB),
         name="grad_hidden",
-    )(grad, near, far, back)
+    )(part_order, grad, near, far, back)
 
 
 def first_back_kernel(
-    g_ref, near_ref, far_ref, normed_ref, normal_ref, inverse_ref, sum_two_ref, level_ref, row_ref,
+    order_ref, g_ref, near_ref, far_ref, normed_ref, normal_ref, inverse_ref, sum_two_ref, level_ref, row_ref,
     sum_ref, low_ref, terms_ref
 ):
     level = level_ref[0:1, 0:1]
     tangent = jnp.tanh(normed_ref[...] / level)
     grad = project(g_ref[...], near_ref, far_ref) * (1.0 - tangent * tangent) + sum_two_ref[...]
     normal = normal_ref[...]
-    grad_sum = norm_back(grad, normal, inverse_ref[...], row_ref[1:2, :])
+    gain = take_blocks(row_ref, order_ref)[1:2, :]
+    grad_sum = norm_back(grad, normal, inverse_ref[...], gain)
     sum_ref[...] = grad_sum
     low_ref[...] = low(grad_sum)
-    add_sums(terms_ref, (grad_sum, grad * normal, grad))
-
-
-def first_back(grad, weights, normed, normal, inverse, sum_two, level, vectors):
+    add_sums(terms_ref, order_ref, (grad_sum, grad * normal, grad))
+
+
+def first_back(grad, weights, normed, normal, inverse, sum_two, level, vectors, order):
     near, far = weights
     tokens, width = normed.shape
     inner = grad.shape[1]
@@ -770,6 +1209,7 @@
         first_back_kernel,
         grid=(tokens // rows,),
         in_specs=[
+            in_smem(),
             block(inner),
             whole(near),
             whole(far),
@@ -789,7 +1229,7 @@
         compiler_params=params(56),
         cost_estimate=cost(2 * tokens * width * inner, 36 * MIB),
         name="first_back",
-    )(grad, near, far, normed, normal, inverse, sum_two, level, vectors)
+    )(order, grad, near, far, normed, normal, inverse, sum_two, level, vectors)
 
 
 def grad_context_kernel(g_ref, near_ref, far_ref, ctx_ref, level_ref, o_ref):
@@ -800,16 +1240,23 @@
     o_ref[...] = low(grad * (1.0 - tangent * tangent))
 
 
-def grad_context_rows(grad, weights, context, level):
+def grad_context_rows(grad, weights, context, level, first):
     near, far = weights
     plane, parts, rows, c = near.shape
+    parts = parts // 2
     tokens, width = grad.shape
-    weight_spec = pl.BlockSpec((plane, None, rows, c), lambda r: (0, r, 0, 0))
+    weight_spec = pl.BlockSpec((plane, None, rows, c), lambda r: (0, r + first, 0, 0))
     block = pl.BlockSpec((tokens, c), lambda r: (0, r))
     return pl.pallas_call(
         grad_context_kernel,
         grid=(parts,),
-        in_specs=[whole(grad), weight_spec, weight_spec, block, whole(level)],
+        in_specs=[
+            whole(grad),
+            weight_spec,
+            weight_spec,
+            pl.BlockSpec((tokens, c), lambda r: (0, r + first)),
+            whole(level),
+        ],
         out_specs=block,
         out_shape=shape_of((tokens, parts * c), BF16),
         compiler_params=params(40),
@@ -818,12 +1265,19 @@
     )(grad, near, far, context, level)
 
 
-def grad_input_kernel(order_ref, q_ref, k_ref, v_ref, near_ref, far_ref, sum_ref, x_ref, level_ref, o_ref):
+def grad_input_kernel(order_ref, *refs):
+    g_refs, (near_ref, far_ref, sum_ref, x_ref, level_ref, o_ref) = refs[:6], refs[6:]
     level = level_ref[0:1, 0:1]
+    half = near_ref.shape[1] // 2
     total = None
-    for i, ref in enumerate((q_ref, k_ref, v_ref)):
-        term = project(ref[...], near_ref.at[:, :, i], far_ref.at[:, :, i])
-        total = term if total is None else total + term
+    for side in range(2):
+        for i in range(3):
+            term = project(
+                g_refs[side * 3 + i][...],
+                near_ref.at[:, side * half : (side + 1) * half, i],
+                far_ref.at[:, side * half : (side + 1) * half, i],
+            )
+            total = term if total is None else total + term
     tangent = jnp.tanh(take_blocks(x_ref, order_ref).astype(F32) / level)
     put_blocks(o_ref, order_ref, low(sum_ref[...] + total * (1.0 - tangent * tangent)))
 
@@ -840,23 +1294,50 @@
     return pl.pallas_call(
         grad_input_kernel,
         grid=(tokens // rows,),
-        in_specs=[
-            in_smem(),
-            block(inner),
-            block(inner),
-            block(inner),
-            whole(near),
-            whole(far),
-            block(width),
-            block(width),
-            whole(level),
-        ],
+        in_specs=[in_smem()]
+        + [block(inner)] * 6
+        + [whole(near), whole(far), block(width), block(width), whole(level)],
         out_specs=block(width),
         out_shape=shape_of((tokens, width), BF16),
         compiler_params=params(48),
-        cost_estimate=cost(6 * tokens * width * inner, 20 * MIB),
+        cost_estimate=cost(12 * tokens * width * inner, 20 * MIB),
         name="grad_input",
     )(order, *grads, near, far, grad_sum, x, level)
+
+
+def place_kernel(turn, order_ref, near_ref, far_ref, o_ref):
+    plane, kinds, rows, c = near_ref.shape
+    for core, ref in enumerate((near_ref, far_ref)):
+        for j in range(plane):
+            here = pl.ds(pl.multiple_of(order_ref[core * plane + j] * rows, rows), rows)
+            if turn:
+                o_ref[:, here] = ref[j, 0].astype(F32).T
+            else:
+                for i in range(kinds):
+                    o_ref[i, here, :] = ref[j, i].astype(F32)
+
+
+def place_grad(sides, blocks, turn):
+    near, far = sides
+    plane, kinds, rows, c = near.shape
+    width = 2 * plane * rows
+    if turn and rows % LANES:
+        split = jnp.concatenate([near, far], axis=0)[:, 0]
+        back = jnp.zeros((2 * plane,), jnp.int32).at[blocks].set(jnp.arange(2 * plane, dtype=jnp.int32))
+        return jnp.take(split, back, axis=0).astype(F32).reshape(width, c).T
+    dims = (c, width) if turn else (kinds, width, c)
+    return pl.pallas_call(
+        partial(place_kernel, turn),
+        grid=(1,),
+        in_specs=[in_smem(), whole(near), whole(far)],
+        out_specs=pl.BlockSpec(dims, lambda s: (0,) * len(dims)),
+        out_shape=shape_of(dims, F32),
+        compiler_params=params(32),
+        name="place_grad",
+    )(blocks.astype(jnp.int32), near, far)
+
+
+HOST_RANK = {qkv_kernel: 2, attend_kernel: 2, hidden_kernel: 1}
 
 
 def doc_segments(doc_lengths, length):
@@ -874,14 +1355,6 @@
 def clip_slope(values, clip_level):
     tangent = jnp.tanh(values / clip_level)
     return 1.0 - tangent * tangent
-
-
-def by_distance(values, axis_name, axis):
-    count, me = lax.axis_size(axis_name), lax.axis_index(axis_name)
-    dims = values.shape
-    split = values.reshape(dims[:axis] + (count, dims[axis] // count) + dims[axis + 1 :])
-    moved = jnp.take(split, me ^ jnp.arange(count), axis=axis)
-    return moved.reshape(dims)
 
 
 def own_block(values, axis):
@@ -923,14 +1396,11 @@
     def restore_rows(values):
         return values if rows % LANES == 0 else restore(values)
 
+    part_order = (part ^ jnp.arange(parts)).astype(jnp.int32)
     x = arrange_rows(layer_input)
     upstream = arrange_rows(grad_output)
-    vectors_one = jnp.zeros((8, width), F32).at[:3].set(
-        arrange(jnp.stack([b_out, gain_one, shift_one]).astype(F32))
-    )
-    vectors_two = jnp.zeros((8, width), F32).at[:3].set(
-        arrange(jnp.stack([b_down, gain_two, shift_two]).astype(F32))
-    )
+    vectors = jnp.stack([b_out, gain_one, shift_one, b_down, gain_two, shift_two, b_out, b_out])
+    vectors = arrange_rows(vectors).astype(F32)
 
     own = [
         own_block(w_qkv, 1),
@@ -952,10 +1422,7 @@
     quant_own = [low(soft_clip(values, level)) for values, level in zip(own, own_levels)]
     slopes = [clip_slope(values, level) for values, level in zip(own, own_levels)]
 
-    weights_qkv = gather(quant_own[0])
-    weights_out, weights_in, weights_down = [
-        tuple(side[:, :, 0] for side in gather(values)) for values in quant_own[1:]
-    ]
+    *weights_qkv, held_out, held_in = first_gather(*quant_own[:3])
     biases = jnp.concatenate([bias_qv.reshape(-1), b_in]).astype(BF16)[None]
     for bit in reversed(range(bits_of("tensor"))):
         other = swap(biases, "tensor", bit)
@@ -970,57 +1437,73 @@
     lengths_here = lax.dynamic_slice_in_dim(doc_lengths, part * held, held, 0)
     segments = doc_segments(lengths_here, SEQ).astype(F32)
     seg_cols, seg_rows = segments[:, :, None], segments[:, None, :]
+    half = parts // 2 * columns
 
     quant_input = quant_rows(x, level_input, order)
-    qkv = qkv_rows(quant_input, weights_qkv, bias_qkv)
-    context, lse, peak = attend(qkv, seg_cols, seg_rows)
+    (qkv,), weights_out = qkv_rows(quant_input, weights_qkv, bias_qkv, held_out)
+    (context, lse, peak), (*weights_in, held_down) = attend(
+        qkv, seg_cols, seg_rows, held_in, quant_own[3]
+    )
     level_context = exchange_all(peak, mesh, "level", ranges[1:2])
+    weights_out = tuple(side[:, :, 0] for side in weights_out)
+    weights_in = tuple(side[:, :, 0] for side in weights_in)
     quant_context, normed, normal_one, inverse_one, peak = first_norm(
-        context, level_context, weights_out, x, vectors_one, order
+        context, level_context, weights_out, x, vectors, order
     )
     level_normed = exchange_all(peak, mesh, "level", ranges[2:3])
-    quant_normed, active, slope, peak = hidden_rows(normed, level_normed, weights_in, bias_hidden)
+    (quant_normed, active, slope, peak), weights_down = hidden_rows(
+        normed, level_normed, weights_in, bias_hidden, held_down
+    )
     level_active = exchange_all(peak, mesh, "level", ranges[3:4])
+    weights_down = tuple(side[:, :, 0] for side in weights_down)
     quant_active, back, output, grad_sum_two, grad_branch, terms_two = second_norm(
-        active, slope, level_active, weights_down, normed, upstream, vectors_two, order
-    )
-
-    def finish(keep, send, slope):
-        return spread(low(scatter(keep, send) * slope))
-
-    down = finish(*weight_grad(grad_branch, [quant_active], parts, plane), slopes[3])
-    grad_hidden, sum_hidden = grad_hidden_rows(grad_branch, weights_down, back)
-    inner = finish(*weight_grad(quant_normed, [grad_hidden], parts, plane), slopes[2])
+        active, slope, level_active, weights_down, normed, upstream, vectors, order
+    )
+
+    down = scatter_all(*weight_grad(grad_branch, [quant_active], parts, plane))
+    grad_branch = tie(grad_branch, next(down))
+    grad_hidden, sum_hidden = grad_hidden_rows(grad_branch, weights_down, back, part_order)
+    grad_hidden = tie(grad_hidden, down.send(sum_hidden))
+    inner = scatter_plane(*weight_grad(quant_normed, [grad_hidden], parts, plane))
+    grad_hidden = tie(grad_hidden, next(inner))
     grad_sum_one, grad_attention, terms_one = first_back(
-        grad_hidden, weights_in, normed, normal_one, inverse_one, grad_sum_two, level_normed, vectors_one
-    )
-    outer = finish(*weight_grad(grad_attention, [quant_context], parts, plane), slopes[1])
-    grad_context = grad_context_rows(grad_attention, weights_out, context, level_context)
-    *grads, sum_qv = attend_back(qkv, grad_context, seg_cols, seg_rows, lse)
-    first = finish(*weight_grad(quant_input, grads, parts, plane), slopes[0])
-    grad_x = grad_input(grads, weights_qkv, grad_sum_one, x, level_input, order)
-
-    back_order = (data ^ jnp.arange(datas)).astype(jnp.int32)
-    back_order = (back_order % 2) * plane + back_order // 2
-
-    def own_order(values):
-        return jnp.take(values, back_order, axis=0).astype(F32)
-
-    grad_w_qkv = own_order(first).transpose(1, 0, 2, 3).reshape(w_qkv.shape)
-    grad_w_in = own_order(inner).reshape(w_in.shape)
-    grad_w_out = own_order(outer).reshape(width, -1).T
-    grad_w_down = own_order(down).reshape(width, -1).T
-
-    sums = jnp.concatenate([restore(terms_one[:3]), restore(terms_two[:3])])
-    sum_qv = jnp.sum(sum_qv, axis=0)[:2]
-    sum_qv = by_distance(sum_qv, "tensor", 1)
-    sum_hidden = by_distance(sum_hidden, "tensor", 1).reshape(-1, width)
-    sums = jnp.concatenate([sums, sum_qv, sum_hidden])
-    padded = jnp.zeros((-(-sums.shape[0] // 8) * 8, width), F32).at[: sums.shape[0]].set(sums)
-    sums = exchange_all(padded, mesh, "sum", ranges[:1])
-    hidden_all = sums[8 : 8 + sum_hidden.shape[0]].reshape(-1)
+        grad_hidden, weights_in, normed, normal_one, inverse_one, grad_sum_two, level_normed, vectors, order
+    )
+    grad_attention = tie(grad_attention, inner.send(terms_one) + down.send(terms_one))
+    outer = scatter_plane(*weight_grad(grad_attention, [quant_context], parts, plane))
+    grad_attention = tie(grad_attention, next(outer))
+    grad_a = grad_context_rows(grad_attention, weights_out, context, level_context, 0)
+    grad_b = grad_context_rows(grad_attention, weights_out, context, level_context, parts // 2)
+    sums_before = jnp.zeros((8, 2 * half), F32)
+    *grads_a, token = attend_back(qkv, grad_a, seg_cols, seg_rows, lse, sums_before, part_order, columns, 0)
+    grads_a[0] = tie(grads_a[0], down.send(token) + outer.send(token))
+    first = scatter_plane(*weight_grad(quant_input, grads_a, parts // 2, plane))
+    grad_b = tie(grad_b, next(first))
+    *grads_b, token = attend_back(qkv, grad_b, seg_cols, seg_rows, lse, token, part_order, columns, half)
+    sum_qv = token
+    grads_b[0] = tie(
+        grads_b[0], inner.send(token) + down.send(token) + outer.send(token) + first.send(token)
+    )
+    raw = weight_grad(quant_input, grads_b, parts // 2, plane)
+    grads_b[0] = tie(grads_b[0], first.send(raw[1]))
+    grad_x = grad_input(grads_a + grads_b, weights_qkv, grad_sum_one, x, level_input, order)
+
+    sums = [terms_one[:3], terms_two[:3], sum_qv[:2], sum_hidden.reshape(-1, width)]
+    if rows % LANES:
+        sums[0], sums[1] = restore(sums[0]), restore(sums[1])
+    sums = jnp.concatenate(sums)
+    padded = jnp.pad(sums, ((0, -sums.shape[0] % 8), (0, 0)))
+    down, inner, outer, first = [run_all(chain, grad_x) for chain in (down, inner, outer, first)]
+    (down, inner, outer, first), sums = finale(
+        low(down * slopes[3]), inner, outer, first, raw, [slopes[0], slopes[2], slopes[1]], padded
+    )
+    hidden_all = sums[8 : 8 + sum_hidden.size // width].reshape(-1)
     grad_bias_qv = lax.dynamic_slice_in_dim(sums[6:8], part * columns, columns, 1)
     grad_b_in = lax.dynamic_slice_in_dim(hidden_all, part * b_in.shape[0], b_in.shape[0], 0)
+    grad_w_down = place_grad(down, blocks, True)
+    grad_w_out = place_grad(outer, blocks, True)
+    grad_w_in = place_grad(inner, blocks, False)[0]
+    grad_w_qkv = place_grad(first, blocks, False)
     new_ranges = jnp.stack(
         [level_input[0, 0], level_context[0, 0], level_normed[0, 0], level_active[0, 0]]
     )

time: 802 us -> 658 us (0.82)
  waiting for transfers between devices: 194 us -> 13.7 us
  Pallas kernels: 327 us -> 458 us
  starting transfers between devices: 85.8 us -> 28.9 us
  other arithmetic: 103 us -> 54.7 us
    ppermute x82 -> x25, waiting for transfers between devices: 194 us -> 13.7 us  [swap(): lax.ppermute(values, axis, [(i, i ^ 1 << bit) for i in range(count)])]
    pallas_call x6 -> x13, Pallas kernels: 150 us -> 300 us  [the longest x3 105 us: run(): results = call(*args, *sources)]
    ppermute x82 -> x25, starting transfers between devices: 85.8 us -> 28.9 us  [swap(): lax.ppermute(values, axis, [(i, i ^ 1 << bit) for i in range(count)])]
    another operation x47 -> x0, other arithmetic: 32.5 us -> none  [the longest x32 17.1 us: spread_plane(): values = jnp.stack([values, other], axis=place)]
    pallas_call x5 -> x4, Pallas kernels: 64.8 us -> 44.2 us  [exchange_all(): pl.pallas_call(partial(exchange_kernel, kind), out_shape=shape_of(dims, F...]
    unnamed x177 -> x213, local copies, waits for them, and re-layouts: 34.3 us -> 53.6 us
    concatenate x11 -> x1, other arithmetic: 18.2 us -> 0.03 us  [local(): sums = jnp.concatenate(sums)]
    gather x11 -> x0, local copies, waits for them, and re-layouts: 13.1 us -> none  [the longest x5 9.42 us: own_order(): return jnp.take(values, back_order, axis=0).astype(F32)]
  transfers between devices with their start and end apart: 82 -> 25, of which waited for: 44 -> 3; matrix products, arithmetic and copies ran while one was open for 15% -> 12% of each run, Pallas kernels for 30% -> 26%
where the time goes in v2:
time: 658 us; the launch traced here: 645 us
  Pallas kernels  458 us (70%)
  local copies, waits for them, and re-layouts  85.8 us (13%)
  other arithmetic  54.7 us (8%)
  starting transfers between devices  28.9 us (4%)
  waiting for transfers between devices  13.7 us (2%)
    pallas_call x3, Pallas kernels, run(): results = call(*args, *sources)  105 us
    pallas_call x1, Pallas kernels, finale(): pl.pallas_call(finale_kernel, in_specs=[vmem] * 8 + [anywhere()] + [vmem]...  67.3 us
    unnamed x213, local copies, waits for them, and re-layouts  53.6 us
    pallas_call x5, Pallas kernels, weight_grad(): pl.pallas_call(partial(weight_grad_kernel, count), grid=(parts, cuts), in...  50.3 us
    pallas_call x1, Pallas kernels, first_gather(): pl.pallas_call(first_gather_kernel, in_specs=[anywhere()] * 3, out_specs=...  44.8 us
    pallas_call x4, Pallas kernels, exchange_all(): pl.pallas_call(partial(exchange_kernel, kind), out_shape=shape_of(dims, F...  44.2 us
    pallas_call x1, Pallas kernels, second_norm(): pl.pallas_call(second_norm_kernel, grid=(tokens // rows,), in_specs=[in_s...  36.5 us
    pallas_call x2, Pallas kernels, attend_back(): pl.pallas_call(partial(attend_back_kernel, c, first), grid=(held, width /...  35.2 us
  transfers between devices with their start and end apart: 25, of which 3 were waited for; matrix products, arithmetic and copies ran while one was open for 12% of the time, Pallas kernels for 26%

profile of v2, /device:TPU:0, one launch (start us, length us, event | category | flops | bytes accessed | tf_op | source)
XLA Modules:
  0.0 644.9 jit_solution(10399291594813730319)
XLA Ops:
  13.2 11.8 %exchange_rows.1 = f32[8,128]{1,0:T(8,128)} custom-call(f32[8,128]{1,0:T(8,128)} %stack.76.x_ref, f32[1]{0:T(128)} %get-tuple-element.227.range_ref), custom_call_target="tpu_custom_call" | custom-call | tf_op jit(solution)/shard_map/exchange_rows/pallas_call | solution.py:115
  42.2 44.8 %first_gather.1 = (bf16[4,4,3,128,256]{4,3,2,1,0:T(8,128)(2,1)S(1)}, bf16[4,4,3,128,256]{4,3,2,1,0:T(8,128)(2,1)S(1)}, bf16[4,1,128,256]{3,2,1,0:T(8,128)(2,1)S(1)}, bf16[4,1,128,1024]{3,2,1,0:T(8,128)(2,1)S(1)}) custom-call(bf16[3,128,256]{2,1,0:T(8,128)(2,1)S(1)} %get-tuple-element.209.first_ref, bf16[1,128,256]{2,1,0:T(8,128)(2,1)S(1)} %get-tuple-element.217.out_ref, ...), custom_call_target="tpu_custom_call" | custom-call | tf_op jit(solution)/shard_map/first_gather/pallas_call | solution.py:465
  105.1 14.6 %qkv.1 = (bf16[3,1024,1024]{2,1,0:T(8,128)(2,1)S(1)}, bf16[4,4,1,128,256]{4,3,2,1,0:T(8,128)(2,1)S(1)}, bf16[4,4,1,128,256]{4,3,2,1,0:T(8,128)(2,1)S(1)}) custom-call(bf16[1024,1024]{1,0:T(8,128)(2,1)S(1)} %copy-done.11, bf16[4,4,3,128,256]{4,3,2,1,0:T(8,128)(2,1)S(1)} %copy-done.35, bf16[4,4,3,128,256]{4,3,2,1,0:T(8,128)(2,1)S(1)} %copy-done.37, ...), custom_call_target="tpu_custom_call" | custom-call | flops 6442450944 | bytes 14680064 | tf_op jit(solution)/shard_map/qkv/pallas_call | solution.py:401
  123.3 45.2 %attend.1 = (f32[1024,1024]{1,0:T(8,128)S(1)}, f32[2,128,512]{2,1,0:T(8,128)S(1)}, f32[8,128]{1,0:T(8,128)S(1)}, bf16[4,4,1,128,1024]{4,3,2,1,0:T(8,128)(2,1)S(1...) custom-call(bf16[3,1024,1024]{2,1,0:T(8,128)(2,1)} %copy-done.53, ...), custom_call_target="tpu_custom_call" | custom-call | flops 30000001024 | bytes 83886080 | tf_op jit(solution)/shard_map/attend/pallas_call | solution.py:401
  174.9 10.8 %exchange_level.3.level_ref = f32[8,128]{1,0:T(8,128)} custom-call(f32[8,128]{1,0:T(8,128)} %copy-done.32, f32[1]{0:T(128)} %get-tuple-element.226.range_ref), custom_call_target="tpu_custom_call" | custom-call | tf_op jit(solution)/shard_map/exchange_level/pallas_call | solution.py:115
  188.4 8.6 %first_norm.1 = (bf16[1024,1024]{1,0:T(8,128)(2,1)S(1)}, f32[1024,1024]{1,0:T(8,128)}, f32[1024,1024]{1,0:T(8,128)}, f32[1024,1]{1,0:T(8,128)S(1)}, f32[8,128]{1,0:T(8,128)S(1)}) custom-call(s32[8]{0:T(128)S(1)} %fusion.50.order_ref, f32[1024,1024]{1,0:T(8,128)} %copy-done.2, f32[8,128]{1,0:T(8,128)S(1)} %copy-done.21, ...), custom_call_target="tpu_custom_call" | custom-call | flops 2147483648 | bytes 20971520 | tf_op jit(solution)/shard_map/first_norm/pallas_call | solution.py:935
  199.7 10.8 %exchange_level.4.refs_1_.level_ref = f32[8,128]{1,0:T(8,128)} custom-call(f32[8,128]{1,0:T(8,128)} %copy-done.33, f32[1]{0:T(128)} %get-tuple-element.228.range_ref), custom_call_target="tpu_custom_call" | custom-call | tf_op jit(solution)/shard_map/exchange_level/pallas_call | solution.py:115
  213.2 45.0 %hidden.1 = (bf16[1024,1024]{1,0:T(8,128)(2,1)S(1)}, f32[1024,4096]{1,0:T(8,128)}, f32[1024,4096]{1,0:T(8,128)}, f32[8,128]{1,0:T(8,128)S(1)}, bf16[4,4,1,128,10...) custom-call(f32[1024,1024]{1,0:T(8,128)} %get-tuple-element.118.refs_0_.normed_ref, f32[8,128]{1,0:T(8,128)S(1)} %copy-done.30, ...), custom_call_target="tpu_custom_call" | custom-call | flops 8589934592 | bytes 52428800 | tf_op jit(solution)/shard_map/hidden/pallas_call | solution.py:401
  258.7 10.8 %exchange_level.5.level_ref = f32[8,128]{1,0:T(8,128)} custom-call(f32[8,128]{1,0:T(8,128)} %copy-done.31, f32[1]{0:T(128)} %get-tuple-element.225.range_ref), custom_call_target="tpu_custom_call" | custom-call | tf_op jit(solution)/shard_map/exchange_level/pallas_call | solution.py:115
  269.6 36.5 %second_norm.1 = (bf16[1024,4096]{1,0:T(8,128)(2,1)}, f32[1024,4096]{1,0:T(8,128)}, bf16[1024,1024]{1,0:T(8,128)(2,1)}, f32[1024,1024]{1,0:T(8,128)}, bf16[1024,1024]{1,0:T(8,128)(2,1)}, /*index=5*/f32[8,1024]{1,0:T(8,128)}) custom-call(s32[8]{0:T(128)} %copy-done.23, f32[1024,4096]{1,0:T(8,128)} %get-tuple-element.123.act_ref, ...), custom_call_target="tpu_custom_call" | custom-call | flops 8589934592 | bytes 83886080 | tf_op jit(solution)/shard_map/second_norm/pallas_call | solution.py:1067
  307.7 15.2 %weight_grad.5 = (f32[4,4,1,128,1024]{4,3,2,1,0:T(8,128)}, bf16[4,4,1,128,1024]{4,3,2,1,0:T(8,128)(2,1)}) custom-call(bf16[1024,1024]{1,0:T(8,128)(2,1)S(1)} %copy-done.39, bf16[1024,4096]{1,0:T(8,128)(2,1)} %get-tuple-element.130.refs_0_), custom_call_target="tpu_custom_call" | custom-call | flops 8589934592 | bytes 41943040 | tf_op jit(solution)/shard_map/weight_grad/pallas_call | solution.py:1126
  322.9 19.4 %grad_hidden.1 = (bf16[1024,4096]{1,0:T(8,128)(2,1)}, f32[4,1024]{1,0:T(4,128)S(1)}) custom-call(s32[4]{0:T(128)S(1)} %iota_xor_fusion.order_ref, bf16[1024,1024]{1,0:T(8,128)(2,1)S(1)} %copy-done.39, bf16[4,4,128,1024]{3,2,1,0:T(8,128)(2,1)} %bitcast.235, bf16[4,4,128,1024]{3,2,1,0:T(8,128)(2,1)} %bitcast.237, f32[1024,4096]{1,0:T(8,128)} %get-tuple-element.133.back_ref), custom_call_target="tpu_custom_call" | custom-call | flops 8589934592 | bytes 35651584 | tf_op jit(solution)/shard_map/grad_hidden/pallas_call | solution.py:1172
  344.9 5.9 bitcast_add_fusion.1
  356.3 15.0 %weight_grad.6 = (f32[4,4,1,128,1024]{4,3,2,1,0:T(8,128)}, bf16[4,4,1,128,1024]{4,3,2,1,0:T(8,128)(2,1)}) custom-call(bf16[1024,1024]{1,0:T(8,128)(2,1)S(1)} %copy-done.57, bf16[1024,4096]{1,0:T(8,128)(2,1)} %get-tuple-element.141.refs_0_.g_ref), custom_call_target="tpu_custom_call" | custom-call | flops 8589934592 | bytes 41943040 | tf_op jit(solution)/shard_map/weight_grad/pallas_call | solution.py:1126
  380.6 18.6 %first_back.1 = (f32[1024,1024]{1,0:T(8,128)}, bf16[1024,1024]{1,0:T(8,128)(2,1)}, f32[8,1024]{1,0:T(8,128)}) custom-call(s32[8]{0:T(128)} %copy-done.23, bf16[1024,4096]{1,0:T(8,128)(2,1)} %get-tuple-element.141.refs_0_.g_ref, bf16[4,4,128,1024]{3,2,1,0:T(8,128)(2,1)} %bitcast.227, bf16[4,4,128,1024]{3,2,1,0:T(8,128)(2,1)} %bitcast.263, ...), custom_call_target="tpu_custom_call" | custom-call | flops 8589934592 | bytes 37748736 | tf_op jit(solution)/shard_map/first_back/pallas_call | solution.py:1208
  409.9 10.1 %bitcast_add_fusion = f32[4,4,1,128,1024]{4,3,1,2,0:T(8,128)} fusion(f32[4,4,1,128,1024]{4,3,2,1,0:T(8,128)} %get-tuple-element.146, bf16[4,4,1,128,1024]{4,3,1,2,0:T(8,128)(2,1)} %collective-permute-done.3), kind=kLoop, calls=%fused_computation | loop fusion | flops 4194304 | bytes 20971520 | tf_op jit(solution)/shard_map/add | solution.py:171
  430.1 5.4 weight_grad.7
  440.2 17.6 %attend_back.2 = (bf16[1024,512]{1,0:T(8,128)(2,1)S(1)}, bf16[1024,512]{1,0:T(8,128)(2,1)S(1)}, bf16[1024,512]{1,0:T(8,128)(2,1)S(1)}, f32[8,1024]{1,0:T(8,128)S(1)}) custom-call(s32[4]{0:T(128)S(1)} %iota_xor_fusion.order_ref, bf16[3,1024,1024]{2,1,0:T(8,128)(2,1)S(1)} %copy-done.54, bf16[3,1024,1024]{2,1,0:T(8,128)(2,1)S(1)} %copy-done.54, ...), custom_call_target="tpu_custom_call" | custom-call | flops 15000000512 | bytes 52428800 | tf_op jit(solution)/shard_map/attend_back/pallas_call | solution.py:837
  469.9 7.2 %weight_grad.8 = (f32[4,2,3,128,256]{4,3,2,1,0:T(8,128)}, bf16[4,2,3,128,256]{4,3,2,1,0:T(8,128)(2,1)S(1)}) custom-call(bf16[1024,1024]{1,0:T(8,128)(2,1)} %copy-done.10, bf16[1024,512]{1,0:T(8,128)(2,1)S(1)} %get-tuple-element.162.refs_0_, bf16[1024,512]{1,0:T(8,128)(2,1)S(1)} %copy-done.49, bf16[1024,512]{1,0:T(8,128)(2,1)S(1)} %copy-done.51), custom_call_target="tpu_custom_call" | custom-call | flops 3221225472 | bytes 15728640 | tf_op jit(solution)/shard_map/weight_grad/pallas_call | solution.py:1126
  479.9 17.6 %attend_back.3 = (bf16[1024,512]{1,0:T(8,128)(2,1)S(1)}, bf16[1024,512]{1,0:T(8,128)(2,1)S(1)}, bf16[1024,512]{1,0:T(8,128)(2,1)S(1)}, f32[8,1024]{1,0:T(8,128)S(1)}) custom-call(s32[4]{0:T(128)S(1)} %iota_xor_fusion.order_ref, bf16[3,1024,1024]{2,1,0:T(8,128)(2,1)S(1)} %copy-done.55, bf16[3,1024,1024]{2,1,0:T(8,128)(2,1)S(1)} %copy-done.55, ...), custom_call_target="tpu_custom_call" | custom-call | flops 15000000512 | bytes 52428800 | tf_op jit(solution)/shard_map/attend_back/pallas_call | solution.py:837
  516.9 7.4 %weight_grad.9 = (f32[4,2,3,128,256]{4,3,2,1,0:T(8,128)}, bf16[4,2,3,128,256]{4,3,2,1,0:T(8,128)(2,1)S(1)}) custom-call(bf16[1024,1024]{1,0:T(8,128)(2,1)} %copy-done.10, bf16[1024,512]{1,0:T(8,128)(2,1)S(1)} %get-tuple-element.182.refs_0_.refs_3_, bf16[1024,512]{1,0:T(8,128)(2,1)S(1)} %get-tuple-element.177.refs_1_.refs_4_, ...), custom_call_target="tpu_custom_call" | custom-call | flops 3221225472 | bytes 15728640 | tf_op jit(solution)/shard_map/weight_grad/pallas_call | solution.py:1126
  532.5 7.0 %collective-permute-done.15 = bf16[2,1,3,128,256]{4,3,2,1,0:T(8,128)(2,1)S(1)} collective-permute-done((bf16[2,1,3,128,256]{4,3,2,1,0:T(8,128)(2,1)S(1)}, bf16[2,1,3,128,256]{4,3,2,1,0:T(8,128)(2,1)S(1)}, u32[]{:S(2)}, u32[]{:S(2)}) %collective-permute-start.15) | collective-permute-done | bytes 393248 | tf_op jit(solution)/shard_map/ppermute | solution.py:142
  540.5 12.5 %grad_input.1 = bf16[1024,1024]{1,0:T(8,128)(2,1)} custom-call(s32[8]{0:T(128)S(1)} %copy-done.24, bf16[1024,512]{1,0:T(8,128)(2,1)S(1)} %copy-done.47, bf16[1024,512]{1,0:T(8,128)(2,1)S(1)} %copy-done.49, bf16[1024,512]{1,0:T(8,128)(2,1)S(1)} %copy-done.51, bf16[1024,512]{1,0:T(8,128)(2,1)S(1)} %get-tuple-element.182.refs_0_.refs_3_, ...), custom_call_target="tpu_custom_call" | custom-call | flops 6442450944 | bytes 20971520 | tf_op jit(solution)/shard_map/grad_input/pallas_call | solution.py:1294
  563.8 67.3 %finale.1 = (bf16[4,1,128,1024]{3,2,1,0:T(8,128)(2,1)S(1)}, bf16[4,1,128,1024]{3,2,1,0:T(8,128)(2,1)}, bf16[4,1,128,1024]{3,2,1,0:T(8,128)(2,1)}, bf16[4,1,128,1...) custom-call(bf16[1,128,1024]{2,1,0:T(8,128)(2,1)S(1)} %fusion.24.dow, ...), custom_call_target="tpu_custom_call" | custom-call | tf_op jit(solution)/shard_map/finale/pallas_call | solution.py:595
  (382 shorter events, 175.7 us)
Async XLA Ops:
  2.5 89.5 %collective-permute-start = (bf16[1,1536]{1,0:T(2,128)(2,1)S(1)}, bf16[1,1536]{1,0:T(2,128)(2,1)S(1)}, u32[]{:S(2)}, u32[]{:S(2)}) collective-permute-start(bf16[1,1536]{1,0:T(2,128)(2,1)S(1)} %broadcast_in_dim.10), channel_id=1, source_target_pairs={{0,2},{1,3},{2,0},{3,1},{4,6},{5,7},{6,4},{7,5},{8,10},{9,11},{10,... | collective-permute-start | bytes 9224 | tf_op jit(solution)/shard_map/ppermute | solution.py:142
  322.9 20.0 %collective-permute-start.2 = (bf16[4,4,1,128,1024]{4,3,1,2,0:T(8,128)(2,1)}, bf16[4,4,1,128,1024]{4,3,1,2,0:T(8,128)(2,1)S(1)}, u32[]{:S(2)}, u32[]{:S(2)}) collective-permute-start(bf16[4,4,1,128,1024]{4,3,1,2,0:T(8,128)(2,1)} %bitcast.261), channel_id=1, source_target_pairs={{0,4},{4,0},{8,12},{12,8},{16,20},{20,16},{24,28},{28,24},{1,5},{5... | collective-permute-start | bytes 12582920 | tf_op jit(solution)/shard_map/ppermute | solution.py:142
  371.3 38.6 %collective-permute-start.3 = (bf16[4,4,1,128,1024]{4,3,1,2,0:T(8,128)(2,1)}, bf16[4,4,1,128,1024]{4,3,1,2,0:T(8,128)(2,1)}, u32[]{:S(2)}, u32[]{:S(2)}) collective-permute-start(bf16[4,4,1,128,1024]{4,3,1,2,0:T(8,128)(2,1)} %bitcast.260), channel_id=1, source_target_pairs={{0,4},{4,0},{8,12},{12,8},{16,20},{20,16},{24,28},{28,24},{1,5},{5... | collective-permute-start | bytes 12582920 | tf_op jit(solution)/shard_map/ppermute | solution.py:142
  371.8 28.9 %collective-permute-start.5 = (bf16[2,2,1,128,1024]{4,3,1,2,0:T(8,128)(2,1)}, bf16[2,2,1,128,1024]{4,3,1,2,0:T(8,128)(2,1)S(1)}, u32[]{:S(2)}, u32[]{:S(2)}) collective-permute-start(bf16[2,2,1,128,1024]{4,3,1,2,0:T(8,128)(2,1)} %fusion.2), channel_id=1, source_target_pairs={{0,8},{4,12},{8,0},{12,4},{16,24},{20,28},{24,16},{28,20},{1,9},{5... | collective-permute-start | bytes 3145736 | tf_op jit(solution)/shard_map/ppermute | solution.py:142
  372.4 29.2 %collective-permute-start.4 = (bf16[2,2,1,128,1024]{4,3,1,2,0:T(8,128)(2,1)}, bf16[2,2,1,128,1024]{4,3,1,2,0:T(8,128)(2,1)}, u32[]{:S(2)}, u32[]{:S(2)}) collective-permute-start(bf16[2,2,1,128,1024]{4,3,1,2,0:T(8,128)(2,1)} %slice.471), channel_id=1, source_target_pairs={{0,16},{4,20},{8,24},{12,28},{16,0},{20,4},{24,8},{28,12},{1,17},{... | collective-permute-start | bytes 3145736 | tf_op jit(solution)/shard_map/ppermute | solution.py:142
  404.3 53.6 %collective-permute-start.7 = (bf16[2,1,128,1024]{3,2,0,1:T(8,128)(2,1)}, bf16[2,1,128,1024]{3,2,0,1:T(8,128)(2,1)S(1)}, u32[]{:S(2)}, u32[]{:S(2)}) collective-permute-start(bf16[2,1,128,1024]{3,2,0,1:T(8,128)(2,1)} %fusion.16), channel_id=1, source_target_pairs={{0,16},{4,20},{8,24},{12,28},{16,0},{20,4},{24,8},{28,12},{1,17},{... | collective-permute-start | bytes 1572872 | tf_op jit(solution)/shard_map/ppermute | solution.py:142
  408.5 49.4 %collective-permute-start.6 = (bf16[2,1,128,1024]{3,2,0,1:T(8,128)(2,1)}, bf16[2,1,128,1024]{3,2,0,1:T(8,128)(2,1)S(1)}, u32[]{:S(2)}, u32[]{:S(2)}) collective-permute-start(bf16[2,1,128,1024]{3,2,0,1:T(8,128)(2,1)} %fusion.15), channel_id=1, source_target_pairs={{0,8},{4,12},{8,0},{12,4},{16,24},{20,28},{24,16},{28,20},{1,9},{5... | collective-permute-start | bytes 1572872 | tf_op jit(solution)/shard_map/ppermute | solution.py:142
  428.0 69.6 %collective-permute-start.10 = (bf16[2,2,1,128,1024]{4,3,1,2,0:T(8,128)(2,1)}, bf16[2,2,1,128,1024]{4,3,1,2,0:T(8,128)(2,1)}, u32[]{:S(2)}, u32[]{:S(2)}) collective-permute-start(bf16[2,2,1,128,1024]{4,3,1,2,0:T(8,128)(2,1)} %fusion.3), channel_id=1, source_target_pairs={{0,8},{4,12},{8,0},{12,4},{16,24},{20,28},{24,16},{28,20},{1,9},{5... | collective-permute-start | bytes 3145736 | tf_op jit(solution)/shard_map/ppermute | solution.py:142
  428.6 72.0 %collective-permute-start.9 = (bf16[2,2,1,128,1024]{4,3,1,2,0:T(8,128)(2,1)}, bf16[2,2,1,128,1024]{4,3,1,2,0:T(8,128)(2,1)}, u32[]{:S(2)}, u32[]{:S(2)}) collective-permute-start(bf16[2,2,1,128,1024]{4,3,1,2,0:T(8,128)(2,1)} %slice.470), channel_id=1, source_target_pairs={{0,16},{4,20},{8,24},{12,28},{16,0},{20,4},{24,8},{28,12},{1,17},{... | collective-permute-start | bytes 3145736 | tf_op jit(solution)/shard_map/ppermute | solution.py:142
  437.3 28.8 %collective-permute-start.8 = (bf16[4,4,1,128,256]{4,3,1,2,0:T(8,128)(2,1)S(1)}, bf16[4,4,1,128,256]{4,3,1,2,0:T(8,128)(2,1)}, u32[]{:S(2)}, u32[]{:S(2)}) collective-permute-start(bf16[4,4,1,128,256]{4,3,1,2,0:T(8,128)(2,1)S(1)} %bitcast.225), channel_id=1, source_target_pairs={{0,4},{4,0},{8,12},{12,8},{16,20},{20,16},{24,28},{28,24},{1,5},{5... | collective-permute-start | bytes 3145736 | tf_op jit(solution)/shard_map/ppermute | solution.py:142
  461.3 44.9 %collective-permute-start.11 = (bf16[1,1,128,1024]{3,2,1,0:T(8,128)(2,1)}, bf16[1,1,128,1024]{3,2,1,0:T(8,128)(2,1)}, u32[]{:S(2)}, u32[]{:S(2)}) collective-permute-start(bf16[1,1,128,1024]{3,2,1,0:T(8,128)(2,1)} %fusion.33), channel_id=1, source_target_pairs={{0,1},{1,0},{2,3},{3,2},{4,5},{5,4},{6,7},{7,6},{8,9},{9,8},{10,11... | collective-permute-start | bytes 786440 | tf_op jit(solution)/shard_map/ppermute | solution.py:142
  462.9 44.1 %collective-permute-start.17 = (bf16[1,1,128,1024]{3,2,1,0:T(8,128)(2,1)}, bf16[1,1,128,1024]{3,2,1,0:T(8,128)(2,1)}, u32[]{:S(2)}, u32[]{:S(2)}) collective-permute-start(bf16[1,1,128,1024]{3,2,1,0:T(8,128)(2,1)} %fusion.32), channel_id=1, source_target_pairs={{0,1},{1,0},{2,3},{3,2},{4,5},{5,4},{6,7},{7,6},{8,9},{9,8},{10,11... | collective-permute-start | bytes 786440 | tf_op jit(solution)/shard_map/ppermute | solution.py:142
  477.1 36.4 %collective-permute-start.14 = (bf16[4,2,3,128,256]{4,3,2,1,0:T(8,128)(2,1)S(1)}, bf16[4,2,3,128,256]{4,3,2,1,0:T(8,128)(2,1)S(1)}, u32[]{:S(2)}, u32[]{:S(2)}) collective-permute-start(bf16[4,2,3,128,256]{4,3,2,1,0:T(8,128)(2,1)S(1)} %get-tuple-element.165), channel_id=1, source_target_pairs={{0,4},{4,0},{8,12},{12,8},{16,20},{20,16},{24,28},{28,24},{1,5},{5... | collective-permute-start | bytes 4718600 | tf_op jit(solution)/shard_map/ppermute | solution.py:142
  497.6 12.5 %collective-permute-start.13 = (bf16[2,2,1,128,256]{4,3,1,2,0:T(8,128)(2,1)S(1)}, bf16[2,2,1,128,256]{4,3,1,2,0:T(8,128)(2,1)S(1)}, u32[]{:S(2)}, u32[]{:S(2)}) collective-permute-start(bf16[2,2,1,128,256]{4,3,1,2,0:T(8,128)(2,1)S(1)} %fusion.35), channel_id=1, source_target_pairs={{0,8},{4,12},{8,0},{12,4},{16,24},{20,28},{24,16},{28,20},{1,9},{5... | collective-permute-start | bytes 786440 | tf_op jit(solution)/shard_map/ppermute | solution.py:142
  500.6 11.0 %collective-permute-start.12 = (bf16[2,2,1,128,256]{4,3,1,2,0:T(8,128)(2,1)S(1)}, bf16[2,2,1,128,256]{4,3,1,2,0:T(8,128)(2,1)S(1)}, u32[]{:S(2)}, u32[]{:S(2)}) collective-permute-start(bf16[2,2,1,128,256]{4,3,1,2,0:T(8,128)(2,1)S(1)} %slice.473), channel_id=1, source_target_pairs={{0,16},{4,20},{8,24},{12,28},{16,0},{20,4},{24,8},{28,12},{1,17},{... | collective-permute-start | bytes 786440 | tf_op jit(solution)/shard_map/ppermute | solution.py:142
  506.2 46.8 %collective-permute-start.20 = (bf16[2,1,128,1024]{3,2,1,0:T(8,128)(2,1)}, bf16[2,1,128,1024]{3,2,1,0:T(8,128)(2,1)}, u32[]{:S(2)}, u32[]{:S(2)}) collective-permute-start(bf16[2,1,128,1024]{3,2,1,0:T(8,128)(2,1)} %fusion.18), channel_id=1, source_target_pairs={{0,16},{4,20},{8,24},{12,28},{16,0},{20,4},{24,8},{28,12},{1,17},{... | collective-permute-start | bytes 1572872 | tf_op jit(solution)/shard_map/ppermute | solution.py:142
  506.9 49.7 %collective-permute-start.19 = (bf16[2,1,128,1024]{3,2,1,0:T(8,128)(2,1)}, bf16[2,1,128,1024]{3,2,1,0:T(8,128)(2,1)S(1)}, u32[]{:S(2)}, u32[]{:S(2)}) collective-permute-start(bf16[2,1,128,1024]{3,2,1,0:T(8,128)(2,1)} %fusion.17), channel_id=1, source_target_pairs={{0,8},{4,12},{8,0},{12,4},{16,24},{20,28},{24,16},{28,20},{1,9},{5... | collective-permute-start | bytes 1572872 | tf_op jit(solution)/shard_map/ppermute | solution.py:142
  510.1 50.6 %collective-permute-start.18 = (bf16[1,128,1024]{2,1,0:T(8,128)(2,1)}, bf16[1,128,1024]{2,1,0:T(8,128)(2,1)}, u32[]{:S(2)}, u32[]{:S(2)}) collective-permute-start(bf16[1,128,1024]{2,1,0:T(8,128)(2,1)} %fusion.34), channel_id=1, source_target_pairs={{0,2},{1,3},{2,0},{3,1},{4,6},{5,7},{6,4},{7,5},{8,10},{9,11},{10,... | collective-permute-start | bytes 786440 | tf_op jit(solution)/shard_map/ppermute | solution.py:142
  514.2 15.2 %collective-permute-start.16 = (bf16[2,1,3,128,256]{4,3,2,1,0:T(8,128)(2,1)S(1)}, bf16[2,1,3,128,256]{4,3,2,1,0:T(8,128)(2,1)S(1)}, u32[]{:S(2)}, u32[]{:S(2)}) collective-permute-start(bf16[2,1,3,128,256]{4,3,2,1,0:T(8,128)(2,1)S(1)} %fusion.27), channel_id=1, source_target_pairs={{0,8},{4,12},{8,0},{12,4},{16,24},{20,28},{24,16},{28,20},{1,9},{5... | collective-permute-start | bytes 1179656 | tf_op jit(solution)/shard_map/ppermute | solution.py:142
  515.4 43.1 %collective-permute-start.22 = (bf16[2,1,128,256]{3,2,1,0:T(8,128)(2,1)}, bf16[2,1,128,256]{3,2,1,0:T(8,128)(2,1)S(1)}, u32[]{:S(2)}, u32[]{:S(2)}) collective-permute-start(bf16[2,1,128,256]{3,2,1,0:T(8,128)(2,1)} %fusion.43), channel_id=1, source_target_pairs={{0,16},{4,20},{8,24},{12,28},{16,0},{20,4},{24,8},{28,12},{1,17},{... | collective-permute-start | bytes 393224 | tf_op jit(solution)/shard_map/ppermute | solution.py:142
  529.4 10.1 %collective-permute-start.15 = (bf16[2,1,3,128,256]{4,3,2,1,0:T(8,128)(2,1)S(1)}, bf16[2,1,3,128,256]{4,3,2,1,0:T(8,128)(2,1)S(1)}, u32[]{:S(2)}, u32[]{:S(2)}) collective-permute-start(bf16[2,1,3,128,256]{4,3,2,1,0:T(8,128)(2,1)S(1)} %slice.472), channel_id=1, source_target_pairs={{0,16},{4,20},{8,24},{12,28},{16,0},{20,4},{24,8},{28,12},{1,17},{... | collective-permute-start | bytes 1179656 | tf_op jit(solution)/shard_map/ppermute | solution.py:142
  539.5 19.6 %collective-permute-start.21 = (bf16[2,1,128,256]{3,2,1,0:T(8,128)(2,1)}, bf16[2,1,128,256]{3,2,1,0:T(8,128)(2,1)S(1)}, u32[]{:S(2)}, u32[]{:S(2)}) collective-permute-start(bf16[2,1,128,256]{3,2,1,0:T(8,128)(2,1)} %fusion.42), channel_id=1, source_target_pairs={{0,8},{4,12},{8,0},{12,4},{16,24},{20,28},{24,16},{28,20},{1,9},{5... | collective-permute-start | bytes 393224 | tf_op jit(solution)/shard_map/ppermute | solution.py:142
  553.1 10.6 %collective-permute-start.24 = (bf16[1,3,128,256]{3,2,1,0:T(8,128)(2,1)}, bf16[1,3,128,256]{3,2,1,0:T(8,128)(2,1)S(1)}, u32[]{:S(2)}, u32[]{:S(2)}) collective-permute-start(bf16[1,3,128,256]{3,2,1,0:T(8,128)(2,1)} %fusion.39), channel_id=1, source_target_pairs={{0,16},{4,20},{8,24},{12,28},{16,0},{20,4},{24,8},{28,12},{1,17},{... | collective-permute-start | bytes 589832 | tf_op jit(solution)/shard_map/ppermute | solution.py:142
  556.6 7.1 %collective-permute-start.23 = (bf16[1,3,128,256]{3,2,1,0:T(8,128)(2,1)S(1)}, bf16[1,3,128,256]{3,2,1,0:T(8,128)(2,1)S(1)}, u32[]{:S(2)}, u32[]{:S(2)}) collective-permute-start(bf16[1,3,128,256]{3,2,1,0:T(8,128)(2,1)S(1)} %fusion.38), channel_id=1, source_target_pairs={{0,8},{4,12},{8,0},{12,4},{16,24},{20,28},{24,16},{28,20},{1,9},{5... | collective-permute-start | bytes 589832 | tf_op jit(solution)/shard_map/ppermute | solution.py:142
  (104 other events, 814.6 us)

commit v3 on v2

v3 whole, which is shorter than its diff:
```python
from functools import partial

import jax
import jax.numpy as jnp
from jax import lax
from jax.experimental import pallas as pl
from jax.experimental.pallas import tpu as pltpu
from jax.sharding import PartitionSpec as P

HD = 64
SEQ = 512
LANES = 128

EPS = 1e-06
DECAY = 0.9
MASKED = -1e30
MESH = pl.DeviceIdType.MESH
F32 = jnp.float32
BF16 = jnp.bfloat16
MIB = 1024 * 1024


def shape_of(dims, kind):
    return jax.ShapeDtypeStruct(dims, kind)


def params(**rest):
    return pltpu.CompilerParams(vmem_limit_bytes=60 * MIB, **rest)


def in_smem():
    return pl.BlockSpec(memory_space=pltpu.SMEM)


def cost(flops, moved):
    return pl.CostEstimate(flops=int(flops), bytes_accessed=int(moved), transcendentals=0)


def dot(first, second):
    return jnp.dot(first, second, preferred_element_type=F32)


def dot_cols(first, second):
    return lax.dot_general(first, second, (((1,), (1,)), ((), ())), preferred_element_type=F32)


def dot_rows(first, second):
    return lax.dot_general(first, second, (((0,), (0,)), ((), ())), preferred_element_type=F32)


def flat(block):
    return block.reshape(block.shape[0] * block.shape[1], block.shape[2])


def exchange_kernel(
    kind, x_ref, range_ref, level_ref, o_ref, near, far, mid, near_send, near_recv, far_send, far_recv
):
    data, part = lax.axis_index("dp"), lax.axis_index("tensor")
    datas, parts = lax.axis_size("dp"), lax.axis_size("tensor")
    barrier = pltpu.get_barrier_semaphore()

    def to_data(step):
        return (lax.rem(data + step, datas), part)

    def to_part(step):
        return (data, lax.rem(part + step, parts))

    def greet(target):
        def run(step, carry):
            pl.semaphore_signal(barrier, inc=1, device_id=target(step), device_id_type=MESH)
            return carry

        return run

    lax.fori_loop(1, datas, greet(to_data), 0)
    lax.fori_loop(1, parts, greet(to_part), 0)
    pl.semaphore_wait(barrier, datas + parts - 2)

    def exchange(source, slots, send, recv, target, count):
        def copy(step):
            return pltpu.make_async_remote_copy(
                src_ref=source,
                dst_ref=slots.at[step],
                send_sem=send.at[step],
                recv_sem=recv.at[step],
                device_id=target(step),
                device_id_type=MESH,
            )

        def start(step, carry):
            copy(step).start()
            return carry

        def finish(step, carry):
            copy(step).wait()
            return carry

        lax.fori_loop(1, count, start, 0)
        slots[0] = source[...]
        lax.fori_loop(1, count, finish, 0)
        return jnp.max(slots[...], axis=0)

    mid[...] = exchange(x_ref, near, near_send, near_recv, to_data, datas)
    total = exchange(mid, far, far_send, far_recv, to_part, parts)
    if kind == "rows":
        total = jnp.broadcast_to(jnp.max(total, axis=1, keepdims=True), total.shape)
    if kind != "rows":
        peak = jnp.max(total, keepdims=True)
        level = DECAY * range_ref[kind] + (1.0 - DECAY) * peak
        places = lax.broadcasted_iota(jnp.int32, total.shape, 0)
        total = jnp.where(places == kind, level, level_ref[...])
    o_ref[...] = total


def exchange_all(values, mesh, kind, previous, levels):
    datas, parts = mesh.shape["dp"], mesh.shape["tensor"]
    dims = values.shape
    copies = pltpu.SemaphoreType.DMA
    vmem = pl.BlockSpec(memory_space=pltpu.VMEM)
    return pl.pallas_call(
        partial(exchange_kernel, kind),
        out_shape=shape_of(dims, F32),
        in_specs=[vmem, in_smem(), vmem],
        out_specs=vmem,
        scratch_shapes=[
            pltpu.VMEM((datas,) + dims, F32),
            pltpu.VMEM((parts,) + dims, F32),
            pltpu.VMEM(dims, F32),
            copies((datas,)),
            copies((datas,)),
            copies((parts,)),
            copies((parts,)),
        ],
        compiler_params=params(
            collective_id={"rows": 0, 1: 1, 2: 7, 3: 8}[kind], has_side_effects=True
        ),
        name="exchange",
    )(values, previous, levels)


def tie(values, others):
    return lax.optimization_barrier((values, *others))[0]


def swap(values, axis, bit, token=None):
    count = lax.axis_size(axis)
    other = lax.ppermute(values, axis, [(i, i ^ (1 << bit)) for i in range(count)])
    return other if token is None else tie(other, [token])


def far_swap(values, r):
    count = lax.axis_size("dp")
    return lax.ppermute(values, "dp", [(i, i ^ r) for i in range(count)])


def bits_of(axis):
    return lax.axis_size(axis).bit_length() - 1


def plane_orders():
    plane = list(range(1, bits_of("dp")))
    return plane, (plane[::-1], plane)


def run_all(chain, token=None):
    try:
        chain.send(token)
        while True:
            next(chain)
    except StopIteration as done:
        return done.value


def low(values):
    return values.astype(BF16)


def first_split(plane_bits):
    _, orders = plane_orders()
    split = []
    for order in orders:
        bit = order[0] - 1
        split.append([[s for s in range(1 << plane_bits) if (s >> bit) & 1 == away] for away in (0, 1)])
    return split


def scatter_plane(keeps, sends, but_last=False):
    plane, orders = plane_orders()
    left = [[bit for bit in plane[::-1] if bit != order[0]] for order in orders]
    sides = [keep.reshape((2,) * len(left[0]) + keep.shape[1:]) for keep in keeps]
    token = yield list(sends)
    for i in range(2):
        other = swap(sends[i], "dp", orders[i][0], token)
        sides[i] = sides[i] + other.reshape(sides[i].shape).astype(F32)
    for step in range(1, len(plane)):
        places = [left[i].index(orders[i][step]) for i in range(2)]
        sends = [low(lax.index_in_dim(sides[i], 1, places[i], keepdims=False)) for i in range(2)]
        if but_last and step == len(plane) - 1:
            return [(lax.index_in_dim(sides[i], 0, places[i], keepdims=False), sends[i]) for i in range(2)]
        token = yield sends
        for i in range(2):
            bit = orders[i][step]
            keep = lax.index_in_dim(sides[i], 0, places[i], keepdims=False)
            sides[i] = keep + swap(sends[i], "dp", bit, token).astype(F32)
            left[i].remove(bit)
    return sides


def scatter_part(keeps, sends):
    sides = yield from scatter_plane(keeps, sends)
    for bit in range(bits_of("tensor") - 1):
        pairs = [values.reshape((-1, 2) + values.shape[1:]) for values in sides]
        sends = [low(values[:, 1]) for values in pairs]
        token = yield sends
        sides = [
            values[:, 0] + swap(send, "tensor", bit, token).astype(F32)
            for values, send in zip(pairs, sends)
        ]
    return [side[0] for side in sides]


def scatter_all(keeps, sends):
    sides = yield from scatter_part(keeps, sends)
    send = low(sides[1])
    token = yield [send]
    return sides[0] + swap(send, "tensor", bits_of("tensor") - 1, token).astype(F32)


def at_distance(axis, r):
    me, index = lax.axis_index(axis), 0
    for bit in range(bits_of(axis)):
        index = index + (me // (1 << bit) + (r >> bit)) % 2 * (1 << bit)
    return index


def plane_moves():
    plane = 1 << (bits_of("dp") - 1)
    if plane == 4:
        return [(1, 2), (2, 4)], [(3, 1, 4, 0), (3, 2, 2, 1)]
    return [(slot, 2 * slot) for slot in range(1, plane)], []


class Mover:
    def __init__(self, send, recv, local):
        self.send, self.recv, self.local = send, recv, local
        self.count, self.local_count = 0, 0

    def remote(self, source, target, axis, r):
        i = self.count
        self.count += 1
        return pltpu.make_async_remote_copy(
            src_ref=source,
            dst_ref=target,
            send_sem=self.send.at[i],
            recv_sem=self.recv.at[i],
            device_id={axis: at_distance(axis, r)},
            device_id_type=MESH,
        )

    def own(self, source, target):
        i = self.local_count
        self.local_count += 1
        return pltpu.make_async_copy(source, target, self.local.at[i])


def greet(distances):
    barrier = pltpu.get_barrier_semaphore()
    for axis, r in distances:
        pl.semaphore_signal(
            barrier, inc=1, device_id={axis: at_distance(axis, r)}, device_id_type=MESH
        )
    pl.semaphore_wait(barrier, len(distances))


def part_distances():
    return [("tensor", r) for r in range(1, 1 << bits_of("tensor"))]


def plane_distances():
    first, second = plane_moves()
    apart = sorted({move[1] for move in first} | {move[2] for move in second} | {1})
    return [("dp", r) for r in apart]


def halves_of(ref, half):
    rows = ref.shape[-2] // 2
    return ref.at[..., half * rows : (half + 1) * rows, :]


def slots(ref, *inner):
    return lambda slot: ref.at[(slot,) + inner]


def low_bit(r):
    return r & -r


class AlongParts:
    def __init__(self, mover, own, place):
        parts = 1 << bits_of("tensor")
        self.copy = mover.own(own, place(0))
        self.moves, self.there = {}, {0}
        for r in range(1, parts):
            rest = r - low_bit(r)
            source = own if rest == 0 else place(rest)
            self.moves[r] = mover.remote(source, place(r), "tensor", low_bit(r))
        self.order = sorted(self.moves, key=lambda r: (bin(r).count("1"), -r))

    def start(self):
        self.copy.start()
        for r in self.order:
            if r == low_bit(r):
                self.moves[r].start()

    def arrive(self, r):
        if r not in self.there:
            self.moves[r].wait_recv()
            self.there.add(r)

    def hand_on(self):
        for r in self.order:
            if r != low_bit(r):
                self.arrive(r - low_bit(r))
                self.moves[r].start()

    def finish(self):
        self.copy.wait()
        for r, move in self.moves.items():
            self.arrive(r)
            move.wait_send()


class OverPlane:
    def __init__(self, mover, held, near, far, given=(), via=None):
        first, second = plane_moves()
        plane = 1 << (bits_of("dp") - 1)
        sources = [held] + (list(given) or [near(slot) for slot, _ in first])
        here = [held] + list(given)
        self.loads = [] if via is None else [mover.own(here[i], via.at[i]) for i in range(len(here))]
        self.copies = [
            mover.own(here[i] if via is None else via.at[i], near(i)) for i in range(len(here))
        ]
        self.first = [] if given else [mover.remote(held, near(slot), "dp", r) for slot, r in first]
        self.second = [
            mover.remote(halves_of(sources[source], half), halves_of(near(slot), half), "dp", r)
            for slot, source, r, half in second
        ]
        sources += [near(slot) for slot in range(len(sources), plane)]
        self.cores = [mover.remote(values, far(i), "dp", 1) for i, values in enumerate(sources)]
        self.early = 1 + len(first)

    def start(self):
        for copy in self.loads or self.copies:
            copy.start()
        for move in self.first:
            move.start()
        self.cores[0].start()

    def relay(self):
        for move in self.first:
            move.wait_recv()
        for move in self.second + self.cores[1 : self.early]:
            move.start()

    def settle(self):
        for load, copy in zip(self.loads, self.copies):
            load.wait()
            copy.start()

    def finish(self):
        for move in self.second:
            move.wait_recv()
        for move in self.cores[self.early :]:
            move.start()
        for move in self.first + self.second:
            move.wait_send()
        for move in self.cores:
            move.wait()
        for copy in self.copies:
            copy.wait()


def plane_counts(given):
    first, second = plane_moves()
    plane = 1 << (bits_of("dp") - 1)
    return len(second) + plane + (0 if given else len(first)), 2 + 2 * given


def copy_semaphores(remote, local):
    copies = pltpu.SemaphoreType.DMA
    return [copies((remote,)), copies((remote,)), copies((local,))]


def anywhere():
    return pl.BlockSpec(memory_space=pltpu.HBM)


def hosting(body, counts, given):
    ins, outs = counts
    sources = sum(1 + count for count in given)

    def kernel(*refs):
        body_ins, held = refs[:ins], list(refs[ins : ins + sources])
        rest = refs[ins + sources :]
        body_outs, sides = rest[:outs], rest[outs : outs + 2 * len(given)]
        body_scratch = rest[outs + 2 * len(given) : -3 - len(given)]
        vias, mover = rest[-3 - len(given) : -3], Mover(*rest[-3:])
        weights = []
        for i, count in enumerate(given):
            own, *there = [held.pop(0) for _ in range(1 + count)]
            near, far = slots(sides[2 * i]), slots(sides[2 * i + 1])
            weights.append((OverPlane(mover, own, near, far, there, vias[i]), count))
        step, steps = 0, 1
        for i in range(HOST_RANK[body]):
            step = step * pl.num_programs(i) + pl.program_id(i)
            steps = steps * pl.num_programs(i)

        @pl.when(step == 0)
        def _():
            greet(plane_distances())
            for weight, count in weights:
                weight.start()
                if count:
                    weight.relay()

        @pl.when(step == steps * 3 // 4)
        def _():
            for weight, count in weights:
                weight.settle()
                if not count:
                    weight.relay()

        body(*body_ins, *body_outs, *body_scratch)

        @pl.when(step == steps - 1)
        def _():
            for weight, _ in weights:
                weight.finish()

    return kernel


def hosted_call(body, weights, cid, *, grid, in_specs, out_specs, out_shape, scratch_shapes=(), **rest):
    plane = 1 << (bits_of("dp") - 1)
    counts = (len(in_specs), len(out_specs))
    given = [len(there) for _, there in weights]
    totals = [sum(column) for column in zip(*[plane_counts(count) for count in given])]
    out_shape, vias, sources = list(out_shape), [], []
    for held, there in weights:
        out_shape += [shape_of((plane,) + held.shape, held.dtype)] * 2
        vias.append(pltpu.VMEM((1 + len(there),) + held.shape, held.dtype))
        sources += [held] + list(there)
    call = pl.pallas_call(
        hosting(body, counts, given),
        grid=grid,
        in_specs=in_specs + [anywhere()] * len(sources),
        out_specs=out_specs + [anywhere()] * 2 * len(weights),
        out_shape=out_shape,
        scratch_shapes=list(scratch_shapes) + vias + copy_semaphores(*totals),
        compiler_params=params(collective_id=cid, has_side_effects=True),
        **rest,
    )

    def run(*args):
        results = call(*args, *sources)
        return results[: counts[1]], results[counts[1] :]

    return run


def first_gather_kernel(
    first_ref, bias_ref, out_ref, in_ref, near, far, held_bias, near_out, far_out, held_in, held_out, send, recv, own
):
    mover = Mover(send, recv, own)
    parts, plane = near.shape[1], near.shape[0]
    moves, relays = plane_moves()
    along = AlongParts(mover, first_ref, lambda r: near.at[0, r])
    sources = [first_ref] + [near.at[0, r] for r in range(1, parts)]
    over = [[mover.remote(sources[r], near.at[slot, r], "dp", d) for slot, d in moves] for r in range(parts)]
    again = [
        [
            mover.remote(halves_of(near.at[source, r], half), halves_of(near.at[slot, r], half), "dp", d)
            for slot, source, d, half in relays
        ]
        for r in range(parts)
    ]
    cores = [
        [mover.remote(sources[r] if slot == 0 else near.at[slot, r], far.at[slot, r], "dp", 1) for slot in range(plane)]
        for r in range(parts)
    ]
    later = [
        AlongParts(mover, source, lambda r, held=held: held.at[r])
        for source, held in ((bias_ref, held_bias), (out_ref, held_out), (in_ref, held_in))
    ]
    outer = OverPlane(mover, held_out, slots(near_out), slots(far_out))
    greet(part_distances() + plane_distances())
    along.start()
    for move in over[0] + cores[0][:1]:
        move.start()
    along.hand_on()
    for units in later[:2]:
        units.start()
    for r in along.order:
        along.arrive(r)
        for move in over[r] + cores[r][:1]:
            move.start()
    for units in later[:2]:
        units.hand_on()
    later[2].start()
    later[1].finish()
    outer.start()
    later[2].hand_on()
    order = [0] + along.order
    for r in order:
        for i, (slot, _) in enumerate(moves):
            over[r][i].wait_recv()
            cores[r][slot].start()
        for move in again[r]:
            move.start()
    outer.relay()
    for r in order:
        for move in again[r]:
            move.wait_recv()
        for slot in range(1 + len(moves), plane):
            cores[r][slot].start()
    along.finish()
    for r in range(parts):
        for move in over[r] + again[r]:
            move.wait_send()
        for move in cores[r]:
            move.wait()
    outer.finish()
    for units in (later[0], later[2]):
        units.finish()


def first_gather(first, biases, outer, inner):
    parts, plane = 1 << bits_of("tensor"), 1 << (bits_of("dp") - 1)
    moves, relays = plane_moves()
    remote = 4 * (parts - 1) + parts * (len(moves) + len(relays) + plane) + plane_counts(0)[0]
    return pl.pallas_call(
        first_gather_kernel,
        in_specs=[pl.BlockSpec(memory_space=pltpu.VMEM)] * 4,
        out_specs=[anywhere()] * 6,
        out_shape=[shape_of((plane, parts) + first.shape, BF16)] * 2
        + [shape_of((parts,) + biases.shape, BF16)]
        + [shape_of((plane, parts) + outer.shape, BF16)] * 2
        + [shape_of((parts,) + inner.shape, BF16)],
        scratch_shapes=[pltpu.VMEM((parts,) + outer.shape, BF16)] + copy_semaphores(remote, 5),
        compiler_params=params(collective_id=3, has_side_effects=True),
        name="first_gather",
    )(first, biases, outer, inner)


class PartSum:
    def __init__(self, mover, distances, send, recv, slope, piece, near, far):
        self.moves = [
            mover.remote(send.at[i], recv.at[i], "tensor", r) for i, r in enumerate(distances)
        ]
        self.over = OverPlane(mover, piece, slots(near), slots(far))
        self.send, self.recv, self.slope, self.piece = send, recv, slope, piece
        self.distances = list(distances)

    def push(self, r, values):
        i = self.distances.index(r)
        self.send[i] = low(values)
        self.moves[i].start()

    def reach(self, own):
        for move in self.moves:
            move.wait_recv()
        total = own + jnp.sum(self.recv[...].astype(F32), axis=0)
        self.piece[...] = low(total * self.slope[...])
        self.over.start()

    def relay(self):
        self.over.relay()

    def finish(self):
        self.over.finish()
        for move in self.moves:
            move.wait_send()


def finale_kernel(
    down_ref, in_a, in_b, out_a, out_b, keep_0, keep_1, keep_2, keep_3, send_0, send_1, send_2, send_3,
    slope_in, slope_out, slope_q, sums_ref, near_d, far_d, near_i, far_i, near_o, far_o, near_q, far_q, sums_out,
    send_i, recv_i, piece_i, send_o, recv_o, piece_o, send_q, recv_q, piece_q, recv_0, recv_1, recv_2, recv_3,
    sums_near, sums_mid, sums_far, send, recv, own
):
    mover = Mover(send, recv, own)
    _, orders = plane_orders()
    quarter = keep_0.shape[0]
    half, parts = 2 * quarter, 4 * quarter
    datas = sums_near.shape[0]
    keeps, sends = (keep_0, keep_1, keep_2, keep_3), (send_0, send_1, send_2, send_3)
    recvs = (recv_0, recv_1, recv_2, recv_3)
    steps = [mover.remote(sends[i], recvs[i], "dp", 1 << orders[i % 2][-1]) for i in range(4)]
    down = OverPlane(mover, down_ref, slots(near_d), slots(far_d))
    inner = PartSum(mover, [half], send_i, recv_i, slope_in, piece_i, near_i, far_i)
    outer = PartSum(mover, range(1, parts), send_o, recv_o, slope_out, piece_o, near_o, far_o)
    first = PartSum(mover, range(1, parts), send_q, recv_q, slope_q, piece_q, near_q, far_q)
    sum_data = [mover.remote(sums_ref, sums_near.at[r], "dp", r) for r in range(1, datas)]
    sum_part = [mover.remote(sums_mid, sums_far.at[r], axis, r) for axis, r in part_distances()]

    def block(r):
        return keeps[r // quarter][r % quarter] + recvs[r // quarter][r % quarter].astype(F32)

    greet([("dp", r) for r in range(1, datas)] + part_distances())
    for step in steps:
        step.start()
    inner.push(half, in_b[...])
    for r in range(1, parts):
        outer.push(r, (out_a if r < half else out_b)[r % half])
    for i in (3, 2, 1, 0):
        steps[i].wait_recv()
        for r in range(i * quarter, (i + 1) * quarter):
            if r:
                first.push(r, block(r))
    down.start()
    for move in sum_data:
        move.start()
    inner.reach(in_a[...])
    outer.reach(out_a[0])
    for move in sum_data:
        move.wait()
    sums_near[0] = sums_ref[...]
    sums_mid[...] = jnp.sum(sums_near[...], axis=0)
    for move in sum_part:
        move.start()
    down.relay()
    inner.relay()
    outer.relay()
    first.reach(block(0))
    for move in sum_part:
        move.wait()
    sums_far[0] = sums_mid[...]
    sums_out[...] = jnp.sum(sums_far[...], axis=0)
    down.finish()
    inner.finish()
    outer.finish()
    first.relay()
    first.finish()
    for step in steps:
        step.wait_send()


def finale(down, inner, outer, first, slopes, sums):
    parts, plane, datas = 1 << bits_of("tensor"), 1 << (bits_of("dp") - 1), 1 << bits_of("dp")
    pieces = [down, slopes[1], slopes[2], slopes[0]]
    remote = 4 + 4 * plane_counts(0)[0] + 3 * (parts - 1) + 1 + datas - 1
    vmem = pl.BlockSpec(memory_space=pltpu.VMEM)
    scratch = []
    for piece, count in zip(pieces[1:], (1, parts - 1, parts - 1)):
        scratch += [pltpu.VMEM((count,) + piece.shape, BF16)] * 2 + [pltpu.VMEM(piece.shape, BF16)]
    scratch += [pltpu.VMEM(first[0][1].shape, BF16)] * 4
    scratch += [
        pltpu.VMEM((datas,) + sums.shape, F32),
        pltpu.VMEM(sums.shape, F32),
        pltpu.VMEM((parts,) + sums.shape, F32),
    ]
    out_shape = []
    for piece in pieces:
        out_shape += [shape_of((plane,) + piece.shape, BF16)] * 2
    keeps, sends = [side[0] for side in first], [side[1] for side in first]
    args = (down, *inner, *outer, *keeps, *sends, slopes[1], slopes[2], slopes[0], sums)
    results = pl.pallas_call(
        finale_kernel,
        in_specs=[vmem] * 9 + [anywhere()] * 4 + [vmem] * 4,
        out_specs=[anywhere()] * 8 + [vmem],
        out_shape=out_shape + [shape_of(sums.shape, F32)],
        scratch_shapes=scratch + copy_semaphores(remote, 4),
        compiler_params=params(collective_id=2, has_side_effects=True),
        name="finale",
    )(*args)
    return [results[2 * i : 2 * i + 2] for i in range(4)], results[8]


def take_blocks(ref, order_ref, here=slice(None)):
    return jnp.concatenate(
        [
            ref[here, pl.ds(pl.multiple_of(order_ref[j] * LANES, LANES), LANES)]
            for j in range(ref.shape[1] // LANES)
        ],
        axis=1,
    )


def put_blocks(ref, order_ref, values):
    for j in range(ref.shape[1] // LANES):
        ref[:, pl.ds(pl.multiple_of(order_ref[j] * LANES, LANES), LANES)] = values[
            :, j * LANES : (j + 1) * LANES
        ]


def fold_peak(values):
    return jnp.max(jnp.abs(values).reshape(-1, 8, LANES), axis=0)


def column_peak(values):
    peak = fold_peak(values[:, :LANES])
    for j in range(1, values.shape[1] // LANES):
        peak = jnp.maximum(peak, fold_peak(values[:, j * LANES : (j + 1) * LANES]))
    return peak


def prepare_kernel(
    order_ref, range_ref, peak_ref, x_ref, qkv_ref, out_ref, in_ref, down_ref, level_ref, quant_ref,
    *refs
):
    level = DECAY * range_ref[0] + (1.0 - DECAY) * peak_ref[6:7, 0:1]
    level_ref[...] = jnp.broadcast_to(level, level_ref.shape)
    for i, ref in enumerate((qkv_ref, out_ref, in_ref, down_ref)):
        for j in range(ref.shape[0]):
            place = j if i == 0 else i + 2
            own = 0.5 * peak_ref[place : place + 1, 0:1]
            tangent = jnp.tanh(ref[j].astype(F32) / own)
            refs[2 * i][j] = low(own * tangent)
            refs[2 * i + 1][j] = 1.0 - tangent * tangent
    rows = 256

    @pl.loop(0, x_ref.shape[0] // rows)
    def _(step):
        here = pl.ds(pl.multiple_of(step * rows, rows), rows)
        x = take_blocks(x_ref, order_ref, here).astype(F32)
        quant_ref[here, :] = low(level * jnp.tanh(x / level))


def prepare(peaks, previous, x, own, order):
    vmem = pl.BlockSpec(memory_space=pltpu.VMEM)
    out_shape = [shape_of((8, LANES), F32), shape_of(x.shape, BF16)]
    for values in own:
        out_shape += [shape_of(values.shape, BF16), shape_of(values.shape, F32)]
    levels, quant, *rest = pl.pallas_call(
        prepare_kernel,
        in_specs=[in_smem(), in_smem()] + [vmem] * 6,
        out_specs=[vmem] * 10,
        out_shape=out_shape,
        compiler_params=params(),
        name="prepare",
    )(order, previous, peaks, x, *own)
    return levels, quant, rest[::2], rest[1::2]


def qkv_kernel(x_ref, near_ref, far_ref, b_ref, o_ref):
    half = x_ref.shape[1] // 2
    total = dot(x_ref[:, :half], flat(near_ref[...])) + dot(x_ref[:, half:], flat(far_ref[...]))
    o_ref[...] = low(total + b_ref[...])


def qkv_rows(x, weights, bias):
    near, far = weights
    plane, parts, kinds, rows, c = near.shape
    tokens, width = x.shape
    weight_spec = pl.BlockSpec((plane, None, None, rows, c), lambda r, i: (0, r, i, 0, 0))
    return pl.pallas_call(
        qkv_kernel,
        grid=(parts, kinds),
        in_specs=[
            pl.BlockSpec((tokens, width), lambda r, i: (0, 0)),
            weight_spec,
            weight_spec,
            pl.BlockSpec((None, 1, c), lambda r, i: (i, 0, r)),
        ],
        out_specs=pl.BlockSpec((None, tokens, c), lambda r, i: (i, 0, r)),
        out_shape=shape_of((kinds, tokens, parts * c), BF16),
        compiler_params=params(),
        cost_estimate=cost(2 * tokens * width * kinds * parts * c, 14 * MIB),
        name="qkv",
    )(x, near, far, bias)


def fill_mask(mask_ref, col_ref, row_ref):
    mask_ref[...] = jnp.where(col_ref[...] == row_ref[...], 0.0, MASKED).astype(F32)


def attend_kernel(
    skip, q_ref, k_ref, v_ref, col_ref, row_ref, lse_before, peak_before, *refs
):
    o_ref, lse_ref, peak_ref, mask_ref, sums_ref = refs[-5:]
    row, pair = pl.program_id(0), pl.program_id(1)
    factor = HD ** (-0.5)

    @pl.when(pair == 0)
    def _():
        fill_mask(mask_ref, col_ref, row_ref)
        sums_ref[...] = lse_before[...].T

    @pl.when((pair == 0) & (row == 0))
    def _():
        peak_ref[...] = peak_before[...]

    rows = 256
    lanes = lax.broadcasted_iota(jnp.int32, (rows, LANES), 1)
    for start in range(0, SEQ, rows):
        here = pl.ds(start, rows)
        q = q_ref[here, :] * jnp.asarray(factor, BF16)
        parts = []
        sums = sums_ref[here, :]
        for head in range(LANES // HD):
            own = lanes // HD == head
            scores = dot_cols(jnp.where(own, q, jnp.zeros_like(q)), k_ref[...]) + mask_ref[here, :]
            row_max = jnp.max(scores, axis=-1, keepdims=True)
            exponent = jnp.exp(scores - row_max)
            totals = jnp.sum(exponent, axis=-1, keepdims=True)
            probs = low(exponent * (1.0 / totals))
            parts.append(dot(probs, v_ref[...]))
            sums = jnp.where(lanes == (pair + skip) * (LANES // HD) + head, row_max + jnp.log(totals), sums)
        context = parts[0]
        for head in range(1, LANES // HD):
            context = jnp.where(lanes // HD == head, parts[head], context)
        o_ref[here, :] = context
        sums_ref[here, :] = sums
        peak_ref[...] = jnp.maximum(peak_ref[...], fold_peak(context))

    @pl.when(pair == pl.num_programs(1) - 1)
    def _():
        lse_ref[...] = sums_ref[...].T


def attend_first_kernel(*refs):
    attend_kernel(0, *refs)


def attend_last_kernel(*refs):
    attend_kernel(pl.num_programs(1), *refs)


def attend(qkv, cols, rows, lse, peak, context=None, weights=()):
    _, tokens, width = qkv.shape
    held = tokens // SEQ
    last = context is not None
    skip = width // LANES // 2 if last else 0

    def side(i):
        return pl.BlockSpec((None, SEQ, LANES), lambda r, j: (i, r, j + skip))

    sums = pl.BlockSpec((None, LANES, SEQ), lambda r, j: (r, 0, 0))
    small = pl.BlockSpec((8, LANES), lambda r, j: (0, 0))
    setup = dict(
        grid=(held, width // LANES // 2),
        in_specs=[
            side(0),
            side(1),
            side(2),
            pl.BlockSpec((None, SEQ, 1), lambda r, j: (r, 0, 0)),
            pl.BlockSpec((None, 1, SEQ), lambda r, j: (r, 0, 0)),
            sums,
            small,
        ],
        out_specs=[pl.BlockSpec((SEQ, LANES), lambda r, j: (r, j + skip)), sums, small],
        out_shape=[
            shape_of((tokens, width), F32),
            shape_of((held, LANES, SEQ), F32),
            shape_of((8, LANES), F32),
        ],
        scratch_shapes=[pltpu.VMEM((SEQ, SEQ), F32), pltpu.VMEM((SEQ, LANES), F32)],
        cost_estimate=cost(15e9, 40 * MIB),
        name="attend",
    )
    args = (qkv, qkv, qkv, cols, rows, lse, peak)
    if not last:
        return pl.pallas_call(attend_first_kernel, compiler_params=params(), **setup)(*args)
    setup["in_specs"].append(anywhere())
    run = hosted_call(
        attend_last_kernel, weights, 5, input_output_aliases={len(args): 0}, **setup
    )
    return run(*args, context)


def attend_back_kernel(
    c, first, order_ref, q_ref, k_ref, v_ref, g_ref, col_ref, row_ref, lse_ref, before_ref, dq_ref, dk_ref,
    dv_ref, sum_ref, mask_ref
):
    pair = pl.program_id(1)

    @pl.when((pair == 0) & (pl.program_id(0) == 0))
    def _():
        sum_ref[...] = before_ref[...]

    factor = HD ** (-0.5)

    @pl.when(pair == 0)
    def _():
        fill_mask(mask_ref, col_ref, row_ref)

    lanes = lax.broadcasted_iota(jnp.int32, (SEQ, LANES), 1)
    q, k, v, g = q_ref[...], k_ref[...], v_ref[...], g_ref[...]
    q_sums, k_sums, v_sums = [], [], []
    for head in range(LANES // HD):
        own = lanes // HD == head
        zero = jnp.zeros_like(q)
        q_own = jnp.where(own, q * jnp.asarray(factor, BF16), zero)
        g_own = jnp.where(own, g, zero)
        logsum = lse_ref[pl.ds((pair + first // LANES) * (LANES // HD) + head, 1), :]
        probs = jnp.exp(dot_cols(k, q_own) + mask_ref[...] - logsum)
        v_sums.append(dot(low(probs), g))
        grad_probs = dot_cols(v, g_own)
        mean_grad = jnp.sum(probs * grad_probs, axis=0, keepdims=True)
        grad_scores = low(factor * probs * (grad_probs - mean_grad))
        k_sums.append(dot(grad_scores, q))
        q_sums.append(dot_rows(grad_scores, k))

    def join(parts):
        joined = parts[0]
        for head in range(1, LANES // HD):
            joined = jnp.where(lanes // HD == head, parts[head], joined)
        return low(joined)

    dq, dv = join(q_sums), join(v_sums)
    dq_ref[...] = dq
    dk_ref[...] = join(k_sums)
    dv_ref[...] = dv
    column = first + pair * LANES
    place = order_ref[column // c] * c + column % c
    here = pl.ds(pl.multiple_of(place, LANES), LANES)
    sum_ref[0:1, here] += jnp.sum(dq.astype(F32), axis=0, keepdims=True)
    sum_ref[1:2, here] += jnp.sum(dv.astype(F32), axis=0, keepdims=True)


def attend_back(qkv, grad, cols, rows, lse, before, part_order, c, first):
    _, tokens, inner = qkv.shape
    width = grad.shape[1]
    held = tokens // SEQ
    skip = first // LANES

    def side(i):
        return pl.BlockSpec((None, SEQ, LANES), lambda r, j: (i, r, j + skip))

    block = pl.BlockSpec((SEQ, LANES), lambda r, j: (r, j))
    sums = pl.BlockSpec((8, inner), lambda r, j: (0, 0))
    return pl.pallas_call(
        partial(attend_back_kernel, c, first),
        grid=(held, width // LANES),
        in_specs=[
            in_smem(),
            side(0),
            side(1),
            side(2),
            block,
            pl.BlockSpec((None, SEQ, 1), lambda r, j: (r, 0, 0)),
            pl.BlockSpec((None, 1, SEQ), lambda r, j: (r, 0, 0)),
            pl.BlockSpec((None, LANES, SEQ), lambda r, j: (r, 0, 0)),
            sums,
        ],
        out_specs=[block, block, block, sums],
        out_shape=[shape_of((tokens, width), BF16)] * 3 + [shape_of((8, inner), F32)],
        scratch_shapes=[pltpu.VMEM((SEQ, SEQ), F32)],
        compiler_params=params(),
        cost_estimate=cost(15e9, 50 * MIB),
        name="attend_back",
    )(part_order, qkv, qkv, qkv, grad, cols, rows, lse, before)


def project(values, *sides):
    halves = []
    for refs in (sides[::2], sides[1::2]):
        total, place = None, 0
        for ref in refs:
            c = ref.shape[3]
            for r in range(ref.shape[1]):
                term = dot_cols(values[:, place : place + c], flat(ref[:, r]))
                total = term if total is None else total + term
                place += c
        halves.append(total)
    return jnp.concatenate(halves, axis=1)


def norm_parts(summed):
    center = summed - jnp.mean(summed, axis=-1, keepdims=True)
    inverse = lax.rsqrt(jnp.mean(center * center, axis=-1, keepdims=True) + EPS)
    return center * inverse, inverse


def norm_back(upstream, normal, inverse, gain):
    scaled = upstream * gain
    return inverse * (
        scaled
        - jnp.mean(scaled, axis=-1, keepdims=True)
        - normal * jnp.mean(scaled * normal, axis=-1, keepdims=True)
    )


def add_sums(ref, order_ref, sums):
    @pl.when(pl.program_id(0) == 0)
    def _():
        ref[...] = jnp.zeros_like(ref)

    for i, values in enumerate(sums):
        total = jnp.sum(values, axis=0, keepdims=True)
        for j in range(ref.shape[1] // LANES):
            here = pl.ds(pl.multiple_of(order_ref[j] * LANES, LANES), LANES)
            ref[i : i + 1, here] += total[:, j * LANES : (j + 1) * LANES]


def first_norm_kernel(
    order_ref, ctx_ref, level_ref, near_ref, far_ref, x_ref, row_ref, quant_ref, normed_ref, normal_ref,
    inverse_ref, peak_ref
):
    level = level_ref[1:2, 0:1]
    quant = low(level * jnp.tanh(ctx_ref[...] / level))
    quant_ref[...] = quant
    vectors = take_blocks(row_ref, order_ref)
    summed = take_blocks(x_ref, order_ref).astype(F32) + project(quant, near_ref, far_ref)
    normal, inverse = norm_parts(summed + vectors[0:1, :])
    normed = normal * vectors[1:2, :] + vectors[2:3, :]
    normed_ref[...] = normed
    normal_ref[...] = normal
    inverse_ref[...] = inverse

    @pl.when(pl.program_id(0) == 0)
    def _():
        peak_ref[...] = jnp.zeros_like(peak_ref)

    peak_ref[...] = jnp.maximum(peak_ref[...], column_peak(normed))


def whole(values):
    dims = values.shape
    return pl.BlockSpec(dims, lambda *steps: (0,) * len(dims))


def first_norm(context, level, weights, x, vectors, order):
    near, far = weights
    tokens, width = x.shape
    inner = context.shape[1]
    rows = 512

    def block(columns):
        return pl.BlockSpec((rows, columns), lambda t: (t, 0))

    return pl.pallas_call(
        first_norm_kernel,
        grid=(tokens // rows,),
        in_specs=[
            in_smem(),
            block(inner),
            whole(level),
            whole(near),
            whole(far),
            block(width),
            whole(vectors),
        ],
        out_specs=[
            block(inner),
            block(width),
            block(width),
            block(1),
            pl.BlockSpec((8, LANES), lambda t: (0, 0)),
        ],
        out_shape=[
            shape_of((tokens, inner), BF16),
            shape_of((tokens, width), F32),
            shape_of((tokens, width), F32),
            shape_of((tokens, 1), F32),
            shape_of((8, LANES), F32),
        ],
        compiler_params=params(),
        cost_estimate=cost(2 * tokens * width * inner, 20 * MIB),
        name="first_norm",
    )(order, context, level, near, far, x, vectors)


def hidden_kernel(normed_ref, level_ref, near_ref, far_ref, b_ref, quant_ref, act_ref, slope_ref, peak_ref):
    half = normed_ref.shape[1] // 2

    @pl.when(pl.program_id(0) == 0)
    def _():
        peak_ref[...] = jnp.zeros_like(peak_ref)
        level = level_ref[2:3, 0:1]
        quant_ref[...] = low(level * jnp.tanh(normed_ref[...] / level))

    hidden = dot(quant_ref[:, :half], flat(near_ref[...]))
    hidden = hidden + dot(quant_ref[:, half:], flat(far_ref[...])) + b_ref[...]
    share = 0.5 + 0.5 * lax.erf(hidden * (0.5**0.5))
    active = hidden * share
    act_ref[...] = active
    slope_ref[...] = share + hidden * ((0.5 / jnp.pi) ** 0.5 * jnp.exp(-0.5 * hidden * hidden))
    peak_ref[...] = jnp.maximum(peak_ref[...], column_peak(active))


def hidden_rows(normed, level, weights, bias, held_down):
    near, far = weights
    plane, parts, rows, c = near.shape
    tokens, width = normed.shape
    step = min(c, 512)
    cuts = c // step
    weight_spec = pl.BlockSpec((plane, None, rows, step), lambda s: (0, s // cuts, 0, s % cuts))
    block = pl.BlockSpec((tokens, step), lambda s: (0, s))
    run = hosted_call(
        hidden_kernel,
        [(held_down, ())],
        6,
        grid=(parts * cuts,),
        in_specs=[
            whole(normed),
            whole(level),
            weight_spec,
            weight_spec,
            pl.BlockSpec((1, step), lambda s: (0, s)),
        ],
        out_specs=[
            pl.BlockSpec((tokens, width), lambda s: (0, 0)),
            block,
            block,
            pl.BlockSpec((8, LANES), lambda s: (0, 0)),
        ],
        out_shape=[
            shape_of((tokens, width), BF16),
            shape_of((tokens, parts * c), F32),
            shape_of((tokens, parts * c), F32),
            shape_of((8, LANES), F32),
        ],
        cost_estimate=cost(2 * tokens * width * parts * c, 50 * MIB),
        name="hidden",
    )
    return run(normed, level, near, far, bias)


def second_norm_kernel(
    order_ref, act_ref, slope_ref, level_ref, near_a, far_a, near_b, far_b, normed_ref, grad_ref, row_ref,
    quant_ref, back_ref, out_ref, sum_ref, branch_ref, terms_ref
):
    level = level_ref[3:4, 0:1]
    tangent = jnp.tanh(act_ref[...] / level)
    quant = low(level * tangent)
    quant_ref[...] = quant
    back_ref[...] = (1.0 - tangent * tangent) * slope_ref[...]
    vectors = take_blocks(row_ref, order_ref)
    summed = normed_ref[...] + project(quant, near_a, far_a, near_b, far_b) + vectors[3:4, :]
    normal, inverse = norm_parts(summed)
    gain = vectors[4:5, :]
    put_blocks(out_ref, order_ref, low(normal * gain + vectors[5:6, :]))
    upstream = take_blocks(grad_ref, order_ref).astype(F32)
    grad_sum = norm_back(upstream, normal, inverse, gain)
    sum_ref[...] = grad_sum
    branch_ref[...] = low(grad_sum)
    add_sums(terms_ref, order_ref, (grad_sum, upstream * normal, upstream))


def second_norm(active, slope, level, weights, normed, grad, vectors, order):
    tokens, width = normed.shape
    inner = active.shape[1]
    rows = 256

    def block(columns):
        return pl.BlockSpec((rows, columns), lambda t: (t, 0))

    return pl.pallas_call(
        second_norm_kernel,
        grid=(tokens // rows,),
        in_specs=[
            in_smem(),
            block(inner),
            block(inner),
            whole(level),
            *[whole(side) for side in weights],
            block(width),
            block(width),
            whole(vectors),
        ],
        out_specs=[
            block(inner),
            block(inner),
            block(width),
            block(width),
            block(width),
            pl.BlockSpec((8, width), lambda t: (0, 0)),
        ],
        out_shape=[
            shape_of((tokens, inner), BF16),
            shape_of((tokens, inner), F32),
            shape_of((tokens, width), BF16),
            shape_of((tokens, width), F32),
            shape_of((tokens, width), BF16),
            shape_of((8, width), F32),
        ],
        compiler_params=params(),
        cost_estimate=cost(2 * tokens * width * inner, 80 * MIB),
        name="second_norm",
    )(order, active, slope, level, *weights, normed, grad, vectors)


def weight_grad_specs(x, grads, parts, plane):
    tokens, width = x.shape
    count = len(grads)
    c = grads[0].shape[1] // parts
    step = min(c, 1024)
    cuts = c // step
    dims = (plane, parts, count, width // (2 * plane), c)
    in_specs = [pl.BlockSpec((tokens, step), lambda r, j: (0, r * cuts + j))] * count
    out_spec = pl.BlockSpec((plane, None, count, dims[3], step), lambda r, j: (0, r, 0, 0, j))
    return dims, (parts, cuts), in_specs, out_spec, 2 * tokens * width * parts * c * count


def weight_send_kernel(count, x_ref, *refs):
    h_refs, (send_ref, turned_ref) = refs[:count], refs[count:]

    @pl.when((pl.program_id(0) == 0) & (pl.program_id(1) == 0))
    def _():
        turned_ref[...] = x_ref[...].T

    for i, h_ref in enumerate(h_refs):
        h = h_ref[...]
        send_ref[:, i] = low(dot(turned_ref[...], h)).reshape(send_ref.shape[0], -1, h.shape[1])


def weight_send(x, grads, parts, plane):
    dims, grid, in_specs, out_spec, flops = weight_grad_specs(x, grads, parts, plane)
    tokens, width = x.shape
    return pl.pallas_call(
        partial(weight_send_kernel, len(grads)),
        grid=grid,
        in_specs=[pl.BlockSpec((tokens, width // 2), lambda r, j: (0, 1))] + in_specs,
        out_specs=out_spec,
        out_shape=shape_of(dims, BF16),
        scratch_shapes=[pltpu.VMEM((width // 2, tokens), BF16)],
        compiler_params=params(),
        cost_estimate=cost(flops / 2, 16 * MIB),
        name="weight_send",
    )(x, *grads)


def weight_keep_kernel(count, split, x_ref, other_ref, *refs):
    h_refs, outs, turned_ref = refs[:count], refs[count:-1], refs[-1]
    half = pl.num_programs(0) // 2

    @pl.when((pl.program_id(0) == 0) & (pl.program_id(1) == 0))
    def _():
        turned_ref[...] = x_ref[...].T

    for side in range(2):

        @pl.when(pl.program_id(0) // half == side)
        def _(side=side):
            keep_ref, send_ref = outs[2 * side : 2 * side + 2]
            for i, h_ref in enumerate(h_refs):
                h = h_ref[...]
                total = dot(turned_ref[...], h).reshape(other_ref.shape[0], -1, h.shape[1])
                for j, slot in enumerate(split[side][0]):
                    keep_ref[j, i] = total[slot] + other_ref[slot, i].astype(F32)
                for j, slot in enumerate(split[side][1]):
                    send_ref[j, i] = low(total[slot] + other_ref[slot, i].astype(F32))


def weight_keep(x, grads, other, parts, plane):
    dims, (_, cuts), in_specs, out_spec, flops = weight_grad_specs(x, grads, parts, plane)
    tokens, width = x.shape
    half = parts // 2
    block = (plane // 2, None, len(grads), dims[3], dims[4] // cuts)
    near = pl.BlockSpec(
        block, lambda r, j: (0, jnp.minimum(r, half - 1), 0, 0, jnp.where(r < half, j, cuts - 1))
    )
    far = pl.BlockSpec(block, lambda r, j: (0, jnp.maximum(r - half, 0), 0, 0, jnp.where(r < half, 0, j)))
    small = (plane // 2, half) + dims[2:]
    keep_a, send_a, keep_b, send_b = pl.pallas_call(
        partial(weight_keep_kernel, len(grads), first_split(bits_of("dp") - 1)),
        grid=(parts, cuts),
        in_specs=[pl.BlockSpec((tokens, width // 2), lambda r, j: (0, 0)), out_spec] + in_specs,
        out_specs=[near, near, far, far],
        out_shape=[shape_of(small, F32), shape_of(small, BF16)] * 2,
        scratch_shapes=[pltpu.VMEM((width // 2, tokens), BF16)],
        compiler_params=params(),
        cost_estimate=cost(flops / 2, 24 * MIB),
        name="weight_keep",
    )(x, other, *grads)
    return [keep_a, keep_b], [send_a, send_b]


def grad_hidden_kernel(cuts, order_ref, g_ref, near_a, far_a, near_b, far_b, back_ref, o_ref, sum_ref):
    half = g_ref.shape[1] // 2
    block = pl.program_id(0)
    columns = back_ref.shape[1]

    @pl.when(block == 0)
    def _():
        sum_ref[...] = jnp.zeros_like(sum_ref)

    for side, (near_ref, far_ref) in enumerate(((near_a, far_a), (near_b, far_b))):

        @pl.when(block * 2 // pl.num_programs(0) == side)
        def _(near_ref=near_ref, far_ref=far_ref):
            grad = dot(g_ref[:, :half], flat(near_ref[...])) + dot(g_ref[:, half:], flat(far_ref[...]))
            grad = low(grad * back_ref[...])
            o_ref[...] = grad
            total = jnp.sum(grad.astype(F32), axis=0, keepdims=True)
            start = pl.multiple_of((block % cuts) * columns, LANES)
            sum_ref[pl.ds(order_ref[block // cuts], 1), pl.ds(start, columns)] = total


def grad_hidden_rows(grad, weights, back, part_order):
    plane, half, rows, c = weights[0].shape
    parts = 2 * half
    tokens, width = grad.shape
    step = min(c, 1024)
    cuts = c // step
    block = (plane, None, rows, step)
    first = pl.BlockSpec(
        block,
        lambda s: (0, jnp.minimum(s // cuts, half - 1), 0, jnp.where(s < half * cuts, s % cuts, cuts - 1)),
    )
    last = pl.BlockSpec(
        block,
        lambda s: (0, jnp.maximum(s // cuts - half, 0), 0, jnp.where(s < half * cuts, 0, s % cuts)),
    )
    block = pl.BlockSpec((tokens, step), lambda s: (0, s))
    return pl.pallas_call(
        partial(grad_hidden_kernel, cuts),
        grid=(parts * cuts,),
        in_specs=[in_smem(), whole(grad), first, first, last, last, block],
        out_specs=[block, pl.BlockSpec((parts, c), lambda s: (0, 0))],
        out_shape=[shape_of((tokens, parts * c), BF16), shape_of((parts, c), F32)],
        compiler_params=params(),
        cost_estimate=cost(2 * tokens * width * parts * c, 34 * MIB),
        name="grad_hidden",
    )(part_order, grad, *weights, back)


def first_back_kernel(
    order_ref, g_ref, near_ref, far_ref, normed_ref, normal_ref, inverse_ref, sum_two_ref, level_ref, row_ref,
    sum_ref, low_ref, terms_ref
):
    level = level_ref[2:3, 0:1]
    tangent = jnp.tanh(normed_ref[...] / level)
    grad = project(g_ref[...], near_ref, far_ref) * (1.0 - tangent * tangent) + sum_two_ref[...]
    normal = normal_ref[...]
    gain = take_blocks(row_ref, order_ref)[1:2, :]
    grad_sum = norm_back(grad, normal, inverse_ref[...], gain)
    sum_ref[...] = grad_sum
    low_ref[...] = low(grad_sum)
    add_sums(terms_ref, order_ref, (grad_sum, grad * normal, grad))


def first_back(grad, weights, normed, normal, inverse, sum_two, level, vectors, order):
    near, far = weights
    tokens, width = normed.shape
    inner = grad.shape[1]
    rows = 256

    def block(columns):
        return pl.BlockSpec((rows, columns), lambda t: (t, 0))

    return pl.pallas_call(
        first_back_kernel,
        grid=(tokens // rows,),
        in_specs=[
            in_smem(),
            block(inner),
            whole(near),
            whole(far),
            block(width),
            block(width),
            block(1),
            block(width),
            whole(level),
            whole(vectors),
        ],
        out_specs=[block(width), block(width), pl.BlockSpec((8, width), lambda t: (0, 0))],
        out_shape=[
            shape_of((tokens, width), F32),
            shape_of((tokens, width), BF16),
            shape_of((8, width), F32),
        ],
        compiler_params=params(),
        cost_estimate=cost(2 * tokens * width * inner, 36 * MIB),
        name="first_back",
    )(order, grad, near, far, normed, normal, inverse, sum_two, level, vectors)


def grad_context_kernel(g_ref, near_ref, far_ref, ctx_ref, level_ref, o_ref):
    half = g_ref.shape[1] // 2
    level = level_ref[1:2, 0:1]
    tangent = jnp.tanh(ctx_ref[...] / level)
    grad = dot(g_ref[:, :half], flat(near_ref[...])) + dot(g_ref[:, half:], flat(far_ref[...]))
    o_ref[...] = low(grad * (1.0 - tangent * tangent))


def grad_context_rows(grad, weights, context, level, first):
    near, far = weights
    plane, parts, rows, c = near.shape
    parts = parts // 2
    tokens, width = grad.shape
    weight_spec = pl.BlockSpec((plane, None, rows, c), lambda r: (0, r + first, 0, 0))
    block = pl.BlockSpec((tokens, c), lambda r: (0, r))
    return pl.pallas_call(
        grad_context_kernel,
        grid=(parts,),
        in_specs=[
            whole(grad),
            weight_spec,
            weight_spec,
            pl.BlockSpec((tokens, c), lambda r: (0, r + first)),
            whole(level),
        ],
        out_specs=block,
        out_shape=shape_of((tokens, parts * c), BF16),
        compiler_params=params(),
        cost_estimate=cost(2 * tokens * width * parts * c, 10 * MIB),
        name="grad_context",
    )(grad, near, far, context, level)


def grad_input_kernel(order_ref, *refs):
    g_refs, (near_ref, far_ref, sum_ref, x_ref, level_ref, o_ref) = refs[:6], refs[6:]
    level = level_ref[0:1, 0:1]
    half = near_ref.shape[1] // 2
    total = None
    for side in range(2):
        for i in range(3):
            term = project(
                g_refs[side * 3 + i][...],
                near_ref.at[:, side * half : (side + 1) * half, i],
                far_ref.at[:, side * half : (side + 1) * half, i],
            )
            total = term if total is None else total + term
    tangent = jnp.tanh(take_blocks(x_ref, order_ref).astype(F32) / level)
    put_blocks(o_ref, order_ref, low(sum_ref[...] + total * (1.0 - tangent * tangent)))


def grad_input(grads, weights, grad_sum, x, level, order):
    near, far = weights
    tokens, width = x.shape
    inner = grads[0].shape[1]
    rows = 256

    def block(columns):
        return pl.BlockSpec((rows, columns), lambda t: (t, 0))

    return pl.pallas_call(
        grad_input_kernel,
        grid=(tokens // rows,),
        in_specs=[in_smem()]
        + [block(inner)] * 6
        + [whole(near), whole(far), block(width), block(width), whole(level)],
        out_specs=block(width),
        out_shape=shape_of((tokens, width), BF16),
        compiler_params=params(),
        cost_estimate=cost(12 * tokens * width * inner, 20 * MIB),
        name="grad_input",
    )(order, *grads, near, far, grad_sum, x, level)


def place_kernel(turns, order_ref, *refs):
    ins, outs = refs[: 2 * len(turns)], refs[2 * len(turns) :]
    core = pl.program_id(0) * 2 // pl.num_programs(0)
    for side in range(2):

        @pl.when(core == side)
        def _(side=side):
            for i, turn in enumerate(turns):
                values = ins[2 * i + side]
                if turn:
                    outs[i][...] = values[0].astype(F32).T
                else:
                    outs[i][...] = values[...].astype(F32)


def place_grads(groups, turns, blocks):
    plane, _, rows, _ = groups[0][0].shape
    width = 2 * plane * rows
    results = [None] * len(groups)
    if rows % LANES:
        back = jnp.zeros((2 * plane,), jnp.int32).at[blocks].set(jnp.arange(2 * plane, dtype=jnp.int32))
        for i, (near, far) in enumerate(groups):
            if turns[i]:
                split = jnp.concatenate([near, far], axis=0)[:, 0]
                results[i] = jnp.take(split, back, axis=0).astype(F32).reshape(width, -1).T
    todo = [i for i in range(len(groups)) if results[i] is None]
    in_specs, out_specs, out_shape, args = [], [], [], []
    for i in todo:
        near, far = groups[i]
        _, kinds, _, c = near.shape
        block = (None, kinds, rows, c)
        in_specs.append(pl.BlockSpec(block, lambda p, order: (jnp.minimum(p, plane - 1), 0, 0, 0)))
        in_specs.append(pl.BlockSpec(block, lambda p, order: (jnp.maximum(p - plane, 0), 0, 0, 0)))
        args += [near, far]
        if turns[i]:
            out_specs.append(pl.BlockSpec((c, rows), lambda p, order: (0, order[p])))
            out_shape.append(shape_of((c, width), F32))
        else:
            out_specs.append(pl.BlockSpec((kinds, rows, c), lambda p, order: (0, order[p], 0)))
            out_shape.append(shape_of((kinds, width, c), F32))
    placed = pl.pallas_call(
        partial(place_kernel, [turns[i] for i in todo]),
        grid_spec=pltpu.PrefetchScalarGridSpec(
            num_scalar_prefetch=1, grid=(2 * plane,), in_specs=in_specs, out_specs=out_specs
        ),
        out_shape=out_shape,
        compiler_params=params(),
        name="place_grads",
    )(blocks.astype(jnp.int32), *args)
    for i, values in zip(todo, placed):
        results[i] = values
    return results


def but_last(keeps, sends):
    return scatter_plane(keeps, sends, True)


def scatter_plane_of(chain, x, grads, other, token, parts, plane):
    return chain(*weight_keep(tie(x, [token]), grads, other, parts, plane))


HOST_RANK = {attend_last_kernel: 2, hidden_kernel: 1}


def doc_segments(doc_lengths, length):
    doc_ends = jnp.cumsum(doc_lengths, axis=1, dtype=jnp.int32)
    places = jnp.arange(length, dtype=jnp.int32)
    return jnp.sum(
        (places[None, :, None] >= doc_ends[:, None, :]).astype(jnp.int32), axis=2, dtype=jnp.int32
    )


def soft_clip(values, clip_level):
    return clip_level * jnp.tanh(values / clip_level)


def clip_slope(values, clip_level):
    tangent = jnp.tanh(values / clip_level)
    return 1.0 - tangent * tangent


def own_block(values, axis):
    rows = values.shape[axis] // lax.axis_size("dp")
    return lax.dynamic_slice_in_dim(values, lax.axis_index("dp") * rows, rows, axis)


def local(
    mesh, layer_input, grad_output, doc_lengths, ranges, w_qkv, bias_qv, w_out, b_out, gain_one,
    shift_one, w_in, b_in, w_down, b_down, gain_two, shift_two
):
    datas, parts = lax.axis_size("dp"), lax.axis_size("tensor")
    data, part = lax.axis_index("dp"), lax.axis_index("tensor")
    plane = datas // 2
    tokens, width = layer_input.shape
    rows = width // datas

    places = jnp.arange(datas)
    distance = (places % plane) * 2 + places // plane
    blocks = data ^ distance
    if rows % LANES == 0:
        per_block = rows // LANES
        order = (blocks[:, None] * per_block + jnp.arange(per_block)).reshape(-1).astype(jnp.int32)
    else:
        order = jnp.arange(width // LANES, dtype=jnp.int32)

    def arrange(values):
        split = values.reshape(values.shape[:-1] + (datas, rows))
        return jnp.take(split, blocks, axis=-2).reshape(values.shape)

    def restore(values):
        split = values.reshape(values.shape[:-1] + (datas, rows))
        back = jnp.zeros((datas,), jnp.int32).at[blocks].set(places.astype(jnp.int32))
        return jnp.take(split, back, axis=-2).reshape(values.shape)

    def arrange_rows(values):
        return values if rows % LANES == 0 else arrange(values)

    def restore_rows(values):
        return values if rows % LANES == 0 else restore(values)

    part_order = (part ^ jnp.arange(parts)).astype(jnp.int32)
    x = arrange_rows(layer_input)
    upstream = arrange_rows(grad_output)
    vectors = jnp.stack([b_out, gain_one, shift_one, b_down, gain_two, shift_two, b_out, b_out])
    vectors = arrange_rows(vectors).astype(F32)

    own = [
        own_block(w_qkv, 1),
        own_block(w_out, 1).T[None],
        own_block(w_in, 0)[None],
        own_block(w_down, 1).T[None],
    ]
    peaks = [jnp.max(jnp.abs(own[0][i].astype(F32)), axis=0) for i in range(3)]
    peaks += [jnp.max(jnp.abs(values[0].astype(F32)), axis=0) for values in own[1:]]
    peaks += [jnp.max(jnp.abs(x.astype(F32)), axis=0)]
    peaks = [jnp.max(values.reshape(-1, LANES), axis=0) for values in peaks]
    peaks = jnp.stack(peaks + [jnp.zeros_like(peaks[0])])
    reached = exchange_all(peaks, mesh, "rows", ranges, peaks)
    levels, quant_input, quant_own, slopes = prepare(reached, ranges, x, own, order)
    biases = jnp.concatenate([bias_qv.reshape(-1), b_in])
    count = biases.shape[0]
    biases = jnp.pad(biases, (0, -count % (16 * LANES))).reshape(-1, LANES)
    near, far, biases, near_out, far_out, held_in = first_gather(quant_own[0], biases, *quant_own[1:3])
    weights_qkv, weights_out = (near, far), (near_out, far_out)
    biases = biases.reshape(parts, -1)[:, :count]
    columns = bias_qv.shape[1]
    bias_q = biases[:, :columns].reshape(1, -1)
    bias_v = biases[:, columns : 2 * columns].reshape(1, -1)
    bias_qkv = jnp.stack([bias_q, jnp.zeros_like(bias_q), bias_v]).astype(F32)
    bias_hidden = biases[:, 2 * columns :].reshape(1, -1).astype(F32)

    held = tokens // SEQ
    lengths_here = lax.dynamic_slice_in_dim(doc_lengths, part * held, held, 0)
    segments = doc_segments(lengths_here, SEQ).astype(F32)
    seg_cols, seg_rows = segments[:, :, None], segments[:, None, :]
    half = parts // 2 * columns

    first_moves, _ = plane_moves()

    def over_plane(values, token):
        values = tie(values, [token])
        return [far_swap(values, r) for _, r in first_moves]

    zero = jnp.zeros((8, LANES), F32)
    there_in = over_plane(held_in, biases)
    held_a = tie(quant_own[3], [biases])[None]
    for bit in reversed(range(bits_of("tensor") - 1)):
        other = swap(held_a, "tensor", bit)
        held_a = jnp.stack([held_a, other], axis=1).reshape((-1,) + held_a.shape[1:])
    qkv = qkv_rows(quant_input, weights_qkv, bias_qkv)
    held_a = tie(held_a, [qkv])
    there_a = over_plane(held_a, qkv)
    held_b = swap(held_a, "tensor", bits_of("tensor") - 1)
    context, lse, peak = attend(qkv, seg_cols, seg_rows, jnp.zeros((held, LANES, SEQ), F32), zero)
    there_in, there_a = [tie(values, [peak]) for values in there_in], [tie(values, [peak]) for values in there_a]
    (context, lse, peak), (*weights_in, near_a, far_a) = attend(
        qkv, seg_cols, seg_rows, lse, peak, context, [(held_in, there_in), (held_a, there_a)]
    )
    weights_in = tuple(side[:, :, 0] for side in weights_in)
    levels = exchange_all(peak, mesh, 1, ranges, levels)
    weights_out = tuple(side[:, :, 0] for side in weights_out)
    quant_context, normed, normal_one, inverse_one, peak = first_norm(
        context, levels, weights_out, x, vectors, order
    )
    levels = exchange_all(peak, mesh, 2, ranges, levels)
    held_b = tie(held_b, [levels])
    (quant_normed, active, slope, peak), (near_b, far_b) = hidden_rows(
        normed, levels, weights_in, bias_hidden, held_b
    )
    levels = exchange_all(peak, mesh, 3, ranges, levels)
    weights_down = [side[:, :, 0] for side in (near_a, far_a, near_b, far_b)]
    quant_active, back, output, grad_sum_two, grad_branch, terms_two = second_norm(
        active, slope, levels, weights_down, normed, upstream, vectors, order
    )

    other = weight_send(grad_branch, [quant_active], parts, plane)
    grad_branch = tie(grad_branch, [other])
    other = swap(other, "dp", 0)
    grad_hidden, sum_hidden = grad_hidden_rows(grad_branch, weights_down, back, part_order)
    down = scatter_plane_of(scatter_all, grad_branch, [quant_active], other, sum_hidden, parts, plane)
    grad_hidden = tie(grad_hidden, next(down))
    other = weight_send(quant_normed, [grad_hidden], parts, plane)
    grad_branch = tie(grad_hidden, [other])
    other = swap(other, "dp", 0)
    grad_sum_one, grad_attention, terms_one = first_back(
        grad_branch, weights_in, normed, normal_one, inverse_one, grad_sum_two, levels, vectors, order
    )
    grad_hidden = tie(grad_hidden, down.send(terms_one))
    inner = scatter_plane_of(scatter_part, quant_normed, [grad_hidden], other, terms_one, parts, plane)
    grad_attention = tie(grad_attention, next(inner))
    other = weight_send(grad_attention, [quant_context], parts, plane)
    grad_context = tie(grad_attention, [other])
    other = swap(other, "dp", 0)
    grad_a = grad_context_rows(grad_context, weights_out, context, levels, 0)
    grad_b = grad_context_rows(grad_context, weights_out, context, levels, parts // 2)
    sums_before = jnp.zeros((8, 2 * half), F32)
    *grads_a, token = attend_back(qkv, grad_a, seg_cols, seg_rows, lse, sums_before, part_order, columns, 0)
    grads_a[0] = tie(grads_a[0], down.send(token))
    outer = scatter_plane_of(scatter_plane, grad_attention, [quant_context], other, token, parts, plane)
    grads_a[0] = tie(grads_a[0], next(outer))
    other = weight_send(quant_input, grads_a, parts // 2, plane)
    grad_b = tie(grad_b, [other])
    other = swap(other, "dp", 0)
    *grads_b, token = attend_back(qkv, grad_b, seg_cols, seg_rows, lse, token, part_order, columns, half)
    sum_qv = token
    grads_b[0] = tie(grads_b[0], inner.send(token) + down.send(token) + outer.send(token))
    other_b = weight_send(quant_input, grads_b, parts // 2, plane)
    grads_a[0] = tie(grads_a[0], [other_b])
    other_b = swap(other_b, "dp", 0)
    first_a = scatter_plane_of(but_last, quant_input, grads_a, other, grads_a[0], parts // 2, plane)
    grads_b[0] = tie(grads_b[0], next(first_a))
    first_b = scatter_plane_of(but_last, quant_input, grads_b, other_b, grads_b[0], parts // 2, plane)
    started = next(first_b) + inner.send(grads_b[0])
    grads_b[0] = tie(grads_b[0], started)
    grad_x = grad_input(grads_a + grads_b, weights_qkv, grad_sum_one, x, levels, order)

    sums = [terms_one[:3], terms_two[:3], sum_qv[:2], sum_hidden.reshape(-1, width)]
    if rows % LANES:
        sums[0], sums[1] = restore(sums[0]), restore(sums[1])
    sums = jnp.concatenate(sums)
    padded = jnp.pad(sums, ((0, -sums.shape[0] % 8), (0, 0)))
    down, inner, outer, first_a, first_b = [
        run_all(chain, grad_x) for chain in (down, inner, outer, first_a, first_b)
    ]
    (down, inner, outer, first), sums = finale(
        low(down * slopes[3]), inner, outer, first_a + first_b, [slopes[0], slopes[2], slopes[1]], padded
    )
    hidden_all = sums[8 : 8 + sum_hidden.size // width].reshape(-1)
    grad_bias_qv = lax.dynamic_slice_in_dim(sums[6:8], part * columns, columns, 1)
    grad_b_in = lax.dynamic_slice_in_dim(hidden_all, part * b_in.shape[0], b_in.shape[0], 0)
    grad_w_down, grad_w_out, grad_w_in, grad_w_qkv = place_grads(
        [down, outer, inner, first], [True, True, False, False], blocks
    )
    grad_w_in = grad_w_in[0]
    new_ranges = levels[:4, 0]
    return (
        restore_rows(output),
        restore_rows(grad_x),
        grad_w_qkv,
        grad_bias_qv,
        grad_w_out,
        sums[0],
        sums[1],
        sums[2],
        grad_w_in,
        grad_b_in,
        grad_w_down,
        sums[3],
        sums[4],
        sums[5],
        new_ranges,
    )


def solution(mesh):
    in_specs = (
        P(("dp", "tensor"), None),
        P(("dp", "tensor"), None),
        P("dp", None),
        P(),
        P(None, None, "tensor"),
        P(None, "tensor"),
        P("tensor", None),
        P(),
        P(),
        P(),
        P(None, "tensor"),
        P("tensor"),
        P("tensor", None),
        P(),
        P(),
        P(),
    )
    out_specs = (
        P(("dp", "tensor"), None),
        P(("dp", "tensor"), None),
        P(None, None, "tensor"),
        P(None, "tensor"),
        P("tensor", None),
        P(),
        P(),
        P(),
        P(None, "tensor"),
        P("tensor"),
        P("tensor", None),
        P(),
        P(),
        P(),
        P(),
    )
    return jax.shard_map(
        partial(local, mesh), mesh=mesh, in_specs=in_specs, out_specs=out_specs, check_vma=False
    )
```

time: 658 us -> 571 us (0.87)
  local copies, waits for them, and re-layouts: 85.8 us -> 33.5 us
  other arithmetic: 54.7 us -> 27.9 us
    pallas_call x12 -> x16, Pallas kernels: 175 us -> 224 us  [the longest x1 56.9 us: finale(): pl.pallas_call(finale_kernel, in_specs=[vmem] * 9 + [anywhere()] * 4 + [v...]
    pallas_call x3 -> x2, Pallas kernels: 105 us -> 56.1 us  [run(): results = call(*args, *sources)]
    unnamed x213 -> x109, local copies, waits for them, and re-layouts: 53.6 us -> 6.56 us
    slice x15 -> x1, local copies, waits for them, and re-layouts: 14 us -> 0.63 us  [local(): new_ranges = levels[:4, 0]]
    add x14 -> x2, other arithmetic: 16.3 us -> 3.24 us  [scatter_plane(): sides[i] = keep + swap(sends[i], 'dp', bit, token).astype(F32)]
    add x4 -> x10, other arithmetic: 17.9 us -> 7.62 us  [scatter_plane(): sides[i] = sides[i] + other.reshape(sides[i].shape).astype(F32)]
    ppermute x25 -> x28, starting transfers between devices: 28.9 us -> 25.2 us  [swap(): lax.ppermute(values, axis, [(i, i ^ 1 << bit) for i in range(count)])]
    ppermute x25 -> x28, waiting for transfers between devices: 13.7 us -> 11 us  [swap(): lax.ppermute(values, axis, [(i, i ^ 1 << bit) for i in range(count)])]
  transfers between devices with their start and end apart: 25 -> 32, of which waited for: 3 -> 6; matrix products, arithmetic and copies ran while one was open for 12% -> 7% of each run, Pallas kernels for 26% -> 40%
where the time goes in v3:
time: 571 us; the launch traced here: 561 us
  Pallas kernels  458 us (80%)
  local copies, waits for them, and re-layouts  33.5 us (6%)
  starting transfers between devices  29.3 us (5%)
  other arithmetic  27.9 us (5%)
  waiting for transfers between devices  11 us (2%)
    pallas_call x1, Pallas kernels, finale(): pl.pallas_call(finale_kernel, in_specs=[vmem] * 9 + [anywhere()] * 4 + [v...  56.9 us
    pallas_call x2, Pallas kernels, run(): results = call(*args, *sources)  56.1 us
    pallas_call x1, Pallas kernels, first_gather(): pl.pallas_call(first_gather_kernel, in_specs=[pl.BlockSpec(memory_space=p...  46.4 us
    pallas_call x4, Pallas kernels, exchange_all(): pl.pallas_call(partial(exchange_kernel, kind), out_shape=shape_of(dims, F...  44.4 us
    pallas_call x5, Pallas kernels, weight_keep(): pl.pallas_call(partial(weight_keep_kernel, len(grads), first_split(bits_o...  38.7 us
    pallas_call x2, Pallas kernels, attend_back(): pl.pallas_call(partial(attend_back_kernel, c, first), grid=(held, width /...  36.3 us
    pallas_call x5, Pallas kernels, weight_send(): pl.pallas_call(partial(weight_send_kernel, len(grads)), grid=grid, in_spe...  33.7 us
    pallas_call x1, Pallas kernels, second_norm(): pl.pallas_call(second_norm_kernel, grid=(tokens // rows,), in_specs=[in_s...  31 us
  transfers between devices with their start and end apart: 32, of which 6 were waited for; matrix products, arithmetic and copies ran while one was open for 7% of the time, Pallas kernels for 40%

profile of v3, /device:TPU:0, one launch (start us, length us, event | category | flops | bytes accessed | tf_op | source)
XLA Modules:
  0.0 561.4 jit_solution(13732370777803146866)
XLA Ops:
  10.5 13.2 %exchange.4.peak_ref = f32[8,128]{1,0:T(8,128)} custom-call(f32[8,128]{1,0:T(8,128)} %stack.67.x_ref.level_ref, f32[4]{0:T(128)} %range_ref.9, f32[8,128]{1,0:T(8,128)} %stack.67.x_ref.level_ref), custom_call_target="tpu_custom_call" | custom-call | tf_op jit(solution)/shard_map/exchange/pallas_call | solution.py:120
  29.2 46.4 %first_gather.1 = (bf16[4,4,3,128,256]{4,3,2,1,0:T(8,128)(2,1)}, bf16[4,4,3,128,256]{4,3,2,1,0:T(8,128)(2,1)}, bf16[4,16,128]{2,1,0:T(8,128)(2,1)}, bf16[4,4,1,1...) custom-call(bf16[3,128,256]{2,1,0:T(8,128)(2,1)} %get-tuple-element.153.first_ref, ...), custom_call_target="tpu_custom_call" | custom-call | tf_op jit(solution)/shard_map/first_gather/pallas_call | solution.py:541
  79.4 14.1 %qkv.1.refs_0_.refs_1_.refs_2_.q_ref.k_ref.v_ref = bf16[3,1024,1024]{2,1,0:T(8,128)(2,1)} custom-call(bf16[1024,1024]{1,0:T(8,128)(2,1)} %get-tuple-element.250.x_ref, bf16[4,4,3,128,256]{4,3,2,1,0:T(8,128)(2,1)} %get-tuple-element.156.near_ref.refs_6_, bf16[4,4,3,128,256]{4,3,2,1,0:T(8,128)(2,1)} %get-tuple-element.157.far_ref.refs_7_, ...), custom_call_target="tpu_custom_call" | custom-call | flops 6442450944 | bytes 14680064 | tf_op jit(solution)/shard_map/qkv/pallas_call | solution.py:756
  98.9 18.4 %attend.2 = (f32[1024,1024]{1,0:T(8,128)}, f32[2,128,512]{2,1,0:T(8,128)}, f32[8,128]{1,0:T(8,128)}) custom-call(bf16[3,1024,1024]{2,1,0:T(8,128)(2,1)} %qkv.1.refs_0_.refs_1_.refs_2_.q_ref.k_ref.v_ref, bf16[3,1024,1024]{2,1,0:T(8,128)(2,1)} %qkv.1.refs_0_.refs_1_.refs_2_.q_ref.k_ref.v_ref, ...), custom_call_target="tpu_custom_call" | custom-call | flops 15000000512 | bytes 41943040 | tf_op jit(solution)/shard_map/attend/pallas_call | solution.py:863
  122.8 25.8 %attend.3 = (f32[1024,1024]{1,0:T(8,128)}, f32[2,128,512]{2,1,0:T(8,128)}, f32[8,128]{1,0:T(8,128)}, bf16[4,4,1,128,1024]{4,3,2,1,0:T(8,128)(2,1)}, bf16[4,4,1,1...) custom-call(bf16[3,1024,1024]{2,1,0:T(8,128)(2,1)} %qkv.1.refs_0_.re, ...), custom_call_target="tpu_custom_call", output_to_operand_aliasing={{0}: (7, {})} | custom-call | flops 15000000512 | bytes 41943040 | tf_op jit(solution)/shard_map/attend/pallas_call | solution.py:465
  148.7 10.4 %exchange.5.level_ref = f32[8,128]{1,0:T(8,128)} custom-call(f32[8,128]{1,0:T(8,128)} %get-tuple-element.173.x_ref, f32[4]{0:T(128)} %range_ref.9, f32[8,128]{1,0:T(8,128)} %get-tuple-element.174.level_ref), custom_call_target="tpu_custom_call" | custom-call | tf_op jit(solution)/shard_map/exchange/pallas_call | solution.py:120
  159.1 9.2 %first_norm.1 = (bf16[1024,1024]{1,0:T(8,128)(2,1)}, f32[1024,1024]{1,0:T(8,128)}, f32[1024,1024]{1,0:T(8,128)}, f32[1024,1]{1,0:T(8,128)}, f32[8,128]{1,0:T(8,128)}) custom-call(s32[8]{0:T(128)} %fusion.42.order_ref, f32[1024,1024]{1,0:T(8,128)} %get-tuple-element.172.ctx_ref, f32[8,128]{1,0:T(8,128)} %exchange.5.level_ref, ...), custom_call_target="tpu_custom_call" | custom-call | flops 2147483648 | bytes 20971520 | tf_op jit(solution)/shard_map/first_norm/pallas_call | solution.py:1032
  168.3 10.4 %exchange.6.refs_1_.level_ref = f32[8,128]{1,0:T(8,128)} custom-call(f32[8,128]{1,0:T(8,128)} %get-tuple-element.178.x_ref, f32[4]{0:T(128)} %range_ref.9, f32[8,128]{1,0:T(8,128)} %exchange.5.level_ref), custom_call_target="tpu_custom_call" | custom-call | tf_op jit(solution)/shard_map/exchange/pallas_call | solution.py:120
  179.5 30.2 %hidden.1 = (bf16[1024,1024]{1,0:T(8,128)(2,1)}, f32[1024,4096]{1,0:T(8,128)}, f32[1024,4096]{1,0:T(8,128)}, f32[8,128]{1,0:T(8,128)}, bf16[4,2,1,128,1024]{4,3,...) custom-call(f32[1024,1024]{1,0:T(8,128)} %get-tuple-element.177.refs_0_.normed_ref, ...), custom_call_target="tpu_custom_call" | custom-call | flops 8589934592 | bytes 52428800 | tf_op jit(solution)/shard_map/hidden/pallas_call | solution.py:465
  209.8 10.4 %exchange.7.level_ref.refs_10_ = f32[8,128]{1,0:T(8,128)} custom-call(f32[8,128]{1,0:T(8,128)} %get-tuple-element.184.x_ref, f32[4]{0:T(128)} %range_ref.9, f32[8,128]{1,0:T(8,128)} %exchange.6.refs_1_.level_ref), custom_call_target="tpu_custom_call" | custom-call | tf_op jit(solution)/shard_map/exchange/pallas_call | solution.py:120
  220.2 31.0 %second_norm.1 = (bf16[1024,4096]{1,0:T(8,128)(2,1)}, f32[1024,4096]{1,0:T(8,128)}, bf16[1024,1024]{1,0:T(8,128)(2,1)}, f32[1024,1024]{1,0:T(8,128)}, bf16[1024,1024]{1,0:T(8,128)(2,1)}, /*index=5*/f32[8,1024]{1,0:T(8,128)}) custom-call(s32[8]{0:T(128)} %fusion.42.order_ref, f32[1024,4096]{1,0:T(8,128)} %get-tuple-element.182.act_ref, ...), custom_call_target="tpu_custom_call" | custom-call | flops 8589934592 | bytes 83886080 | tf_op jit(solution)/shard_map/second_norm/pallas_call | solution.py:1149
  251.2 9.1 %weight_send.5 = bf16[4,4,1,128,1024]{4,3,2,1,0:T(8,128)(2,1)} custom-call(bf16[1024,1024]{1,0:T(8,128)(2,1)} %get-tuple-element.196.x_ref.g_ref, bf16[1024,4096]{1,0:T(8,128)(2,1)} %get-tuple-element.191.refs_0_), custom_call_target="tpu_custom_call" | custom-call | flops 4294967296 | bytes 16777216 | tf_op jit(solution)/shard_map/weight_send/pallas_call | solution.py:1211
  260.8 16.9 %grad_hidden.1 = (bf16[1024,4096]{1,0:T(8,128)(2,1)}, f32[4,1024]{1,0:T(4,128)}) custom-call(s32[4]{0:T(128)} %iota_xor_fusion.order_ref, bf16[1024,1024]{1,0:T(8,128)(2,1)} %get-tuple-element.196.x_ref.g_ref, bf16[4,2,128,1024]{3,2,1,0:T(8,128)(2,1)} %bitcast.223, bf16[4,2,128,1024]{3,2,1,0:T(8,128)(2,1)} %bitcast.225, bf16[4,2,128,1024]{3,2,1,0:T(8,128)(2,1)} %bitcast.227, ...), custom_call_target="tpu_custom_call" | custom-call | flops 8589934592 | bytes 35651584 | tf_op jit(solution)/shard_map/grad_hidden/pallas_call | solution.py:1307
  277.7 10.7 %weight_keep.5 = (f32[2,2,1,128,1024]{4,3,2,1,0:T(8,128)}, bf16[2,2,1,128,1024]{4,3,2,1,0:T(8,128)(2,1)}, f32[2,2,1,128,1024]{4,3,2,1,0:T(8,128)}, bf16[2,2,1,128,1024]{4,3,2,1,0:T(8,128)(2,1)}) custom-call(bf16[1024,1024]{1,0:T(8,128)(2,1)} %get-tuple-element.196.x_ref.g_ref, bf16[4,4,1,128,1024]{4,3,2,1,0:T(8,128)(2,1)} %collective-permute-done.6.other_ref, ...), custom_call_target="tpu_custom_call" | custom-call | flops 4294967296 | bytes 25165824 | tf_op jit(solution)/shard_map/weight_keep/pallas_call | solution.py:1256
  288.5 9.2 %weight_send.6 = bf16[4,4,1,128,1024]{4,3,2,1,0:T(8,128)(2,1)} custom-call(bf16[1024,1024]{1,0:T(8,128)(2,1)} %get-tuple-element.207.x_ref, bf16[1024,4096]{1,0:T(8,128)(2,1)} %get-tuple-element.212.refs_0_.g_ref), custom_call_target="tpu_custom_call" | custom-call | flops 4294967296 | bytes 16777216 | tf_op jit(solution)/shard_map/weight_send/pallas_call | solution.py:1211
  300.3 18.5 %first_back.1 = (f32[1024,1024]{1,0:T(8,128)}, bf16[1024,1024]{1,0:T(8,128)(2,1)}, f32[8,1024]{1,0:T(8,128)}) custom-call(s32[8]{0:T(128)} %fusion.42.order_ref, bf16[1024,4096]{1,0:T(8,128)(2,1)} %get-tuple-element.212.refs_0_.g_ref, bf16[4,4,128,1024]{3,2,1,0:T(8,128)(2,1)} %bitcast.260, bf16[4,4,128,1024]{3,2,1,0:T(8,128)(2,1)} %bitcast.262, ...), custom_call_target="tpu_custom_call" | custom-call | flops 8589934592 | bytes 37748736 | tf_op jit(solution)/shard_map/first_back/pallas_call | solution.py:1343
  331.8 10.6 %weight_keep.6 = (f32[2,2,1,128,1024]{4,3,2,1,0:T(8,128)}, bf16[2,2,1,128,1024]{4,3,2,1,0:T(8,128)(2,1)}, f32[2,2,1,128,1024]{4,3,2,1,0:T(8,128)}, bf16[2,2,1,128,1024]{4,3,2,1,0:T(8,128)(2,1)}) custom-call(bf16[1024,1024]{1,0:T(8,128)(2,1)} %get-tuple-element.207.x_ref, bf16[4,4,1,128,1024]{4,3,2,1,0:T(8,128)(2,1)} %collective-permute-done.7.other_ref, ...), custom_call_target="tpu_custom_call" | custom-call | flops 4294967296 | bytes 25165824 | tf_op jit(solution)/shard_map/weight_keep/pallas_call | solution.py:1256
  352.5 18.2 %attend_back.2 = (bf16[1024,512]{1,0:T(8,128)(2,1)}, bf16[1024,512]{1,0:T(8,128)(2,1)}, bf16[1024,512]{1,0:T(8,128)(2,1)}, f32[8,1024]{1,0:T(8,128)}) custom-call(s32[4]{0:T(128)} %iota_xor_fusion.order_ref, bf16[3,1024,1024]{2,1,0:T(8,128)(2,1)} %qkv.1.refs_0_.refs_1_.refs_2_.q_ref.k_ref.v_ref, ...), custom_call_target="tpu_custom_call" | custom-call | flops 15000000512 | bytes 52428800 | tf_op jit(solution)/shard_map/attend_back/pallas_call | solution.py:932
  391.7 18.1 %attend_back.3 = (bf16[1024,512]{1,0:T(8,128)(2,1)}, bf16[1024,512]{1,0:T(8,128)(2,1)}, bf16[1024,512]{1,0:T(8,128)(2,1)}, f32[8,1024]{1,0:T(8,128)}) custom-call(s32[4]{0:T(128)} %iota_xor_fusion.order_ref, bf16[3,1024,1024]{2,1,0:T(8,128)(2,1)} %qkv.1.refs_0_.refs_1_.refs_2_.q_ref.k_ref.v_ref, ...), custom_call_target="tpu_custom_call" | custom-call | flops 15000000512 | bytes 52428800 | tf_op jit(solution)/shard_map/attend_back/pallas_call | solution.py:932
  434.5 6.0 %weight_keep.8 = (f32[2,1,3,128,256]{4,3,2,1,0:T(8,128)}, bf16[2,1,3,128,256]{4,3,2,1,0:T(8,128)(2,1)}, f32[2,1,3,128,256]{4,3,2,1,0:T(8,128)}, bf16[2,1,3,128,256]{4,3,2,1,0:T(8,128)(2,1)}) custom-call(bf16[1024,1024]{1,0:T(8,128)(2,1)} %get-tuple-element.250.x_ref, bf16[4,2,3,128,256]{4,3,2,1,0:T(8,128)(2,1)} %collective-permute-done.18.other_ref, ...), custom_call_target="tpu_custom_call" | custom-call | flops 1610612736 | bytes 25165824 | tf_op jit(solution)/shard_map/weight_keep/pallas_call | solution.py:1256
  447.4 5.8 %weight_keep.9 = (f32[2,1,3,128,256]{4,3,2,1,0:T(8,128)}, bf16[2,1,3,128,256]{4,3,2,1,0:T(8,128)(2,1)}, f32[2,1,3,128,256]{4,3,2,1,0:T(8,128)}, bf16[2,1,3,128,256]{4,3,2,1,0:T(8,128)(2,1)}) custom-call(bf16[1024,1024]{1,0:T(8,128)(2,1)} %get-tuple-element.250.x_ref, bf16[4,2,3,128,256]{4,3,2,1,0:T(8,128)(2,1)} %collective-permute-done.19.other_ref, ...), custom_call_target="tpu_custom_call" | custom-call | flops 1610612736 | bytes 25165824 | tf_op jit(solution)/shard_map/weight_keep/pallas_call | solution.py:1256
  453.2 12.9 %grad_input.1 = bf16[1024,1024]{1,0:T(8,128)(2,1)} custom-call(s32[8]{0:T(128)} %fusion.42.order_ref, bf16[1024,512]{1,0:T(8,128)(2,1)} %get-tuple-element.245.refs_0_, bf16[1024,512]{1,0:T(8,128)(2,1)} %get-tuple-element.228.refs_1_, bf16[1024,512]{1,0:T(8,128)(2,1)} %get-tuple-element.229.refs_2_, bf16[1024,512]{1,0:T(8,128)(2,1)} %get-tuple-element.255.refs_0_.refs_3_, ...), custom_call_target="tpu_custom_call" | custom-call | flops 6442450944 | bytes 20971520 | tf_op jit(solution)/shard_map/grad_input/pallas_call | solution.py:1429
  489.2 56.9 %finale.1 = (bf16[4,1,128,1024]{3,2,1,0:T(8,128)(2,1)}, bf16[4,1,128,1024]{3,2,1,0:T(8,128)(2,1)}, bf16[4,1,128,1024]{3,2,1,0:T(8,128)(2,1)}, bf16[4,1,128,1024]...) custom-call(bf16[1,128,1024]{2,1,0:T(8,128)(2,1)} %fusion.20.down_re, ...), custom_call_target="tpu_custom_call" | custom-call | tf_op jit(solution)/shard_map/finale/pallas_call | solution.py:667
  550.5 10.5 %place_grads.1 = (f32[1024,1024]{1,0:T(8,128)}, f32[256,1024]{1,0:T(8,128)}, f32[1,1024,1024]{2,1,0:T(8,128)}, f32[3,1024,256]{2,1,0:T(8,128)}) custom-call(s32[8]{0:T(128)} %fusion.42.order_ref, bf16[4,1,128,1024]{3,2,1,0:T(8,128)(2,1)} %get-tuple-element.276.refs_0_, bf16[4,1,128,1024]{3,2,1,0:T(8,128)(2,1)} %get-tuple-element.277.refs_1_, ...), custom_call_target="tpu_custom_call" | custom-call | tf_op jit(solution)/shard_map/place_grads/pallas_call | solution.py:1483
  (272 shorter events, 136.4 us)
Async XLA Ops:
  76.4 45.3 %collective-permute-start.1 = (bf16[4,1,128,1024]{3,2,1,0:T(8,128)(2,1)}, bf16[4,1,128,1024]{3,2,1,0:T(8,128)(2,1)S(1)}, u32[]{:S(2)}, u32[]{:S(2)}) collective-permute-start(bf16[4,1,128,1024]{3,2,1,0:T(8,128)(2,1)} %get-tuple-element.163.refs_8_), channel_id=1, source_target_pairs={{0,16},{4,20},{8,24},{12,28},{16,0},{20,4},{24,8},{28,12},{1,17},{... | collective-permute-start | bytes 3145736 | tf_op jit(solution)/shard_map/ppermute | solution.py:153
  77.8 43.9 %collective-permute-start = (bf16[4,1,128,1024]{3,2,1,0:T(8,128)(2,1)}, bf16[4,1,128,1024]{3,2,1,0:T(8,128)(2,1)}, u32[]{:S(2)}, u32[]{:S(2)}) collective-permute-start(bf16[4,1,128,1024]{3,2,1,0:T(8,128)(2,1)} %get-tuple-element.163.refs_8_), channel_id=1, source_target_pairs={{0,8},{4,12},{8,0},{12,4},{16,24},{20,28},{24,16},{28,20},{1,9},{5... | collective-permute-start | bytes 3145736 | tf_op jit(solution)/shard_map/ppermute | solution.py:153
  95.3 26.4 %collective-permute-start.4 = (bf16[2,1,128,1024]{3,2,1,0:T(8,128)(2,1)S(1)}, bf16[2,1,128,1024]{3,2,1,0:T(8,128)(2,1)S(1)}, u32[]{:S(2)}, u32[]{:S(2)}) collective-permute-start(bf16[2,1,128,1024]{3,2,1,0:T(8,128)(2,1)S(1)} %maximum_bitcast_fusion.refs_11_), channel_id=1, source_target_pairs={{0,16},{4,20},{8,24},{12,28},{16,0},{20,4},{24,8},{28,12},{1,17},{... | collective-permute-start | bytes 1572872 | tf_op jit(solution)/shard_map/ppermute | solution.py:153
  96.7 24.9 %collective-permute-start.3 = (bf16[2,1,128,1024]{3,2,1,0:T(8,128)(2,1)S(1)}, bf16[2,1,128,1024]{3,2,1,0:T(8,128)(2,1)}, u32[]{:S(2)}, u32[]{:S(2)}) collective-permute-start(bf16[2,1,128,1024]{3,2,1,0:T(8,128)(2,1)S(1)} %maximum_bitcast_fusion.refs_11_), channel_id=1, source_target_pairs={{0,8},{4,12},{8,0},{12,4},{16,24},{20,28},{24,16},{28,20},{1,9},{5... | collective-permute-start | bytes 1572872 | tf_op jit(solution)/shard_map/ppermute | solution.py:153
  118.7 60.0 %collective-permute-start.5 = (bf16[2,1,128,1024]{3,2,1,0:T(8,128)(2,1)S(1)}, bf16[2,1,128,1024]{3,2,1,0:T(8,128)(2,1)S(1)}, u32[]{:S(2)}, u32[]{:S(2)}) collective-permute-start(bf16[2,1,128,1024]{3,2,1,0:T(8,128)(2,1)S(1)} %maximum_bitcast_fusion.refs_11_), channel_id=1, source_target_pairs={{0,2},{1,3},{2,0},{3,1},{4,6},{5,7},{6,4},{7,5},{8,10},{9,11},{10,... | collective-permute-start | bytes 1572872 | tf_op jit(solution)/shard_map/ppermute | solution.py:147
  260.3 17.4 %collective-permute-start.6 = (bf16[4,4,1,128,1024]{4,3,2,1,0:T(8,128)(2,1)}, bf16[4,4,1,128,1024]{4,3,2,1,0:T(8,128)(2,1)}, u32[]{:S(2)}, u32[]{:S(2)}) collective-permute-start(bf16[4,4,1,128,1024]{4,3,2,1,0:T(8,128)(2,1)} %weight_send.5), channel_id=1, source_target_pairs={{0,4},{4,0},{8,12},{12,8},{16,20},{20,16},{24,28},{28,24},{1,5},{5... | collective-permute-start | bytes 12582920 | tf_op jit(solution)/shard_map/ppermute | solution.py:147
  297.7 34.2 %collective-permute-start.7 = (bf16[4,4,1,128,1024]{4,3,2,1,0:T(8,128)(2,1)}, bf16[4,4,1,128,1024]{4,3,2,1,0:T(8,128)(2,1)}, u32[]{:S(2)}, u32[]{:S(2)}) collective-permute-start(bf16[4,4,1,128,1024]{4,3,2,1,0:T(8,128)(2,1)} %weight_send.6), channel_id=1, source_target_pairs={{0,4},{4,0},{8,12},{12,8},{16,20},{20,16},{24,28},{28,24},{1,5},{5... | collective-permute-start | bytes 12582920 | tf_op jit(solution)/shard_map/ppermute | solution.py:147
  298.2 25.3 %collective-permute-start.9 = (bf16[2,2,1,128,1024]{4,3,1,2,0:T(8,128)(2,1)}, bf16[2,2,1,128,1024]{4,3,1,2,0:T(8,128)(2,1)S(1)}, u32[]{:S(2)}, u32[]{:S(2)}) collective-permute-start(bf16[2,2,1,128,1024]{4,3,1,2,0:T(8,128)(2,1)} %bitcast.37), channel_id=1, source_target_pairs={{0,8},{4,12},{8,0},{12,4},{16,24},{20,28},{24,16},{28,20},{1,9},{5... | collective-permute-start | bytes 3145736 | tf_op jit(solution)/shard_map/ppermute | solution.py:147
  299.6 24.8 %collective-permute-start.8 = (bf16[2,2,1,128,1024]{4,3,1,2,0:T(8,128)(2,1)S(1)}, bf16[2,2,1,128,1024]{4,3,1,2,0:T(8,128)(2,1)S(1)}, u32[]{:S(2)}, u32[]{:S(2)}) collective-permute-start(bf16[2,2,1,128,1024]{4,3,1,2,0:T(8,128)(2,1)S(1)} %bitcast.256), channel_id=1, source_target_pairs={{0,16},{4,20},{8,24},{12,28},{16,0},{20,4},{24,8},{28,12},{1,17},{... | collective-permute-start | bytes 3145736 | tf_op jit(solution)/shard_map/ppermute | solution.py:147
  327.8 43.0 %collective-permute-start.11 = (bf16[2,1,128,1024]{3,2,0,1:T(8,128)(2,1)}, bf16[2,1,128,1024]{3,2,0,1:T(8,128)(2,1)S(1)}, u32[]{:S(2)}, u32[]{:S(2)}) collective-permute-start(bf16[2,1,128,1024]{3,2,0,1:T(8,128)(2,1)} %fusion.9), channel_id=1, source_target_pairs={{0,16},{4,20},{8,24},{12,28},{16,0},{20,4},{24,8},{28,12},{1,17},{... | collective-permute-start | bytes 1572872 | tf_op jit(solution)/shard_map/ppermute | solution.py:147
  331.0 39.8 %collective-permute-start.10 = (bf16[2,1,128,1024]{3,2,0,1:T(8,128)(2,1)S(1)}, bf16[2,1,128,1024]{3,2,0,1:T(8,128)(2,1)S(1)}, u32[]{:S(2)}, u32[]{:S(2)}) collective-permute-start(bf16[2,1,128,1024]{3,2,0,1:T(8,128)(2,1)S(1)} %fusion.8), channel_id=1, source_target_pairs={{0,8},{4,12},{8,0},{12,4},{16,24},{20,28},{24,16},{28,20},{1,9},{5... | collective-permute-start | bytes 1572872 | tf_op jit(solution)/shard_map/ppermute | solution.py:147
  347.5 33.4 %collective-permute-start.12 = (bf16[4,4,1,128,256]{4,3,2,1,0:T(8,128)(2,1)}, bf16[4,4,1,128,256]{4,3,2,1,0:T(8,128)(2,1)}, u32[]{:S(2)}, u32[]{:S(2)}) collective-permute-start(bf16[4,4,1,128,256]{4,3,2,1,0:T(8,128)(2,1)} %weight_send.7), channel_id=1, source_target_pairs={{0,4},{4,0},{8,12},{12,8},{16,20},{20,16},{24,28},{28,24},{1,5},{5... | collective-permute-start | bytes 3145736 | tf_op jit(solution)/shard_map/ppermute | solution.py:147
  371.7 46.5 %collective-permute-start.15 = (bf16[1,1,128,1024]{3,2,1,0:T(8,128)(2,1)}, bf16[1,1,128,1024]{3,2,1,0:T(8,128)(2,1)}, u32[]{:S(2)}, u32[]{:S(2)}) collective-permute-start(bf16[1,1,128,1024]{3,2,1,0:T(8,128)(2,1)} %fusion.24), channel_id=1, source_target_pairs={{0,1},{1,0},{2,3},{3,2},{4,5},{5,4},{6,7},{7,6},{8,9},{9,8},{10,11... | collective-permute-start | bytes 786440 | tf_op jit(solution)/shard_map/ppermute | solution.py:147
  373.8 57.7 %collective-permute-start.22 = (bf16[1,1,128,1024]{3,2,1,0:T(8,128)(2,1)}, bf16[1,1,128,1024]{3,2,1,0:T(8,128)(2,1)S(1)}, u32[]{:S(2)}, u32[]{:S(2)}) collective-permute-start(bf16[1,1,128,1024]{3,2,1,0:T(8,128)(2,1)} %fusion.23), channel_id=1, source_target_pairs={{0,1},{1,0},{2,3},{3,2},{4,5},{5,4},{6,7},{7,6},{8,9},{9,8},{10,11... | collective-permute-start | bytes 786440 | tf_op jit(solution)/shard_map/ppermute | solution.py:147
  374.7 35.1 %collective-permute-start.14 = (bf16[2,2,1,128,1024]{4,3,1,2,0:T(8,128)(2,1)S(1)}, bf16[2,2,1,128,1024]{4,3,1,2,0:T(8,128)(2,1)S(1)}, u32[]{:S(2)}, u32[]{:S(2)}) collective-permute-start(bf16[2,2,1,128,1024]{4,3,1,2,0:T(8,128)(2,1)S(1)} %bitcast.255), channel_id=1, source_target_pairs={{0,8},{4,12},{8,0},{12,4},{16,24},{20,28},{24,16},{28,20},{1,9},{5... | collective-permute-start | bytes 3145736 | tf_op jit(solution)/shard_map/ppermute | solution.py:147
  375.9 38.7 %collective-permute-start.13 = (bf16[2,2,1,128,1024]{4,3,1,2,0:T(8,128)(2,1)}, bf16[2,2,1,128,1024]{4,3,1,2,0:T(8,128)(2,1)}, u32[]{:S(2)}, u32[]{:S(2)}) collective-permute-start(bf16[2,2,1,128,1024]{4,3,1,2,0:T(8,128)(2,1)} %bitcast.46), channel_id=1, source_target_pairs={{0,16},{4,20},{8,24},{12,28},{16,0},{20,4},{24,8},{28,12},{1,17},{... | collective-permute-start | bytes 3145736 | tf_op jit(solution)/shard_map/ppermute | solution.py:147
  391.7 41.7 %collective-permute-start.18 = (bf16[4,2,3,128,256]{4,3,2,1,0:T(8,128)(2,1)}, bf16[4,2,3,128,256]{4,3,2,1,0:T(8,128)(2,1)}, u32[]{:S(2)}, u32[]{:S(2)}) collective-permute-start(bf16[4,2,3,128,256]{4,3,2,1,0:T(8,128)(2,1)} %weight_send.8), channel_id=1, source_target_pairs={{0,4},{4,0},{8,12},{12,8},{16,20},{20,16},{24,28},{28,24},{1,5},{5... | collective-permute-start | bytes 4718600 | tf_op jit(solution)/shard_map/ppermute | solution.py:147
  420.3 20.2 %collective-permute-start.21 = (bf16[2,1,128,1024]{3,2,0,1:T(8,128)(2,1)}, bf16[2,1,128,1024]{3,2,0,1:T(8,128)(2,1)}, u32[]{:S(2)}, u32[]{:S(2)}) collective-permute-start(bf16[2,1,128,1024]{3,2,0,1:T(8,128)(2,1)} %fusion.11), channel_id=1, source_target_pairs={{0,16},{4,20},{8,24},{12,28},{16,0},{20,4},{24,8},{28,12},{1,17},{... | collective-permute-start | bytes 1572872 | tf_op jit(solution)/shard_map/ppermute | solution.py:147
  421.5 20.0 %collective-permute-start.20 = (bf16[2,1,128,1024]{3,2,0,1:T(8,128)(2,1)}, bf16[2,1,128,1024]{3,2,0,1:T(8,128)(2,1)}, u32[]{:S(2)}, u32[]{:S(2)}) collective-permute-start(bf16[2,1,128,1024]{3,2,0,1:T(8,128)(2,1)} %fusion.10), channel_id=1, source_target_pairs={{0,8},{4,12},{8,0},{12,4},{16,24},{20,28},{24,16},{28,20},{1,9},{5... | collective-permute-start | bytes 1572872 | tf_op jit(solution)/shard_map/ppermute | solution.py:147
  431.5 44.1 %collective-permute-start.23 = (bf16[1,128,1024]{2,1,0:T(8,128)(2,1)}, bf16[1,128,1024]{2,1,0:T(8,128)(2,1)}, u32[]{:S(2)}, u32[]{:S(2)}) collective-permute-start(bf16[1,128,1024]{2,1,0:T(8,128)(2,1)} %fusion.25), channel_id=1, source_target_pairs={{0,2},{1,3},{2,0},{3,1},{4,6},{5,7},{6,4},{7,5},{8,10},{9,11},{10,... | collective-permute-start | bytes 786440 | tf_op jit(solution)/shard_map/ppermute | solution.py:147
  433.4 35.7 %collective-permute-start.27 = (bf16[2,1,128,256]{3,2,1,0:T(8,128)(2,1)}, bf16[2,1,128,256]{3,2,1,0:T(8,128)(2,1)}, u32[]{:S(2)}, u32[]{:S(2)}) collective-permute-start(bf16[2,1,128,256]{3,2,1,0:T(8,128)(2,1)} %fusion.35), channel_id=1, source_target_pairs={{0,16},{4,20},{8,24},{12,28},{16,0},{20,4},{24,8},{28,12},{1,17},{... | collective-permute-start | bytes 393224 | tf_op jit(solution)/shard_map/ppermute | solution.py:147
  440.5 31.2 %collective-permute-start.26 = (bf16[2,1,128,256]{3,2,1,0:T(8,128)(2,1)}, bf16[2,1,128,256]{3,2,1,0:T(8,128)(2,1)}, u32[]{:S(2)}, u32[]{:S(2)}) collective-permute-start(bf16[2,1,128,256]{3,2,1,0:T(8,128)(2,1)} %fusion.34), channel_id=1, source_target_pairs={{0,8},{4,12},{8,0},{12,4},{16,24},{20,28},{24,16},{28,20},{1,9},{5... | collective-permute-start | bytes 393224 | tf_op jit(solution)/shard_map/ppermute | solution.py:147
  441.4 37.6 %collective-permute-start.29 = (bf16[2,1,3,128,256]{4,3,2,1,0:T(8,128)(2,1)}, bf16[2,1,3,128,256]{4,3,2,1,0:T(8,128)(2,1)S(1)}, u32[]{:S(2)}, u32[]{:S(2)}) collective-permute-start(bf16[2,1,3,128,256]{4,3,2,1,0:T(8,128)(2,1)} %get-tuple-element.248), channel_id=1, source_target_pairs={{0,8},{4,12},{8,0},{12,4},{16,24},{20,28},{24,16},{28,20},{1,9},{5... | collective-permute-start | bytes 1179656 | tf_op jit(solution)/shard_map/ppermute | solution.py:147
  446.5 19.6 %collective-permute-start.25 = (bf16[1,1,128,1024]{3,2,1,0:T(8,128)(2,1)}, bf16[1,1,128,1024]{3,2,1,0:T(8,128)(2,1)}, u32[]{:S(2)}, u32[]{:S(2)}) collective-permute-start(bf16[1,1,128,1024]{3,2,1,0:T(8,128)(2,1)} %fusion.27), channel_id=1, source_target_pairs={{0,1},{1,0},{2,3},{3,2},{4,5},{5,4},{6,7},{7,6},{8,9},{9,8},{10,11... | collective-permute-start | bytes 786440 | tf_op jit(solution)/shard_map/ppermute | solution.py:147
  (59 other events, 596.7 us)

commit v4 on v3

--- a/solution.py
+++ b/solution.py
@@ -33,7 +33,7 @@
 
 
 def cost(flops, moved):
-    return pl.CostEstimate(flops=int(flops), bytes_accessed=int(moved), transcendentals=0)
+    return pl.CostEstimate(flops=int(flops) // 1000, bytes_accessed=int(moved) // 1000, transcendentals=0)
 
 
 def dot(first, second):
@@ -50,92 +50,6 @@
 
 def flat(block):
     return block.reshape(block.shape[0] * block.shape[1], block.shape[2])
-
-
-def exchange_kernel(
-    kind, x_ref, range_ref, level_ref, o_ref, near, far, mid, near_send, near_recv, far_send, far_recv
-):
-    data, part = lax.axis_index("dp"), lax.axis_index("tensor")
-    datas, parts = lax.axis_size("dp"), lax.axis_size("tensor")
-    barrier = pltpu.get_barrier_semaphore()
-
-    def to_data(step):
-        return (lax.rem(data + step, datas), part)
-
-    def to_part(step):
-        return (data, lax.rem(part + step, parts))
-
-    def greet(target):
-        def run(step, carry):
-            pl.semaphore_signal(barrier, inc=1, device_id=target(step), device_id_type=MESH)
-            return carry
-
-        return run
-
-    lax.fori_loop(1, datas, greet(to_data), 0)
-    lax.fori_loop(1, parts, greet(to_part), 0)
-    pl.semaphore_wait(barrier, datas + parts - 2)
-
-    def exchange(source, slots, send, recv, target, count):
-        def copy(step):
-            return pltpu.make_async_remote_copy(
-                src_ref=source,
-                dst_ref=slots.at[step],
-                send_sem=send.at[step],
-                recv_sem=recv.at[step],
-                device_id=target(step),
-                device_id_type=MESH,
-            )
-
-        def start(step, carry):
-            copy(step).start()
-            return carry
-
-        def finish(step, carry):
-            copy(step).wait()
-            return carry
-
-        lax.fori_loop(1, count, start, 0)
-        slots[0] = source[...]
-        lax.fori_loop(1, count, finish, 0)
-        return jnp.max(slots[...], axis=0)
-
-    mid[...] = exchange(x_ref, near, near_send, near_recv, to_data, datas)
-    total = exchange(mid, far, far_send, far_recv, to_part, parts)
-    if kind == "rows":
-        total = jnp.broadcast_to(jnp.max(total, axis=1, keepdims=True), total.shape)
-    if kind != "rows":
-        peak = jnp.max(total, keepdims=True)
-        level = DECAY * range_ref[kind] + (1.0 - DECAY) * peak
-        places = lax.broadcasted_iota(jnp.int32, total.shape, 0)
-        total = jnp.where(places == kind, level, level_ref[...])
-    o_ref[...] = total
-
-
-def exchange_all(values, mesh, kind, previous, levels):
-    datas, parts = mesh.shape["dp"], mesh.shape["tensor"]
-    dims = values.shape
-    copies = pltpu.SemaphoreType.DMA
-    vmem = pl.BlockSpec(memory_space=pltpu.VMEM)
-    return pl.pallas_call(
-        partial(exchange_kernel, kind),
-        out_shape=shape_of(dims, F32),
-        in_specs=[vmem, in_smem(), vmem],
-        out_specs=vmem,
-        scratch_shapes=[
-            pltpu.VMEM((datas,) + dims, F32),
-            pltpu.VMEM((parts,) + dims, F32),
-            pltpu.VMEM(dims, F32),
-            copies((datas,)),
-            copies((datas,)),
-            copies((parts,)),
-            copies((parts,)),
-        ],
-        compiler_params=params(
-            collective_id={"rows": 0, 1: 1, 2: 7, 3: 8}[kind], has_side_effects=True
-        ),
-        name="exchange",
-    )(values, previous, levels)
 
 
 def tie(values, others):
@@ -184,46 +98,38 @@
     return split
 
 
-def scatter_plane(keeps, sends, but_last=False):
+def scatter_plane(keeps, sends, left_over=False):
     plane, orders = plane_orders()
     left = [[bit for bit in plane[::-1] if bit != order[0]] for order in orders]
     sides = [keep.reshape((2,) * len(left[0]) + keep.shape[1:]) for keep in keeps]
-    token = yield list(sends)
-    for i in range(2):
-        other = swap(sends[i], "dp", orders[i][0], token)
-        sides[i] = sides[i] + other.reshape(sides[i].shape).astype(F32)
-    for step in range(1, len(plane)):
-        places = [left[i].index(orders[i][step]) for i in range(2)]
-        sends = [low(lax.index_in_dim(sides[i], 1, places[i], keepdims=False)) for i in range(2)]
-        if but_last and step == len(plane) - 1:
-            return [(lax.index_in_dim(sides[i], 0, places[i], keepdims=False), sends[i]) for i in range(2)]
+    sends = [send.reshape(side.shape) for side, send in zip(sides, sends)]
+    for step in range(len(plane)):
+        if step:
+            places = [left[i].index(orders[i][step]) for i in range(2)]
+            sends = [low(lax.index_in_dim(sides[i], 1, places[i], keepdims=False)) for i in range(2)]
+            sides = [lax.index_in_dim(sides[i], 0, places[i], keepdims=False) for i in range(2)]
+            for i in range(2):
+                left[i].remove(orders[i][step])
         token = yield sends
-        for i in range(2):
-            bit = orders[i][step]
-            keep = lax.index_in_dim(sides[i], 0, places[i], keepdims=False)
-            sides[i] = keep + swap(sends[i], "dp", bit, token).astype(F32)
-            left[i].remove(bit)
+        others = [swap(sends[i], "dp", orders[i][step], token) for i in range(2)]
+        if left_over and step == len(plane) - 2:
+            return list(zip(sides, others))
+        sides = [side + other.astype(F32) for side, other in zip(sides, others)]
     return sides
 
 
-def scatter_part(keeps, sends):
+def scatter_all(keeps, sends):
     sides = yield from scatter_plane(keeps, sends)
-    for bit in range(bits_of("tensor") - 1):
+    last = bits_of("tensor") - 1
+    for bit in range(last):
         pairs = [values.reshape((-1, 2) + values.shape[1:]) for values in sides]
         sends = [low(values[:, 1]) for values in pairs]
         token = yield sends
-        sides = [
-            values[:, 0] + swap(send, "tensor", bit, token).astype(F32)
-            for values, send in zip(pairs, sends)
-        ]
-    return [side[0] for side in sides]
-
-
-def scatter_all(keeps, sends):
-    sides = yield from scatter_part(keeps, sends)
-    send = low(sides[1])
+        others = [swap(send, "tensor", bit, token) for send in sends]
+        sides = [values[:, 0] + other.astype(F32) for values, other in zip(pairs, others)]
+    send = low(sides[1][0])
     token = yield [send]
-    return sides[0] + swap(send, "tensor", bits_of("tensor") - 1, token).astype(F32)
+    return sides[0][0], swap(send, "tensor", last, token)
 
 
 def at_distance(axis, r):
@@ -395,16 +301,54 @@
     return pl.BlockSpec(memory_space=pltpu.HBM)
 
 
-def hosting(body, counts, given):
+def all_distances():
+    return [("dp", r) for r in range(1, 1 << bits_of("dp"))] + part_distances()
+
+
+class Peaks:
+    def __init__(self, mover, mine, near, mid, far):
+        self.mine, self.near, self.mid, self.far = mine, near, mid, far
+        self.first = [mover.remote(mine, near.at[r], "dp", r) for r in range(1, near.shape[0])]
+        self.second = [mover.remote(mid, far.at[r], axis, r) for axis, r in part_distances()]
+
+    def reach(self, values):
+        self.mine[...] = values
+        for moves, source, held in (
+            (self.first, self.mine, self.near),
+            (self.second, self.mid, self.far),
+        ):
+            for move in moves:
+                move.start()
+            held[0] = source[...]
+            for move in moves:
+                move.wait()
+            values = jnp.max(held[...], axis=0)
+            self.mid[...] = values
+        return values
+
+
+def peak_scratch():
+    datas, parts = 1 << bits_of("dp"), 1 << bits_of("tensor")
+    tile = (8, LANES)
+    return [pltpu.VMEM(dims, F32) for dims in (tile, (datas,) + tile, tile, (parts,) + tile)]
+
+
+def peak_moves():
+    return (1 << bits_of("dp")) + (1 << bits_of("tensor")) - 2
+
+
+def hosting(body, counts, given, row, peak):
     ins, outs = counts
     sources = sum(1 + count for count in given)
 
     def kernel(*refs):
-        body_ins, held = refs[:ins], list(refs[ins : ins + sources])
-        rest = refs[ins + sources :]
-        body_outs, sides = rest[:outs], rest[outs : outs + 2 * len(given)]
-        body_scratch = rest[outs + 2 * len(given) : -3 - len(given)]
-        vias, mover = rest[-3 - len(given) : -3], Mover(*rest[-3:])
+        body_ins, (range_ref, before_ref) = refs[:ins], refs[ins : ins + 2]
+        held, rest = list(refs[ins + 2 : ins + 2 + sources]), refs[ins + 2 + sources :]
+        body_outs, level_ref = rest[:outs], rest[outs]
+        sides, rest = rest[outs + 1 : outs + 1 + 2 * len(given)], rest[outs + 1 + 2 * len(given) :]
+        body_scratch, vias = rest[: -7 - len(given)], rest[-7 - len(given) : -7]
+        mover = Mover(*rest[-3:])
+        peaks = Peaks(mover, *rest[-7:-3])
         weights = []
         for i, count in enumerate(given):
             own, *there = [held.pop(0) for _ in range(1 + count)]
@@ -417,7 +361,7 @@
 
         @pl.when(step == 0)
         def _():
-            greet(plane_distances())
+            greet(all_distances())
             for weight, count in weights:
                 weight.start()
                 if count:
@@ -436,34 +380,39 @@
         def _():
             for weight, _ in weights:
                 weight.finish()
+            largest = jnp.max(peaks.reach(body_outs[peak][...]), keepdims=True)
+            level = DECAY * range_ref[row] + (1.0 - DECAY) * largest
+            places = lax.broadcasted_iota(jnp.int32, level_ref.shape, 0)
+            level_ref[...] = jnp.where(places == row, level, before_ref[...])
 
     return kernel
 
 
-def hosted_call(body, weights, cid, *, grid, in_specs, out_specs, out_shape, scratch_shapes=(), **rest):
+def hosted_call(body, weights, cid, ranges, levels, row, peak, *, grid, in_specs, out_specs, out_shape, scratch_shapes=(), **rest):
     plane = 1 << (bits_of("dp") - 1)
     counts = (len(in_specs), len(out_specs))
     given = [len(there) for _, there in weights]
-    totals = [sum(column) for column in zip(*[plane_counts(count) for count in given])]
-    out_shape, vias, sources = list(out_shape), [], []
+    totals = [sum(column) for column in zip((peak_moves(), 1), *[plane_counts(count) for count in given])]
+    small = pl.BlockSpec((8, LANES), lambda *steps: (0, 0))
+    out_shape, vias, sources = out_shape + [shape_of((8, LANES), F32)], [], []
     for held, there in weights:
         out_shape += [shape_of((plane,) + held.shape, held.dtype)] * 2
         vias.append(pltpu.VMEM((1 + len(there),) + held.shape, held.dtype))
         sources += [held] + list(there)
     call = pl.pallas_call(
-        hosting(body, counts, given),
+        hosting(body, counts, given, row, peak),
         grid=grid,
-        in_specs=in_specs + [anywhere()] * len(sources),
-        out_specs=out_specs + [anywhere()] * 2 * len(weights),
+        in_specs=in_specs + [in_smem(), small] + [anywhere()] * len(sources),
+        out_specs=out_specs + [small] + [anywhere()] * 2 * len(weights),
         out_shape=out_shape,
-        scratch_shapes=list(scratch_shapes) + vias + copy_semaphores(*totals),
+        scratch_shapes=list(scratch_shapes) + vias + peak_scratch() + copy_semaphores(*totals),
         compiler_params=params(collective_id=cid, has_side_effects=True),
         **rest,
     )
 
     def run(*args):
-        results = call(*args, *sources)
-        return results[: counts[1]], results[counts[1] :]
+        results = call(*args, ranges, levels, *sources)
+        return results[: counts[1]], results[counts[1]], results[counts[1] + 1 :]
 
     return run
 
@@ -552,128 +501,158 @@
     )(first, biases, outer, inner)
 
 
-class PartSum:
-    def __init__(self, mover, distances, send, recv, slope, piece, near, far):
-        self.moves = [
-            mover.remote(send.at[i], recv.at[i], "tensor", r) for i, r in enumerate(distances)
-        ]
-        self.over = OverPlane(mover, piece, slots(near), slots(far))
-        self.send, self.recv, self.slope, self.piece = send, recv, slope, piece
-        self.distances = list(distances)
-
-    def push(self, r, values):
-        i = self.distances.index(r)
-        self.send[i] = low(values)
-        self.moves[i].start()
-
-    def reach(self, own):
-        for move in self.moves:
-            move.wait_recv()
-        total = own + jnp.sum(self.recv[...].astype(F32), axis=0)
-        self.piece[...] = low(total * self.slope[...])
-        self.over.start()
-
-    def relay(self):
-        self.over.relay()
-
-    def finish(self):
-        self.over.finish()
-        for move in self.moves:
-            move.wait_send()
+CHUNK = 2
 
 
 def finale_kernel(
-    down_ref, in_a, in_b, out_a, out_b, keep_0, keep_1, keep_2, keep_3, send_0, send_1, send_2, send_3,
-    slope_in, slope_out, slope_q, sums_ref, near_d, far_d, near_i, far_i, near_o, far_o, near_q, far_q, sums_out,
-    send_i, recv_i, piece_i, send_o, recv_o, piece_o, send_q, recv_q, piece_q, recv_0, recv_1, recv_2, recv_3,
-    sums_near, sums_mid, sums_far, send, recv, own
+    down_sum, down_more, in_sum, in_more, keep_0, more_0, keep_1, more_1, keep_2, more_2, keep_3, more_3,
+    slope_q, slope_in, slope_down, sums_ref, near_d, far_d, near_i, far_i, near_q, far_q, sums_out,
+    piece_d, piece_i, send_q, recv_q, piece_q, send_p, recv_p, sums_near, sums_mid, sums_far, send, recv, own
 ):
     mover = Mover(send, recv, own)
     _, orders = plane_orders()
-    quarter = keep_0.shape[0]
-    half, parts = 2 * quarter, 4 * quarter
-    datas = sums_near.shape[0]
-    keeps, sends = (keep_0, keep_1, keep_2, keep_3), (send_0, send_1, send_2, send_3)
-    recvs = (recv_0, recv_1, recv_2, recv_3)
-    steps = [mover.remote(sends[i], recvs[i], "dp", 1 << orders[i % 2][-1]) for i in range(4)]
-    down = OverPlane(mover, down_ref, slots(near_d), slots(far_d))
-    inner = PartSum(mover, [half], send_i, recv_i, slope_in, piece_i, near_i, far_i)
-    outer = PartSum(mover, range(1, parts), send_o, recv_o, slope_out, piece_o, near_o, far_o)
-    first = PartSum(mover, range(1, parts), send_q, recv_q, slope_q, piece_q, near_q, far_q)
-    sum_data = [mover.remote(sums_ref, sums_near.at[r], "dp", r) for r in range(1, datas)]
+    keeps, mores = (keep_0, keep_1, keep_2, keep_3), (more_0, more_1, more_2, more_3)
+    quarter, kinds = keep_0.shape[1:3]
+    parts, datas, chunks = 4 * quarter, sums_near.shape[0], kinds // CHUNK
+    steps = [
+        [mover.remote(send_p.at[k, i], recv_p.at[k, i], "dp", 1 << orders[i % 2][-1]) for i in range(4)]
+        for k in range(chunks)
+    ]
+    along = [
+        [mover.remote(send_q.at[k, r - 1], recv_q.at[k, r - 1], axis, r) for axis, r in part_distances()]
+        for k in range(chunks)
+    ]
+    down = OverPlane(mover, piece_d, slots(near_d), slots(far_d))
+    inner = OverPlane(mover, piece_i, slots(near_i), slots(far_i))
+    first = [
+        OverPlane(
+            mover,
+            piece_q.at[k],
+            slots(near_q, pl.ds(k * CHUNK, CHUNK)),
+            slots(far_q, pl.ds(k * CHUNK, CHUNK)),
+        )
+        for k in range(chunks)
+    ]
+    me = lax.axis_index("dp")
+    sum_data = [
+        mover.remote(sums_ref.at[at_distance("dp", r)], sums_near.at[r], "dp", r) for r in range(1, datas)
+    ]
+    sum_back = [mover.remote(sums_out.at[me], sums_out.at[me], "dp", r) for r in range(1, datas)]
     sum_part = [mover.remote(sums_mid, sums_far.at[r], axis, r) for axis, r in part_distances()]
 
-    def block(r):
-        return keeps[r // quarter][r % quarter] + recvs[r // quarter][r % quarter].astype(F32)
+    def kinds_of(k):
+        return slice(k * CHUNK, (k + 1) * CHUNK)
+
+    def block(k, r):
+        i, j = r // quarter, r % quarter
+        here = keeps[i][0, j, kinds_of(k)] + mores[i][0, j, kinds_of(k)].astype(F32)
+        return here + recv_p[k, i, j].astype(F32)
+
+    def reach(k):
+        total = block(k, 0)
+        for r in range(1, parts):
+            along[k][r - 1].wait_recv()
+            total = total + recv_q[k, r - 1].astype(F32)
+        piece_q[k] = low(total * slope_q[kinds_of(k)])
+        first[k].start()
 
     greet([("dp", r) for r in range(1, datas)] + part_distances())
-    for step in steps:
-        step.start()
-    inner.push(half, in_b[...])
-    for r in range(1, parts):
-        outer.push(r, (out_a if r < half else out_b)[r % half])
-    for i in (3, 2, 1, 0):
-        steps[i].wait_recv()
-        for r in range(i * quarter, (i + 1) * quarter):
-            if r:
-                first.push(r, block(r))
-    down.start()
     for move in sum_data:
         move.start()
-    inner.reach(in_a[...])
-    outer.reach(out_a[0])
+    for k in range(chunks):
+        for i in (3, 2, 1, 0):
+            more = mores[i][1, :, kinds_of(k)].astype(F32)
+            send_p[k, i] = low(keeps[i][1, :, kinds_of(k)] + more)
+            steps[k][i].start()
+    piece_d[...] = low((down_sum[...] + down_more[...].astype(F32)) * slope_down[...])
+    piece_i[...] = low((in_sum[...] + in_more[...].astype(F32)) * slope_in[...])
+    for k in range(chunks):
+        for i in (3, 2, 1, 0):
+            steps[k][i].wait_recv()
+            for r in range(i * quarter, (i + 1) * quarter):
+                if r:
+                    send_q[k, r - 1] = low(block(k, r))
+                    along[k][r - 1].start()
+    down.start()
+    inner.start()
     for move in sum_data:
         move.wait()
-    sums_near[0] = sums_ref[...]
+    sums_near[0] = sums_ref[me]
     sums_mid[...] = jnp.sum(sums_near[...], axis=0)
     for move in sum_part:
         move.start()
+    reach(0)
     down.relay()
     inner.relay()
-    outer.relay()
-    first.reach(block(0))
+    for k in range(1, chunks):
+        reach(k)
+        first[k - 1].relay()
     for move in sum_part:
         move.wait()
     sums_far[0] = sums_mid[...]
-    sums_out[...] = jnp.sum(sums_far[...], axis=0)
+    sums_out[me] = jnp.sum(sums_far[...], axis=0)
+    for move in sum_back:
+        move.start()
     down.finish()
     inner.finish()
-    outer.finish()
-    first.relay()
-    first.finish()
-    for step in steps:
-        step.wait_send()
-
-
-def finale(down, inner, outer, first, slopes, sums):
+    first[chunks - 1].relay()
+    for move in sum_back:
+        move.wait()
+    for unit in first:
+        unit.finish()
+    for group in steps + along:
+        for move in group:
+            move.wait_send()
+
+
+def finale(down, inner, first, slopes, sums):
     parts, plane, datas = 1 << bits_of("tensor"), 1 << (bits_of("dp") - 1), 1 << bits_of("dp")
-    pieces = [down, slopes[1], slopes[2], slopes[0]]
-    remote = 4 + 4 * plane_counts(0)[0] + 3 * (parts - 1) + 1 + datas - 1
+    pieces = [slopes[2], slopes[1], slopes[0]]
+    _, quarter, kinds, rows, c = first[0][0].shape
+    chunks = kinds // CHUNK
+    remote = chunks * (4 + parts - 1) + (2 + chunks) * plane_counts(0)[0] + 2 * (datas - 1) + parts - 1
+    dims = sums.shape
+    sums = sums.reshape(datas, -1, LANES)
+    own = sums.shape[1:]
     vmem = pl.BlockSpec(memory_space=pltpu.VMEM)
-    scratch = []
-    for piece, count in zip(pieces[1:], (1, parts - 1, parts - 1)):
-        scratch += [pltpu.VMEM((count,) + piece.shape, BF16)] * 2 + [pltpu.VMEM(piece.shape, BF16)]
-    scratch += [pltpu.VMEM(first[0][1].shape, BF16)] * 4
+    scratch = [pltpu.VMEM(piece.shape, BF16) for piece in pieces[:2]]
+    scratch += [pltpu.VMEM((chunks, parts - 1, CHUNK, rows, c), BF16)] * 2
+    scratch += [pltpu.VMEM((chunks, CHUNK, rows, c), BF16)]
+    scratch += [pltpu.VMEM((chunks, 4, quarter, CHUNK, rows, c), BF16)] * 2
     scratch += [
-        pltpu.VMEM((datas,) + sums.shape, F32),
         pltpu.VMEM(sums.shape, F32),
-        pltpu.VMEM((parts,) + sums.shape, F32),
+        pltpu.VMEM(own, F32),
+        pltpu.VMEM((parts,) + own, F32),
     ]
     out_shape = []
     for piece in pieces:
         out_shape += [shape_of((plane,) + piece.shape, BF16)] * 2
-    keeps, sends = [side[0] for side in first], [side[1] for side in first]
-    args = (down, *inner, *outer, *keeps, *sends, slopes[1], slopes[2], slopes[0], sums)
+    args = [*down, *inner]
+    for pair in first:
+        args += list(pair)
+    args += [*slopes, sums]
     results = pl.pallas_call(
         finale_kernel,
-        in_specs=[vmem] * 9 + [anywhere()] * 4 + [vmem] * 4,
-        out_specs=[anywhere()] * 8 + [vmem],
+        in_specs=[vmem] * len(args),
+        out_specs=[anywhere()] * 6 + [vmem],
         out_shape=out_shape + [shape_of(sums.shape, F32)],
-        scratch_shapes=scratch + copy_semaphores(remote, 4),
+        scratch_shapes=scratch + copy_semaphores(remote, 2 + chunks),
         compiler_params=params(collective_id=2, has_side_effects=True),
         name="finale",
     )(*args)
-    return [results[2 * i : 2 * i + 2] for i in range(4)], results[8]
+    return [results[2 * i : 2 * i + 2] for i in range(3)], results[6].reshape(dims)
+
+
+class Order:
+    def __init__(self, width):
+        self.rows = width // (1 << bits_of("dp"))
+
+    def __getitem__(self, j):
+        if self.rows % LANES:
+            return j
+        plane, each = 1 << (bits_of("dp") - 1), self.rows // LANES
+        place = j // each
+        return at_distance("dp", place % plane * 2 + place // plane) * each + j % each
 
 
 def take_blocks(ref, order_ref, here=slice(None)):
@@ -704,42 +683,68 @@
     return peak
 
 
+def lane_peak(values):
+    return jnp.max(column_peak(values), axis=0, keepdims=True)
+
+
 def prepare_kernel(
-    order_ref, range_ref, peak_ref, x_ref, qkv_ref, out_ref, in_ref, down_ref, level_ref, quant_ref,
-    *refs
+    range_ref, x_ref, qkv_ref, out_ref, in_ref, down_ref, level_ref, quant_ref, *refs
 ):
-    level = DECAY * range_ref[0] + (1.0 - DECAY) * peak_ref[6:7, 0:1]
+    peaks = Peaks(Mover(*refs[-3:-1], None), *refs[-7:-3])
+    greet(all_distances())
+    order = Order(x_ref.shape[1])
+    rows = 256
+    steps = x_ref.shape[0] // rows
+
+    def largest(step, peak):
+        here = pl.ds(pl.multiple_of(step * rows, rows), rows)
+        return jnp.maximum(peak, column_peak(x_ref[here, :].astype(F32)))
+
+    own = [qkv_ref[j].astype(F32) for j in range(3)]
+    own += [ref[0].astype(F32) for ref in (out_ref, in_ref, down_ref)]
+    found = [lane_peak(values) for values in own]
+    inputs = lax.fori_loop(0, steps, largest, jnp.zeros((8, LANES), F32))
+    found.append(jnp.max(inputs, axis=0, keepdims=True))
+    found.append(jnp.zeros((1, LANES), F32))
+    reached = jnp.max(peaks.reach(jnp.concatenate(found, axis=0)), axis=1, keepdims=True)
+    level = DECAY * range_ref[0] + (1.0 - DECAY) * reached[6:7, :]
     level_ref[...] = jnp.broadcast_to(level, level_ref.shape)
-    for i, ref in enumerate((qkv_ref, out_ref, in_ref, down_ref)):
-        for j in range(ref.shape[0]):
-            place = j if i == 0 else i + 2
-            own = 0.5 * peak_ref[place : place + 1, 0:1]
-            tangent = jnp.tanh(ref[j].astype(F32) / own)
-            refs[2 * i][j] = low(own * tangent)
-            refs[2 * i + 1][j] = 1.0 - tangent * tangent
-    rows = 256
-
-    @pl.loop(0, x_ref.shape[0] // rows)
+    for i, values in enumerate(own):
+        bound = 0.5 * reached[i : i + 1, :]
+        tangent = jnp.tanh(values / bound)
+        quant, slope = low(bound * tangent), 1.0 - tangent * tangent
+        if i < 4:
+            refs[4][i] = slope
+        else:
+            refs[1 + i][0] = slope
+        if i < 3:
+            refs[0][i] = quant
+        else:
+            refs[i - 2][0] = quant
+
+    @pl.loop(0, steps)
     def _(step):
         here = pl.ds(pl.multiple_of(step * rows, rows), rows)
-        x = take_blocks(x_ref, order_ref, here).astype(F32)
+        x = take_blocks(x_ref, order, here).astype(F32)
         quant_ref[here, :] = low(level * jnp.tanh(x / level))
 
 
-def prepare(peaks, previous, x, own, order):
+def prepare(ranges, x, own):
     vmem = pl.BlockSpec(memory_space=pltpu.VMEM)
     out_shape = [shape_of((8, LANES), F32), shape_of(x.shape, BF16)]
-    for values in own:
-        out_shape += [shape_of(values.shape, BF16), shape_of(values.shape, F32)]
+    out_shape += [shape_of(values.shape, BF16) for values in own]
+    out_shape += [shape_of((4,) + own[0].shape[1:], F32)]
+    out_shape += [shape_of(values.shape, F32) for values in own[2:]]
     levels, quant, *rest = pl.pallas_call(
         prepare_kernel,
-        in_specs=[in_smem(), in_smem()] + [vmem] * 6,
-        out_specs=[vmem] * 10,
+        in_specs=[in_smem()] + [vmem] * 5,
+        out_specs=[vmem] * 9,
         out_shape=out_shape,
-        compiler_params=params(),
+        scratch_shapes=peak_scratch() + copy_semaphores(peak_moves(), 1),
+        compiler_params=params(collective_id=0, has_side_effects=True),
         name="prepare",
-    )(order, previous, peaks, x, *own)
-    return levels, quant, rest[::2], rest[1::2]
+    )(ranges, x, *own)
+    return levels, quant, rest[:4], rest[4:]
 
 
 def qkv_kernel(x_ref, near_ref, far_ref, b_ref, o_ref):
@@ -770,12 +775,22 @@
     )(x, near, far, bias)
 
 
-def fill_mask(mask_ref, col_ref, row_ref):
-    mask_ref[...] = jnp.where(col_ref[...] == row_ref[...], 0.0, MASKED).astype(F32)
+def fill_mask(mask_ref, ends_ref):
+    row = pl.program_id(0)
+
+    def segments(dims, axis):
+        places = lax.broadcasted_iota(jnp.int32, dims, axis)
+        count = jnp.zeros(dims, jnp.int32)
+        for j in range(ends_ref.shape[1]):
+            count = count + (places >= ends_ref[row, j]).astype(jnp.int32)
+        return count
+
+    same = segments((SEQ, 1), 0) == segments((1, SEQ), 1)
+    mask_ref[...] = jnp.where(same, 0.0, MASKED).astype(F32)
 
 
 def attend_kernel(
-    skip, q_ref, k_ref, v_ref, col_ref, row_ref, lse_before, peak_before, *refs
+    skip, ends_ref, q_ref, k_ref, v_ref, *refs
 ):
     o_ref, lse_ref, peak_ref, mask_ref, sums_ref = refs[-5:]
     row, pair = pl.program_id(0), pl.program_id(1)
@@ -783,12 +798,12 @@
 
     @pl.when(pair == 0)
     def _():
-        fill_mask(mask_ref, col_ref, row_ref)
-        sums_ref[...] = lse_before[...].T
+        fill_mask(mask_ref, ends_ref)
+        sums_ref[...] = jnp.zeros_like(sums_ref) if skip == 0 else refs[0][...].T
 
     @pl.when((pair == 0) & (row == 0))
     def _():
-        peak_ref[...] = peak_before[...]
+        peak_ref[...] = jnp.zeros_like(peak_ref) if skip == 0 else refs[1][...]
 
     rows = 256
     lanes = lax.broadcasted_iota(jnp.int32, (rows, LANES), 1)
@@ -826,7 +841,7 @@
     attend_kernel(pl.num_programs(1), *refs)
 
 
-def attend(qkv, cols, rows, lse, peak, context=None, weights=()):
+def attend(qkv, ends, lse=None, peak=None, context=None, weights=(), ranges=None, levels=None):
     _, tokens, width = qkv.shape
     held = tokens // SEQ
     last = context is not None
@@ -839,15 +854,7 @@
     small = pl.BlockSpec((8, LANES), lambda r, j: (0, 0))
     setup = dict(
         grid=(held, width // LANES // 2),
-        in_specs=[
-            side(0),
-            side(1),
-            side(2),
-            pl.BlockSpec((None, SEQ, 1), lambda r, j: (r, 0, 0)),
-            pl.BlockSpec((None, 1, SEQ), lambda r, j: (r, 0, 0)),
-            sums,
-            small,
-        ],
+        in_specs=[in_smem(), side(0), side(1), side(2)],
         out_specs=[pl.BlockSpec((SEQ, LANES), lambda r, j: (r, j + skip)), sums, small],
         out_shape=[
             shape_of((tokens, width), F32),
@@ -858,18 +865,18 @@
         cost_estimate=cost(15e9, 40 * MIB),
         name="attend",
     )
-    args = (qkv, qkv, qkv, cols, rows, lse, peak)
+    args = (ends, qkv, qkv, qkv)
     if not last:
         return pl.pallas_call(attend_first_kernel, compiler_params=params(), **setup)(*args)
-    setup["in_specs"].append(anywhere())
+    setup["in_specs"] += [sums, small, anywhere()]
     run = hosted_call(
-        attend_last_kernel, weights, 5, input_output_aliases={len(args): 0}, **setup
-    )
-    return run(*args, context)
+        attend_last_kernel, weights, 5, ranges, levels, 1, 2, input_output_aliases={6: 0}, **setup
+    )
+    return run(*args, lse, peak, context)
 
 
 def attend_back_kernel(
-    c, first, order_ref, q_ref, k_ref, v_ref, g_ref, col_ref, row_ref, lse_ref, before_ref, dq_ref, dk_ref,
+    c, first, order_ref, ends_ref, q_ref, k_ref, v_ref, g_ref, lse_ref, before_ref, dq_ref, dk_ref,
     dv_ref, sum_ref, mask_ref
 ):
     pair = pl.program_id(1)
@@ -882,7 +889,7 @@
 
     @pl.when(pair == 0)
     def _():
-        fill_mask(mask_ref, col_ref, row_ref)
+        fill_mask(mask_ref, ends_ref)
 
     lanes = lax.broadcasted_iota(jnp.int32, (SEQ, LANES), 1)
     q, k, v, g = q_ref[...], k_ref[...], v_ref[...], g_ref[...]
@@ -918,9 +925,9 @@
     sum_ref[1:2, here] += jnp.sum(dv.astype(F32), axis=0, keepdims=True)
 
 
-def attend_back(qkv, grad, cols, rows, lse, before, part_order, c, first):
+def attend_back(qkv, grad, ends, lse, before, part_order, c, first):
     _, tokens, inner = qkv.shape
-    width = grad.shape[1]
+    width = inner // 2
     held = tokens // SEQ
     skip = first // LANES
 
@@ -934,12 +941,11 @@
         grid=(held, width // LANES),
         in_specs=[
             in_smem(),
+            in_smem(),
             side(0),
             side(1),
             side(2),
-            block,
-            pl.BlockSpec((None, SEQ, 1), lambda r, j: (r, 0, 0)),
-            pl.BlockSpec((None, 1, SEQ), lambda r, j: (r, 0, 0)),
+            pl.BlockSpec((SEQ, LANES), lambda r, j: (r, j + skip)),
             pl.BlockSpec((None, LANES, SEQ), lambda r, j: (r, 0, 0)),
             sums,
         ],
@@ -949,7 +955,7 @@
         compiler_params=params(),
         cost_estimate=cost(15e9, 50 * MIB),
         name="attend_back",
-    )(part_order, qkv, qkv, qkv, grad, cols, rows, lse, before)
+    )(part_order, ends, qkv, qkv, qkv, grad, lse, before)
 
 
 def project(values, *sides):
@@ -994,14 +1000,15 @@
 
 
 def first_norm_kernel(
-    order_ref, ctx_ref, level_ref, near_ref, far_ref, x_ref, row_ref, quant_ref, normed_ref, normal_ref,
+    ctx_ref, level_ref, near_ref, far_ref, x_ref, row_ref, quant_ref, normed_ref, normal_ref,
     inverse_ref, peak_ref
 ):
     level = level_ref[1:2, 0:1]
     quant = low(level * jnp.tanh(ctx_ref[...] / level))
     quant_ref[...] = quant
-    vectors = take_blocks(row_ref, order_ref)
-    summed = take_blocks(x_ref, order_ref).astype(F32) + project(quant, near_ref, far_ref)
+    order = Order(x_ref.shape[1])
+    vectors = take_blocks(row_ref, order)
+    summed = take_blocks(x_ref, order).astype(F32) + project(quant, near_ref, far_ref)
     normal, inverse = norm_parts(summed + vectors[0:1, :])
     normed = normal * vectors[1:2, :] + vectors[2:3, :]
     normed_ref[...] = normed
@@ -1020,7 +1027,7 @@
     return pl.BlockSpec(dims, lambda *steps: (0,) * len(dims))
 
 
-def first_norm(context, level, weights, x, vectors, order):
+def first_norm(context, level, weights, x, vectors, ranges):
     near, far = weights
     tokens, width = x.shape
     inner = context.shape[1]
@@ -1029,11 +1036,16 @@
     def block(columns):
         return pl.BlockSpec((rows, columns), lambda t: (t, 0))
 
-    return pl.pallas_call(
+    run = hosted_call(
         first_norm_kernel,
+        [],
+        7,
+        ranges,
+        level,
+        2,
+        4,
         grid=(tokens // rows,),
         in_specs=[
-            in_smem(),
             block(inner),
             whole(level),
             whole(near),
@@ -1055,10 +1067,10 @@
             shape_of((tokens, 1), F32),
             shape_of((8, LANES), F32),
         ],
-        compiler_params=params(),
         cost_estimate=cost(2 * tokens * width * inner, 20 * MIB),
         name="first_norm",
-    )(order, context, level, near, far, x, vectors)
+    )
+    return run(context, level, near, far, x, vectors)
 
 
 def hidden_kernel(normed_ref, level_ref, near_ref, far_ref, b_ref, quant_ref, act_ref, slope_ref, peak_ref):
@@ -1079,7 +1091,7 @@
     peak_ref[...] = jnp.maximum(peak_ref[...], column_peak(active))
 
 
-def hidden_rows(normed, level, weights, bias, held_down):
+def hidden_rows(normed, level, weights, bias, held_down, ranges):
     near, far = weights
     plane, parts, rows, c = near.shape
     tokens, width = normed.shape
@@ -1091,6 +1103,10 @@
         hidden_kernel,
         [(held_down, ())],
         6,
+        ranges,
+        level,
+        3,
+        3,
         grid=(parts * cuts,),
         in_specs=[
             whole(normed),
@@ -1181,54 +1197,60 @@
     )(order, active, slope, level, *weights, normed, grad, vectors)
 
 
-def weight_grad_specs(x, grads, parts, plane):
-    tokens, width = x.shape
-    count = len(grads)
-    c = grads[0].shape[1] // parts
+def weight_specs(xs, products, parts, plane, c):
+    tokens, width = xs[0].shape
+    count = len(products)
     step = min(c, 1024)
     cuts = c // step
     dims = (plane, parts, count, width // (2 * plane), c)
-    in_specs = [pl.BlockSpec((tokens, step), lambda r, j: (0, r * cuts + j))] * count
+    in_specs = [
+        pl.BlockSpec((tokens, step), lambda r, j, first=first: (0, (r + first) * cuts + j))
+        for _, _, first in products
+    ]
     out_spec = pl.BlockSpec((plane, None, count, dims[3], step), lambda r, j: (0, r, 0, 0, j))
-    return dims, (parts, cuts), in_specs, out_spec, 2 * tokens * width * parts * c * count
-
-
-def weight_send_kernel(count, x_ref, *refs):
-    h_refs, (send_ref, turned_ref) = refs[:count], refs[count:]
-
+    estimate = cost(tokens * width * parts * c * count, 20 * MIB)
+    return dims, (parts, cuts), in_specs, out_spec, estimate
+
+
+def turn_once(x_refs, turned_refs):
     @pl.when((pl.program_id(0) == 0) & (pl.program_id(1) == 0))
     def _():
-        turned_ref[...] = x_ref[...].T
-
+        for x_ref, turned_ref in zip(x_refs, turned_refs):
+            turned_ref[...] = x_ref[...].T
+
+
+def weight_send_kernel(count, which, *refs):
+    x_refs, h_refs = refs[:count], refs[count : count + len(which)]
+    send_ref, turned = refs[count + len(which)], refs[count + len(which) + 1 :]
+    turn_once(x_refs, turned)
     for i, h_ref in enumerate(h_refs):
         h = h_ref[...]
-        send_ref[:, i] = low(dot(turned_ref[...], h)).reshape(send_ref.shape[0], -1, h.shape[1])
-
-
-def weight_send(x, grads, parts, plane):
-    dims, grid, in_specs, out_spec, flops = weight_grad_specs(x, grads, parts, plane)
-    tokens, width = x.shape
+        total = dot(turned[which[i]][...], h)
+        send_ref[:, i] = low(total).reshape(send_ref.shape[0], -1, h.shape[1])
+
+
+def weight_send(xs, products, parts, plane, c):
+    dims, grid, in_specs, out_spec, estimate = weight_specs(xs, products, parts, plane, c)
+    tokens, width = xs[0].shape
     return pl.pallas_call(
-        partial(weight_send_kernel, len(grads)),
+        partial(weight_send_kernel, len(xs), [product[0] for product in products]),
         grid=grid,
-        in_specs=[pl.BlockSpec((tokens, width // 2), lambda r, j: (0, 1))] + in_specs,
+        in_specs=[pl.BlockSpec((tokens, width // 2), lambda r, j: (0, 1))] * len(xs) + in_specs,
         out_specs=out_spec,
         out_shape=shape_of(dims, BF16),
-        scratch_shapes=[pltpu.VMEM((width // 2, tokens), BF16)],
+        scratch_shapes=[pltpu.VMEM((width // 2, tokens), BF16)] * len(xs),
         compiler_params=params(),
-        cost_estimate=cost(flops / 2, 16 * MIB),
+        cost_estimate=estimate,
         name="weight_send",
-    )(x, *grads)
-
-
-def weight_keep_kernel(count, split, x_ref, other_ref, *refs):
-    h_refs, outs, turned_ref = refs[:count], refs[count:-1], refs[-1]
+    )(*xs, *[product[1] for product in products])
+
+
+def weight_keep_kernel(count, which, split, *refs):
+    x_refs, other_ref = refs[:count], refs[count]
+    h_refs = refs[count + 1 : count + 1 + len(which)]
+    outs, turned = refs[count + 1 + len(which) : -count], refs[-count:]
     half = pl.num_programs(0) // 2
-
-    @pl.when((pl.program_id(0) == 0) & (pl.program_id(1) == 0))
-    def _():
-        turned_ref[...] = x_ref[...].T
-
+    turn_once(x_refs, turned)
     for side in range(2):
 
         @pl.when(pl.program_id(0) // half == side)
@@ -1236,34 +1258,37 @@
             keep_ref, send_ref = outs[2 * side : 2 * side + 2]
             for i, h_ref in enumerate(h_refs):
                 h = h_ref[...]
-                total = dot(turned_ref[...], h).reshape(other_ref.shape[0], -1, h.shape[1])
+                total = dot(turned[which[i]][...], h).reshape(other_ref.shape[0], -1, h.shape[1])
                 for j, slot in enumerate(split[side][0]):
                     keep_ref[j, i] = total[slot] + other_ref[slot, i].astype(F32)
                 for j, slot in enumerate(split[side][1]):
                     send_ref[j, i] = low(total[slot] + other_ref[slot, i].astype(F32))
 
 
-def weight_keep(x, grads, other, parts, plane):
-    dims, (_, cuts), in_specs, out_spec, flops = weight_grad_specs(x, grads, parts, plane)
-    tokens, width = x.shape
+def weight_keep(xs, products, other, parts, plane, c):
+    dims, (_, cuts), in_specs, out_spec, estimate = weight_specs(xs, products, parts, plane, c)
+    tokens, width = xs[0].shape
     half = parts // 2
-    block = (plane // 2, None, len(grads), dims[3], dims[4] // cuts)
+    block = (plane // 2, None, dims[2], dims[3], c // cuts)
     near = pl.BlockSpec(
         block, lambda r, j: (0, jnp.minimum(r, half - 1), 0, 0, jnp.where(r < half, j, cuts - 1))
     )
     far = pl.BlockSpec(block, lambda r, j: (0, jnp.maximum(r - half, 0), 0, 0, jnp.where(r < half, 0, j)))
     small = (plane // 2, half) + dims[2:]
+    which = [product[0] for product in products]
     keep_a, send_a, keep_b, send_b = pl.pallas_call(
-        partial(weight_keep_kernel, len(grads), first_split(bits_of("dp") - 1)),
+        partial(weight_keep_kernel, len(xs), which, first_split(bits_of("dp") - 1)),
         grid=(parts, cuts),
-        in_specs=[pl.BlockSpec((tokens, width // 2), lambda r, j: (0, 0)), out_spec] + in_specs,
+        in_specs=[pl.BlockSpec((tokens, width // 2), lambda r, j: (0, 0))] * len(xs)
+        + [out_spec]
+        + in_specs,
         out_specs=[near, near, far, far],
         out_shape=[shape_of(small, F32), shape_of(small, BF16)] * 2,
-        scratch_shapes=[pltpu.VMEM((width // 2, tokens), BF16)],
+        scratch_shapes=[pltpu.VMEM((width // 2, tokens), BF16)] * len(xs),
         compiler_params=params(),
-        cost_estimate=cost(flops / 2, 24 * MIB),
+        cost_estimate=estimate,
         name="weight_keep",
-    )(x, other, *grads)
+    )(*xs, other, *[product[1] for product in products])
     return [keep_a, keep_b], [send_a, send_b]
 
 
@@ -1375,12 +1400,11 @@
     o_ref[...] = low(grad * (1.0 - tangent * tangent))
 
 
-def grad_context_rows(grad, weights, context, level, first):
+def grad_context_rows(grad, weights, context, level):
     near, far = weights
     plane, parts, rows, c = near.shape
-    parts = parts // 2
     tokens, width = grad.shape
-    weight_spec = pl.BlockSpec((plane, None, rows, c), lambda r: (0, r + first, 0, 0))
+    weight_spec = pl.BlockSpec((plane, None, rows, c), lambda r: (0, r, 0, 0))
     block = pl.BlockSpec((tokens, c), lambda r: (0, r))
     return pl.pallas_call(
         grad_context_kernel,
@@ -1389,7 +1413,7 @@
             whole(grad),
             weight_spec,
             weight_spec,
-            pl.BlockSpec((tokens, c), lambda r: (0, r + first)),
+            block,
             whole(level),
         ],
         out_specs=block,
@@ -1440,86 +1464,76 @@
     )(order, *grads, near, far, grad_sum, x, level)
 
 
-def place_kernel(turns, order_ref, *refs):
-    ins, outs = refs[: 2 * len(turns)], refs[2 * len(turns) :]
-    core = pl.program_id(0) * 2 // pl.num_programs(0)
-    for side in range(2):
-
-        @pl.when(core == side)
-        def _(side=side):
-            for i, turn in enumerate(turns):
-                values = ins[2 * i + side]
-                if turn:
-                    outs[i][...] = values[0].astype(F32).T
-                else:
-                    outs[i][...] = values[...].astype(F32)
-
-
-def place_grads(groups, turns, blocks):
-    plane, _, rows, _ = groups[0][0].shape
+def place_kernel(turned, order_ref, *refs):
+    d_refs, i_refs, q_refs = refs[:2], refs[2:4], refs[4:6]
+    in_out, qkv_out, *turned_outs = refs[6:]
+    step = pl.program_id(0)
+    plane, _, rows, _ = i_refs[0].shape
+    for core in range(2):
+        for j in range(plane):
+            here = pl.ds(pl.multiple_of(order_ref[core * plane + j] * rows, rows), rows)
+            in_out[0, here, :] = i_refs[core][j, 0].astype(F32)
+            if turned:
+                turned_outs[0][:, here] = d_refs[core][j, 0].astype(F32).T
+
+            @pl.when(step < 3)
+            def _(core=core, j=j, here=here):
+                qkv_out[0, here, :] = q_refs[core][j, 0].astype(F32)
+
+            if turned:
+
+                @pl.when(step == 3)
+                def _(core=core, j=j, here=here):
+                    turned_outs[1][:, here] = q_refs[core][j, 0].astype(F32).T
+
+
+def place_grads(down, inner, first, blocks):
+    plane, _, rows, c = inner[0].shape
+    columns = first[0].shape[3]
     width = 2 * plane * rows
-    results = [None] * len(groups)
-    if rows % LANES:
-        back = jnp.zeros((2 * plane,), jnp.int32).at[blocks].set(jnp.arange(2 * plane, dtype=jnp.int32))
-        for i, (near, far) in enumerate(groups):
-            if turns[i]:
-                split = jnp.concatenate([near, far], axis=0)[:, 0]
-                results[i] = jnp.take(split, back, axis=0).astype(F32).reshape(width, -1).T
-    todo = [i for i in range(len(groups)) if results[i] is None]
-    in_specs, out_specs, out_shape, args = [], [], [], []
-    for i in todo:
-        near, far = groups[i]
-        _, kinds, _, c = near.shape
-        block = (None, kinds, rows, c)
-        in_specs.append(pl.BlockSpec(block, lambda p, order: (jnp.minimum(p, plane - 1), 0, 0, 0)))
-        in_specs.append(pl.BlockSpec(block, lambda p, order: (jnp.maximum(p - plane, 0), 0, 0, 0)))
-        args += [near, far]
-        if turns[i]:
-            out_specs.append(pl.BlockSpec((c, rows), lambda p, order: (0, order[p])))
-            out_shape.append(shape_of((c, width), F32))
-        else:
-            out_specs.append(pl.BlockSpec((kinds, rows, c), lambda p, order: (0, order[p], 0)))
-            out_shape.append(shape_of((kinds, width, c), F32))
-    placed = pl.pallas_call(
-        partial(place_kernel, [turns[i] for i in todo]),
-        grid_spec=pltpu.PrefetchScalarGridSpec(
-            num_scalar_prefetch=1, grid=(2 * plane,), in_specs=in_specs, out_specs=out_specs
-        ),
+    turned = rows % LANES == 0
+    cut = c // 4
+
+    def piece(size, index):
+        return [pl.BlockSpec((plane, 1, rows, size), index)] * 2
+
+    out_specs = [
+        pl.BlockSpec((1, width, cut), lambda p: (0, 0, p)),
+        pl.BlockSpec((1, width, columns), lambda p: (jnp.minimum(p, 2), 0, 0)),
+    ]
+    out_shape = [shape_of((1, width, c), F32), shape_of((3, width, columns), F32)]
+    if turned:
+        out_specs.append(pl.BlockSpec((cut, width), lambda p: (p, 0)))
+        out_specs.append(pl.BlockSpec((columns, width), lambda p: (0, 0)))
+        out_shape += [shape_of((c, width), F32), shape_of((columns, width), F32)]
+    inner_grad, qkv_grad, *rest = pl.pallas_call(
+        partial(place_kernel, turned),
+        grid=(4,),
+        in_specs=[in_smem()]
+        + piece(cut, lambda p: (0, 0, 0, p)) * 2
+        + piece(columns, lambda p: (0, p, 0, 0)),
+        out_specs=out_specs,
         out_shape=out_shape,
         compiler_params=params(),
         name="place_grads",
-    )(blocks.astype(jnp.int32), *args)
-    for i, values in zip(todo, placed):
-        results[i] = values
-    return results
-
-
-def but_last(keeps, sends):
+    )(blocks.astype(jnp.int32), *down, *inner, *first)
+    if not turned:
+        back = jnp.zeros((2 * plane,), jnp.int32).at[blocks].set(jnp.arange(2 * plane, dtype=jnp.int32))
+        for near, far in (down, [side[:, 3:] for side in first]):
+            split = jnp.concatenate([near, far], axis=0)[:, 0]
+            rest.append(jnp.take(split, back, axis=0).astype(F32).reshape(width, -1).T)
+    return inner_grad[0], qkv_grad, rest[0], rest[1]
+
+
+def left_over(keeps, sends):
     return scatter_plane(keeps, sends, True)
 
 
-def scatter_plane_of(chain, x, grads, other, token, parts, plane):
-    return chain(*weight_keep(tie(x, [token]), grads, other, parts, plane))
-
-
-HOST_RANK = {attend_last_kernel: 2, hidden_kernel: 1}
-
-
-def doc_segments(doc_lengths, length):
-    doc_ends = jnp.cumsum(doc_lengths, axis=1, dtype=jnp.int32)
-    places = jnp.arange(length, dtype=jnp.int32)
-    return jnp.sum(
-        (places[None, :, None] >= doc_ends[:, None, :]).astype(jnp.int32), axis=2, dtype=jnp.int32
-    )
-
-
-def soft_clip(values, clip_level):
-    return clip_level * jnp.tanh(values / clip_level)
-
-
-def clip_slope(values, clip_level):
-    tangent = jnp.tanh(values / clip_level)
-    return 1.0 - tangent * tangent
+def scatter_grad(chain, xs, products, other, token, parts, plane, c):
+    return chain(*weight_keep([tie(xs[0], [token])] + xs[1:], products, other, parts, plane, c))
+
+
+HOST_RANK = {first_norm_kernel: 1, attend_last_kernel: 2, hidden_kernel: 1}
 
 
 def own_block(values, axis):
@@ -1573,13 +1587,7 @@
         own_block(w_in, 0)[None],
         own_block(w_down, 1).T[None],
     ]
-    peaks = [jnp.max(jnp.abs(own[0][i].astype(F32)), axis=0) for i in range(3)]
-    peaks += [jnp.max(jnp.abs(values[0].astype(F32)), axis=0) for values in own[1:]]
-    peaks += [jnp.max(jnp.abs(x.astype(F32)), axis=0)]
-    peaks = [jnp.max(values.reshape(-1, LANES), axis=0) for values in peaks]
-    peaks = jnp.stack(peaks + [jnp.zeros_like(peaks[0])])
-    reached = exchange_all(peaks, mesh, "rows", ranges, peaks)
-    levels, quant_input, quant_own, slopes = prepare(reached, ranges, x, own, order)
+    levels, quant_input, quant_own, slopes = prepare(ranges, x, own)
     biases = jnp.concatenate([bias_qv.reshape(-1), b_in])
     count = biases.shape[0]
     biases = jnp.pad(biases, (0, -count % (16 * LANES))).reshape(-1, LANES)
@@ -1594,8 +1602,7 @@
 
     held = tokens // SEQ
     lengths_here = lax.dynamic_slice_in_dim(doc_lengths, part * held, held, 0)
-    segments = doc_segments(lengths_here, SEQ).astype(F32)
-    seg_cols, seg_rows = segments[:, :, None], segments[:, None, :]
+    ends = jnp.cumsum(lengths_here, axis=1, dtype=jnp.int32)
     half = parts // 2 * columns
 
     first_moves, _ = plane_moves()
@@ -1604,7 +1611,6 @@
         values = tie(values, [token])
         return [far_swap(values, r) for _, r in first_moves]
 
-    zero = jnp.zeros((8, LANES), F32)
     there_in = over_plane(held_in, biases)
     held_a = tie(quant_own[3], [biases])[None]
     for bit in reversed(range(bits_of("tensor") - 1)):
@@ -1614,87 +1620,86 @@
     held_a = tie(held_a, [qkv])
     there_a = over_plane(held_a, qkv)
     held_b = swap(held_a, "tensor", bits_of("tensor") - 1)
-    context, lse, peak = attend(qkv, seg_cols, seg_rows, jnp.zeros((held, LANES, SEQ), F32), zero)
+    context, lse, peak = attend(qkv, ends)
     there_in, there_a = [tie(values, [peak]) for values in there_in], [tie(values, [peak]) for values in there_a]
-    (context, lse, peak), (*weights_in, near_a, far_a) = attend(
-        qkv, seg_cols, seg_rows, lse, peak, context, [(held_in, there_in), (held_a, there_a)]
+    (context, lse, _), levels, (*weights_in, near_a, far_a) = attend(
+        qkv, ends, lse, peak, context, [(held_in, there_in), (held_a, there_a)], ranges, levels
     )
     weights_in = tuple(side[:, :, 0] for side in weights_in)
-    levels = exchange_all(peak, mesh, 1, ranges, levels)
     weights_out = tuple(side[:, :, 0] for side in weights_out)
-    quant_context, normed, normal_one, inverse_one, peak = first_norm(
-        context, levels, weights_out, x, vectors, order
-    )
-    levels = exchange_all(peak, mesh, 2, ranges, levels)
+    (quant_context, normed, normal_one, inverse_one, _), levels, _ = first_norm(
+        context, levels, weights_out, x, vectors, ranges
+    )
     held_b = tie(held_b, [levels])
-    (quant_normed, active, slope, peak), (near_b, far_b) = hidden_rows(
-        normed, levels, weights_in, bias_hidden, held_b
-    )
-    levels = exchange_all(peak, mesh, 3, ranges, levels)
+    (quant_normed, active, slope, _), levels, (near_b, far_b) = hidden_rows(
+        normed, levels, weights_in, bias_hidden, held_b, ranges
+    )
     weights_down = [side[:, :, 0] for side in (near_a, far_a, near_b, far_b)]
     quant_active, back, output, grad_sum_two, grad_branch, terms_two = second_norm(
         active, slope, levels, weights_down, normed, upstream, vectors, order
     )
 
-    other = weight_send(grad_branch, [quant_active], parts, plane)
-    grad_branch = tie(grad_branch, [other])
+    wide = b_in.shape[0]
+    other = weight_send([grad_branch], [(0, quant_active, 0)], parts, plane, wide)
+    grad_after = tie(grad_branch, [other])
     other = swap(other, "dp", 0)
-    grad_hidden, sum_hidden = grad_hidden_rows(grad_branch, weights_down, back, part_order)
-    down = scatter_plane_of(scatter_all, grad_branch, [quant_active], other, sum_hidden, parts, plane)
+    grad_hidden, sum_hidden = grad_hidden_rows(grad_after, weights_down, back, part_order)
+    down = scatter_grad(
+        scatter_all, [grad_branch], [(0, quant_active, 0)], other, sum_hidden, parts, plane, wide
+    )
     grad_hidden = tie(grad_hidden, next(down))
-    other = weight_send(quant_normed, [grad_hidden], parts, plane)
-    grad_branch = tie(grad_hidden, [other])
+    other = weight_send([quant_normed], [(0, grad_hidden, 0)], parts, plane, wide)
+    grad_after = tie(grad_hidden, [other])
     other = swap(other, "dp", 0)
     grad_sum_one, grad_attention, terms_one = first_back(
-        grad_branch, weights_in, normed, normal_one, inverse_one, grad_sum_two, levels, vectors, order
+        grad_after, weights_in, normed, normal_one, inverse_one, grad_sum_two, levels, vectors, order
     )
     grad_hidden = tie(grad_hidden, down.send(terms_one))
-    inner = scatter_plane_of(scatter_part, quant_normed, [grad_hidden], other, terms_one, parts, plane)
-    grad_attention = tie(grad_attention, next(inner))
-    other = weight_send(grad_attention, [quant_context], parts, plane)
-    grad_context = tie(grad_attention, [other])
-    other = swap(other, "dp", 0)
-    grad_a = grad_context_rows(grad_context, weights_out, context, levels, 0)
-    grad_b = grad_context_rows(grad_context, weights_out, context, levels, parts // 2)
+    inner = scatter_grad(
+        scatter_all, [quant_normed], [(0, grad_hidden, 0)], other, terms_one, parts, plane, wide
+    )
+    grad_after = tie(grad_attention, next(inner))
+    grad_context = grad_context_rows(grad_after, weights_out, context, levels)
+    grad_context = tie(grad_context, down.send(grad_context))
     sums_before = jnp.zeros((8, 2 * half), F32)
-    *grads_a, token = attend_back(qkv, grad_a, seg_cols, seg_rows, lse, sums_before, part_order, columns, 0)
-    grads_a[0] = tie(grads_a[0], down.send(token))
-    outer = scatter_plane_of(scatter_plane, grad_attention, [quant_context], other, token, parts, plane)
-    grads_a[0] = tie(grads_a[0], next(outer))
-    other = weight_send(quant_input, grads_a, parts // 2, plane)
-    grad_b = tie(grad_b, [other])
-    other = swap(other, "dp", 0)
-    *grads_b, token = attend_back(qkv, grad_b, seg_cols, seg_rows, lse, token, part_order, columns, half)
+    *grads, token = attend_back(
+        qkv, grad_context, ends, lse, sums_before, part_order, columns, 0
+    )
+    grads_a = grads
+    xs = [quant_input, grad_attention]
+    products_a = [(0, grad, 0) for grad in grads] + [(1, quant_context, 0)]
+    other_a = weight_send(xs, products_a, parts // 2, plane, columns)
+    token_a = other_a
+    grad_context = tie(grad_context, inner.send(token_a) + down.send(token_a))
+    other_a = swap(other_a, "dp", 0)
+    *grads, token = attend_back(
+        qkv, grad_context, ends, lse, token, part_order, columns, half
+    )
     sum_qv = token
-    grads_b[0] = tie(grads_b[0], inner.send(token) + down.send(token) + outer.send(token))
-    other_b = weight_send(quant_input, grads_b, parts // 2, plane)
-    grads_a[0] = tie(grads_a[0], [other_b])
+    down = run_all(down, token)
+    grads[0] = tie(grads[0], inner.send(token) + [down[1]])
+    products_b = [(0, grad, 0) for grad in grads] + [(1, quant_context, parts // 2)]
+    other_b = weight_send(xs, products_b, parts // 2, plane, columns)
+    token = other_b
     other_b = swap(other_b, "dp", 0)
-    first_a = scatter_plane_of(but_last, quant_input, grads_a, other, grads_a[0], parts // 2, plane)
-    grads_b[0] = tie(grads_b[0], next(first_a))
-    first_b = scatter_plane_of(but_last, quant_input, grads_b, other_b, grads_b[0], parts // 2, plane)
-    started = next(first_b) + inner.send(grads_b[0])
-    grads_b[0] = tie(grads_b[0], started)
-    grad_x = grad_input(grads_a + grads_b, weights_qkv, grad_sum_one, x, levels, order)
+    first_a = scatter_grad(left_over, xs, products_a, other_a, token, parts // 2, plane, columns)
+    started = next(first_a)
+    first_b = scatter_grad(left_over, xs, products_b, other_b, started[0], parts // 2, plane, columns)
+    started = next(first_b) + inner.send(started[0])
+    grads[0] = tie(grads[0], started)
+    grad_x = grad_input(grads_a + grads, weights_qkv, grad_sum_one, x, levels, order)
 
     sums = [terms_one[:3], terms_two[:3], sum_qv[:2], sum_hidden.reshape(-1, width)]
     if rows % LANES:
         sums[0], sums[1] = restore(sums[0]), restore(sums[1])
     sums = jnp.concatenate(sums)
     padded = jnp.pad(sums, ((0, -sums.shape[0] % 8), (0, 0)))
-    down, inner, outer, first_a, first_b = [
-        run_all(chain, grad_x) for chain in (down, inner, outer, first_a, first_b)
-    ]
-    (down, inner, outer, first), sums = finale(
-        low(down * slopes[3]), inner, outer, first_a + first_b, [slopes[0], slopes[2], slopes[1]], padded
-    )
+    inner, first_a, first_b = [run_all(chain, grad_x) for chain in (inner, first_a, first_b)]
+    (down, inner, first), sums = finale(down, inner, first_a + first_b, slopes, padded)
     hidden_all = sums[8 : 8 + sum_hidden.size // width].reshape(-1)
     grad_bias_qv = lax.dynamic_slice_in_dim(sums[6:8], part * columns, columns, 1)
     grad_b_in = lax.dynamic_slice_in_dim(hidden_all, part * b_in.shape[0], b_in.shape[0], 0)
-    grad_w_down, grad_w_out, grad_w_in, grad_w_qkv = place_grads(
-        [down, outer, inner, first], [True, True, False, False], blocks
-    )
-    grad_w_in = grad_w_in[0]
+    grad_w_in, grad_w_qkv, grad_w_down, grad_w_out = place_grads(down, inner, first, blocks)
     new_ranges = levels[:4, 0]
     return (
         restore_rows(output),

time: 571 us -> 533 us (0.933)
  Pallas kernels: 458 us -> 439 us
  other arithmetic: 27.9 us -> 16.8 us
    pallas_call x20 -> x14, Pallas kernels: 254 us -> 239 us  [the longest x3 92.2 us: run(): results = call(*args, ranges, levels, *sources)]
    unnamed x109 -> x76, local copies, waits for them, and re-layouts: 6.56 us -> 13.1 us
    convert_element_type x14 -> x7, local copies, waits for them, and re-layouts: 9.97 us -> 4.24 us  [low(): return values.astype(BF16)]
    ppermute x28 -> x24, starting transfers between devices: 25.2 us -> 22.6 us  [swap(): lax.ppermute(values, axis, [(i, i ^ 1 << bit) for i in range(count)])]
    ppermute x28 -> x24, waiting for transfers between devices: 11 us -> 11.5 us  [swap(): lax.ppermute(values, axis, [(i, i ^ 1 << bit) for i in range(count)])]
  transfers between devices with their start and end apart: 32 -> 28, of which waited for: 6 -> 3; matrix products, arithmetic and copies ran while one was open for 7% -> 5% of each run, Pallas kernels for 40% -> 41%
where the time goes in v4:
time: 533 us; the launch traced here: 525 us
  Pallas kernels  439 us (82%)
  local copies, waits for them, and re-layouts  28.5 us (5%)
  starting transfers between devices  26.7 us (5%)
  other arithmetic  16.8 us (3%)
  waiting for transfers between devices  11.5 us (2%)
    pallas_call x3, Pallas kernels, run(): results = call(*args, ranges, levels, *sources)  92.2 us
    pallas_call x1, Pallas kernels, finale(): pl.pallas_call(finale_kernel, in_specs=[vmem] * len(args), out_specs=[any...  51.1 us
    pallas_call x1, Pallas kernels, first_gather(): pl.pallas_call(first_gather_kernel, in_specs=[pl.BlockSpec(memory_space=p...  46.4 us
    pallas_call x4, Pallas kernels, weight_keep(): pl.pallas_call(partial(weight_keep_kernel, len(xs), which, first_split(bi...  36.6 us
    pallas_call x2, Pallas kernels, attend_back(): pl.pallas_call(partial(attend_back_kernel, c, first), grid=(held, width /...  36.1 us
    pallas_call x4, Pallas kernels, weight_send(): pl.pallas_call(partial(weight_send_kernel, len(xs), [product[0] for produ...  31.4 us
    pallas_call x1, Pallas kernels, second_norm(): pl.pallas_call(second_norm_kernel, grid=(tokens // rows,), in_specs=[in_s...  31 us
    ppermute x24, starting transfers between devices, swap(): lax.ppermute(values, axis, [(i, i ^ 1 << bit) for i in range(count)])  22.6 us
  transfers between devices with their start and end apart: 28, of which 3 were waited for; matrix products, arithmetic and copies ran while one was open for 5% of the time, Pallas kernels for 41%

profile of v4, /device:TPU:0, one launch (start us, length us, event | category | flops | bytes accessed | tf_op | source)
XLA Modules:
  0.0 524.7 jit_solution(8610390132198377731)
XLA Ops:
  8.7 17.1 %prepare.1 = (f32[8,128]{1,0:T(8,128)}, bf16[1024,1024]{1,0:T(8,128)(2,1)}, bf16[3,128,256]{2,1,0:T(8,128)(2,1)}, bf16[1,128,256]{2,1,0:T(8,128)(2,1)}, bf16[1,1...) custom-call(f32[4]{0:T(128)} %refs_5_.1, ...), custom_call_target="tpu_custom_call" | custom-call | tf_op jit(solution)/shard_map/prepare/pallas_call | solution.py:738
  25.8 46.4 %first_gather.1 = (bf16[4,4,3,128,256]{4,3,2,1,0:T(8,128)(2,1)}, bf16[4,4,3,128,256]{4,3,2,1,0:T(8,128)(2,1)}, bf16[4,16,128]{2,1,0:T(8,128)(2,1)}, bf16[4,4,1,1...) custom-call(bf16[3,128,256]{2,1,0:T(8,128)(2,1)} %get-tuple-element.138.first_ref, ...), custom_call_target="tpu_custom_call" | custom-call | tf_op jit(solution)/shard_map/first_gather/pallas_call | solution.py:490
  75.8 14.1 %qkv.1.refs_1_.refs_2_.refs_3_.q_ref.k_ref.v_ref = bf16[3,1024,1024]{2,1,0:T(8,128)(2,1)} custom-call(bf16[1024,1024]{1,0:T(8,128)(2,1)} %get-tuple-element.226.x_ref.refs_0_, bf16[4,4,3,128,256]{4,3,2,1,0:T(8,128)(2,1)} %get-tuple-element.141.near_ref.refs_6_, bf16[4,4,3,128,256]{4,3,2,1,0:T(8,128)(2,1)} %get-tuple-element.142.far_ref.refs_7_, ...), custom_call_target="tpu_custom_call" | custom-call | flops 6442450 | bytes 14680 | tf_op jit(solution)/shard_map/qkv/pallas_call | solution.py:761
  97.3 18.1 %attend.2 = (f32[1024,1024]{1,0:T(8,128)}, f32[2,128,512]{2,1,0:T(8,128)}, f32[8,128]{1,0:T(8,128)}) custom-call(s32[2,4]{1,0:T(2,128)} %reduce_window_sum.11.refs_0_.ends_ref, bf16[3,1024,1024]{2,1,0:T(8,128)(2,1)} %qkv.1.refs_1_.refs_2_.refs_3_.q_ref.k_ref.v_ref, bf16[3,1024,1024]{2,1,0:T(8,128)(2,1)} %qkv.1.refs_1_.refs_2_.refs_3_.q_ref.k_ref.v_ref, ...), custom_call_target="tpu_custom_call" | custom-call | flops 15000000 | bytes 41943 | tf_op jit(solution)/shard_map/attend/pallas_call | solution.py:870
  117.3 33.9 %attend.3 = (f32[1024,1024]{1,0:T(8,128)}, f32[2,128,512]{2,1,0:T(8,128)}, f32[8,128]{1,0:T(8,128)}, f32[8,128]{1,0:T(8,128)}, bf16[4,4,1,128,1024]{4,3,2,1,0:T(...) custom-call(s32[2,4]{1,0:T(2,128)} %reduce_window_sum.11.refs_0_.end, ...), custom_call_target="tpu_custom_call", output_to_operand_aliasing={{0}: (6, {})} | custom-call | flops 15000000 | bytes 41943 | tf_op jit(solution)/shard_map/attend/pallas_call | solution.py:414
  151.2 19.4 %first_norm.1 = (bf16[1024,1024]{1,0:T(8,128)(2,1)}, f32[1024,1024]{1,0:T(8,128)}, f32[1024,1024]{1,0:T(8,128)}, f32[1024,1]{1,0:T(8,128)}, f32[8,128]{1,0:T(8,128)}, /*index=5*/f32[8,128]{1,0:T(8,128)}) custom-call(f32[1024,1024]{1,0:T(8,128)} %get-tuple-element.158.refs_0_.ctx_ref, f32[8,128]{1,0:T(8,128)} %get-tuple-element.159.refs_1_.refs_7_, ...), custom_call_target="tpu_custom_call" | custom-call | flops 2147483 | bytes 20971 | tf_op jit(solution)/shard_map/first_norm/pallas_call | solution.py:414
  171.4 38.9 %hidden.1 = (bf16[1024,1024]{1,0:T(8,128)(2,1)}, f32[1024,4096]{1,0:T(8,128)}, f32[1024,4096]{1,0:T(8,128)}, f32[8,128]{1,0:T(8,128)}, f32[8,128]{1,0:T(8,128)},...) custom-call(f32[1024,1024]{1,0:T(8,128)} %get-tuple-element.162.refs_0_.normed_ref, ...), custom_call_target="tpu_custom_call" | custom-call | flops 8589934 | bytes 52428 | tf_op jit(solution)/shard_map/hidden/pallas_call | solution.py:414
  210.3 31.0 %second_norm.1 = (bf16[1024,4096]{1,0:T(8,128)(2,1)}, f32[1024,4096]{1,0:T(8,128)}, bf16[1024,1024]{1,0:T(8,128)(2,1)}, f32[1024,1024]{1,0:T(8,128)}, bf16[1024,1024]{1,0:T(8,128)(2,1)}, /*index=5*/f32[8,1024]{1,0:T(8,128)}) custom-call(s32[8]{0:T(128)} %fusion.32.order_ref, f32[1024,4096]{1,0:T(8,128)} %get-tuple-element.167.act_ref, ...), custom_call_target="tpu_custom_call" | custom-call | flops 8589934 | bytes 83886 | tf_op jit(solution)/shard_map/second_norm/pallas_call | solution.py:1165
  241.4 9.1 %weight_send.4 = bf16[4,4,1,128,1024]{4,3,2,1,0:T(8,128)(2,1)} custom-call(bf16[1024,1024]{1,0:T(8,128)(2,1)} %get-tuple-element.181.refs_0_.g_ref, bf16[1024,4096]{1,0:T(8,128)(2,1)} %get-tuple-element.176.refs_1_.refs_2_), custom_call_target="tpu_custom_call" | custom-call | flops 4294967 | bytes 20971 | tf_op jit(solution)/shard_map/weight_send/pallas_call | solution.py:1235
  251.0 16.9 %grad_hidden.1 = (bf16[1024,4096]{1,0:T(8,128)(2,1)}, f32[4,1024]{1,0:T(4,128)}) custom-call(s32[4]{0:T(128)} %iota_xor_fusion.order_ref, bf16[1024,1024]{1,0:T(8,128)(2,1)} %get-tuple-element.181.refs_0_.g_ref, bf16[4,2,128,1024]{3,2,1,0:T(8,128)(2,1)} %bitcast.143, bf16[4,2,128,1024]{3,2,1,0:T(8,128)(2,1)} %bitcast.145, ...), custom_call_target="tpu_custom_call" | custom-call | flops 8589934 | bytes 35651 | tf_op jit(solution)/shard_map/grad_hidden/pallas_call | solution.py:1332
  267.9 10.8 %weight_keep.4 = (f32[2,2,1,128,1024]{4,3,2,1,0:T(8,128)}, bf16[2,2,1,128,1024]{4,3,2,1,0:T(8,128)(2,1)}, f32[2,2,1,128,1024]{4,3,2,1,0:T(8,128)}, bf16[2,2,1,128,1024]{4,3,2,1,0:T(8,128)(2,1)}) custom-call(bf16[1024,1024]{1,0:T(8,128)(2,1)} %get-tuple-element.181.refs_0_.g_ref, bf16[4,4,1,128,1024]{4,3,2,1,0:T(8,128)(2,1)} %collective-permute-done.6.refs_1_, ...), custom_call_target="tpu_custom_call" | custom-call | flops 4294967 | bytes 20971 | tf_op jit(solution)/shard_map/weight_keep/pallas_call | solution.py:1279
  278.7 9.1 %weight_send.5 = bf16[4,4,1,128,1024]{4,3,2,1,0:T(8,128)(2,1)} custom-call(bf16[1024,1024]{1,0:T(8,128)(2,1)} %get-tuple-element.192.refs_0_, bf16[1024,4096]{1,0:T(8,128)(2,1)} %get-tuple-element.197.refs_1_.g_ref.refs_2_), custom_call_target="tpu_custom_call" | custom-call | flops 4294967 | bytes 20971 | tf_op jit(solution)/shard_map/weight_send/pallas_call | solution.py:1235
  290.4 18.6 %first_back.1 = (f32[1024,1024]{1,0:T(8,128)}, bf16[1024,1024]{1,0:T(8,128)(2,1)}, f32[8,1024]{1,0:T(8,128)}) custom-call(s32[8]{0:T(128)} %fusion.32.order_ref, bf16[1024,4096]{1,0:T(8,128)(2,1)} %get-tuple-element.197.refs_1_.g_ref.refs_2_, bf16[4,4,128,1024]{3,2,1,0:T(8,128)(2,1)} %bitcast.139, bf16[4,4,128,1024]{3,2,1,0:T(8,128)(2,1)} %bitcast.141, ...), custom_call_target="tpu_custom_call" | custom-call | flops 8589934 | bytes 37748 | tf_op jit(solution)/shard_map/first_back/pallas_call | solution.py:1368
  320.9 10.6 %weight_keep.5 = (f32[2,2,1,128,1024]{4,3,2,1,0:T(8,128)}, bf16[2,2,1,128,1024]{4,3,2,1,0:T(8,128)(2,1)}, f32[2,2,1,128,1024]{4,3,2,1,0:T(8,128)}, bf16[2,2,1,128,1024]{4,3,2,1,0:T(8,128)(2,1)}) custom-call(bf16[1024,1024]{1,0:T(8,128)(2,1)} %get-tuple-element.192.refs_0_, bf16[4,4,1,128,1024]{4,3,2,1,0:T(8,128)(2,1)} %collective-permute-done.7.refs_1_, ...), custom_call_target="tpu_custom_call" | custom-call | flops 4294967 | bytes 20971 | tf_op jit(solution)/shard_map/weight_keep/pallas_call | solution.py:1279
  331.5 6.8 %grad_context.1.g_ref = bf16[1024,1024]{1,0:T(8,128)(2,1)} custom-call(bf16[1024,1024]{1,0:T(8,128)(2,1)} %get-tuple-element.200.g_ref.refs_1_, bf16[4,4,128,256]{3,2,1,0:T(8,128)(2,1)} %bitcast.151, bf16[4,4,128,256]{3,2,1,0:T(8,128)(2,1)} %bitcast.153, f32[1024,1024]{1,0:T(8,128)} %get-tuple-element.158.refs_0_.ctx_ref, ...), custom_call_target="tpu_custom_call" | custom-call | flops 2147483 | bytes 10485 | tf_op jit(solution)/shard_map/grad_context/pallas_call | solution.py:1409
  344.0 18.1 %attend_back.2 = (bf16[1024,512]{1,0:T(8,128)(2,1)}, bf16[1024,512]{1,0:T(8,128)(2,1)}, bf16[1024,512]{1,0:T(8,128)(2,1)}, f32[8,1024]{1,0:T(8,128)}) custom-call(s32[4]{0:T(128)} %iota_xor_fusion.order_ref, s32[2,4]{1,0:T(2,128)} %reduce_window_sum.11.refs_0_.ends_ref, bf16[3,1024,1024]{2,1,0:T(8,128)(2,1)} %qkv.1.refs_1_.refs_2_.refs_3_.q_ref.k_ref.v_ref, ...), custom_call_target="tpu_custom_call" | custom-call | flops 15000000 | bytes 52428 | tf_op jit(solution)/shard_map/attend_back/pallas_call | solution.py:939
  362.1 6.6 %weight_send.6 = bf16[4,2,4,128,256]{4,3,2,1,0:T(8,128)(2,1)} custom-call(bf16[1024,1024]{1,0:T(8,128)(2,1)} %get-tuple-element.226.x_ref.refs_0_, bf16[1024,1024]{1,0:T(8,128)(2,1)} %get-tuple-element.200.g_ref.refs_1_, bf16[1024,512]{1,0:T(8,128)(2,1)} %get-tuple-element.205.refs_2_.refs_3_.refs_0_, ...), custom_call_target="tpu_custom_call" | custom-call | flops 2147483 | bytes 20971 | tf_op jit(solution)/shard_map/weight_send/pallas_call | solution.py:1235
  382.0 18.0 %attend_back.3 = (bf16[1024,512]{1,0:T(8,128)(2,1)}, bf16[1024,512]{1,0:T(8,128)(2,1)}, bf16[1024,512]{1,0:T(8,128)(2,1)}, f32[8,1024]{1,0:T(8,128)}) custom-call(s32[4]{0:T(128)} %iota_xor_fusion.order_ref, s32[2,4]{1,0:T(2,128)} %reduce_window_sum.11.refs_0_.ends_ref, bf16[3,1024,1024]{2,1,0:T(8,128)(2,1)} %qkv.1.refs_1_.refs_2_.refs_3_.q_ref.k_ref.v_ref, ...), custom_call_target="tpu_custom_call" | custom-call | flops 15000000 | bytes 52428 | tf_op jit(solution)/shard_map/attend_back/pallas_call | solution.py:939
  404.0 6.6 %weight_send.7 = bf16[4,2,4,128,256]{4,3,2,1,0:T(8,128)(2,1)} custom-call(bf16[1024,1024]{1,0:T(8,128)(2,1)} %get-tuple-element.226.x_ref.refs_0_, bf16[1024,1024]{1,0:T(8,128)(2,1)} %get-tuple-element.200.g_ref.refs_1_, bf16[1024,512]{1,0:T(8,128)(2,1)} %get-tuple-element.230.refs_2_.refs_3_, bf16[1024,512]{1,0:T(8,128)(2,1)} %get-tuple-element.222.refs_3_.refs_4_, ...), custom_call_target="tpu_custom_call" | custom-call | flops 2147483 | bytes 20971 | tf_op jit(solution)/shard_map/weight_send/pallas_call | solution.py:1235
  422.0 7.4 %weight_keep.6 = (f32[2,1,4,128,256]{4,3,2,1,0:T(8,128)}, bf16[2,1,4,128,256]{4,3,2,1,0:T(8,128)(2,1)}, f32[2,1,4,128,256]{4,3,2,1,0:T(8,128)}, bf16[2,1,4,128,256]{4,3,2,1,0:T(8,128)(2,1)}) custom-call(bf16[1024,1024]{1,0:T(8,128)(2,1)} %get-tuple-element.226.x_ref.refs_0_, bf16[1024,1024]{1,0:T(8,128)(2,1)} %get-tuple-element.200.g_ref.refs_1_, ...), custom_call_target="tpu_custom_call" | custom-call | flops 2147483 | bytes 20971 | tf_op jit(solution)/shard_map/weight_keep/pallas_call | solution.py:1279
  431.5 7.8 %weight_keep.7 = (f32[2,1,4,128,256]{4,3,2,1,0:T(8,128)}, bf16[2,1,4,128,256]{4,3,2,1,0:T(8,128)(2,1)}, f32[2,1,4,128,256]{4,3,2,1,0:T(8,128)}, bf16[2,1,4,128,256]{4,3,2,1,0:T(8,128)(2,1)}) custom-call(bf16[1024,1024]{1,0:T(8,128)(2,1)} %get-tuple-element.226.x_ref.refs_0_, bf16[1024,1024]{1,0:T(8,128)(2,1)} %get-tuple-element.200.g_ref.refs_1_, ...), custom_call_target="tpu_custom_call" | custom-call | flops 2147483 | bytes 20971 | tf_op jit(solution)/shard_map/weight_keep/pallas_call | solution.py:1279
  445.0 12.8 %grad_input.1 = bf16[1024,1024]{1,0:T(8,128)(2,1)} custom-call(s32[8]{0:T(128)} %fusion.32.order_ref, bf16[1024,512]{1,0:T(8,128)(2,1)} %get-tuple-element.205.refs_2_.refs_3_.refs_0_, bf16[1024,512]{1,0:T(8,128)(2,1)} %get-tuple-element.206.refs_3_.refs_4_.refs_1_, bf16[1024,512]{1,0:T(8,128)(2,1)} %get-tuple-element.207.refs_4_.refs_5_.refs_2_, ...), custom_call_target="tpu_custom_call" | custom-call | flops 6442450 | bytes 20971 | tf_op jit(solution)/shard_map/grad_input/pallas_call | solution.py:1453
  458.9 51.1 %finale.1 = (bf16[4,1,128,1024]{3,2,1,0:T(8,128)(2,1)}, bf16[4,1,128,1024]{3,2,1,0:T(8,128)(2,1)}, bf16[4,1,128,1024]{3,2,1,0:T(8,128)(2,1)}, bf16[4,1,128,1024]...) custom-call(f32[1,128,1024]{2,1,0:T(8,128)} %fusion.15.down_sum, ...), custom_call_target="tpu_custom_call" | custom-call | tf_op jit(solution)/shard_map/finale/pallas_call | solution.py:634
  514.1 10.2 %place_grads.1 = (f32[1,1024,1024]{2,1,0:T(8,128)}, f32[3,1024,256]{2,1,0:T(8,128)}, f32[1024,1024]{1,0:T(8,128)}, f32[256,1024]{1,0:T(8,128)}) custom-call(s32[8]{0:T(128)} %fusion.32.order_ref, bf16[4,1,128,1024]{3,2,1,0:T(8,128)(2,1)} %get-tuple-element.248.refs_0_, bf16[4,1,128,1024]{3,2,1,0:T(8,128)(2,1)} %get-tuple-element.249.refs_1_, ...), custom_call_target="tpu_custom_call" | custom-call | tf_op jit(solution)/shard_map/place_grads/pallas_call | solution.py:1509
  (189 shorter events, 83.5 us)
Async XLA Ops:
  72.9 43.1 %collective-permute-start.1 = (bf16[4,1,128,1024]{3,2,1,0:T(8,128)(2,1)}, bf16[4,1,128,1024]{3,2,1,0:T(8,128)(2,1)S(1)}, u32[]{:S(2)}, u32[]{:S(2)}) collective-permute-start(bf16[4,1,128,1024]{3,2,1,0:T(8,128)(2,1)} %get-tuple-element.149.refs_9_), channel_id=1, source_target_pairs={{0,16},{4,20},{8,24},{12,28},{16,0},{20,4},{24,8},{28,12},{1,17},{... | collective-permute-start | bytes 3145736 | tf_op jit(solution)/shard_map/ppermute | solution.py:67
  74.4 41.6 %collective-permute-start = (bf16[4,1,128,1024]{3,2,1,0:T(8,128)(2,1)}, bf16[4,1,128,1024]{3,2,1,0:T(8,128)(2,1)S(1)}, u32[]{:S(2)}, u32[]{:S(2)}) collective-permute-start(bf16[4,1,128,1024]{3,2,1,0:T(8,128)(2,1)} %get-tuple-element.149.refs_9_), channel_id=1, source_target_pairs={{0,8},{4,12},{8,0},{12,4},{16,24},{20,28},{24,16},{28,20},{1,9},{5... | collective-permute-start | bytes 3145736 | tf_op jit(solution)/shard_map/ppermute | solution.py:67
  90.0 25.9 %collective-permute-start.4 = (bf16[2,1,128,1024]{3,2,1,0:T(8,128)(2,1)S(1)}, bf16[2,1,128,1024]{3,2,1,0:T(8,128)(2,1)}, u32[]{:S(2)}, u32[]{:S(2)}) collective-permute-start(bf16[2,1,128,1024]{3,2,1,0:T(8,128)(2,1)S(1)} %maximum_bitcast_fusion.refs_12_), channel_id=1, source_target_pairs={{0,16},{4,20},{8,24},{12,28},{16,0},{20,4},{24,8},{28,12},{1,17},{... | collective-permute-start | bytes 1572872 | tf_op jit(solution)/shard_map/ppermute | solution.py:67
  91.5 24.4 %collective-permute-start.3 = (bf16[2,1,128,1024]{3,2,1,0:T(8,128)(2,1)S(1)}, bf16[2,1,128,1024]{3,2,1,0:T(8,128)(2,1)}, u32[]{:S(2)}, u32[]{:S(2)}) collective-permute-start(bf16[2,1,128,1024]{3,2,1,0:T(8,128)(2,1)S(1)} %maximum_bitcast_fusion.refs_12_), channel_id=1, source_target_pairs={{0,8},{4,12},{8,0},{12,4},{16,24},{20,28},{24,16},{28,20},{1,9},{5... | collective-permute-start | bytes 1572872 | tf_op jit(solution)/shard_map/ppermute | solution.py:67
  92.1 78.5 %collective-permute-start.5 = (bf16[2,1,128,1024]{3,2,1,0:T(8,128)(2,1)S(1)}, bf16[2,1,128,1024]{3,2,1,0:T(8,128)(2,1)S(1)}, u32[]{:S(2)}, u32[]{:S(2)}) collective-permute-start(bf16[2,1,128,1024]{3,2,1,0:T(8,128)(2,1)S(1)} %maximum_bitcast_fusion.refs_12_), channel_id=1, source_target_pairs={{0,2},{1,3},{2,0},{3,1},{4,6},{5,7},{6,4},{7,5},{8,10},{9,11},{10,... | collective-permute-start | bytes 1572872 | tf_op jit(solution)/shard_map/ppermute | solution.py:61
  250.5 17.4 %collective-permute-start.6 = (bf16[4,4,1,128,1024]{4,3,2,1,0:T(8,128)(2,1)}, bf16[4,4,1,128,1024]{4,3,2,1,0:T(8,128)(2,1)}, u32[]{:S(2)}, u32[]{:S(2)}) collective-permute-start(bf16[4,4,1,128,1024]{4,3,2,1,0:T(8,128)(2,1)} %weight_send.4), channel_id=1, source_target_pairs={{0,4},{4,0},{8,12},{12,8},{16,20},{20,16},{24,28},{28,24},{1,5},{5... | collective-permute-start | bytes 12582920 | tf_op jit(solution)/shard_map/ppermute | solution.py:61
  287.8 33.1 %collective-permute-start.7 = (bf16[4,4,1,128,1024]{4,3,2,1,0:T(8,128)(2,1)}, bf16[4,4,1,128,1024]{4,3,2,1,0:T(8,128)(2,1)}, u32[]{:S(2)}, u32[]{:S(2)}) collective-permute-start(bf16[4,4,1,128,1024]{4,3,2,1,0:T(8,128)(2,1)} %weight_send.5), channel_id=1, source_target_pairs={{0,4},{4,0},{8,12},{12,8},{16,20},{20,16},{24,28},{28,24},{1,5},{5... | collective-permute-start | bytes 12582920 | tf_op jit(solution)/shard_map/ppermute | solution.py:61
  288.3 25.3 %collective-permute-start.9 = (bf16[2,2,1,128,1024]{4,3,1,2,0:T(8,128)(2,1)}, bf16[2,2,1,128,1024]{4,3,1,2,0:T(8,128)(2,1)S(1)}, u32[]{:S(2)}, u32[]{:S(2)}) collective-permute-start(bf16[2,2,1,128,1024]{4,3,1,2,0:T(8,128)(2,1)} %bitcast.22), channel_id=1, source_target_pairs={{0,8},{4,12},{8,0},{12,4},{16,24},{20,28},{24,16},{28,20},{1,9},{5... | collective-permute-start | bytes 3145736 | tf_op jit(solution)/shard_map/ppermute | solution.py:61
  288.9 25.1 %collective-permute-start.8 = (bf16[2,2,1,128,1024]{4,3,1,2,0:T(8,128)(2,1)}, bf16[2,2,1,128,1024]{4,3,1,2,0:T(8,128)(2,1)}, u32[]{:S(2)}, u32[]{:S(2)}) collective-permute-start(bf16[2,2,1,128,1024]{4,3,1,2,0:T(8,128)(2,1)} %bitcast.19), channel_id=1, source_target_pairs={{0,16},{4,20},{8,24},{12,28},{16,0},{20,4},{24,8},{28,12},{1,17},{... | collective-permute-start | bytes 3145736 | tf_op jit(solution)/shard_map/ppermute | solution.py:61
  318.9 19.5 %collective-permute-start.11 = (bf16[2,1,128,1024]{3,2,0,1:T(8,128)(2,1)}, bf16[2,1,128,1024]{3,2,0,1:T(8,128)(2,1)S(1)}, u32[]{:S(2)}, u32[]{:S(2)}) collective-permute-start(bf16[2,1,128,1024]{3,2,0,1:T(8,128)(2,1)} %get-tuple-element.268), channel_id=1, source_target_pairs={{0,16},{4,20},{8,24},{12,28},{16,0},{20,4},{24,8},{28,12},{1,17},{... | collective-permute-start | bytes 1572872 | tf_op jit(solution)/shard_map/ppermute | solution.py:61
  320.3 20.8 %collective-permute-start.10 = (bf16[2,1,128,1024]{3,2,0,1:T(8,128)(2,1)S(1)}, bf16[2,1,128,1024]{3,2,0,1:T(8,128)(2,1)S(1)}, u32[]{:S(2)}, u32[]{:S(2)}) collective-permute-start(bf16[2,1,128,1024]{3,2,0,1:T(8,128)(2,1)S(1)} %get-tuple-element.267), channel_id=1, source_target_pairs={{0,8},{4,12},{8,0},{12,4},{16,24},{20,28},{24,16},{28,20},{1,9},{5... | collective-permute-start | bytes 1572872 | tf_op jit(solution)/shard_map/ppermute | solution.py:61
  338.3 34.4 %collective-permute-start.13 = (bf16[2,2,1,128,1024]{4,3,1,2,0:T(8,128)(2,1)}, bf16[2,2,1,128,1024]{4,3,1,2,0:T(8,128)(2,1)}, u32[]{:S(2)}, u32[]{:S(2)}) collective-permute-start(bf16[2,2,1,128,1024]{4,3,1,2,0:T(8,128)(2,1)} %bitcast.173), channel_id=1, source_target_pairs={{0,8},{4,12},{8,0},{12,4},{16,24},{20,28},{24,16},{28,20},{1,9},{5... | collective-permute-start | bytes 3145736 | tf_op jit(solution)/shard_map/ppermute | solution.py:61
  341.2 27.5 %collective-permute-start.14 = (bf16[1,1,128,1024]{3,2,1,0:T(8,128)(2,1)S(1)}, bf16[1,1,128,1024]{3,2,1,0:T(8,128)(2,1)}, u32[]{:S(2)}, u32[]{:S(2)}) collective-permute-start(bf16[1,1,128,1024]{3,2,1,0:T(8,128)(2,1)S(1)} %fusion.21), channel_id=1, source_target_pairs={{0,1},{1,0},{2,3},{3,2},{4,5},{5,4},{6,7},{7,6},{8,9},{9,8},{10,11... | collective-permute-start | bytes 786440 | tf_op jit(solution)/shard_map/ppermute | solution.py:61
  342.1 34.0 %collective-permute-start.12 = (bf16[2,2,1,128,1024]{4,3,1,2,0:T(8,128)(2,1)}, bf16[2,2,1,128,1024]{4,3,1,2,0:T(8,128)(2,1)}, u32[]{:S(2)}, u32[]{:S(2)}) collective-permute-start(bf16[2,2,1,128,1024]{4,3,1,2,0:T(8,128)(2,1)} %bitcast.31), channel_id=1, source_target_pairs={{0,16},{4,20},{8,24},{12,28},{16,0},{20,4},{24,8},{28,12},{1,17},{... | collective-permute-start | bytes 3145736 | tf_op jit(solution)/shard_map/ppermute | solution.py:61
  368.7 53.3 %collective-permute-start.18 = (bf16[4,2,4,128,256]{4,3,2,1,0:T(8,128)(2,1)}, bf16[4,2,4,128,256]{4,3,2,1,0:T(8,128)(2,1)}, u32[]{:S(2)}, u32[]{:S(2)}) collective-permute-start(bf16[4,2,4,128,256]{4,3,2,1,0:T(8,128)(2,1)} %weight_send.6), channel_id=1, source_target_pairs={{0,4},{4,0},{8,12},{12,8},{16,20},{20,16},{24,28},{28,24},{1,5},{5... | collective-permute-start | bytes 6291464 | tf_op jit(solution)/shard_map/ppermute | solution.py:61
  370.4 29.6 %collective-permute-start.17 = (bf16[1,128,1024]{2,1,0:T(8,128)(2,1)}, bf16[1,128,1024]{2,1,0:T(8,128)(2,1)S(1)}, u32[]{:S(2)}, u32[]{:S(2)}) collective-permute-start(bf16[1,128,1024]{2,1,0:T(8,128)(2,1)} %fusion.22), channel_id=1, source_target_pairs={{0,2},{1,3},{2,0},{3,1},{4,6},{5,7},{6,4},{7,5},{8,10},{9,11},{10,... | collective-permute-start | bytes 786440 | tf_op jit(solution)/shard_map/ppermute | solution.py:61
  376.1 24.0 %collective-permute-start.16 = (bf16[2,1,128,1024]{3,2,0,1:T(8,128)(2,1)}, bf16[2,1,128,1024]{3,2,0,1:T(8,128)(2,1)S(1)}, u32[]{:S(2)}, u32[]{:S(2)}) collective-permute-start(bf16[2,1,128,1024]{3,2,0,1:T(8,128)(2,1)} %fusion.11), channel_id=1, source_target_pairs={{0,16},{4,20},{8,24},{12,28},{16,0},{20,4},{24,8},{28,12},{1,17},{... | collective-permute-start | bytes 1572872 | tf_op jit(solution)/shard_map/ppermute | solution.py:61
  381.4 18.8 %collective-permute-start.15 = (bf16[2,1,128,1024]{3,2,0,1:T(8,128)(2,1)}, bf16[2,1,128,1024]{3,2,0,1:T(8,128)(2,1)}, u32[]{:S(2)}, u32[]{:S(2)}) collective-permute-start(bf16[2,1,128,1024]{3,2,0,1:T(8,128)(2,1)} %fusion.10), channel_id=1, source_target_pairs={{0,8},{4,12},{8,0},{12,4},{16,24},{20,28},{24,16},{28,20},{1,9},{5... | collective-permute-start | bytes 1572872 | tf_op jit(solution)/shard_map/ppermute | solution.py:61
  410.6 20.9 %collective-permute-start.19 = (bf16[4,2,4,128,256]{4,3,2,1,0:T(8,128)(2,1)}, bf16[4,2,4,128,256]{4,3,2,1,0:T(8,128)(2,1)}, u32[]{:S(2)}, u32[]{:S(2)}) collective-permute-start(bf16[4,2,4,128,256]{4,3,2,1,0:T(8,128)(2,1)} %weight_send.7), channel_id=1, source_target_pairs={{0,4},{4,0},{8,12},{12,8},{16,20},{20,16},{24,28},{28,24},{1,5},{5... | collective-permute-start | bytes 6291464 | tf_op jit(solution)/shard_map/ppermute | solution.py:61
  411.3 19.6 %collective-permute-start.20 = (bf16[1,1,128,1024]{3,2,1,0:T(8,128)(2,1)S(1)}, bf16[1,1,128,1024]{3,2,1,0:T(8,128)(2,1)S(1)}, u32[]{:S(2)}, u32[]{:S(2)}) collective-permute-start(bf16[1,1,128,1024]{3,2,1,0:T(8,128)(2,1)S(1)} %fusion.24), channel_id=1, source_target_pairs={{0,1},{1,0},{2,3},{3,2},{4,5},{5,4},{6,7},{7,6},{8,9},{9,8},{10,11... | collective-permute-start | bytes 786440 | tf_op jit(solution)/shard_map/ppermute | solution.py:61
  419.8 22.3 %collective-permute-start.22 = (bf16[1,1,128,1024]{3,2,1,0:T(8,128)(2,1)}, bf16[1,1,128,1024]{3,2,1,0:T(8,128)(2,1)S(1)}, u32[]{:S(2)}, u32[]{:S(2)}) collective-permute-start(bf16[1,1,128,1024]{3,2,1,0:T(8,128)(2,1)} %fusion.23), channel_id=1, source_target_pairs={{0,1},{1,0},{2,3},{3,2},{4,5},{5,4},{6,7},{7,6},{8,9},{9,8},{10,11... | collective-permute-start | bytes 786440 | tf_op jit(solution)/shard_map/ppermute | solution.py:61
  429.5 28.4 %collective-permute-start.24 = (bf16[2,1,4,128,256]{4,3,2,1,0:T(8,128)(2,1)}, bf16[2,1,4,128,256]{4,3,2,1,0:T(8,128)(2,1)S(1)}, u32[]{:S(2)}, u32[]{:S(2)}) collective-permute-start(bf16[2,1,4,128,256]{4,3,2,1,0:T(8,128)(2,1)} %get-tuple-element.225), channel_id=1, source_target_pairs={{0,16},{4,20},{8,24},{12,28},{16,0},{20,4},{24,8},{28,12},{1,17},{... | collective-permute-start | bytes 1572872 | tf_op jit(solution)/shard_map/ppermute | solution.py:61
  430.9 26.9 %collective-permute-start.25 = (bf16[2,1,4,128,256]{4,3,2,1,0:T(8,128)(2,1)}, bf16[2,1,4,128,256]{4,3,2,1,0:T(8,128)(2,1)S(1)}, u32[]{:S(2)}, u32[]{:S(2)}) collective-permute-start(bf16[2,1,4,128,256]{4,3,2,1,0:T(8,128)(2,1)} %get-tuple-element.238), channel_id=1, source_target_pairs={{0,8},{4,12},{8,0},{12,4},{16,24},{20,28},{24,16},{28,20},{1,9},{5... | collective-permute-start | bytes 1572872 | tf_op jit(solution)/shard_map/ppermute | solution.py:61
  439.3 18.6 %collective-permute-start.27 = (bf16[2,1,4,128,256]{4,3,2,1,0:T(8,128)(2,1)}, bf16[2,1,4,128,256]{4,3,2,1,0:T(8,128)(2,1)}, u32[]{:S(2)}, u32[]{:S(2)}) collective-permute-start(bf16[2,1,4,128,256]{4,3,2,1,0:T(8,128)(2,1)} %get-tuple-element.228), channel_id=1, source_target_pairs={{0,8},{4,12},{8,0},{12,4},{16,24},{20,28},{24,16},{28,20},{1,9},{5... | collective-permute-start | bytes 1572872 | tf_op jit(solution)/shard_map/ppermute | solution.py:61
  (39 other events, 377.6 us)

commit v5 on v4

--- a/solution.py
+++ b/solution.py
@@ -123,9 +123,9 @@
     last = bits_of("tensor") - 1
     for bit in range(last):
         pairs = [values.reshape((-1, 2) + values.shape[1:]) for values in sides]
-        sends = [low(values[:, 1]) for values in pairs]
-        token = yield sends
-        others = [swap(send, "tensor", bit, token) for send in sends]
+        send = jnp.concatenate([low(values[:, 1]) for values in pairs])
+        token = yield [send]
+        others = jnp.split(swap(send, "tensor", bit, token), 2)
         sides = [values[:, 0] + other.astype(F32) for values, other in zip(pairs, others)]
     send = low(sides[1][0])
     token = yield [send]
@@ -805,7 +805,7 @@
     def _():
         peak_ref[...] = jnp.zeros_like(peak_ref) if skip == 0 else refs[1][...]
 
-    rows = 256
+    rows = SEQ
     lanes = lax.broadcasted_iota(jnp.int32, (rows, LANES), 1)
     for start in range(0, SEQ, rows):
         here = pl.ds(start, rows)
@@ -893,25 +893,26 @@
 
     lanes = lax.broadcasted_iota(jnp.int32, (SEQ, LANES), 1)
     q, k, v, g = q_ref[...], k_ref[...], v_ref[...], g_ref[...]
-    q_sums, k_sums, v_sums = [], [], []
-    for head in range(LANES // HD):
+    heads, zero = LANES // HD, jnp.zeros((SEQ, LANES), BF16)
+    probs, grad_scores = [], []
+    for head in range(heads):
         own = lanes // HD == head
-        zero = jnp.zeros_like(q)
         q_own = jnp.where(own, q * jnp.asarray(factor, BF16), zero)
         g_own = jnp.where(own, g, zero)
-        logsum = lse_ref[pl.ds((pair + first // LANES) * (LANES // HD) + head, 1), :]
-        probs = jnp.exp(dot_cols(k, q_own) + mask_ref[...] - logsum)
-        v_sums.append(dot(low(probs), g))
+        logsum = lse_ref[pl.ds((pair + first // LANES) * heads + head, 1), :]
+        prob = jnp.exp(dot_cols(k, q_own) + mask_ref[...] - logsum)
         grad_probs = dot_cols(v, g_own)
-        mean_grad = jnp.sum(probs * grad_probs, axis=0, keepdims=True)
-        grad_scores = low(factor * probs * (grad_probs - mean_grad))
-        k_sums.append(dot(grad_scores, q))
-        q_sums.append(dot_rows(grad_scores, k))
+        mean_grad = jnp.sum(prob * grad_probs, axis=0, keepdims=True)
+        probs.append(low(prob))
+        grad_scores.append(low(factor * prob * (grad_probs - mean_grad)))
+    v_sums = dot(jnp.concatenate(probs, axis=0), g)
+    k_sums = dot(jnp.concatenate(grad_scores, axis=0), q)
+    q_sums = dot_rows(jnp.concatenate(grad_scores, axis=1), k)
 
     def join(parts):
-        joined = parts[0]
-        for head in range(1, LANES // HD):
-            joined = jnp.where(lanes // HD == head, parts[head], joined)
+        joined = parts[:SEQ]
+        for head in range(1, heads):
+            joined = jnp.where(lanes // HD == head, parts[head * SEQ : (head + 1) * SEQ], joined)
         return low(joined)
 
     dq, dv = join(q_sums), join(v_sums)
@@ -1134,14 +1135,12 @@
 
 
 def second_norm_kernel(
-    order_ref, act_ref, slope_ref, level_ref, near_a, far_a, near_b, far_b, normed_ref, grad_ref, row_ref,
-    quant_ref, back_ref, out_ref, sum_ref, branch_ref, terms_ref
+    order_ref, act_ref, level_ref, near_a, far_a, near_b, far_b, normed_ref, grad_ref, row_ref,
+    quant_ref, out_ref, sum_ref, branch_ref, terms_ref
 ):
     level = level_ref[3:4, 0:1]
-    tangent = jnp.tanh(act_ref[...] / level)
-    quant = low(level * tangent)
+    quant = low(level * jnp.tanh(act_ref[...] / level))
     quant_ref[...] = quant
-    back_ref[...] = (1.0 - tangent * tangent) * slope_ref[...]
     vectors = take_blocks(row_ref, order_ref)
     summed = normed_ref[...] + project(quant, near_a, far_a, near_b, far_b) + vectors[3:4, :]
     normal, inverse = norm_parts(summed)
@@ -1154,7 +1153,7 @@
     add_sums(terms_ref, order_ref, (grad_sum, upstream * normal, upstream))
 
 
-def second_norm(active, slope, level, weights, normed, grad, vectors, order):
+def second_norm(active, level, weights, normed, grad, vectors, order):
     tokens, width = normed.shape
     inner = active.shape[1]
     rows = 256
@@ -1167,7 +1166,6 @@
         grid=(tokens // rows,),
         in_specs=[
             in_smem(),
-            block(inner),
             block(inner),
             whole(level),
             *[whole(side) for side in weights],
@@ -1177,7 +1175,6 @@
         ],
         out_specs=[
             block(inner),
-            block(inner),
             block(width),
             block(width),
             block(width),
@@ -1185,7 +1182,6 @@
         ],
         out_shape=[
             shape_of((tokens, inner), BF16),
-            shape_of((tokens, inner), F32),
             shape_of((tokens, width), BF16),
             shape_of((tokens, width), F32),
             shape_of((tokens, width), BF16),
@@ -1194,7 +1190,7 @@
         compiler_params=params(),
         cost_estimate=cost(2 * tokens * width * inner, 80 * MIB),
         name="second_norm",
-    )(order, active, slope, level, *weights, normed, grad, vectors)
+    )(order, active, level, *weights, normed, grad, vectors)
 
 
 def weight_specs(xs, products, parts, plane, c):
@@ -1292,10 +1288,13 @@
     return [keep_a, keep_b], [send_a, send_b]
 
 
-def grad_hidden_kernel(cuts, order_ref, g_ref, near_a, far_a, near_b, far_b, back_ref, o_ref, sum_ref):
+def grad_hidden_kernel(
+    cuts, order_ref, g_ref, near_a, far_a, near_b, far_b, act_ref, slope_ref, level_ref, o_ref, sum_ref
+):
     half = g_ref.shape[1] // 2
     block = pl.program_id(0)
-    columns = back_ref.shape[1]
+    columns = act_ref.shape[1]
+    level = level_ref[3:4, 0:1]
 
     @pl.when(block == 0)
     def _():
@@ -1306,14 +1305,15 @@
         @pl.when(block * 2 // pl.num_programs(0) == side)
         def _(near_ref=near_ref, far_ref=far_ref):
             grad = dot(g_ref[:, :half], flat(near_ref[...])) + dot(g_ref[:, half:], flat(far_ref[...]))
-            grad = low(grad * back_ref[...])
+            tangent = jnp.tanh(act_ref[...] / level)
+            grad = low(grad * ((1.0 - tangent * tangent) * slope_ref[...]))
             o_ref[...] = grad
             total = jnp.sum(grad.astype(F32), axis=0, keepdims=True)
             start = pl.multiple_of((block % cuts) * columns, LANES)
             sum_ref[pl.ds(order_ref[block // cuts], 1), pl.ds(start, columns)] = total
 
 
-def grad_hidden_rows(grad, weights, back, part_order):
+def grad_hidden_rows(grad, weights, active, slope, level, part_order):
     plane, half, rows, c = weights[0].shape
     parts = 2 * half
     tokens, width = grad.shape
@@ -1332,13 +1332,13 @@
     return pl.pallas_call(
         partial(grad_hidden_kernel, cuts),
         grid=(parts * cuts,),
-        in_specs=[in_smem(), whole(grad), first, first, last, last, block],
+        in_specs=[in_smem(), whole(grad), first, first, last, last, block, block, whole(level)],
         out_specs=[block, pl.BlockSpec((parts, c), lambda s: (0, 0))],
         out_shape=[shape_of((tokens, parts * c), BF16), shape_of((parts, c), F32)],
         compiler_params=params(),
         cost_estimate=cost(2 * tokens * width * parts * c, 34 * MIB),
         name="grad_hidden",
-    )(part_order, grad, *weights, back)
+    )(part_order, grad, *weights, active, slope, level)
 
 
 def first_back_kernel(
@@ -1635,15 +1635,17 @@
         normed, levels, weights_in, bias_hidden, held_b, ranges
     )
     weights_down = [side[:, :, 0] for side in (near_a, far_a, near_b, far_b)]
-    quant_active, back, output, grad_sum_two, grad_branch, terms_two = second_norm(
-        active, slope, levels, weights_down, normed, upstream, vectors, order
+    quant_active, output, grad_sum_two, grad_branch, terms_two = second_norm(
+        active, levels, weights_down, normed, upstream, vectors, order
     )
 
     wide = b_in.shape[0]
     other = weight_send([grad_branch], [(0, quant_active, 0)], parts, plane, wide)
     grad_after = tie(grad_branch, [other])
     other = swap(other, "dp", 0)
-    grad_hidden, sum_hidden = grad_hidden_rows(grad_after, weights_down, back, part_order)
+    grad_hidden, sum_hidden = grad_hidden_rows(
+        grad_after, weights_down, active, slope, levels, part_order
+    )
     down = scatter_grad(
         scatter_all, [grad_branch], [(0, quant_active, 0)], other, sum_hidden, parts, plane, wide
     )

time: 533 us -> 515 us (0.966)
  Pallas kernels: 439 us -> 428 us
    pallas_call x1, Pallas kernels: 31 us -> 22 us  [second_norm(): pl.pallas_call(second_norm_kernel, grid=(tokens // rows,), in_specs=[in_s...]
    ppermute x24 -> x22, starting transfers between devices: 22.6 us -> 19.1 us  [swap(): lax.ppermute(values, axis, [(i, i ^ 1 << bit) for i in range(count)])]
    unnamed x76 -> x84, local copies, waits for them, and re-layouts: 13.1 us -> 14.2 us
    ppermute x24 -> x22, waiting for transfers between devices: 11.5 us -> 11.2 us  [swap(): lax.ppermute(values, axis, [(i, i ^ 1 << bit) for i in range(count)])]
  transfers between devices with their start and end apart: 28 -> 26, of which waited for: 3 -> 3; matrix products, arithmetic and copies ran while one was open for 5% -> 4% of each run, Pallas kernels for 41% -> 42%
where the time goes in v5:
time: 515 us; the launch traced here: 507 us
  Pallas kernels  428 us (83%)
  local copies, waits for them, and re-layouts  27.4 us (5%)
  starting transfers between devices  23.2 us (5%)
  other arithmetic  15.9 us (3%)
  waiting for transfers between devices  11.2 us (2%)
    pallas_call x3, Pallas kernels, run(): results = call(*args, ranges, levels, *sources)  90.6 us
    pallas_call x1, Pallas kernels, finale(): pl.pallas_call(finale_kernel, in_specs=[vmem] * len(args), out_specs=[any...  51.6 us
    pallas_call x1, Pallas kernels, first_gather(): pl.pallas_call(first_gather_kernel, in_specs=[pl.BlockSpec(memory_space=p...  46.4 us
    pallas_call x4, Pallas kernels, weight_keep(): pl.pallas_call(partial(weight_keep_kernel, len(xs), which, first_split(bi...  36.2 us
    pallas_call x2, Pallas kernels, attend_back(): pl.pallas_call(partial(attend_back_kernel, c, first), grid=(held, width /...  34.4 us
    pallas_call x4, Pallas kernels, weight_send(): pl.pallas_call(partial(weight_send_kernel, len(xs), [product[0] for produ...  31.8 us
    pallas_call x1, Pallas kernels, second_norm(): pl.pallas_call(second_norm_kernel, grid=(tokens // rows,), in_specs=[in_s...  22 us
    pallas_call x1, Pallas kernels, grad_hidden_rows(): pl.pallas_call(partial(grad_hidden_kernel, cuts), grid=(parts * cuts,), i...  21.2 us
  transfers between devices with their start and end apart: 26, of which 3 were waited for; matrix products, arithmetic and copies ran while one was open for 4% of the time, Pallas kernels for 42%

profile of v5, /device:TPU:0, one launch (start us, length us, event | category | flops | bytes accessed | tf_op | source)
XLA Modules:
  0.0 507.2 jit_solution(5745544812477591641)
XLA Ops:
  8.7 17.2 %prepare.1 = (f32[8,128]{1,0:T(8,128)}, bf16[1024,1024]{1,0:T(8,128)(2,1)}, bf16[3,128,256]{2,1,0:T(8,128)(2,1)}, bf16[1,128,256]{2,1,0:T(8,128)(2,1)}, bf16[1,1...) custom-call(f32[4]{0:T(128)} %refs_5_.1, ...), custom_call_target="tpu_custom_call" | custom-call | tf_op jit(solution)/shard_map/prepare/pallas_call | solution.py:738
  25.8 46.4 %first_gather.1 = (bf16[4,4,3,128,256]{4,3,2,1,0:T(8,128)(2,1)}, bf16[4,4,3,128,256]{4,3,2,1,0:T(8,128)(2,1)}, bf16[4,16,128]{2,1,0:T(8,128)(2,1)}, bf16[4,4,1,1...) custom-call(bf16[3,128,256]{2,1,0:T(8,128)(2,1)} %get-tuple-element.135.first_ref, ...), custom_call_target="tpu_custom_call" | custom-call | tf_op jit(solution)/shard_map/first_gather/pallas_call | solution.py:490
  75.9 14.1 %qkv.1.refs_1_.refs_2_.refs_3_.q_ref.k_ref.v_ref = bf16[3,1024,1024]{2,1,0:T(8,128)(2,1)} custom-call(bf16[1024,1024]{1,0:T(8,128)(2,1)} %get-tuple-element.222.x_ref.refs_0_, bf16[4,4,3,128,256]{4,3,2,1,0:T(8,128)(2,1)} %get-tuple-element.138.near_ref.refs_6_, bf16[4,4,3,128,256]{4,3,2,1,0:T(8,128)(2,1)} %get-tuple-element.139.far_ref.refs_7_, ...), custom_call_target="tpu_custom_call" | custom-call | flops 6442450 | bytes 14680 | tf_op jit(solution)/shard_map/qkv/pallas_call | solution.py:761
  97.3 13.7 %attend.2 = (f32[1024,1024]{1,0:T(8,128)}, f32[2,128,512]{2,1,0:T(8,128)}, f32[8,128]{1,0:T(8,128)}) custom-call(s32[2,4]{1,0:T(2,128)} %reduce_window_sum.11.refs_0_.ends_ref, bf16[3,1024,1024]{2,1,0:T(8,128)(2,1)} %qkv.1.refs_1_.refs_2_.refs_3_.q_ref.k_ref.v_ref, bf16[3,1024,1024]{2,1,0:T(8,128)(2,1)} %qkv.1.refs_1_.refs_2_.refs_3_.q_ref.k_ref.v_ref, ...), custom_call_target="tpu_custom_call" | custom-call | flops 15000000 | bytes 41943 | tf_op jit(solution)/shard_map/attend/pallas_call | solution.py:870
  112.9 32.1 %attend.3 = (f32[1024,1024]{1,0:T(8,128)}, f32[2,128,512]{2,1,0:T(8,128)}, f32[8,128]{1,0:T(8,128)}, f32[8,128]{1,0:T(8,128)}, bf16[4,4,1,128,1024]{4,3,2,1,0:T(...) custom-call(s32[2,4]{1,0:T(2,128)} %reduce_window_sum.11.refs_0_.end, ...), custom_call_target="tpu_custom_call", output_to_operand_aliasing={{0}: (6, {})} | custom-call | flops 15000000 | bytes 41943 | tf_op jit(solution)/shard_map/attend/pallas_call | solution.py:414
  145.1 19.4 %first_norm.1 = (bf16[1024,1024]{1,0:T(8,128)(2,1)}, f32[1024,1024]{1,0:T(8,128)}, f32[1024,1024]{1,0:T(8,128)}, f32[1024,1]{1,0:T(8,128)}, f32[8,128]{1,0:T(8,128)}, /*index=5*/f32[8,128]{1,0:T(8,128)}) custom-call(f32[1024,1024]{1,0:T(8,128)} %get-tuple-element.155.refs_0_.ctx_ref, f32[8,128]{1,0:T(8,128)} %get-tuple-element.156.refs_1_.refs_7_, ...), custom_call_target="tpu_custom_call" | custom-call | flops 2147483 | bytes 20971 | tf_op jit(solution)/shard_map/first_norm/pallas_call | solution.py:414
  165.3 39.1 %hidden.1 = (bf16[1024,1024]{1,0:T(8,128)(2,1)}, f32[1024,4096]{1,0:T(8,128)}, f32[1024,4096]{1,0:T(8,128)}, f32[8,128]{1,0:T(8,128)}, f32[8,128]{1,0:T(8,128)},...) custom-call(f32[1024,1024]{1,0:T(8,128)} %get-tuple-element.159.refs_0_.normed_ref, ...), custom_call_target="tpu_custom_call" | custom-call | flops 8589934 | bytes 52428 | tf_op jit(solution)/shard_map/hidden/pallas_call | solution.py:414
  204.4 22.0 %second_norm.1 = (bf16[1024,4096]{1,0:T(8,128)(2,1)}, bf16[1024,1024]{1,0:T(8,128)(2,1)}, f32[1024,1024]{1,0:T(8,128)}, bf16[1024,1024]{1,0:T(8,128)(2,1)}, f32[8,1024]{1,0:T(8,128)}) custom-call(s32[8]{0:T(128)} %fusion.32.order_ref, f32[1024,4096]{1,0:T(8,128)} %get-tuple-element.164.act_ref, f32[8,128]{1,0:T(8,128)} %get-tuple-element.165.level_ref.refs_10_, ...), custom_call_target="tpu_custom_call" | custom-call | flops 8589934 | bytes 83886 | tf_op jit(solution)/shard_map/second_norm/pallas_call | solution.py:1164
  226.4 9.1 %weight_send.4 = bf16[4,4,1,128,1024]{4,3,2,1,0:T(8,128)(2,1)} custom-call(bf16[1024,1024]{1,0:T(8,128)(2,1)} %get-tuple-element.177.refs_0_.g_ref, bf16[1024,4096]{1,0:T(8,128)(2,1)} %get-tuple-element.172.refs_1_.refs_2_), custom_call_target="tpu_custom_call" | custom-call | flops 4294967 | bytes 20971 | tf_op jit(solution)/shard_map/weight_send/pallas_call | solution.py:1231
  236.0 21.2 %grad_hidden.1 = (bf16[1024,4096]{1,0:T(8,128)(2,1)}, f32[4,1024]{1,0:T(4,128)}) custom-call(s32[4]{0:T(128)} %iota_xor_fusion.order_ref, bf16[1024,1024]{1,0:T(8,128)(2,1)} %get-tuple-element.177.refs_0_.g_ref, bf16[4,2,128,1024]{3,2,1,0:T(8,128)(2,1)} %bitcast.143, bf16[4,2,128,1024]{3,2,1,0:T(8,128)(2,1)} %bitcast.145, ...), custom_call_target="tpu_custom_call" | custom-call | flops 8589934 | bytes 35651 | tf_op jit(solution)/shard_map/grad_hidden/pallas_call | solution.py:1332
  257.3 10.6 %weight_keep.4 = (f32[2,2,1,128,1024]{4,3,2,1,0:T(8,128)}, bf16[2,2,1,128,1024]{4,3,2,1,0:T(8,128)(2,1)}, f32[2,2,1,128,1024]{4,3,2,1,0:T(8,128)}, bf16[2,2,1,128,1024]{4,3,2,1,0:T(8,128)(2,1)}) custom-call(bf16[1024,1024]{1,0:T(8,128)(2,1)} %get-tuple-element.177.refs_0_.g_ref, bf16[4,4,1,128,1024]{4,3,2,1,0:T(8,128)(2,1)} %collective-permute-done.6.refs_1_, ...), custom_call_target="tpu_custom_call" | custom-call | flops 4294967 | bytes 20971 | tf_op jit(solution)/shard_map/weight_keep/pallas_call | solution.py:1275
  267.9 9.2 %weight_send.5 = bf16[4,4,1,128,1024]{4,3,2,1,0:T(8,128)(2,1)} custom-call(bf16[1024,1024]{1,0:T(8,128)(2,1)} %get-tuple-element.188.refs_0_, bf16[1024,4096]{1,0:T(8,128)(2,1)} %get-tuple-element.193.refs_1_.g_ref.refs_2_), custom_call_target="tpu_custom_call" | custom-call | flops 4294967 | bytes 20971 | tf_op jit(solution)/shard_map/weight_send/pallas_call | solution.py:1231
  279.7 18.7 %first_back.1 = (f32[1024,1024]{1,0:T(8,128)}, bf16[1024,1024]{1,0:T(8,128)(2,1)}, f32[8,1024]{1,0:T(8,128)}) custom-call(s32[8]{0:T(128)} %fusion.32.order_ref, bf16[1024,4096]{1,0:T(8,128)(2,1)} %get-tuple-element.193.refs_1_.g_ref.refs_2_, bf16[4,4,128,1024]{3,2,1,0:T(8,128)(2,1)} %bitcast.139, bf16[4,4,128,1024]{3,2,1,0:T(8,128)(2,1)} %bitcast.141, ...), custom_call_target="tpu_custom_call" | custom-call | flops 8589934 | bytes 37748 | tf_op jit(solution)/shard_map/first_back/pallas_call | solution.py:1368
  312.1 10.7 %weight_keep.5 = (f32[2,2,1,128,1024]{4,3,2,1,0:T(8,128)}, bf16[2,2,1,128,1024]{4,3,2,1,0:T(8,128)(2,1)}, f32[2,2,1,128,1024]{4,3,2,1,0:T(8,128)}, bf16[2,2,1,128,1024]{4,3,2,1,0:T(8,128)(2,1)}) custom-call(bf16[1024,1024]{1,0:T(8,128)(2,1)} %get-tuple-element.188.refs_0_, bf16[4,4,1,128,1024]{4,3,2,1,0:T(8,128)(2,1)} %collective-permute-done.7.refs_1_, ...), custom_call_target="tpu_custom_call" | custom-call | flops 4294967 | bytes 20971 | tf_op jit(solution)/shard_map/weight_keep/pallas_call | solution.py:1275
  322.7 6.8 %grad_context.1.g_ref = bf16[1024,1024]{1,0:T(8,128)(2,1)} custom-call(bf16[1024,1024]{1,0:T(8,128)(2,1)} %get-tuple-element.196.g_ref.refs_1_, bf16[4,4,128,256]{3,2,1,0:T(8,128)(2,1)} %bitcast.151, bf16[4,4,128,256]{3,2,1,0:T(8,128)(2,1)} %bitcast.153, f32[1024,1024]{1,0:T(8,128)} %get-tuple-element.155.refs_0_.ctx_ref, ...), custom_call_target="tpu_custom_call" | custom-call | flops 2147483 | bytes 10485 | tf_op jit(solution)/shard_map/grad_context/pallas_call | solution.py:1409
  334.7 17.1 %attend_back.2 = (bf16[1024,512]{1,0:T(8,128)(2,1)}, bf16[1024,512]{1,0:T(8,128)(2,1)}, bf16[1024,512]{1,0:T(8,128)(2,1)}, f32[8,1024]{1,0:T(8,128)}) custom-call(s32[4]{0:T(128)} %iota_xor_fusion.order_ref, s32[2,4]{1,0:T(2,128)} %reduce_window_sum.11.refs_0_.ends_ref, bf16[3,1024,1024]{2,1,0:T(8,128)(2,1)} %qkv.1.refs_1_.refs_2_.refs_3_.q_ref.k_ref.v_ref, ...), custom_call_target="tpu_custom_call" | custom-call | flops 15000000 | bytes 52428 | tf_op jit(solution)/shard_map/attend_back/pallas_call | solution.py:940
  351.8 6.6 %weight_send.6 = bf16[4,2,4,128,256]{4,3,2,1,0:T(8,128)(2,1)} custom-call(bf16[1024,1024]{1,0:T(8,128)(2,1)} %get-tuple-element.222.x_ref.refs_0_, bf16[1024,1024]{1,0:T(8,128)(2,1)} %get-tuple-element.196.g_ref.refs_1_, bf16[1024,512]{1,0:T(8,128)(2,1)} %get-tuple-element.201.refs_2_.refs_3_.refs_0_, ...), custom_call_target="tpu_custom_call" | custom-call | flops 2147483 | bytes 20971 | tf_op jit(solution)/shard_map/weight_send/pallas_call | solution.py:1231
  369.8 17.2 %attend_back.3 = (bf16[1024,512]{1,0:T(8,128)(2,1)}, bf16[1024,512]{1,0:T(8,128)(2,1)}, bf16[1024,512]{1,0:T(8,128)(2,1)}, f32[8,1024]{1,0:T(8,128)}) custom-call(s32[4]{0:T(128)} %iota_xor_fusion.order_ref, s32[2,4]{1,0:T(2,128)} %reduce_window_sum.11.refs_0_.ends_ref, bf16[3,1024,1024]{2,1,0:T(8,128)(2,1)} %qkv.1.refs_1_.refs_2_.refs_3_.q_ref.k_ref.v_ref, ...), custom_call_target="tpu_custom_call" | custom-call | flops 15000000 | bytes 52428 | tf_op jit(solution)/shard_map/attend_back/pallas_call | solution.py:940
  390.0 6.8 %weight_send.7 = bf16[4,2,4,128,256]{4,3,2,1,0:T(8,128)(2,1)} custom-call(bf16[1024,1024]{1,0:T(8,128)(2,1)} %get-tuple-element.222.x_ref.refs_0_, bf16[1024,1024]{1,0:T(8,128)(2,1)} %get-tuple-element.196.g_ref.refs_1_, bf16[1024,512]{1,0:T(8,128)(2,1)} %get-tuple-element.226.refs_2_.refs_3_, bf16[1024,512]{1,0:T(8,128)(2,1)} %get-tuple-element.218.refs_3_.refs_4_, ...), custom_call_target="tpu_custom_call" | custom-call | flops 2147483 | bytes 20971 | tf_op jit(solution)/shard_map/weight_send/pallas_call | solution.py:1231
  397.4 7.4 %weight_keep.6 = (f32[2,1,4,128,256]{4,3,2,1,0:T(8,128)}, bf16[2,1,4,128,256]{4,3,2,1,0:T(8,128)(2,1)}, f32[2,1,4,128,256]{4,3,2,1,0:T(8,128)}, bf16[2,1,4,128,256]{4,3,2,1,0:T(8,128)(2,1)}) custom-call(bf16[1024,1024]{1,0:T(8,128)(2,1)} %get-tuple-element.222.x_ref.refs_0_, bf16[1024,1024]{1,0:T(8,128)(2,1)} %get-tuple-element.196.g_ref.refs_1_, ...), custom_call_target="tpu_custom_call" | custom-call | flops 2147483 | bytes 20971 | tf_op jit(solution)/shard_map/weight_keep/pallas_call | solution.py:1275
  411.8 7.5 %weight_keep.7 = (f32[2,1,4,128,256]{4,3,2,1,0:T(8,128)}, bf16[2,1,4,128,256]{4,3,2,1,0:T(8,128)(2,1)}, f32[2,1,4,128,256]{4,3,2,1,0:T(8,128)}, bf16[2,1,4,128,256]{4,3,2,1,0:T(8,128)(2,1)}) custom-call(bf16[1024,1024]{1,0:T(8,128)(2,1)} %get-tuple-element.222.x_ref.refs_0_, bf16[1024,1024]{1,0:T(8,128)(2,1)} %get-tuple-element.196.g_ref.refs_1_, ...), custom_call_target="tpu_custom_call" | custom-call | flops 2147483 | bytes 20971 | tf_op jit(solution)/shard_map/weight_keep/pallas_call | solution.py:1275
  426.8 12.8 %grad_input.1 = bf16[1024,1024]{1,0:T(8,128)(2,1)} custom-call(s32[8]{0:T(128)} %fusion.32.order_ref, bf16[1024,512]{1,0:T(8,128)(2,1)} %get-tuple-element.201.refs_2_.refs_3_.refs_0_, bf16[1024,512]{1,0:T(8,128)(2,1)} %get-tuple-element.202.refs_3_.refs_4_.refs_1_, bf16[1024,512]{1,0:T(8,128)(2,1)} %get-tuple-element.203.refs_4_.refs_5_.refs_2_, ...), custom_call_target="tpu_custom_call" | custom-call | flops 6442450 | bytes 20971 | tf_op jit(solution)/shard_map/grad_input/pallas_call | solution.py:1453
  440.8 51.6 %finale.1 = (bf16[4,1,128,1024]{3,2,1,0:T(8,128)(2,1)}, bf16[4,1,128,1024]{3,2,1,0:T(8,128)(2,1)}, bf16[4,1,128,1024]{3,2,1,0:T(8,128)(2,1)}, bf16[4,1,128,1024]...) custom-call(f32[1,128,1024]{2,1,0:T(8,128)} %get-tuple-element.255.d, ...), custom_call_target="tpu_custom_call" | custom-call | tf_op jit(solution)/shard_map/finale/pallas_call | solution.py:634
  496.5 10.2 %place_grads.1 = (f32[1,1024,1024]{2,1,0:T(8,128)}, f32[3,1024,256]{2,1,0:T(8,128)}, f32[1024,1024]{1,0:T(8,128)}, f32[256,1024]{1,0:T(8,128)}) custom-call(s32[8]{0:T(128)} %fusion.32.order_ref, bf16[4,1,128,1024]{3,2,1,0:T(8,128)(2,1)} %get-tuple-element.242.refs_0_, bf16[4,1,128,1024]{3,2,1,0:T(8,128)(2,1)} %get-tuple-element.243.refs_1_, ...), custom_call_target="tpu_custom_call" | custom-call | tf_op jit(solution)/shard_map/place_grads/pallas_call | solution.py:1509
  (193 shorter events, 77.7 us)
Async XLA Ops:
  73.0 38.7 %collective-permute-start.1 = (bf16[4,1,128,1024]{3,2,1,0:T(8,128)(2,1)}, bf16[4,1,128,1024]{3,2,1,0:T(8,128)(2,1)S(1)}, u32[]{:S(2)}, u32[]{:S(2)}) collective-permute-start(bf16[4,1,128,1024]{3,2,1,0:T(8,128)(2,1)} %get-tuple-element.146.refs_9_), channel_id=1, source_target_pairs={{0,16},{4,20},{8,24},{12,28},{16,0},{20,4},{24,8},{28,12},{1,17},{... | collective-permute-start | bytes 3145736 | tf_op jit(solution)/shard_map/ppermute | solution.py:67
  74.4 37.2 %collective-permute-start = (bf16[4,1,128,1024]{3,2,1,0:T(8,128)(2,1)}, bf16[4,1,128,1024]{3,2,1,0:T(8,128)(2,1)S(1)}, u32[]{:S(2)}, u32[]{:S(2)}) collective-permute-start(bf16[4,1,128,1024]{3,2,1,0:T(8,128)(2,1)} %get-tuple-element.146.refs_9_), channel_id=1, source_target_pairs={{0,8},{4,12},{8,0},{12,4},{16,24},{20,28},{24,16},{28,20},{1,9},{5... | collective-permute-start | bytes 3145736 | tf_op jit(solution)/shard_map/ppermute | solution.py:67
  90.1 21.5 %collective-permute-start.4 = (bf16[2,1,128,1024]{3,2,1,0:T(8,128)(2,1)S(1)}, bf16[2,1,128,1024]{3,2,1,0:T(8,128)(2,1)}, u32[]{:S(2)}, u32[]{:S(2)}) collective-permute-start(bf16[2,1,128,1024]{3,2,1,0:T(8,128)(2,1)S(1)} %maximum_bitcast_fusion.refs_12_), channel_id=1, source_target_pairs={{0,16},{4,20},{8,24},{12,28},{16,0},{20,4},{24,8},{28,12},{1,17},{... | collective-permute-start | bytes 1572872 | tf_op jit(solution)/shard_map/ppermute | solution.py:67
  91.6 20.1 %collective-permute-start.3 = (bf16[2,1,128,1024]{3,2,1,0:T(8,128)(2,1)S(1)}, bf16[2,1,128,1024]{3,2,1,0:T(8,128)(2,1)}, u32[]{:S(2)}, u32[]{:S(2)}) collective-permute-start(bf16[2,1,128,1024]{3,2,1,0:T(8,128)(2,1)S(1)} %maximum_bitcast_fusion.refs_12_), channel_id=1, source_target_pairs={{0,8},{4,12},{8,0},{12,4},{16,24},{20,28},{24,16},{28,20},{1,9},{5... | collective-permute-start | bytes 1572872 | tf_op jit(solution)/shard_map/ppermute | solution.py:67
  92.1 72.3 %collective-permute-start.5 = (bf16[2,1,128,1024]{3,2,1,0:T(8,128)(2,1)S(1)}, bf16[2,1,128,1024]{3,2,1,0:T(8,128)(2,1)S(1)}, u32[]{:S(2)}, u32[]{:S(2)}) collective-permute-start(bf16[2,1,128,1024]{3,2,1,0:T(8,128)(2,1)S(1)} %maximum_bitcast_fusion.refs_12_), channel_id=1, source_target_pairs={{0,2},{1,3},{2,0},{3,1},{4,6},{5,7},{6,4},{7,5},{8,10},{9,11},{10,... | collective-permute-start | bytes 1572872 | tf_op jit(solution)/shard_map/ppermute | solution.py:61
  235.5 21.8 %collective-permute-start.6 = (bf16[4,4,1,128,1024]{4,3,2,1,0:T(8,128)(2,1)}, bf16[4,4,1,128,1024]{4,3,2,1,0:T(8,128)(2,1)}, u32[]{:S(2)}, u32[]{:S(2)}) collective-permute-start(bf16[4,4,1,128,1024]{4,3,2,1,0:T(8,128)(2,1)} %weight_send.4), channel_id=1, source_target_pairs={{0,4},{4,0},{8,12},{12,8},{16,20},{20,16},{24,28},{28,24},{1,5},{5... | collective-permute-start | bytes 12582920 | tf_op jit(solution)/shard_map/ppermute | solution.py:61
  277.1 35.0 %collective-permute-start.7 = (bf16[4,4,1,128,1024]{4,3,2,1,0:T(8,128)(2,1)}, bf16[4,4,1,128,1024]{4,3,2,1,0:T(8,128)(2,1)}, u32[]{:S(2)}, u32[]{:S(2)}) collective-permute-start(bf16[4,4,1,128,1024]{4,3,2,1,0:T(8,128)(2,1)} %weight_send.5), channel_id=1, source_target_pairs={{0,4},{4,0},{8,12},{12,8},{16,20},{20,16},{24,28},{28,24},{1,5},{5... | collective-permute-start | bytes 12582920 | tf_op jit(solution)/shard_map/ppermute | solution.py:61
  277.6 25.3 %collective-permute-start.9 = (bf16[2,2,1,128,1024]{4,3,1,2,0:T(8,128)(2,1)}, bf16[2,2,1,128,1024]{4,3,1,2,0:T(8,128)(2,1)S(1)}, u32[]{:S(2)}, u32[]{:S(2)}) collective-permute-start(bf16[2,2,1,128,1024]{4,3,1,2,0:T(8,128)(2,1)} %bitcast.22), channel_id=1, source_target_pairs={{0,8},{4,12},{8,0},{12,4},{16,24},{20,28},{24,16},{28,20},{1,9},{5... | collective-permute-start | bytes 3145736 | tf_op jit(solution)/shard_map/ppermute | solution.py:61
  279.1 24.8 %collective-permute-start.8 = (bf16[2,2,1,128,1024]{4,3,1,2,0:T(8,128)(2,1)S(1)}, bf16[2,2,1,128,1024]{4,3,1,2,0:T(8,128)(2,1)S(1)}, u32[]{:S(2)}, u32[]{:S(2)}) collective-permute-start(bf16[2,2,1,128,1024]{4,3,1,2,0:T(8,128)(2,1)S(1)} %bitcast.173), channel_id=1, source_target_pairs={{0,16},{4,20},{8,24},{12,28},{16,0},{20,4},{24,8},{28,12},{1,17},{... | collective-permute-start | bytes 3145736 | tf_op jit(solution)/shard_map/ppermute | solution.py:61
  310.1 19.5 %collective-permute-start.10 = (bf16[2,1,128,1024]{3,2,0,1:T(8,128)(2,1)S(1)}, bf16[2,1,128,1024]{3,2,0,1:T(8,128)(2,1)}, u32[]{:S(2)}, u32[]{:S(2)}) collective-permute-start(bf16[2,1,128,1024]{3,2,0,1:T(8,128)(2,1)S(1)} %get-tuple-element.265), channel_id=1, source_target_pairs={{0,8},{4,12},{8,0},{12,4},{16,24},{20,28},{24,16},{28,20},{1,9},{5... | collective-permute-start | bytes 1572872 | tf_op jit(solution)/shard_map/ppermute | solution.py:61
  310.6 20.5 %collective-permute-start.11 = (bf16[2,1,128,1024]{3,2,0,1:T(8,128)(2,1)}, bf16[2,1,128,1024]{3,2,0,1:T(8,128)(2,1)S(1)}, u32[]{:S(2)}, u32[]{:S(2)}) collective-permute-start(bf16[2,1,128,1024]{3,2,0,1:T(8,128)(2,1)} %get-tuple-element.266), channel_id=1, source_target_pairs={{0,16},{4,20},{8,24},{12,28},{16,0},{20,4},{24,8},{28,12},{1,17},{... | collective-permute-start | bytes 1572872 | tf_op jit(solution)/shard_map/ppermute | solution.py:61
  331.3 30.9 %collective-permute-start.13 = (bf16[2,2,1,128,1024]{4,3,1,2,0:T(8,128)(2,1)}, bf16[2,2,1,128,1024]{4,3,1,2,0:T(8,128)(2,1)S(1)}, u32[]{:S(2)}, u32[]{:S(2)}) collective-permute-start(bf16[2,2,1,128,1024]{4,3,1,2,0:T(8,128)(2,1)} %bitcast.34), channel_id=1, source_target_pairs={{0,8},{4,12},{8,0},{12,4},{16,24},{20,28},{24,16},{28,20},{1,9},{5... | collective-permute-start | bytes 3145736 | tf_op jit(solution)/shard_map/ppermute | solution.py:61
  332.0 30.3 %collective-permute-start.12 = (bf16[2,2,1,128,1024]{4,3,1,2,0:T(8,128)(2,1)}, bf16[2,2,1,128,1024]{4,3,1,2,0:T(8,128)(2,1)}, u32[]{:S(2)}, u32[]{:S(2)}) collective-permute-start(bf16[2,2,1,128,1024]{4,3,1,2,0:T(8,128)(2,1)} %bitcast.31), channel_id=1, source_target_pairs={{0,16},{4,20},{8,24},{12,28},{16,0},{20,4},{24,8},{28,12},{1,17},{... | collective-permute-start | bytes 3145736 | tf_op jit(solution)/shard_map/ppermute | solution.py:61
  333.5 25.0 %collective-permute-start.14 = (bf16[2,1,128,1024]{3,2,1,0:T(8,128)(2,1)S(1)}, bf16[2,1,128,1024]{3,2,1,0:T(8,128)(2,1)}, u32[]{:S(2)}, u32[]{:S(2)}) collective-permute-start(bf16[2,1,128,1024]{3,2,1,0:T(8,128)(2,1)S(1)} %pad_maximum_fusion), channel_id=1, source_target_pairs={{0,1},{1,0},{2,3},{3,2},{4,5},{5,4},{6,7},{7,6},{8,9},{9,8},{10,11... | collective-permute-start | bytes 1572872 | tf_op jit(solution)/shard_map/ppermute | solution.py:61
  358.5 39.0 %collective-permute-start.18 = (bf16[4,2,4,128,256]{4,3,2,1,0:T(8,128)(2,1)}, bf16[4,2,4,128,256]{4,3,2,1,0:T(8,128)(2,1)}, u32[]{:S(2)}, u32[]{:S(2)}) collective-permute-start(bf16[4,2,4,128,256]{4,3,2,1,0:T(8,128)(2,1)} %weight_send.6), channel_id=1, source_target_pairs={{0,4},{4,0},{8,12},{12,8},{16,20},{20,16},{24,28},{28,24},{1,5},{5... | collective-permute-start | bytes 6291464 | tf_op jit(solution)/shard_map/ppermute | solution.py:61
  360.7 26.3 %collective-permute-start.17 = (bf16[1,128,1024]{2,1,0:T(8,128)(2,1)}, bf16[1,128,1024]{2,1,0:T(8,128)(2,1)S(1)}, u32[]{:S(2)}, u32[]{:S(2)}) collective-permute-start(bf16[1,128,1024]{2,1,0:T(8,128)(2,1)} %get-tuple-element.256), channel_id=1, source_target_pairs={{0,2},{1,3},{2,0},{3,1},{4,6},{5,7},{6,4},{7,5},{8,10},{9,11},{10,... | collective-permute-start | bytes 786440 | tf_op jit(solution)/shard_map/ppermute | solution.py:61
  365.0 22.1 %collective-permute-start.15 = (bf16[2,1,128,1024]{3,2,0,1:T(8,128)(2,1)S(1)}, bf16[2,1,128,1024]{3,2,0,1:T(8,128)(2,1)S(1)}, u32[]{:S(2)}, u32[]{:S(2)}) collective-permute-start(bf16[2,1,128,1024]{3,2,0,1:T(8,128)(2,1)S(1)} %fusion.10), channel_id=1, source_target_pairs={{0,8},{4,12},{8,0},{12,4},{16,24},{20,28},{24,16},{28,20},{1,9},{5... | collective-permute-start | bytes 1572872 | tf_op jit(solution)/shard_map/ppermute | solution.py:61
  368.4 18.9 %collective-permute-start.16 = (bf16[2,1,128,1024]{3,2,0,1:T(8,128)(2,1)}, bf16[2,1,128,1024]{3,2,0,1:T(8,128)(2,1)}, u32[]{:S(2)}, u32[]{:S(2)}) collective-permute-start(bf16[2,1,128,1024]{3,2,0,1:T(8,128)(2,1)} %fusion.11), channel_id=1, source_target_pairs={{0,16},{4,20},{8,24},{12,28},{16,0},{20,4},{24,8},{28,12},{1,17},{... | collective-permute-start | bytes 1572872 | tf_op jit(solution)/shard_map/ppermute | solution.py:61
  396.8 15.0 %collective-permute-start.19 = (bf16[4,2,4,128,256]{4,3,2,1,0:T(8,128)(2,1)}, bf16[4,2,4,128,256]{4,3,2,1,0:T(8,128)(2,1)}, u32[]{:S(2)}, u32[]{:S(2)}) collective-permute-start(bf16[4,2,4,128,256]{4,3,2,1,0:T(8,128)(2,1)} %weight_send.7), channel_id=1, source_target_pairs={{0,4},{4,0},{8,12},{12,8},{16,20},{20,16},{24,28},{28,24},{1,5},{5... | collective-permute-start | bytes 6291464 | tf_op jit(solution)/shard_map/ppermute | solution.py:61
  404.9 34.8 %collective-permute-start.22 = (bf16[2,1,4,128,256]{4,3,2,1,0:T(8,128)(2,1)}, bf16[2,1,4,128,256]{4,3,2,1,0:T(8,128)(2,1)S(1)}, u32[]{:S(2)}, u32[]{:S(2)}) collective-permute-start(bf16[2,1,4,128,256]{4,3,2,1,0:T(8,128)(2,1)} %get-tuple-element.221), channel_id=1, source_target_pairs={{0,16},{4,20},{8,24},{12,28},{16,0},{20,4},{24,8},{28,12},{1,17},{... | collective-permute-start | bytes 1572872 | tf_op jit(solution)/shard_map/ppermute | solution.py:61
  411.2 28.5 %collective-permute-start.23 = (bf16[2,1,4,128,256]{4,3,2,1,0:T(8,128)(2,1)}, bf16[2,1,4,128,256]{4,3,2,1,0:T(8,128)(2,1)S(1)}, u32[]{:S(2)}, u32[]{:S(2)}) collective-permute-start(bf16[2,1,4,128,256]{4,3,2,1,0:T(8,128)(2,1)} %get-tuple-element.232), channel_id=1, source_target_pairs={{0,8},{4,12},{8,0},{12,4},{16,24},{20,28},{24,16},{28,20},{1,9},{5... | collective-permute-start | bytes 1572872 | tf_op jit(solution)/shard_map/ppermute | solution.py:61
  419.4 20.3 %collective-permute-start.25 = (bf16[2,1,4,128,256]{4,3,2,1,0:T(8,128)(2,1)}, bf16[2,1,4,128,256]{4,3,2,1,0:T(8,128)(2,1)S(1)}, u32[]{:S(2)}, u32[]{:S(2)}) collective-permute-start(bf16[2,1,4,128,256]{4,3,2,1,0:T(8,128)(2,1)} %get-tuple-element.224), channel_id=1, source_target_pairs={{0,8},{4,12},{8,0},{12,4},{16,24},{20,28},{24,16},{28,20},{1,9},{5... | collective-permute-start | bytes 1572872 | tf_op jit(solution)/shard_map/ppermute | solution.py:61
  420.8 18.9 %collective-permute-start.24 = (bf16[2,1,4,128,256]{4,3,2,1,0:T(8,128)(2,1)}, bf16[2,1,4,128,256]{4,3,2,1,0:T(8,128)(2,1)}, u32[]{:S(2)}, u32[]{:S(2)}) collective-permute-start(bf16[2,1,4,128,256]{4,3,2,1,0:T(8,128)(2,1)} %get-tuple-element.223), channel_id=1, source_target_pairs={{0,16},{4,20},{8,24},{12,28},{16,0},{20,4},{24,8},{28,12},{1,17},{... | collective-permute-start | bytes 1572872 | tf_op jit(solution)/shard_map/ppermute | solution.py:61
  423.4 16.2 %collective-permute-start.21 = (bf16[1,128,1024]{2,1,0:T(8,128)(2,1)S(1)}, bf16[1,128,1024]{2,1,0:T(8,128)(2,1)S(1)}, u32[]{:S(2)}, u32[]{:S(2)}) collective-permute-start(bf16[1,128,1024]{2,1,0:T(8,128)(2,1)S(1)} %get-tuple-element.254), channel_id=1, source_target_pairs={{0,2},{1,3},{2,0},{3,1},{4,6},{5,7},{6,4},{7,5},{8,10},{9,11},{10,... | collective-permute-start | bytes 786440 | tf_op jit(solution)/shard_map/ppermute | solution.py:61
  (41 other events, 313.5 us)

commit v6 on v5

--- a/solution.py
+++ b/solution.py
@@ -169,13 +169,23 @@
         return pltpu.make_async_copy(source, target, self.local.at[i])
 
 
-def greet(distances):
-    barrier = pltpu.get_barrier_semaphore()
+def call_out(distances):
     for axis, r in distances:
         pl.semaphore_signal(
-            barrier, inc=1, device_id={axis: at_distance(axis, r)}, device_id_type=MESH
+            pltpu.get_barrier_semaphore(),
+            inc=1,
+            device_id={axis: at_distance(axis, r)},
+            device_id_type=MESH,
         )
-    pl.semaphore_wait(barrier, len(distances))
+
+
+def await_all(distances):
+    pl.semaphore_wait(pltpu.get_barrier_semaphore(), len(distances))
+
+
+def greet(distances):
+    call_out(distances)
+    await_all(distances)
 
 
 def part_distances():
@@ -273,11 +283,13 @@
             load.wait()
             copy.start()
 
-    def finish(self):
+    def complete(self):
         for move in self.second:
             move.wait_recv()
         for move in self.cores[self.early :]:
             move.start()
+
+    def finish(self):
         for move in self.first + self.second:
             move.wait_send()
         for move in self.cores:
@@ -361,13 +373,15 @@
 
         @pl.when(step == 0)
         def _():
-            greet(all_distances())
+            call_out(all_distances())
+            if weights:
+                await_all(all_distances())
             for weight, count in weights:
                 weight.start()
                 if count:
                     weight.relay()
 
-        @pl.when(step == steps * 3 // 4)
+        @pl.when(step == steps * 5 // 8)
         def _():
             for weight, count in weights:
                 weight.settle()
@@ -378,12 +392,16 @@
 
         @pl.when(step == steps - 1)
         def _():
+            if not weights:
+                await_all(all_distances())
             for weight, _ in weights:
-                weight.finish()
+                weight.complete()
             largest = jnp.max(peaks.reach(body_outs[peak][...]), keepdims=True)
             level = DECAY * range_ref[row] + (1.0 - DECAY) * largest
             places = lax.broadcasted_iota(jnp.int32, level_ref.shape, 0)
             level_ref[...] = jnp.where(places == row, level, before_ref[...])
+            for weight, _ in weights:
+                weight.finish()
 
     return kernel
 
@@ -478,6 +496,7 @@
             move.wait_send()
         for move in cores[r]:
             move.wait()
+    outer.complete()
     outer.finish()
     for units in (later[0], later[2]):
         units.finish()
@@ -556,13 +575,16 @@
         piece_q[k] = low(total * slope_q[kinds_of(k)])
         first[k].start()
 
-    greet([("dp", r) for r in range(1, datas)] + part_distances())
+    call_out(all_distances())
+    for k in range(chunks):
+        for i in (3, 2, 1, 0):
+            more = mores[i][1, :, kinds_of(k)].astype(F32)
+            send_p[k, i] = low(keeps[i][1, :, kinds_of(k)] + more)
+    await_all(all_distances())
     for move in sum_data:
         move.start()
     for k in range(chunks):
         for i in (3, 2, 1, 0):
-            more = mores[i][1, :, kinds_of(k)].astype(F32)
-            send_p[k, i] = low(keeps[i][1, :, kinds_of(k)] + more)
             steps[k][i].start()
     piece_d[...] = low((down_sum[...] + down_more[...].astype(F32)) * slope_down[...])
     piece_i[...] = low((in_sum[...] + in_more[...].astype(F32)) * slope_in[...])
@@ -593,12 +615,12 @@
     sums_out[me] = jnp.sum(sums_far[...], axis=0)
     for move in sum_back:
         move.start()
-    down.finish()
-    inner.finish()
     first[chunks - 1].relay()
+    for unit in [down, inner] + first:
+        unit.complete()
     for move in sum_back:
         move.wait()
-    for unit in first:
+    for unit in [down, inner] + first:
         unit.finish()
     for group in steps + along:
         for move in group:
@@ -691,7 +713,7 @@
     range_ref, x_ref, qkv_ref, out_ref, in_ref, down_ref, level_ref, quant_ref, *refs
 ):
     peaks = Peaks(Mover(*refs[-3:-1], None), *refs[-7:-3])
-    greet(all_distances())
+    call_out(all_distances())
     order = Order(x_ref.shape[1])
     rows = 256
     steps = x_ref.shape[0] // rows
@@ -706,7 +728,9 @@
     inputs = lax.fori_loop(0, steps, largest, jnp.zeros((8, LANES), F32))
     found.append(jnp.max(inputs, axis=0, keepdims=True))
     found.append(jnp.zeros((1, LANES), F32))
-    reached = jnp.max(peaks.reach(jnp.concatenate(found, axis=0)), axis=1, keepdims=True)
+    found = jnp.concatenate(found, axis=0)
+    await_all(all_distances())
+    reached = jnp.max(peaks.reach(found), axis=1, keepdims=True)
     level = DECAY * range_ref[0] + (1.0 - DECAY) * reached[6:7, :]
     level_ref[...] = jnp.broadcast_to(level, level_ref.shape)
     for i, values in enumerate(own):
@@ -749,25 +773,26 @@
 
 def qkv_kernel(x_ref, near_ref, far_ref, b_ref, o_ref):
     half = x_ref.shape[1] // 2
-    total = dot(x_ref[:, :half], flat(near_ref[...])) + dot(x_ref[:, half:], flat(far_ref[...]))
-    o_ref[...] = low(total + b_ref[...])
+    for i in range(o_ref.shape[0]):
+        total = dot(x_ref[:, :half], flat(near_ref[:, i])) + dot(x_ref[:, half:], flat(far_ref[:, i]))
+        o_ref[i] = low(total + b_ref[i])
 
 
 def qkv_rows(x, weights, bias):
     near, far = weights
     plane, parts, kinds, rows, c = near.shape
     tokens, width = x.shape
-    weight_spec = pl.BlockSpec((plane, None, None, rows, c), lambda r, i: (0, r, i, 0, 0))
+    weight_spec = pl.BlockSpec((plane, None, kinds, rows, c), lambda r: (0, r, 0, 0, 0))
     return pl.pallas_call(
         qkv_kernel,
-        grid=(parts, kinds),
+        grid=(parts,),
         in_specs=[
-            pl.BlockSpec((tokens, width), lambda r, i: (0, 0)),
+            pl.BlockSpec((tokens, width), lambda r: (0, 0)),
             weight_spec,
             weight_spec,
-            pl.BlockSpec((None, 1, c), lambda r, i: (i, 0, r)),
+            pl.BlockSpec((kinds, 1, c), lambda r: (0, 0, r)),
         ],
-        out_specs=pl.BlockSpec((None, tokens, c), lambda r, i: (i, 0, r)),
+        out_specs=pl.BlockSpec((kinds, tokens, c), lambda r: (0, 0, r)),
         out_shape=shape_of((kinds, tokens, parts * c), BF16),
         compiler_params=params(),
         cost_estimate=cost(2 * tokens * width * kinds * parts * c, 14 * MIB),

time: 515 us -> 507 us (0.984)
  Pallas kernels: 428 us -> 417 us
    pallas_call x3, Pallas kernels: 90.6 us -> 83.3 us  [run(): results = call(*args, ranges, levels, *sources)]
  transfers between devices with their start and end apart: 26 -> 26, of which waited for: 3 -> 5; matrix products, arithmetic and copies ran while one was open for 4% -> 4% of each run, Pallas kernels for 42% -> 41%
where the time goes in v6:
time: 507 us; the launch traced here: 499 us
  Pallas kernels  417 us (82%)
  local copies, waits for them, and re-layouts  27.4 us (5%)
  starting transfers between devices  24.1 us (5%)
  other arithmetic  15.9 us (3%)
  waiting for transfers between devices  12.9 us (3%)
    pallas_call x3, Pallas kernels, run(): results = call(*args, ranges, levels, *sources)  83.3 us
    pallas_call x1, Pallas kernels, finale(): pl.pallas_call(finale_kernel, in_specs=[vmem] * len(args), out_specs=[any...  51.6 us
    pallas_call x1, Pallas kernels, first_gather(): pl.pallas_call(first_gather_kernel, in_specs=[pl.BlockSpec(memory_space=p...  46.4 us
    pallas_call x4, Pallas kernels, weight_keep(): pl.pallas_call(partial(weight_keep_kernel, len(xs), which, first_split(bi...  36.2 us
    pallas_call x2, Pallas kernels, attend_back(): pl.pallas_call(partial(attend_back_kernel, c, first), grid=(held, width /...  34.4 us
    pallas_call x4, Pallas kernels, weight_send(): pl.pallas_call(partial(weight_send_kernel, len(xs), [product[0] for produ...  31.8 us
    pallas_call x1, Pallas kernels, second_norm(): pl.pallas_call(second_norm_kernel, grid=(tokens // rows,), in_specs=[in_s...  22 us
    pallas_call x1, Pallas kernels, grad_hidden_rows(): pl.pallas_call(partial(grad_hidden_kernel, cuts), grid=(parts * cuts,), i...  21.2 us
  transfers between devices with their start and end apart: 26, of which 5 were waited for; matrix products, arithmetic and copies ran while one was open for 4% of the time, Pallas kernels for 41%

profile of v6, /device:TPU:0, one launch (start us, length us, event | category | flops | bytes accessed | tf_op | source)
XLA Modules:
  0.0 498.8 jit_solution(9964414950169447201)
XLA Ops:
  8.7 16.7 %prepare.1 = (f32[8,128]{1,0:T(8,128)}, bf16[1024,1024]{1,0:T(8,128)(2,1)}, bf16[3,128,256]{2,1,0:T(8,128)(2,1)}, bf16[1,128,256]{2,1,0:T(8,128)(2,1)}, bf16[1,1...) custom-call(f32[4]{0:T(128)} %refs_5_.1, ...), custom_call_target="tpu_custom_call" | custom-call | tf_op jit(solution)/shard_map/prepare/pallas_call | solution.py:762
  25.4 46.4 %first_gather.1 = (bf16[4,4,3,128,256]{4,3,2,1,0:T(8,128)(2,1)}, bf16[4,4,3,128,256]{4,3,2,1,0:T(8,128)(2,1)}, bf16[4,16,128]{2,1,0:T(8,128)(2,1)}, bf16[4,4,1,1...) custom-call(bf16[3,128,256]{2,1,0:T(8,128)(2,1)} %get-tuple-element.135.first_ref, ...), custom_call_target="tpu_custom_call" | custom-call | tf_op jit(solution)/shard_map/first_gather/pallas_call | solution.py:509
  75.4 10.8 %qkv.1.refs_1_.refs_2_.refs_3_.q_ref.k_ref.v_ref = bf16[3,1024,1024]{2,1,0:T(8,128)(2,1)} custom-call(bf16[1024,1024]{1,0:T(8,128)(2,1)} %get-tuple-element.222.x_ref.refs_0_, bf16[4,4,3,128,256]{4,3,2,1,0:T(8,128)(2,1)} %get-tuple-element.138.near_ref.refs_6_, bf16[4,4,3,128,256]{4,3,2,1,0:T(8,128)(2,1)} %get-tuple-element.139.far_ref.refs_7_, ...), custom_call_target="tpu_custom_call" | custom-call | flops 6442450 | bytes 14680 | tf_op jit(solution)/shard_map/qkv/pallas_call | solution.py:786
  93.6 13.7 %attend.2 = (f32[1024,1024]{1,0:T(8,128)}, f32[2,128,512]{2,1,0:T(8,128)}, f32[8,128]{1,0:T(8,128)}) custom-call(s32[2,4]{1,0:T(2,128)} %reduce_window_sum.11.refs_0_.ends_ref, bf16[3,1024,1024]{2,1,0:T(8,128)(2,1)} %qkv.1.refs_1_.refs_2_.refs_3_.q_ref.k_ref.v_ref, bf16[3,1024,1024]{2,1,0:T(8,128)(2,1)} %qkv.1.refs_1_.refs_2_.refs_3_.q_ref.k_ref.v_ref, ...), custom_call_target="tpu_custom_call" | custom-call | flops 15000000 | bytes 41943 | tf_op jit(solution)/shard_map/attend/pallas_call | solution.py:895
  111.8 30.2 %attend.3 = (f32[1024,1024]{1,0:T(8,128)}, f32[2,128,512]{2,1,0:T(8,128)}, f32[8,128]{1,0:T(8,128)}, f32[8,128]{1,0:T(8,128)}, bf16[4,4,1,128,1024]{4,3,2,1,0:T(...) custom-call(s32[2,4]{1,0:T(2,128)} %reduce_window_sum.11.refs_0_.end, ...), custom_call_target="tpu_custom_call", output_to_operand_aliasing={{0}: (6, {})} | custom-call | flops 15000000 | bytes 41943 | tf_op jit(solution)/shard_map/attend/pallas_call | solution.py:432
  142.1 17.0 %first_norm.1 = (bf16[1024,1024]{1,0:T(8,128)(2,1)}, f32[1024,1024]{1,0:T(8,128)}, f32[1024,1024]{1,0:T(8,128)}, f32[1024,1]{1,0:T(8,128)}, f32[8,128]{1,0:T(8,128)}, /*index=5*/f32[8,128]{1,0:T(8,128)}) custom-call(f32[1024,1024]{1,0:T(8,128)} %get-tuple-element.155.refs_0_.ctx_ref, f32[8,128]{1,0:T(8,128)} %get-tuple-element.156.refs_1_.refs_7_, ...), custom_call_target="tpu_custom_call" | custom-call | flops 2147483 | bytes 20971 | tf_op jit(solution)/shard_map/first_norm/pallas_call | solution.py:432
  159.9 36.0 %hidden.1 = (bf16[1024,1024]{1,0:T(8,128)(2,1)}, f32[1024,4096]{1,0:T(8,128)}, f32[1024,4096]{1,0:T(8,128)}, f32[8,128]{1,0:T(8,128)}, f32[8,128]{1,0:T(8,128)},...) custom-call(f32[1024,1024]{1,0:T(8,128)} %get-tuple-element.159.refs_0_.normed_ref, ...), custom_call_target="tpu_custom_call" | custom-call | flops 8589934 | bytes 52428 | tf_op jit(solution)/shard_map/hidden/pallas_call | solution.py:432
  196.0 22.0 %second_norm.1 = (bf16[1024,4096]{1,0:T(8,128)(2,1)}, bf16[1024,1024]{1,0:T(8,128)(2,1)}, f32[1024,1024]{1,0:T(8,128)}, bf16[1024,1024]{1,0:T(8,128)(2,1)}, f32[8,1024]{1,0:T(8,128)}) custom-call(s32[8]{0:T(128)} %fusion.32.order_ref, f32[1024,4096]{1,0:T(8,128)} %get-tuple-element.164.act_ref, f32[8,128]{1,0:T(8,128)} %get-tuple-element.165.level_ref.refs_10_, ...), custom_call_target="tpu_custom_call" | custom-call | flops 8589934 | bytes 83886 | tf_op jit(solution)/shard_map/second_norm/pallas_call | solution.py:1189
  218.0 9.1 %weight_send.4 = bf16[4,4,1,128,1024]{4,3,2,1,0:T(8,128)(2,1)} custom-call(bf16[1024,1024]{1,0:T(8,128)(2,1)} %get-tuple-element.177.refs_0_.g_ref, bf16[1024,4096]{1,0:T(8,128)(2,1)} %get-tuple-element.172.refs_1_.refs_2_), custom_call_target="tpu_custom_call" | custom-call | flops 4294967 | bytes 20971 | tf_op jit(solution)/shard_map/weight_send/pallas_call | solution.py:1256
  227.6 21.2 %grad_hidden.1 = (bf16[1024,4096]{1,0:T(8,128)(2,1)}, f32[4,1024]{1,0:T(4,128)}) custom-call(s32[4]{0:T(128)} %iota_xor_fusion.order_ref, bf16[1024,1024]{1,0:T(8,128)(2,1)} %get-tuple-element.177.refs_0_.g_ref, bf16[4,2,128,1024]{3,2,1,0:T(8,128)(2,1)} %bitcast.143, bf16[4,2,128,1024]{3,2,1,0:T(8,128)(2,1)} %bitcast.145, ...), custom_call_target="tpu_custom_call" | custom-call | flops 8589934 | bytes 35651 | tf_op jit(solution)/shard_map/grad_hidden/pallas_call | solution.py:1357
  248.9 10.6 %weight_keep.4 = (f32[2,2,1,128,1024]{4,3,2,1,0:T(8,128)}, bf16[2,2,1,128,1024]{4,3,2,1,0:T(8,128)(2,1)}, f32[2,2,1,128,1024]{4,3,2,1,0:T(8,128)}, bf16[2,2,1,128,1024]{4,3,2,1,0:T(8,128)(2,1)}) custom-call(bf16[1024,1024]{1,0:T(8,128)(2,1)} %get-tuple-element.177.refs_0_.g_ref, bf16[4,4,1,128,1024]{4,3,2,1,0:T(8,128)(2,1)} %collective-permute-done.6.refs_1_, ...), custom_call_target="tpu_custom_call" | custom-call | flops 4294967 | bytes 20971 | tf_op jit(solution)/shard_map/weight_keep/pallas_call | solution.py:1300
  259.5 9.2 %weight_send.5 = bf16[4,4,1,128,1024]{4,3,2,1,0:T(8,128)(2,1)} custom-call(bf16[1024,1024]{1,0:T(8,128)(2,1)} %get-tuple-element.188.refs_0_, bf16[1024,4096]{1,0:T(8,128)(2,1)} %get-tuple-element.193.refs_1_.g_ref.refs_2_), custom_call_target="tpu_custom_call" | custom-call | flops 4294967 | bytes 20971 | tf_op jit(solution)/shard_map/weight_send/pallas_call | solution.py:1256
  271.3 18.7 %first_back.1 = (f32[1024,1024]{1,0:T(8,128)}, bf16[1024,1024]{1,0:T(8,128)(2,1)}, f32[8,1024]{1,0:T(8,128)}) custom-call(s32[8]{0:T(128)} %fusion.32.order_ref, bf16[1024,4096]{1,0:T(8,128)(2,1)} %get-tuple-element.193.refs_1_.g_ref.refs_2_, bf16[4,4,128,1024]{3,2,1,0:T(8,128)(2,1)} %bitcast.139, bf16[4,4,128,1024]{3,2,1,0:T(8,128)(2,1)} %bitcast.141, ...), custom_call_target="tpu_custom_call" | custom-call | flops 8589934 | bytes 37748 | tf_op jit(solution)/shard_map/first_back/pallas_call | solution.py:1393
  303.7 10.7 %weight_keep.5 = (f32[2,2,1,128,1024]{4,3,2,1,0:T(8,128)}, bf16[2,2,1,128,1024]{4,3,2,1,0:T(8,128)(2,1)}, f32[2,2,1,128,1024]{4,3,2,1,0:T(8,128)}, bf16[2,2,1,128,1024]{4,3,2,1,0:T(8,128)(2,1)}) custom-call(bf16[1024,1024]{1,0:T(8,128)(2,1)} %get-tuple-element.188.refs_0_, bf16[4,4,1,128,1024]{4,3,2,1,0:T(8,128)(2,1)} %collective-permute-done.7.refs_1_, ...), custom_call_target="tpu_custom_call" | custom-call | flops 4294967 | bytes 20971 | tf_op jit(solution)/shard_map/weight_keep/pallas_call | solution.py:1300
  314.3 6.8 %grad_context.1.g_ref = bf16[1024,1024]{1,0:T(8,128)(2,1)} custom-call(bf16[1024,1024]{1,0:T(8,128)(2,1)} %get-tuple-element.196.g_ref.refs_1_, bf16[4,4,128,256]{3,2,1,0:T(8,128)(2,1)} %bitcast.151, bf16[4,4,128,256]{3,2,1,0:T(8,128)(2,1)} %bitcast.153, f32[1024,1024]{1,0:T(8,128)} %get-tuple-element.155.refs_0_.ctx_ref, ...), custom_call_target="tpu_custom_call" | custom-call | flops 2147483 | bytes 10485 | tf_op jit(solution)/shard_map/grad_context/pallas_call | solution.py:1434
  326.3 17.1 %attend_back.2 = (bf16[1024,512]{1,0:T(8,128)(2,1)}, bf16[1024,512]{1,0:T(8,128)(2,1)}, bf16[1024,512]{1,0:T(8,128)(2,1)}, f32[8,1024]{1,0:T(8,128)}) custom-call(s32[4]{0:T(128)} %iota_xor_fusion.order_ref, s32[2,4]{1,0:T(2,128)} %reduce_window_sum.11.refs_0_.ends_ref, bf16[3,1024,1024]{2,1,0:T(8,128)(2,1)} %qkv.1.refs_1_.refs_2_.refs_3_.q_ref.k_ref.v_ref, ...), custom_call_target="tpu_custom_call" | custom-call | flops 15000000 | bytes 52428 | tf_op jit(solution)/shard_map/attend_back/pallas_call | solution.py:965
  343.4 6.6 %weight_send.6 = bf16[4,2,4,128,256]{4,3,2,1,0:T(8,128)(2,1)} custom-call(bf16[1024,1024]{1,0:T(8,128)(2,1)} %get-tuple-element.222.x_ref.refs_0_, bf16[1024,1024]{1,0:T(8,128)(2,1)} %get-tuple-element.196.g_ref.refs_1_, bf16[1024,512]{1,0:T(8,128)(2,1)} %get-tuple-element.201.refs_2_.refs_3_.refs_0_, ...), custom_call_target="tpu_custom_call" | custom-call | flops 2147483 | bytes 20971 | tf_op jit(solution)/shard_map/weight_send/pallas_call | solution.py:1256
  360.4 17.2 %attend_back.3 = (bf16[1024,512]{1,0:T(8,128)(2,1)}, bf16[1024,512]{1,0:T(8,128)(2,1)}, bf16[1024,512]{1,0:T(8,128)(2,1)}, f32[8,1024]{1,0:T(8,128)}) custom-call(s32[4]{0:T(128)} %iota_xor_fusion.order_ref, s32[2,4]{1,0:T(2,128)} %reduce_window_sum.11.refs_0_.ends_ref, bf16[3,1024,1024]{2,1,0:T(8,128)(2,1)} %qkv.1.refs_1_.refs_2_.refs_3_.q_ref.k_ref.v_ref, ...), custom_call_target="tpu_custom_call" | custom-call | flops 15000000 | bytes 52428 | tf_op jit(solution)/shard_map/attend_back/pallas_call | solution.py:965
  380.6 6.8 %weight_send.7 = bf16[4,2,4,128,256]{4,3,2,1,0:T(8,128)(2,1)} custom-call(bf16[1024,1024]{1,0:T(8,128)(2,1)} %get-tuple-element.222.x_ref.refs_0_, bf16[1024,1024]{1,0:T(8,128)(2,1)} %get-tuple-element.196.g_ref.refs_1_, bf16[1024,512]{1,0:T(8,128)(2,1)} %get-tuple-element.226.refs_2_.refs_3_, bf16[1024,512]{1,0:T(8,128)(2,1)} %get-tuple-element.218.refs_3_.refs_4_, ...), custom_call_target="tpu_custom_call" | custom-call | flops 2147483 | bytes 20971 | tf_op jit(solution)/shard_map/weight_send/pallas_call | solution.py:1256
  389.0 7.4 %weight_keep.6 = (f32[2,1,4,128,256]{4,3,2,1,0:T(8,128)}, bf16[2,1,4,128,256]{4,3,2,1,0:T(8,128)(2,1)}, f32[2,1,4,128,256]{4,3,2,1,0:T(8,128)}, bf16[2,1,4,128,256]{4,3,2,1,0:T(8,128)(2,1)}) custom-call(bf16[1024,1024]{1,0:T(8,128)(2,1)} %get-tuple-element.222.x_ref.refs_0_, bf16[1024,1024]{1,0:T(8,128)(2,1)} %get-tuple-element.196.g_ref.refs_1_, ...), custom_call_target="tpu_custom_call" | custom-call | flops 2147483 | bytes 20971 | tf_op jit(solution)/shard_map/weight_keep/pallas_call | solution.py:1300
  403.1 7.5 %weight_keep.7 = (f32[2,1,4,128,256]{4,3,2,1,0:T(8,128)}, bf16[2,1,4,128,256]{4,3,2,1,0:T(8,128)(2,1)}, f32[2,1,4,128,256]{4,3,2,1,0:T(8,128)}, bf16[2,1,4,128,256]{4,3,2,1,0:T(8,128)(2,1)}) custom-call(bf16[1024,1024]{1,0:T(8,128)(2,1)} %get-tuple-element.222.x_ref.refs_0_, bf16[1024,1024]{1,0:T(8,128)(2,1)} %get-tuple-element.196.g_ref.refs_1_, ...), custom_call_target="tpu_custom_call" | custom-call | flops 2147483 | bytes 20971 | tf_op jit(solution)/shard_map/weight_keep/pallas_call | solution.py:1300
  418.4 12.8 %grad_input.1 = bf16[1024,1024]{1,0:T(8,128)(2,1)} custom-call(s32[8]{0:T(128)} %fusion.32.order_ref, bf16[1024,512]{1,0:T(8,128)(2,1)} %get-tuple-element.201.refs_2_.refs_3_.refs_0_, bf16[1024,512]{1,0:T(8,128)(2,1)} %get-tuple-element.202.refs_3_.refs_4_.refs_1_, bf16[1024,512]{1,0:T(8,128)(2,1)} %get-tuple-element.203.refs_4_.refs_5_.refs_2_, ...), custom_call_target="tpu_custom_call" | custom-call | flops 6442450 | bytes 20971 | tf_op jit(solution)/shard_map/grad_input/pallas_call | solution.py:1478
  432.4 51.6 %finale.1 = (bf16[4,1,128,1024]{3,2,1,0:T(8,128)(2,1)}, bf16[4,1,128,1024]{3,2,1,0:T(8,128)(2,1)}, bf16[4,1,128,1024]{3,2,1,0:T(8,128)(2,1)}, bf16[4,1,128,1024]...) custom-call(f32[1,128,1024]{2,1,0:T(8,128)} %get-tuple-element.255.d, ...), custom_call_target="tpu_custom_call" | custom-call | tf_op jit(solution)/shard_map/finale/pallas_call | solution.py:656
  488.1 10.2 %place_grads.1 = (f32[1,1024,1024]{2,1,0:T(8,128)}, f32[3,1024,256]{2,1,0:T(8,128)}, f32[1024,1024]{1,0:T(8,128)}, f32[256,1024]{1,0:T(8,128)}) custom-call(s32[8]{0:T(128)} %fusion.32.order_ref, bf16[4,1,128,1024]{3,2,1,0:T(8,128)(2,1)} %get-tuple-element.242.refs_0_, bf16[4,1,128,1024]{3,2,1,0:T(8,128)(2,1)} %get-tuple-element.243.refs_1_, ...), custom_call_target="tpu_custom_call" | custom-call | tf_op jit(solution)/shard_map/place_grads/pallas_call | solution.py:1534
  (193 shorter events, 80.3 us)
Async XLA Ops:
  72.5 38.0 %collective-permute-start.1 = (bf16[4,1,128,1024]{3,2,1,0:T(8,128)(2,1)}, bf16[4,1,128,1024]{3,2,1,0:T(8,128)(2,1)S(1)}, u32[]{:S(2)}, u32[]{:S(2)}) collective-permute-start(bf16[4,1,128,1024]{3,2,1,0:T(8,128)(2,1)} %get-tuple-element.146.refs_9_), channel_id=1, source_target_pairs={{0,16},{4,20},{8,24},{12,28},{16,0},{20,4},{24,8},{28,12},{1,17},{... | collective-permute-start | bytes 3145736 | tf_op jit(solution)/shard_map/ppermute | solution.py:67
  74.0 36.5 %collective-permute-start = (bf16[4,1,128,1024]{3,2,1,0:T(8,128)(2,1)}, bf16[4,1,128,1024]{3,2,1,0:T(8,128)(2,1)S(1)}, u32[]{:S(2)}, u32[]{:S(2)}) collective-permute-start(bf16[4,1,128,1024]{3,2,1,0:T(8,128)(2,1)} %get-tuple-element.146.refs_9_), channel_id=1, source_target_pairs={{0,8},{4,12},{8,0},{12,4},{16,24},{20,28},{24,16},{28,20},{1,9},{5... | collective-permute-start | bytes 3145736 | tf_op jit(solution)/shard_map/ppermute | solution.py:67
  86.3 23.0 %collective-permute-start.4 = (bf16[2,1,128,1024]{3,2,1,0:T(8,128)(2,1)S(1)}, bf16[2,1,128,1024]{3,2,1,0:T(8,128)(2,1)}, u32[]{:S(2)}, u32[]{:S(2)}) collective-permute-start(bf16[2,1,128,1024]{3,2,1,0:T(8,128)(2,1)S(1)} %maximum_bitcast_fusion.refs_12_), channel_id=1, source_target_pairs={{0,16},{4,20},{8,24},{12,28},{16,0},{20,4},{24,8},{28,12},{1,17},{... | collective-permute-start | bytes 1572872 | tf_op jit(solution)/shard_map/ppermute | solution.py:67
  87.8 22.7 %collective-permute-start.3 = (bf16[2,1,128,1024]{3,2,1,0:T(8,128)(2,1)S(1)}, bf16[2,1,128,1024]{3,2,1,0:T(8,128)(2,1)}, u32[]{:S(2)}, u32[]{:S(2)}) collective-permute-start(bf16[2,1,128,1024]{3,2,1,0:T(8,128)(2,1)S(1)} %maximum_bitcast_fusion.refs_12_), channel_id=1, source_target_pairs={{0,8},{4,12},{8,0},{12,4},{16,24},{20,28},{24,16},{28,20},{1,9},{5... | collective-permute-start | bytes 1572872 | tf_op jit(solution)/shard_map/ppermute | solution.py:67
  88.4 70.7 %collective-permute-start.5 = (bf16[2,1,128,1024]{3,2,1,0:T(8,128)(2,1)S(1)}, bf16[2,1,128,1024]{3,2,1,0:T(8,128)(2,1)S(1)}, u32[]{:S(2)}, u32[]{:S(2)}) collective-permute-start(bf16[2,1,128,1024]{3,2,1,0:T(8,128)(2,1)S(1)} %maximum_bitcast_fusion.refs_12_), channel_id=1, source_target_pairs={{0,2},{1,3},{2,0},{3,1},{4,6},{5,7},{6,4},{7,5},{8,10},{9,11},{10,... | collective-permute-start | bytes 1572872 | tf_op jit(solution)/shard_map/ppermute | solution.py:61
  227.1 21.8 %collective-permute-start.6 = (bf16[4,4,1,128,1024]{4,3,2,1,0:T(8,128)(2,1)}, bf16[4,4,1,128,1024]{4,3,2,1,0:T(8,128)(2,1)}, u32[]{:S(2)}, u32[]{:S(2)}) collective-permute-start(bf16[4,4,1,128,1024]{4,3,2,1,0:T(8,128)(2,1)} %weight_send.4), channel_id=1, source_target_pairs={{0,4},{4,0},{8,12},{12,8},{16,20},{20,16},{24,28},{28,24},{1,5},{5... | collective-permute-start | bytes 12582920 | tf_op jit(solution)/shard_map/ppermute | solution.py:61
  268.7 35.0 %collective-permute-start.7 = (bf16[4,4,1,128,1024]{4,3,2,1,0:T(8,128)(2,1)}, bf16[4,4,1,128,1024]{4,3,2,1,0:T(8,128)(2,1)}, u32[]{:S(2)}, u32[]{:S(2)}) collective-permute-start(bf16[4,4,1,128,1024]{4,3,2,1,0:T(8,128)(2,1)} %weight_send.5), channel_id=1, source_target_pairs={{0,4},{4,0},{8,12},{12,8},{16,20},{20,16},{24,28},{28,24},{1,5},{5... | collective-permute-start | bytes 12582920 | tf_op jit(solution)/shard_map/ppermute | solution.py:61
  269.2 25.3 %collective-permute-start.9 = (bf16[2,2,1,128,1024]{4,3,1,2,0:T(8,128)(2,1)}, bf16[2,2,1,128,1024]{4,3,1,2,0:T(8,128)(2,1)S(1)}, u32[]{:S(2)}, u32[]{:S(2)}) collective-permute-start(bf16[2,2,1,128,1024]{4,3,1,2,0:T(8,128)(2,1)} %bitcast.22), channel_id=1, source_target_pairs={{0,8},{4,12},{8,0},{12,4},{16,24},{20,28},{24,16},{28,20},{1,9},{5... | collective-permute-start | bytes 3145736 | tf_op jit(solution)/shard_map/ppermute | solution.py:61
  270.7 24.8 %collective-permute-start.8 = (bf16[2,2,1,128,1024]{4,3,1,2,0:T(8,128)(2,1)S(1)}, bf16[2,2,1,128,1024]{4,3,1,2,0:T(8,128)(2,1)S(1)}, u32[]{:S(2)}, u32[]{:S(2)}) collective-permute-start(bf16[2,2,1,128,1024]{4,3,1,2,0:T(8,128)(2,1)S(1)} %bitcast.173), channel_id=1, source_target_pairs={{0,16},{4,20},{8,24},{12,28},{16,0},{20,4},{24,8},{28,12},{1,17},{... | collective-permute-start | bytes 3145736 | tf_op jit(solution)/shard_map/ppermute | solution.py:61
  301.7 19.5 %collective-permute-start.10 = (bf16[2,1,128,1024]{3,2,0,1:T(8,128)(2,1)S(1)}, bf16[2,1,128,1024]{3,2,0,1:T(8,128)(2,1)}, u32[]{:S(2)}, u32[]{:S(2)}) collective-permute-start(bf16[2,1,128,1024]{3,2,0,1:T(8,128)(2,1)S(1)} %get-tuple-element.265), channel_id=1, source_target_pairs={{0,8},{4,12},{8,0},{12,4},{16,24},{20,28},{24,16},{28,20},{1,9},{5... | collective-permute-start | bytes 1572872 | tf_op jit(solution)/shard_map/ppermute | solution.py:61
  302.2 20.5 %collective-permute-start.11 = (bf16[2,1,128,1024]{3,2,0,1:T(8,128)(2,1)}, bf16[2,1,128,1024]{3,2,0,1:T(8,128)(2,1)S(1)}, u32[]{:S(2)}, u32[]{:S(2)}) collective-permute-start(bf16[2,1,128,1024]{3,2,0,1:T(8,128)(2,1)} %get-tuple-element.266), channel_id=1, source_target_pairs={{0,16},{4,20},{8,24},{12,28},{16,0},{20,4},{24,8},{28,12},{1,17},{... | collective-permute-start | bytes 1572872 | tf_op jit(solution)/shard_map/ppermute | solution.py:61
  322.9 29.9 %collective-permute-start.13 = (bf16[2,2,1,128,1024]{4,3,1,2,0:T(8,128)(2,1)}, bf16[2,2,1,128,1024]{4,3,1,2,0:T(8,128)(2,1)S(1)}, u32[]{:S(2)}, u32[]{:S(2)}) collective-permute-start(bf16[2,2,1,128,1024]{4,3,1,2,0:T(8,128)(2,1)} %bitcast.34), channel_id=1, source_target_pairs={{0,8},{4,12},{8,0},{12,4},{16,24},{20,28},{24,16},{28,20},{1,9},{5... | collective-permute-start | bytes 3145736 | tf_op jit(solution)/shard_map/ppermute | solution.py:61
  323.5 29.3 %collective-permute-start.12 = (bf16[2,2,1,128,1024]{4,3,1,2,0:T(8,128)(2,1)}, bf16[2,2,1,128,1024]{4,3,1,2,0:T(8,128)(2,1)}, u32[]{:S(2)}, u32[]{:S(2)}) collective-permute-start(bf16[2,2,1,128,1024]{4,3,1,2,0:T(8,128)(2,1)} %bitcast.31), channel_id=1, source_target_pairs={{0,16},{4,20},{8,24},{12,28},{16,0},{20,4},{24,8},{28,12},{1,17},{... | collective-permute-start | bytes 3145736 | tf_op jit(solution)/shard_map/ppermute | solution.py:61
  325.1 25.0 %collective-permute-start.14 = (bf16[2,1,128,1024]{3,2,1,0:T(8,128)(2,1)S(1)}, bf16[2,1,128,1024]{3,2,1,0:T(8,128)(2,1)}, u32[]{:S(2)}, u32[]{:S(2)}) collective-permute-start(bf16[2,1,128,1024]{3,2,1,0:T(8,128)(2,1)S(1)} %pad_maximum_fusion), channel_id=1, source_target_pairs={{0,1},{1,0},{2,3},{3,2},{4,5},{5,4},{6,7},{7,6},{8,9},{9,8},{10,11... | collective-permute-start | bytes 1572872 | tf_op jit(solution)/shard_map/ppermute | solution.py:61
  350.1 38.9 %collective-permute-start.18 = (bf16[4,2,4,128,256]{4,3,2,1,0:T(8,128)(2,1)}, bf16[4,2,4,128,256]{4,3,2,1,0:T(8,128)(2,1)}, u32[]{:S(2)}, u32[]{:S(2)}) collective-permute-start(bf16[4,2,4,128,256]{4,3,2,1,0:T(8,128)(2,1)} %weight_send.6), channel_id=1, source_target_pairs={{0,4},{4,0},{8,12},{12,8},{16,20},{20,16},{24,28},{28,24},{1,5},{5... | collective-permute-start | bytes 6291464 | tf_op jit(solution)/shard_map/ppermute | solution.py:61
  352.3 25.3 %collective-permute-start.17 = (bf16[1,128,1024]{2,1,0:T(8,128)(2,1)}, bf16[1,128,1024]{2,1,0:T(8,128)(2,1)S(1)}, u32[]{:S(2)}, u32[]{:S(2)}) collective-permute-start(bf16[1,128,1024]{2,1,0:T(8,128)(2,1)} %get-tuple-element.256), channel_id=1, source_target_pairs={{0,2},{1,3},{2,0},{3,1},{4,6},{5,7},{6,4},{7,5},{8,10},{9,11},{10,... | collective-permute-start | bytes 786440 | tf_op jit(solution)/shard_map/ppermute | solution.py:61
  355.6 22.1 %collective-permute-start.15 = (bf16[2,1,128,1024]{3,2,0,1:T(8,128)(2,1)S(1)}, bf16[2,1,128,1024]{3,2,0,1:T(8,128)(2,1)S(1)}, u32[]{:S(2)}, u32[]{:S(2)}) collective-permute-start(bf16[2,1,128,1024]{3,2,0,1:T(8,128)(2,1)S(1)} %fusion.10), channel_id=1, source_target_pairs={{0,8},{4,12},{8,0},{12,4},{16,24},{20,28},{24,16},{28,20},{1,9},{5... | collective-permute-start | bytes 1572872 | tf_op jit(solution)/shard_map/ppermute | solution.py:61
  359.7 18.2 %collective-permute-start.16 = (bf16[2,1,128,1024]{3,2,0,1:T(8,128)(2,1)}, bf16[2,1,128,1024]{3,2,0,1:T(8,128)(2,1)}, u32[]{:S(2)}, u32[]{:S(2)}) collective-permute-start(bf16[2,1,128,1024]{3,2,0,1:T(8,128)(2,1)} %fusion.11), channel_id=1, source_target_pairs={{0,16},{4,20},{8,24},{12,28},{16,0},{20,4},{24,8},{28,12},{1,17},{... | collective-permute-start | bytes 1572872 | tf_op jit(solution)/shard_map/ppermute | solution.py:61
  387.4 15.7 %collective-permute-start.19 = (bf16[4,2,4,128,256]{4,3,2,1,0:T(8,128)(2,1)}, bf16[4,2,4,128,256]{4,3,2,1,0:T(8,128)(2,1)}, u32[]{:S(2)}, u32[]{:S(2)}) collective-permute-start(bf16[4,2,4,128,256]{4,3,2,1,0:T(8,128)(2,1)} %weight_send.7), channel_id=1, source_target_pairs={{0,4},{4,0},{8,12},{12,8},{16,20},{20,16},{24,28},{28,24},{1,5},{5... | collective-permute-start | bytes 6291464 | tf_op jit(solution)/shard_map/ppermute | solution.py:61
  396.4 34.8 %collective-permute-start.22 = (bf16[2,1,4,128,256]{4,3,2,1,0:T(8,128)(2,1)}, bf16[2,1,4,128,256]{4,3,2,1,0:T(8,128)(2,1)S(1)}, u32[]{:S(2)}, u32[]{:S(2)}) collective-permute-start(bf16[2,1,4,128,256]{4,3,2,1,0:T(8,128)(2,1)} %get-tuple-element.221), channel_id=1, source_target_pairs={{0,16},{4,20},{8,24},{12,28},{16,0},{20,4},{24,8},{28,12},{1,17},{... | collective-permute-start | bytes 1572872 | tf_op jit(solution)/shard_map/ppermute | solution.py:61
  401.7 29.5 %collective-permute-start.23 = (bf16[2,1,4,128,256]{4,3,2,1,0:T(8,128)(2,1)}, bf16[2,1,4,128,256]{4,3,2,1,0:T(8,128)(2,1)S(1)}, u32[]{:S(2)}, u32[]{:S(2)}) collective-permute-start(bf16[2,1,4,128,256]{4,3,2,1,0:T(8,128)(2,1)} %get-tuple-element.232), channel_id=1, source_target_pairs={{0,8},{4,12},{8,0},{12,4},{16,24},{20,28},{24,16},{28,20},{1,9},{5... | collective-permute-start | bytes 1572872 | tf_op jit(solution)/shard_map/ppermute | solution.py:61
  410.6 20.7 %collective-permute-start.25 = (bf16[2,1,4,128,256]{4,3,2,1,0:T(8,128)(2,1)}, bf16[2,1,4,128,256]{4,3,2,1,0:T(8,128)(2,1)S(1)}, u32[]{:S(2)}, u32[]{:S(2)}) collective-permute-start(bf16[2,1,4,128,256]{4,3,2,1,0:T(8,128)(2,1)} %get-tuple-element.224), channel_id=1, source_target_pairs={{0,8},{4,12},{8,0},{12,4},{16,24},{20,28},{24,16},{28,20},{1,9},{5... | collective-permute-start | bytes 1572872 | tf_op jit(solution)/shard_map/ppermute | solution.py:61
  411.3 19.9 %collective-permute-start.24 = (bf16[2,1,4,128,256]{4,3,2,1,0:T(8,128)(2,1)}, bf16[2,1,4,128,256]{4,3,2,1,0:T(8,128)(2,1)}, u32[]{:S(2)}, u32[]{:S(2)}) collective-permute-start(bf16[2,1,4,128,256]{4,3,2,1,0:T(8,128)(2,1)} %get-tuple-element.223), channel_id=1, source_target_pairs={{0,16},{4,20},{8,24},{12,28},{16,0},{20,4},{24,8},{28,12},{1,17},{... | collective-permute-start | bytes 1572872 | tf_op jit(solution)/shard_map/ppermute | solution.py:61
  414.6 16.6 %collective-permute-start.21 = (bf16[1,128,1024]{2,1,0:T(8,128)(2,1)S(1)}, bf16[1,128,1024]{2,1,0:T(8,128)(2,1)S(1)}, u32[]{:S(2)}, u32[]{:S(2)}) collective-permute-start(bf16[1,128,1024]{2,1,0:T(8,128)(2,1)S(1)} %get-tuple-element.254), channel_id=1, source_target_pairs={{0,2},{1,3},{2,0},{3,1},{4,6},{5,7},{6,4},{7,5},{8,10},{9,11},{10,... | collective-permute-start | bytes 786440 | tf_op jit(solution)/shard_map/ppermute | solution.py:61
  (41 other events, 286.2 us)

commit v7 on v6

--- a/solution.py
+++ b/solution.py
@@ -33,7 +33,7 @@
 
 
 def cost(flops, moved):
-    return pl.CostEstimate(flops=int(flops) // 1000, bytes_accessed=int(moved) // 1000, transcendentals=0)
+    return pl.CostEstimate(flops=int(flops) // 30, bytes_accessed=int(moved) // 30, transcendentals=0)
 
 
 def dot(first, second):
@@ -588,6 +588,8 @@
             steps[k][i].start()
     piece_d[...] = low((down_sum[...] + down_more[...].astype(F32)) * slope_down[...])
     piece_i[...] = low((in_sum[...] + in_more[...].astype(F32)) * slope_in[...])
+    down.start()
+    inner.start()
     for k in range(chunks):
         for i in (3, 2, 1, 0):
             steps[k][i].wait_recv()
@@ -595,8 +597,6 @@
                 if r:
                     send_q[k, r - 1] = low(block(k, r))
                     along[k][r - 1].start()
-    down.start()
-    inner.start()
     for move in sum_data:
         move.wait()
     sums_near[0] = sums_ref[me]

time: 507 us -> 505 us (level)
  no operation moved by 1% of the time
where the time goes in v7:
time: 505 us; the launch traced here: 497 us
  Pallas kernels  415 us (82%)
  local copies, waits for them, and re-layouts  27.4 us (5%)
  starting transfers between devices  24.1 us (5%)
  other arithmetic  15.9 us (3%)
  waiting for transfers between devices  12.9 us (3%)
    pallas_call x3, Pallas kernels, run(): results = call(*args, ranges, levels, *sources)  83.3 us
    pallas_call x1, Pallas kernels, finale(): pl.pallas_call(finale_kernel, in_specs=[vmem] * len(args), out_specs=[any...  49.5 us
    pallas_call x1, Pallas kernels, first_gather(): pl.pallas_call(first_gather_kernel, in_specs=[pl.BlockSpec(memory_space=p...  46.4 us
    pallas_call x4, Pallas kernels, weight_keep(): pl.pallas_call(partial(weight_keep_kernel, len(xs), which, first_split(bi...  36.2 us
    pallas_call x2, Pallas kernels, attend_back(): pl.pallas_call(partial(attend_back_kernel, c, first), grid=(held, width /...  34.4 us
    pallas_call x4, Pallas kernels, weight_send(): pl.pallas_call(partial(weight_send_kernel, len(xs), [product[0] for produ...  31.8 us
    pallas_call x1, Pallas kernels, second_norm(): pl.pallas_call(second_norm_kernel, grid=(tokens // rows,), in_specs=[in_s...  22 us
    pallas_call x1, Pallas kernels, grad_hidden_rows(): pl.pallas_call(partial(grad_hidden_kernel, cuts), grid=(parts * cuts,), i...  21.2 us
  transfers between devices with their start and end apart: 26, of which 5 were waited for; matrix products, arithmetic and copies ran while one was open for 4% of the time, Pallas kernels for 41%

profile of v7, /device:TPU:0, one launch (start us, length us, event | category | flops | bytes accessed | tf_op | source)
XLA Modules:
  0.0 496.6 jit_solution(639534847234071200)
XLA Ops:
  8.7 16.7 %prepare.1 = (f32[8,128]{1,0:T(8,128)}, bf16[1024,1024]{1,0:T(8,128)(2,1)}, bf16[3,128,256]{2,1,0:T(8,128)(2,1)}, bf16[1,128,256]{2,1,0:T(8,128)(2,1)}, bf16[1,1...) custom-call(f32[4]{0:T(128)} %refs_5_.1, ...), custom_call_target="tpu_custom_call" | custom-call | tf_op jit(solution)/shard_map/prepare/pallas_call | solution.py:762
  25.4 46.4 %first_gather.1 = (bf16[4,4,3,128,256]{4,3,2,1,0:T(8,128)(2,1)}, bf16[4,4,3,128,256]{4,3,2,1,0:T(8,128)(2,1)}, bf16[4,16,128]{2,1,0:T(8,128)(2,1)}, bf16[4,4,1,1...) custom-call(bf16[3,128,256]{2,1,0:T(8,128)(2,1)} %get-tuple-element.135.first_ref, ...), custom_call_target="tpu_custom_call" | custom-call | tf_op jit(solution)/shard_map/first_gather/pallas_call | solution.py:509
  75.4 10.8 %qkv.1.refs_1_.refs_2_.refs_3_.q_ref.k_ref.v_ref = bf16[3,1024,1024]{2,1,0:T(8,128)(2,1)} custom-call(bf16[1024,1024]{1,0:T(8,128)(2,1)} %get-tuple-element.222.x_ref.refs_0_, bf16[4,4,3,128,256]{4,3,2,1,0:T(8,128)(2,1)} %get-tuple-element.138.near_ref.refs_6_, bf16[4,4,3,128,256]{4,3,2,1,0:T(8,128)(2,1)} %get-tuple-element.139.far_ref.refs_7_, ...), custom_call_target="tpu_custom_call" | custom-call | flops 214748368 | bytes 489335 | tf_op jit(solution)/shard_map/qkv/pallas_call | solution.py:786
  93.6 13.7 %attend.2 = (f32[1024,1024]{1,0:T(8,128)}, f32[2,128,512]{2,1,0:T(8,128)}, f32[8,128]{1,0:T(8,128)}) custom-call(s32[2,4]{1,0:T(2,128)} %reduce_window_sum.11.refs_0_.ends_ref, bf16[3,1024,1024]{2,1,0:T(8,128)(2,1)} %qkv.1.refs_1_.refs_2_.refs_3_.q_ref.k_ref.v_ref, bf16[3,1024,1024]{2,1,0:T(8,128)(2,1)} %qkv.1.refs_1_.refs_2_.refs_3_.q_ref.k_ref.v_ref, ...), custom_call_target="tpu_custom_call" | custom-call | flops 500000000 | bytes 1398101 | tf_op jit(solution)/shard_map/attend/pallas_call | solution.py:895
  111.8 30.2 %attend.3 = (f32[1024,1024]{1,0:T(8,128)}, f32[2,128,512]{2,1,0:T(8,128)}, f32[8,128]{1,0:T(8,128)}, f32[8,128]{1,0:T(8,128)}, bf16[4,4,1,128,1024]{4,3,2,1,0:T(...) custom-call(s32[2,4]{1,0:T(2,128)} %reduce_window_sum.11.refs_0_.end, ...), custom_call_target="tpu_custom_call", output_to_operand_aliasing={{0}: (6, {})} | custom-call | flops 500000000 | bytes 1398101 | tf_op jit(solution)/shard_map/attend/pallas_call | solution.py:432
  142.1 17.0 %first_norm.1 = (bf16[1024,1024]{1,0:T(8,128)(2,1)}, f32[1024,1024]{1,0:T(8,128)}, f32[1024,1024]{1,0:T(8,128)}, f32[1024,1]{1,0:T(8,128)}, f32[8,128]{1,0:T(8,128)}, /*index=5*/f32[8,128]{1,0:T(8,128)}) custom-call(f32[1024,1024]{1,0:T(8,128)} %get-tuple-element.155.refs_0_.ctx_ref, f32[8,128]{1,0:T(8,128)} %get-tuple-element.156.refs_1_.refs_7_, ...), custom_call_target="tpu_custom_call" | custom-call | flops 71582784 | bytes 699050 | tf_op jit(solution)/shard_map/first_norm/pallas_call | solution.py:432
  159.9 36.0 %hidden.1 = (bf16[1024,1024]{1,0:T(8,128)(2,1)}, f32[1024,4096]{1,0:T(8,128)}, f32[1024,4096]{1,0:T(8,128)}, f32[8,128]{1,0:T(8,128)}, f32[8,128]{1,0:T(8,128)},...) custom-call(f32[1024,1024]{1,0:T(8,128)} %get-tuple-element.159.refs_0_.normed_ref, ...), custom_call_target="tpu_custom_call" | custom-call | flops 286331168 | bytes 1747626 | tf_op jit(solution)/shard_map/hidden/pallas_call | solution.py:432
  196.0 22.0 %second_norm.1 = (bf16[1024,4096]{1,0:T(8,128)(2,1)}, bf16[1024,1024]{1,0:T(8,128)(2,1)}, f32[1024,1024]{1,0:T(8,128)}, bf16[1024,1024]{1,0:T(8,128)(2,1)}, f32[8,1024]{1,0:T(8,128)}) custom-call(s32[8]{0:T(128)} %fusion.32.order_ref, f32[1024,4096]{1,0:T(8,128)} %get-tuple-element.164.act_ref, f32[8,128]{1,0:T(8,128)} %get-tuple-element.165.level_ref.refs_10_, ...), custom_call_target="tpu_custom_call" | custom-call | flops 286331168 | bytes 2796202 | tf_op jit(solution)/shard_map/second_norm/pallas_call | solution.py:1189
  218.0 9.1 %weight_send.4 = bf16[4,4,1,128,1024]{4,3,2,1,0:T(8,128)(2,1)} custom-call(bf16[1024,1024]{1,0:T(8,128)(2,1)} %get-tuple-element.177.refs_0_.g_ref, bf16[1024,4096]{1,0:T(8,128)(2,1)} %get-tuple-element.172.refs_1_.refs_2_), custom_call_target="tpu_custom_call" | custom-call | flops 143165568 | bytes 699050 | tf_op jit(solution)/shard_map/weight_send/pallas_call | solution.py:1256
  227.6 21.2 %grad_hidden.1 = (bf16[1024,4096]{1,0:T(8,128)(2,1)}, f32[4,1024]{1,0:T(4,128)}) custom-call(s32[4]{0:T(128)} %iota_xor_fusion.order_ref, bf16[1024,1024]{1,0:T(8,128)(2,1)} %get-tuple-element.177.refs_0_.g_ref, bf16[4,2,128,1024]{3,2,1,0:T(8,128)(2,1)} %bitcast.143, bf16[4,2,128,1024]{3,2,1,0:T(8,128)(2,1)} %bitcast.145, ...), custom_call_target="tpu_custom_call" | custom-call | flops 286331168 | bytes 1188386 | tf_op jit(solution)/shard_map/grad_hidden/pallas_call | solution.py:1357
  248.9 10.6 %weight_keep.4 = (f32[2,2,1,128,1024]{4,3,2,1,0:T(8,128)}, bf16[2,2,1,128,1024]{4,3,2,1,0:T(8,128)(2,1)}, f32[2,2,1,128,1024]{4,3,2,1,0:T(8,128)}, bf16[2,2,1,128,1024]{4,3,2,1,0:T(8,128)(2,1)}) custom-call(bf16[1024,1024]{1,0:T(8,128)(2,1)} %get-tuple-element.177.refs_0_.g_ref, bf16[4,4,1,128,1024]{4,3,2,1,0:T(8,128)(2,1)} %collective-permute-done.6.refs_1_, ...), custom_call_target="tpu_custom_call" | custom-call | flops 143165568 | bytes 699050 | tf_op jit(solution)/shard_map/weight_keep/pallas_call | solution.py:1300
  259.5 9.2 %weight_send.5 = bf16[4,4,1,128,1024]{4,3,2,1,0:T(8,128)(2,1)} custom-call(bf16[1024,1024]{1,0:T(8,128)(2,1)} %get-tuple-element.188.refs_0_, bf16[1024,4096]{1,0:T(8,128)(2,1)} %get-tuple-element.193.refs_1_.g_ref.refs_2_), custom_call_target="tpu_custom_call" | custom-call | flops 143165568 | bytes 699050 | tf_op jit(solution)/shard_map/weight_send/pallas_call | solution.py:1256
  271.3 18.7 %first_back.1 = (f32[1024,1024]{1,0:T(8,128)}, bf16[1024,1024]{1,0:T(8,128)(2,1)}, f32[8,1024]{1,0:T(8,128)}) custom-call(s32[8]{0:T(128)} %fusion.32.order_ref, bf16[1024,4096]{1,0:T(8,128)(2,1)} %get-tuple-element.193.refs_1_.g_ref.refs_2_, bf16[4,4,128,1024]{3,2,1,0:T(8,128)(2,1)} %bitcast.139, bf16[4,4,128,1024]{3,2,1,0:T(8,128)(2,1)} %bitcast.141, ...), custom_call_target="tpu_custom_call" | custom-call | flops 286331168 | bytes 1258291 | tf_op jit(solution)/shard_map/first_back/pallas_call | solution.py:1393
  303.7 10.7 %weight_keep.5 = (f32[2,2,1,128,1024]{4,3,2,1,0:T(8,128)}, bf16[2,2,1,128,1024]{4,3,2,1,0:T(8,128)(2,1)}, f32[2,2,1,128,1024]{4,3,2,1,0:T(8,128)}, bf16[2,2,1,128,1024]{4,3,2,1,0:T(8,128)(2,1)}) custom-call(bf16[1024,1024]{1,0:T(8,128)(2,1)} %get-tuple-element.188.refs_0_, bf16[4,4,1,128,1024]{4,3,2,1,0:T(8,128)(2,1)} %collective-permute-done.7.refs_1_, ...), custom_call_target="tpu_custom_call" | custom-call | flops 143165568 | bytes 699050 | tf_op jit(solution)/shard_map/weight_keep/pallas_call | solution.py:1300
  314.3 6.8 %grad_context.1.g_ref = bf16[1024,1024]{1,0:T(8,128)(2,1)} custom-call(bf16[1024,1024]{1,0:T(8,128)(2,1)} %get-tuple-element.196.g_ref.refs_1_, bf16[4,4,128,256]{3,2,1,0:T(8,128)(2,1)} %bitcast.151, bf16[4,4,128,256]{3,2,1,0:T(8,128)(2,1)} %bitcast.153, f32[1024,1024]{1,0:T(8,128)} %get-tuple-element.155.refs_0_.ctx_ref, ...), custom_call_target="tpu_custom_call" | custom-call | flops 71582784 | bytes 349525 | tf_op jit(solution)/shard_map/grad_context/pallas_call | solution.py:1434
  326.3 17.1 %attend_back.2 = (bf16[1024,512]{1,0:T(8,128)(2,1)}, bf16[1024,512]{1,0:T(8,128)(2,1)}, bf16[1024,512]{1,0:T(8,128)(2,1)}, f32[8,1024]{1,0:T(8,128)}) custom-call(s32[4]{0:T(128)} %iota_xor_fusion.order_ref, s32[2,4]{1,0:T(2,128)} %reduce_window_sum.11.refs_0_.ends_ref, bf16[3,1024,1024]{2,1,0:T(8,128)(2,1)} %qkv.1.refs_1_.refs_2_.refs_3_.q_ref.k_ref.v_ref, ...), custom_call_target="tpu_custom_call" | custom-call | flops 500000000 | bytes 1747626 | tf_op jit(solution)/shard_map/attend_back/pallas_call | solution.py:965
  343.4 6.6 %weight_send.6 = bf16[4,2,4,128,256]{4,3,2,1,0:T(8,128)(2,1)} custom-call(bf16[1024,1024]{1,0:T(8,128)(2,1)} %get-tuple-element.222.x_ref.refs_0_, bf16[1024,1024]{1,0:T(8,128)(2,1)} %get-tuple-element.196.g_ref.refs_1_, bf16[1024,512]{1,0:T(8,128)(2,1)} %get-tuple-element.201.refs_2_.refs_3_.refs_0_, ...), custom_call_target="tpu_custom_call" | custom-call | flops 71582784 | bytes 699050 | tf_op jit(solution)/shard_map/weight_send/pallas_call | solution.py:1256
  360.4 17.2 %attend_back.3 = (bf16[1024,512]{1,0:T(8,128)(2,1)}, bf16[1024,512]{1,0:T(8,128)(2,1)}, bf16[1024,512]{1,0:T(8,128)(2,1)}, f32[8,1024]{1,0:T(8,128)}) custom-call(s32[4]{0:T(128)} %iota_xor_fusion.order_ref, s32[2,4]{1,0:T(2,128)} %reduce_window_sum.11.refs_0_.ends_ref, bf16[3,1024,1024]{2,1,0:T(8,128)(2,1)} %qkv.1.refs_1_.refs_2_.refs_3_.q_ref.k_ref.v_ref, ...), custom_call_target="tpu_custom_call" | custom-call | flops 500000000 | bytes 1747626 | tf_op jit(solution)/shard_map/attend_back/pallas_call | solution.py:965
  380.6 6.8 %weight_send.7 = bf16[4,2,4,128,256]{4,3,2,1,0:T(8,128)(2,1)} custom-call(bf16[1024,1024]{1,0:T(8,128)(2,1)} %get-tuple-element.222.x_ref.refs_0_, bf16[1024,1024]{1,0:T(8,128)(2,1)} %get-tuple-element.196.g_ref.refs_1_, bf16[1024,512]{1,0:T(8,128)(2,1)} %get-tuple-element.226.refs_2_.refs_3_, bf16[1024,512]{1,0:T(8,128)(2,1)} %get-tuple-element.218.refs_3_.refs_4_, ...), custom_call_target="tpu_custom_call" | custom-call | flops 71582784 | bytes 699050 | tf_op jit(solution)/shard_map/weight_send/pallas_call | solution.py:1256
  389.0 7.4 %weight_keep.6 = (f32[2,1,4,128,256]{4,3,2,1,0:T(8,128)}, bf16[2,1,4,128,256]{4,3,2,1,0:T(8,128)(2,1)}, f32[2,1,4,128,256]{4,3,2,1,0:T(8,128)}, bf16[2,1,4,128,256]{4,3,2,1,0:T(8,128)(2,1)}) custom-call(bf16[1024,1024]{1,0:T(8,128)(2,1)} %get-tuple-element.222.x_ref.refs_0_, bf16[1024,1024]{1,0:T(8,128)(2,1)} %get-tuple-element.196.g_ref.refs_1_, ...), custom_call_target="tpu_custom_call" | custom-call | flops 71582784 | bytes 699050 | tf_op jit(solution)/shard_map/weight_keep/pallas_call | solution.py:1300
  403.1 7.5 %weight_keep.7 = (f32[2,1,4,128,256]{4,3,2,1,0:T(8,128)}, bf16[2,1,4,128,256]{4,3,2,1,0:T(8,128)(2,1)}, f32[2,1,4,128,256]{4,3,2,1,0:T(8,128)}, bf16[2,1,4,128,256]{4,3,2,1,0:T(8,128)(2,1)}) custom-call(bf16[1024,1024]{1,0:T(8,128)(2,1)} %get-tuple-element.222.x_ref.refs_0_, bf16[1024,1024]{1,0:T(8,128)(2,1)} %get-tuple-element.196.g_ref.refs_1_, ...), custom_call_target="tpu_custom_call" | custom-call | flops 71582784 | bytes 699050 | tf_op jit(solution)/shard_map/weight_keep/pallas_call | solution.py:1300
  418.4 12.8 %grad_input.1 = bf16[1024,1024]{1,0:T(8,128)(2,1)} custom-call(s32[8]{0:T(128)} %fusion.32.order_ref, bf16[1024,512]{1,0:T(8,128)(2,1)} %get-tuple-element.201.refs_2_.refs_3_.refs_0_, bf16[1024,512]{1,0:T(8,128)(2,1)} %get-tuple-element.202.refs_3_.refs_4_.refs_1_, bf16[1024,512]{1,0:T(8,128)(2,1)} %get-tuple-element.203.refs_4_.refs_5_.refs_2_, ...), custom_call_target="tpu_custom_call" | custom-call | flops 214748368 | bytes 699050 | tf_op jit(solution)/shard_map/grad_input/pallas_call | solution.py:1478
  432.4 49.5 %finale.1 = (bf16[4,1,128,1024]{3,2,1,0:T(8,128)(2,1)}, bf16[4,1,128,1024]{3,2,1,0:T(8,128)(2,1)}, bf16[4,1,128,1024]{3,2,1,0:T(8,128)(2,1)}, bf16[4,1,128,1024]...) custom-call(f32[1,128,1024]{2,1,0:T(8,128)} %get-tuple-element.255.d, ...), custom_call_target="tpu_custom_call" | custom-call | tf_op jit(solution)/shard_map/finale/pallas_call | solution.py:656
  486.0 10.2 %place_grads.1 = (f32[1,1024,1024]{2,1,0:T(8,128)}, f32[3,1024,256]{2,1,0:T(8,128)}, f32[1024,1024]{1,0:T(8,128)}, f32[256,1024]{1,0:T(8,128)}) custom-call(s32[8]{0:T(128)} %fusion.32.order_ref, bf16[4,1,128,1024]{3,2,1,0:T(8,128)(2,1)} %get-tuple-element.242.refs_0_, bf16[4,1,128,1024]{3,2,1,0:T(8,128)(2,1)} %get-tuple-element.243.refs_1_, ...), custom_call_target="tpu_custom_call" | custom-call | tf_op jit(solution)/shard_map/place_grads/pallas_call | solution.py:1534
  (193 shorter events, 80.3 us)
Async XLA Ops:
  72.5 38.0 %collective-permute-start.1 = (bf16[4,1,128,1024]{3,2,1,0:T(8,128)(2,1)}, bf16[4,1,128,1024]{3,2,1,0:T(8,128)(2,1)S(1)}, u32[]{:S(2)}, u32[]{:S(2)}) collective-permute-start(bf16[4,1,128,1024]{3,2,1,0:T(8,128)(2,1)} %get-tuple-element.146.refs_9_), channel_id=1, source_target_pairs={{0,16},{4,20},{8,24},{12,28},{16,0},{20,4},{24,8},{28,12},{1,17},{... | collective-permute-start | bytes 3145736 | tf_op jit(solution)/shard_map/ppermute | solution.py:67
  74.0 36.5 %collective-permute-start = (bf16[4,1,128,1024]{3,2,1,0:T(8,128)(2,1)}, bf16[4,1,128,1024]{3,2,1,0:T(8,128)(2,1)S(1)}, u32[]{:S(2)}, u32[]{:S(2)}) collective-permute-start(bf16[4,1,128,1024]{3,2,1,0:T(8,128)(2,1)} %get-tuple-element.146.refs_9_), channel_id=1, source_target_pairs={{0,8},{4,12},{8,0},{12,4},{16,24},{20,28},{24,16},{28,20},{1,9},{5... | collective-permute-start | bytes 3145736 | tf_op jit(solution)/shard_map/ppermute | solution.py:67
  86.3 23.0 %collective-permute-start.4 = (bf16[2,1,128,1024]{3,2,1,0:T(8,128)(2,1)S(1)}, bf16[2,1,128,1024]{3,2,1,0:T(8,128)(2,1)}, u32[]{:S(2)}, u32[]{:S(2)}) collective-permute-start(bf16[2,1,128,1024]{3,2,1,0:T(8,128)(2,1)S(1)} %maximum_bitcast_fusion.refs_12_), channel_id=1, source_target_pairs={{0,16},{4,20},{8,24},{12,28},{16,0},{20,4},{24,8},{28,12},{1,17},{... | collective-permute-start | bytes 1572872 | tf_op jit(solution)/shard_map/ppermute | solution.py:67
  87.8 22.7 %collective-permute-start.3 = (bf16[2,1,128,1024]{3,2,1,0:T(8,128)(2,1)S(1)}, bf16[2,1,128,1024]{3,2,1,0:T(8,128)(2,1)}, u32[]{:S(2)}, u32[]{:S(2)}) collective-permute-start(bf16[2,1,128,1024]{3,2,1,0:T(8,128)(2,1)S(1)} %maximum_bitcast_fusion.refs_12_), channel_id=1, source_target_pairs={{0,8},{4,12},{8,0},{12,4},{16,24},{20,28},{24,16},{28,20},{1,9},{5... | collective-permute-start | bytes 1572872 | tf_op jit(solution)/shard_map/ppermute | solution.py:67
  88.4 70.7 %collective-permute-start.5 = (bf16[2,1,128,1024]{3,2,1,0:T(8,128)(2,1)S(1)}, bf16[2,1,128,1024]{3,2,1,0:T(8,128)(2,1)S(1)}, u32[]{:S(2)}, u32[]{:S(2)}) collective-permute-start(bf16[2,1,128,1024]{3,2,1,0:T(8,128)(2,1)S(1)} %maximum_bitcast_fusion.refs_12_), channel_id=1, source_target_pairs={{0,2},{1,3},{2,0},{3,1},{4,6},{5,7},{6,4},{7,5},{8,10},{9,11},{10,... | collective-permute-start | bytes 1572872 | tf_op jit(solution)/shard_map/ppermute | solution.py:61
  227.1 21.8 %collective-permute-start.6 = (bf16[4,4,1,128,1024]{4,3,2,1,0:T(8,128)(2,1)}, bf16[4,4,1,128,1024]{4,3,2,1,0:T(8,128)(2,1)}, u32[]{:S(2)}, u32[]{:S(2)}) collective-permute-start(bf16[4,4,1,128,1024]{4,3,2,1,0:T(8,128)(2,1)} %weight_send.4), channel_id=1, source_target_pairs={{0,4},{4,0},{8,12},{12,8},{16,20},{20,16},{24,28},{28,24},{1,5},{5... | collective-permute-start | bytes 12582920 | tf_op jit(solution)/shard_map/ppermute | solution.py:61
  268.7 35.0 %collective-permute-start.7 = (bf16[4,4,1,128,1024]{4,3,2,1,0:T(8,128)(2,1)}, bf16[4,4,1,128,1024]{4,3,2,1,0:T(8,128)(2,1)}, u32[]{:S(2)}, u32[]{:S(2)}) collective-permute-start(bf16[4,4,1,128,1024]{4,3,2,1,0:T(8,128)(2,1)} %weight_send.5), channel_id=1, source_target_pairs={{0,4},{4,0},{8,12},{12,8},{16,20},{20,16},{24,28},{28,24},{1,5},{5... | collective-permute-start | bytes 12582920 | tf_op jit(solution)/shard_map/ppermute | solution.py:61
  269.2 25.3 %collective-permute-start.9 = (bf16[2,2,1,128,1024]{4,3,1,2,0:T(8,128)(2,1)}, bf16[2,2,1,128,1024]{4,3,1,2,0:T(8,128)(2,1)S(1)}, u32[]{:S(2)}, u32[]{:S(2)}) collective-permute-start(bf16[2,2,1,128,1024]{4,3,1,2,0:T(8,128)(2,1)} %bitcast.22), channel_id=1, source_target_pairs={{0,8},{4,12},{8,0},{12,4},{16,24},{20,28},{24,16},{28,20},{1,9},{5... | collective-permute-start | bytes 3145736 | tf_op jit(solution)/shard_map/ppermute | solution.py:61
  270.7 24.8 %collective-permute-start.8 = (bf16[2,2,1,128,1024]{4,3,1,2,0:T(8,128)(2,1)S(1)}, bf16[2,2,1,128,1024]{4,3,1,2,0:T(8,128)(2,1)S(1)}, u32[]{:S(2)}, u32[]{:S(2)}) collective-permute-start(bf16[2,2,1,128,1024]{4,3,1,2,0:T(8,128)(2,1)S(1)} %bitcast.173), channel_id=1, source_target_pairs={{0,16},{4,20},{8,24},{12,28},{16,0},{20,4},{24,8},{28,12},{1,17},{... | collective-permute-start | bytes 3145736 | tf_op jit(solution)/shard_map/ppermute | solution.py:61
  301.7 19.5 %collective-permute-start.10 = (bf16[2,1,128,1024]{3,2,0,1:T(8,128)(2,1)S(1)}, bf16[2,1,128,1024]{3,2,0,1:T(8,128)(2,1)}, u32[]{:S(2)}, u32[]{:S(2)}) collective-permute-start(bf16[2,1,128,1024]{3,2,0,1:T(8,128)(2,1)S(1)} %get-tuple-element.265), channel_id=1, source_target_pairs={{0,8},{4,12},{8,0},{12,4},{16,24},{20,28},{24,16},{28,20},{1,9},{5... | collective-permute-start | bytes 1572872 | tf_op jit(solution)/shard_map/ppermute | solution.py:61
  302.2 20.5 %collective-permute-start.11 = (bf16[2,1,128,1024]{3,2,0,1:T(8,128)(2,1)}, bf16[2,1,128,1024]{3,2,0,1:T(8,128)(2,1)S(1)}, u32[]{:S(2)}, u32[]{:S(2)}) collective-permute-start(bf16[2,1,128,1024]{3,2,0,1:T(8,128)(2,1)} %get-tuple-element.266), channel_id=1, source_target_pairs={{0,16},{4,20},{8,24},{12,28},{16,0},{20,4},{24,8},{28,12},{1,17},{... | collective-permute-start | bytes 1572872 | tf_op jit(solution)/shard_map/ppermute | solution.py:61
  322.9 29.9 %collective-permute-start.13 = (bf16[2,2,1,128,1024]{4,3,1,2,0:T(8,128)(2,1)}, bf16[2,2,1,128,1024]{4,3,1,2,0:T(8,128)(2,1)S(1)}, u32[]{:S(2)}, u32[]{:S(2)}) collective-permute-start(bf16[2,2,1,128,1024]{4,3,1,2,0:T(8,128)(2,1)} %bitcast.34), channel_id=1, source_target_pairs={{0,8},{4,12},{8,0},{12,4},{16,24},{20,28},{24,16},{28,20},{1,9},{5... | collective-permute-start | bytes 3145736 | tf_op jit(solution)/shard_map/ppermute | solution.py:61
  323.5 29.3 %collective-permute-start.12 = (bf16[2,2,1,128,1024]{4,3,1,2,0:T(8,128)(2,1)}, bf16[2,2,1,128,1024]{4,3,1,2,0:T(8,128)(2,1)}, u32[]{:S(2)}, u32[]{:S(2)}) collective-permute-start(bf16[2,2,1,128,1024]{4,3,1,2,0:T(8,128)(2,1)} %bitcast.31), channel_id=1, source_target_pairs={{0,16},{4,20},{8,24},{12,28},{16,0},{20,4},{24,8},{28,12},{1,17},{... | collective-permute-start | bytes 3145736 | tf_op jit(solution)/shard_map/ppermute | solution.py:61
  325.1 25.0 %collective-permute-start.14 = (bf16[2,1,128,1024]{3,2,1,0:T(8,128)(2,1)S(1)}, bf16[2,1,128,1024]{3,2,1,0:T(8,128)(2,1)}, u32[]{:S(2)}, u32[]{:S(2)}) collective-permute-start(bf16[2,1,128,1024]{3,2,1,0:T(8,128)(2,1)S(1)} %pad_maximum_fusion), channel_id=1, source_target_pairs={{0,1},{1,0},{2,3},{3,2},{4,5},{5,4},{6,7},{7,6},{8,9},{9,8},{10,11... | collective-permute-start | bytes 1572872 | tf_op jit(solution)/shard_map/ppermute | solution.py:61
  350.1 38.9 %collective-permute-start.18 = (bf16[4,2,4,128,256]{4,3,2,1,0:T(8,128)(2,1)}, bf16[4,2,4,128,256]{4,3,2,1,0:T(8,128)(2,1)}, u32[]{:S(2)}, u32[]{:S(2)}) collective-permute-start(bf16[4,2,4,128,256]{4,3,2,1,0:T(8,128)(2,1)} %weight_send.6), channel_id=1, source_target_pairs={{0,4},{4,0},{8,12},{12,8},{16,20},{20,16},{24,28},{28,24},{1,5},{5... | collective-permute-start | bytes 6291464 | tf_op jit(solution)/shard_map/ppermute | solution.py:61
  352.3 25.3 %collective-permute-start.17 = (bf16[1,128,1024]{2,1,0:T(8,128)(2,1)}, bf16[1,128,1024]{2,1,0:T(8,128)(2,1)S(1)}, u32[]{:S(2)}, u32[]{:S(2)}) collective-permute-start(bf16[1,128,1024]{2,1,0:T(8,128)(2,1)} %get-tuple-element.256), channel_id=1, source_target_pairs={{0,2},{1,3},{2,0},{3,1},{4,6},{5,7},{6,4},{7,5},{8,10},{9,11},{10,... | collective-permute-start | bytes 786440 | tf_op jit(solution)/shard_map/ppermute | solution.py:61
  355.6 22.1 %collective-permute-start.15 = (bf16[2,1,128,1024]{3,2,0,1:T(8,128)(2,1)S(1)}, bf16[2,1,128,1024]{3,2,0,1:T(8,128)(2,1)S(1)}, u32[]{:S(2)}, u32[]{:S(2)}) collective-permute-start(bf16[2,1,128,1024]{3,2,0,1:T(8,128)(2,1)S(1)} %fusion.10), channel_id=1, source_target_pairs={{0,8},{4,12},{8,0},{12,4},{16,24},{20,28},{24,16},{28,20},{1,9},{5... | collective-permute-start | bytes 1572872 | tf_op jit(solution)/shard_map/ppermute | solution.py:61
  359.7 18.2 %collective-permute-start.16 = (bf16[2,1,128,1024]{3,2,0,1:T(8,128)(2,1)}, bf16[2,1,128,1024]{3,2,0,1:T(8,128)(2,1)}, u32[]{:S(2)}, u32[]{:S(2)}) collective-permute-start(bf16[2,1,128,1024]{3,2,0,1:T(8,128)(2,1)} %fusion.11), channel_id=1, source_target_pairs={{0,16},{4,20},{8,24},{12,28},{16,0},{20,4},{24,8},{28,12},{1,17},{... | collective-permute-start | bytes 1572872 | tf_op jit(solution)/shard_map/ppermute | solution.py:61
  387.4 15.7 %collective-permute-start.19 = (bf16[4,2,4,128,256]{4,3,2,1,0:T(8,128)(2,1)}, bf16[4,2,4,128,256]{4,3,2,1,0:T(8,128)(2,1)}, u32[]{:S(2)}, u32[]{:S(2)}) collective-permute-start(bf16[4,2,4,128,256]{4,3,2,1,0:T(8,128)(2,1)} %weight_send.7), channel_id=1, source_target_pairs={{0,4},{4,0},{8,12},{12,8},{16,20},{20,16},{24,28},{28,24},{1,5},{5... | collective-permute-start | bytes 6291464 | tf_op jit(solution)/shard_map/ppermute | solution.py:61
  396.4 34.8 %collective-permute-start.22 = (bf16[2,1,4,128,256]{4,3,2,1,0:T(8,128)(2,1)}, bf16[2,1,4,128,256]{4,3,2,1,0:T(8,128)(2,1)S(1)}, u32[]{:S(2)}, u32[]{:S(2)}) collective-permute-start(bf16[2,1,4,128,256]{4,3,2,1,0:T(8,128)(2,1)} %get-tuple-element.221), channel_id=1, source_target_pairs={{0,16},{4,20},{8,24},{12,28},{16,0},{20,4},{24,8},{28,12},{1,17},{... | collective-permute-start | bytes 1572872 | tf_op jit(solution)/shard_map/ppermute | solution.py:61
  401.7 29.5 %collective-permute-start.23 = (bf16[2,1,4,128,256]{4,3,2,1,0:T(8,128)(2,1)}, bf16[2,1,4,128,256]{4,3,2,1,0:T(8,128)(2,1)S(1)}, u32[]{:S(2)}, u32[]{:S(2)}) collective-permute-start(bf16[2,1,4,128,256]{4,3,2,1,0:T(8,128)(2,1)} %get-tuple-element.232), channel_id=1, source_target_pairs={{0,8},{4,12},{8,0},{12,4},{16,24},{20,28},{24,16},{28,20},{1,9},{5... | collective-permute-start | bytes 1572872 | tf_op jit(solution)/shard_map/ppermute | solution.py:61
  410.6 20.7 %collective-permute-start.25 = (bf16[2,1,4,128,256]{4,3,2,1,0:T(8,128)(2,1)}, bf16[2,1,4,128,256]{4,3,2,1,0:T(8,128)(2,1)S(1)}, u32[]{:S(2)}, u32[]{:S(2)}) collective-permute-start(bf16[2,1,4,128,256]{4,3,2,1,0:T(8,128)(2,1)} %get-tuple-element.224), channel_id=1, source_target_pairs={{0,8},{4,12},{8,0},{12,4},{16,24},{20,28},{24,16},{28,20},{1,9},{5... | collective-permute-start | bytes 1572872 | tf_op jit(solution)/shard_map/ppermute | solution.py:61
  411.3 19.9 %collective-permute-start.24 = (bf16[2,1,4,128,256]{4,3,2,1,0:T(8,128)(2,1)}, bf16[2,1,4,128,256]{4,3,2,1,0:T(8,128)(2,1)}, u32[]{:S(2)}, u32[]{:S(2)}) collective-permute-start(bf16[2,1,4,128,256]{4,3,2,1,0:T(8,128)(2,1)} %get-tuple-element.223), channel_id=1, source_target_pairs={{0,16},{4,20},{8,24},{12,28},{16,0},{20,4},{24,8},{28,12},{1,17},{... | collective-permute-start | bytes 1572872 | tf_op jit(solution)/shard_map/ppermute | solution.py:61
  414.6 16.6 %collective-permute-start.21 = (bf16[1,128,1024]{2,1,0:T(8,128)(2,1)S(1)}, bf16[1,128,1024]{2,1,0:T(8,128)(2,1)S(1)}, u32[]{:S(2)}, u32[]{:S(2)}) collective-permute-start(bf16[1,128,1024]{2,1,0:T(8,128)(2,1)S(1)} %get-tuple-element.254), channel_id=1, source_target_pairs={{0,2},{1,3},{2,0},{3,1},{4,6},{5,7},{6,4},{7,5},{8,10},{9,11},{10,... | collective-permute-start | bytes 786440 | tf_op jit(solution)/shard_map/ppermute | solution.py:61
  (41 other events, 286.2 us)
